TPU v7x, 32 devices: a whole 2x2x4 slice. The times are simulated.
32 devices in a mesh: groups: 2 (over x), ctx: 16 (over z, y, core).
Axes of the slice: x: 2, y: 2, z: 4, core: 2. Of those that a mesh axis runs over, the one named last changes fastest.
Arguments:
- features: bfloat16 [64, 16, 24, 192], P(('groups', 'ctx')), parts along dimension 0, may hold values from -6 to 6
- clip_ids: int32 [64], P('groups'), parts along dimension 0, may hold values from 0 to 7, never falling along the last dimension, each value on 1 to 8 neighbouring positions
- gain_first: float32 [192], replicated, may hold values from 0.1 to 1.9
- weight_first: bfloat16 [27, 192, 192], P(None, None, 'ctx'), may hold values from -0.078125 to 0.078125
- gain_second: float32 [192], replicated, may hold values from 0.1 to 1.9
- weight_second: bfloat16 [27, 192, 192], P(None, None, 'ctx'), may hold values from -0.078125 to 0.078125
- gain_third: float32 [192], replicated, may hold values from 0.1 to 1.9
- weight_out: bfloat16 [27, 192, 16], replicated, may hold values from -0.078125 to 0.078125
- embed_weight: bfloat16 [64, 3072], replicated, may hold values from -0.75 to 0.75
- shift_mod: float32 [3072], replicated, may hold values from -3 to 3
- scale_mod: float32 [3072], replicated, may hold values from -0.5 to 0.5
- token_order: int32 [6144], P(('groups', 'ctx')), parts along dimension 0, may hold values from 0 to 3071, each once
Outputs:
- tokens_out: bfloat16 [6144, 3072], P(('groups', 'ctx')), parts along dimension 0
There are 2 independent parts, one for each index of `groups`. A program takes and returns all parts, laid end to end along the dimension named above; an argument that names none is the same for every part. Nothing has to cross between parts.
Inputs may be any that keep to these rules, and one draw needn't show every extreme that they name: `clip_ids`: clip ids never fall along the frames and start at 0; each clip spans 1 to 8 frames, and some clip spans exactly 8. `token_order`: each patch index appears exactly once.
All inputs are finite; a program needn't handle non-finite values.
Results may differ from a plain program's by a relative error of at most 0.014.
Values may be sent and summed in bfloat16 or wider, within the bound.
No kernel may reach another device: no remote copies, remote signals or barrier semaphores. Data moves between devices by JAX's collectives and lax.ppermute only.
A program may use at most 128 MiB of HBM per device.

v0:
```python
import jax
import jax.numpy as jnp
from jax import lax
from jax.sharding import PartitionSpec as P


def shifted_2(value, axis, steps):
    count = lax.axis_size(axis)
    first, last = (max(0, -steps), min(count, count - steps))
    return lax.ppermute(value, axis, [(source, source + steps) for source in range(first, last)])


def clip_masks(clip_ids, device, frames):
    positions = device * frames - 2 + jnp.arange(frames + 2, dtype=jnp.int32)
    looked = jnp.where(positions >= 0, clip_ids[jnp.maximum(positions, 0)], -1)
    current = looked[2:]
    return jnp.stack([looked[frame_tap : frame_tap + frames] == current for frame_tap in range(3)])


def conv_block(extended, kept_mask, weight):
    frames = kept_mask.shape[1]
    height, breadth, channels = (extended.shape[1], extended.shape[2], extended.shape[3])
    padded = jnp.pad(extended, ((0, 0), (1, 1), (1, 1), (0, 0)))
    summed = jnp.zeros((frames * height * breadth, weight.shape[2]), jnp.float32)
    for frame_tap in range(3):
        source = jnp.where(
            kept_mask[frame_tap][:, None, None, None],
            padded[frame_tap : frame_tap + frames],
            jnp.zeros((), extended.dtype),
        )
        for row_tap in range(3):
            for col_tap in range(3):
                shifted = source[
                    :, row_tap : row_tap + height, col_tap : col_tap + breadth, :
                ].reshape(-1, channels)
                summed = summed + jnp.dot(
                    shifted,
                    weight[frame_tap * 9 + row_tap * 3 + col_tap],
                    preferred_element_type=jnp.float32,
                )
    return summed


def with_rim(values):
    rim = shifted_2(values, "ctx", 1)
    return jnp.concatenate([rim, values], axis=0)


def conv_columns(extended, kept_mask, weight_shard):
    return conv_block(extended, kept_mask, lax.all_gather(weight_shard, "ctx", axis=2, tiled=True))


def rms_silu(values, gain_vector):
    values = values.astype(jnp.float32)
    normed = (
        values * lax.rsqrt(jnp.mean(values * values, axis=-1, keepdims=True) + 1e-06) * gain_vector
    )
    return jax.nn.silu(normed).astype(jnp.bfloat16)


def to_patches(latents):
    frames, height, breadth, latent_depth = latents.shape
    grid = latents.reshape(frames, height // 2, 2, breadth // 2, 2, latent_depth).transpose(
        0, 1, 3, 2, 4, 5
    )
    return grid.reshape(frames * (height // 2) * (breadth // 2), 4 * latent_depth)


def modulate(ordered, embed_weight, shift_mod, scale_mod):
    embedded = jnp.dot(ordered, embed_weight, preferred_element_type=jnp.float32)
    center = jnp.mean(embedded, axis=-1, keepdims=True)
    centered = embedded - center
    variance = jnp.mean(centered * centered, axis=-1, keepdims=True)
    normed = centered * lax.rsqrt(variance + 1e-06)
    return (normed * (1.0 + scale_mod) + shift_mod).astype(jnp.bfloat16)


def body(
    features,
    clip_ids,
    gain_first,
    weight_first,
    gain_second,
    weight_second,
    gain_third,
    weight_out,
    embed_weight,
    shift_mod,
    scale_mod,
    token_order,
):
    frames, height, breadth, channels = features.shape
    kept_mask = clip_masks(clip_ids, lax.axis_index("ctx"), frames)

    def convolve(values, weight_shard):
        extended = with_rim(values)
        summed = conv_columns(extended, kept_mask, weight_shard)
        return summed.reshape(frames, height, breadth, channels)

    first_in = rms_silu(features, gain_first)
    first_out = convolve(first_in, weight_first).astype(jnp.bfloat16)
    second_in = rms_silu(first_out, gain_second)
    block_out = (features.astype(jnp.float32) + convolve(second_in, weight_second)).astype(
        jnp.bfloat16
    )
    head_in = rms_silu(block_out, gain_third)
    latents = (
        conv_block(with_rim(head_in), kept_mask, weight_out)
        .reshape(frames, height, breadth, -1)
        .astype(jnp.bfloat16)
    )
    patches = to_patches(latents)
    all_patches = lax.all_gather(patches, "ctx", axis=0, tiled=True)
    ordered = all_patches[token_order]
    return modulate(ordered, embed_weight, shift_mod, scale_mod)


def solution(mesh):
    in_specs = (
        P(("groups", "ctx"), None, None, None),
        P("groups"),
        P(),
        P(None, None, "ctx"),
        P(),
        P(None, None, "ctx"),
        P(),
        P(),
        P(),
        P(),
        P(),
        P(("groups", "ctx")),
    )
    out_specs = P(("groups", "ctx"), None)
    return jax.shard_map(body, mesh=mesh, in_specs=in_specs, out_specs=out_specs, check_vma=False)
```

profile of v0, /device:TPU:0, one launch (start us, length us, event | category | flops | bytes accessed | tf_op | source)
XLA Modules:
  0.0 207.4 jit_solution(17634757845780341969)
XLA Ops:
  7.3 1.2 fusion.31
  8.5 1.3 fusion.38
  9.8 2.4 %collective-permute-start = (bf16[2,16,24,192]{3,2,1,0:T(8,128)(2,1)S(1)}, bf16[2,16,24,192]{3,2,1,0:T(8,128)(2,1)S(1)}, u32[]{:S(2)}, u32[]{:S(2)}) collective-permute-start(bf16[2,16,24,192]{3,2,1,0:T(8,128)(2,1)S(1)} %fusion.38), channel_id=1, source_target_pairs={{0,1},{1,2},{2,3},{3,4},{4,5},{5,6},{6,7},{7,8},{8,9},{9,10},{10,1... | collective-permute-start | bytes 884744 | tf_op jit(solution)/shard_map/ppermute | solution.py:10
  12.3 1.3 gather_fusion
  13.6 1.2 compare_select_fusion
  16.1 2.1 %fusion.168 = (bf16[2,16,24,192]{3,2,1,0:T(8,128)(2,1)}, bf16[2,16,24,192]{3,2,1,0:T(8,128)(2,1)}, bf16[2,16,24,192]{3,2,1,0:T(8,128)(2,1)}, bf16[2,16,24,192]{3...) fusion(bf16[4,18,26,192]{3,2,1,0:T(8,128)(2,1)S(1)} %fusion.14), kind=kLoop, calls=%fused_computation.275 | loop fusion | bytes 4718592 | tf_op jit(solution)/shard_map/slice | solution.py:33
  18.4 3.3 %fusion.173 = (bf16[2,16,24,192]{3,2,1,0:T(8,128)(2,1)}, bf16[2,16,24,192]{3,2,1,0:T(8,128)(2,1)}, bf16[2,16,24,192]{3,2,1,0:T(8,128)(2,1)}, bf16[2,16,24,192]{3...) fusion(bf16[2,18,26,192]{3,2,1,0:T(8,128)(2,1)S(1)} %get-tuple-, ...), kind=kLoop, calls=%fused_computation.280 | loop fusion | bytes 10616832 | tf_op jit(solution)/shard_map/slice | solution.py:33
  21.8 35.8 %all-gather.4.cloned.1.call-done = bf16[27,192,192]{1,0,2:T(8,128)(2,1)} async-done(((bf16[27,192,12]{1,0,2:T(8,128)(2,1)}), bf16[27,192,192]{1,0,2:T(8,128)(2,1)}) %all-gather.4.cloned.1.call-update) | async-done | bytes 1990672 | tf_op jit(solution)/shard_map/all_gather | solution.py:50
  57.6 7.2 %fusion.165 = (bf16[1,192,192]{1,0,2:T(2,128)(2,1)}, bf16[1,192,192]{1,0,2:T(2,128)(2,1)}, bf16[1,192,192]{1,0,2:T(2,128)(2,1)}, bf16[1,192,192]{1,0,2:T(2,128)(...) fusion(bf16[27,192,192]{1,0,2:T(8,128)(2,1)} %all-gather.4.clon, ...), kind=kLoop, calls=%fused_computation.272 | loop fusion | bytes 1179648 | tf_op jit(solution)/shard_map/slice | solution.py:38
  64.7 1.7 copy.83
  66.4 1.7 copy.84
  68.1 1.7 copy.85
  69.8 1.7 copy.86
  71.5 1.7 copy.87
  73.2 1.7 copy.88
  74.8 1.7 copy.89
  76.5 1.7 copy.90
  78.2 4.9 %fusion.164 = (bf16[1,192,192]{1,0,2:T(2,128)(2,1)}, bf16[1,192,192]{1,0,2:T(2,128)(2,1)}, bf16[1,192,192]{1,0,2:T(2,128)(2,1)}, bf16[1,192,192]{1,0,2:T(2,128)(...) fusion(bf16[27,192,192]{1,0,2:T(8,128)(2,1)S(1)} %copy-done.2), kind=kLoop, calls=%fused_computation.271 | loop fusion | bytes 2801664 | tf_op jit(solution)/shard_map/slice | solution.py:38
  83.1 1.1 copy.91
  84.3 1.1 copy.92
  85.3 1.0 copy.93
  86.4 1.0 copy.94
  87.4 1.0 copy.95
  88.5 1.0 copy.96
  89.6 1.7 copy.97
  91.3 1.3 fusion.97
  99.1 1.7 copy.100
  100.9 0.8 copy.101
  102.9 1.3 convolution_add_fusion.37
  108.7 2.9 %collective-permute-start.1 = (bf16[2,16,24,192]{3,2,1,0:T(8,128)(2,1)S(1)}, bf16[2,16,24,192]{3,2,1,0:T(8,128)(2,1)}, u32[]{:S(2)}, u32[]{:S(2)}) collective-permute-start(bf16[2,16,24,192]{3,2,1,0:T(8,128)(2,1)S(1)} %multiply_convert_fusion), channel_id=1, source_target_pairs={{0,1},{1,2},{2,3},{3,4},{4,5},{5,6},{6,7},{7,8},{8,9},{9,10},{10,1... | collective-permute-start | bytes 884744 | tf_op jit(solution)/shard_map/ppermute | solution.py:10
  111.6 9.6 %fusion.162 = (bf16[1,192,192]{1,0,2:T(2,128)(2,1)S(1)}, bf16[1,192,192]{1,0,2:T(2,128)(2,1)S(1)}, bf16[1,192,192]{1,0,2:T(2,128)(2,1)S(1)}, bf16[1,192,192]{1,0...) fusion(bf16[27,192,192]{1,0,2:T(8,128)(2,1)} %all-gather.6.clon, ...), kind=kLoop, calls=%fused_computation.269 | loop fusion | bytes 2801664 | tf_op jit(solution)/shard_map/slice | solution.py:38
  121.2 1.4 fusion.163
  124.9 0.8 copy.113
  128.8 1.7 copy.118
  130.5 1.7 copy.119
  132.2 1.7 copy.120
  133.9 1.7 copy.121
  135.6 1.7 copy.122
  137.2 1.7 copy.123
  138.9 1.7 copy.124
  140.6 1.7 copy.125
  145.1 1.5 fusion.13
  146.7 0.8 slice_select_fusion.2
  158.6 2.0 collective-permute-start.2
  160.8 0.8 collective-permute-done.2
  170.9 26.0 %all-gather = bf16[16,192,64]{1,2,0:T(8,128)(2,1)S(1)} all-gather(bf16[1,192,64]{1,2,0:T(8,128)(2,1)S(1)} %reshape.421), channel_id=1, replica_groups=mesh['groups'=2,'ctx'=16] {'ctx'}, dimensions={0}, use_global_device_ids=true | all-gather | bytes 417792 | tf_op jit(solution)/shard_map/all_gather | solution.py:113
  197.3 0.8 gather_fusion.1
  199.1 1.5 add_convert_fusion
  (325 shorter events, 43.8 us)
Async XLA Ops:
  6.5 191.6 %copy-start = (bf16[64,3072]{1,0:T(8,128)(2,1)S(1)}, bf16[64,3072]{1,0:T(8,128)(2,1)}, u32[]{:S(2)}) copy-start(bf16[64,3072]{1,0:T(8,128)(2,1)} %param.20) | copy-start | bytes 1179652
  6.5 51.0 %all-gather.4.cloned.1.call-start = ((), (), s32[]{:S(2)}) async-start(), calls=%async_computation | async-start | bytes 3342336 | tf_op jit(solution)/shard_map/all_gather | solution.py:50
  7.3 104.3 %all-gather.6.cloned.1.call-start = ((), (), s32[]{:S(2)}) async-start(), calls=%async_computation.1 | async-start | bytes 3342336 | tf_op jit(solution)/shard_map/all_gather | solution.py:50
  9.8 8.4 %copy-start.4 = (bf16[2,16,24,192]{3,2,1,0:T(8,128)(2,1)}, bf16[2,16,24,192]{3,2,1,0:T(8,128)(2,1)S(1)}, u32[]{:S(2)}) copy-start(bf16[2,16,24,192]{3,2,1,0:T(8,128)(2,1)S(1)} %fusion.38) | copy-start | bytes 884740
  9.8 5.8 %collective-permute-start = (bf16[2,16,24,192]{3,2,1,0:T(8,128)(2,1)S(1)}, bf16[2,16,24,192]{3,2,1,0:T(8,128)(2,1)S(1)}, u32[]{:S(2)}, u32[]{:S(2)}) collective-permute-start(bf16[2,16,24,192]{3,2,1,0:T(8,128)(2,1)S(1)} %fusion.38), channel_id=1, source_target_pairs={{0,1},{1,2},{2,3},{3,4},{4,5},{5,6},{6,7},{7,8},{8,9},{9,10},{10,1... | collective-permute-start | bytes 884744 | tf_op jit(solution)/shard_map/ppermute | solution.py:10
  14.9 3.4 %copy-start.81 = (pred[2]{0:T(512)(128)(4,1)}, pred[2]{0:T(512)(128)(4,1)S(1)}, u32[]{:S(2)}) copy-start(pred[2]{0:T(512)(128)(4,1)S(1)} %get-tuple-element.143) | copy-start | bytes 10
  14.9 3.4 %copy-start.83 = (pred[2]{0:T(512)(128)(4,1)}, pred[2]{0:T(512)(128)(4,1)S(1)}, u32[]{:S(2)}) copy-start(pred[2]{0:T(512)(128)(4,1)S(1)} %get-tuple-element.144) | copy-start | bytes 10
  57.6 20.6 %copy-start.2 = (bf16[27,192,192]{1,0,2:T(8,128)(2,1)S(1)}, bf16[27,192,192]{1,0,2:T(8,128)(2,1)}, u32[]{:S(2)}) copy-start(bf16[27,192,192]{1,0,2:T(8,128)(2,1)} %all-gather.4.cloned.1.call-done) | copy-start | bytes 5971972
  83.1 9.5 %copy-start.22 = (bf16[2,16,24,192]{3,2,1,0:T(8,128)(2,1)S(1)}, bf16[2,16,24,192]{3,2,1,0:T(8,128)(2,1)}, u32[]{:S(2)}) copy-start(bf16[2,16,24,192]{3,2,1,0:T(8,128)(2,1)} %get-tuple-element.150) | copy-start | bytes 884740
  83.1 9.5 %copy-start.75 = (bf16[1,192,192]{2,1,0:T(8,128)(2,1)S(1)}, bf16[1,192,192]{2,1,0:T(8,128)(2,1)}, u32[]{:S(2)}) copy-start(bf16[1,192,192]{2,1,0:T(8,128)(2,1)} %copy.84) | copy-start | bytes 221188
  83.1 9.8 %copy-start.21 = (bf16[2,16,24,192]{3,2,1,0:T(8,128)(2,1)S(1)}, bf16[2,16,24,192]{3,2,1,0:T(8,128)(2,1)}, u32[]{:S(2)}) copy-start(bf16[2,16,24,192]{3,2,1,0:T(8,128)(2,1)} %get-tuple-element.151) | copy-start | bytes 884740
  83.1 9.8 %copy-start.74 = (bf16[1,192,192]{2,1,0:T(8,128)(2,1)S(1)}, bf16[1,192,192]{2,1,0:T(8,128)(2,1)}, u32[]{:S(2)}) copy-start(bf16[1,192,192]{2,1,0:T(8,128)(2,1)} %copy.85) | copy-start | bytes 221188
  89.5 3.8 %copy-start.20 = (bf16[2,16,24,192]{3,2,1,0:T(8,128)(2,1)S(1)}, bf16[2,16,24,192]{3,2,1,0:T(8,128)(2,1)}, u32[]{:S(2)}) copy-start(bf16[2,16,24,192]{3,2,1,0:T(8,128)(2,1)} %get-tuple-element.152) | copy-start | bytes 884740
  89.5 3.8 %copy-start.72 = (bf16[1,192,192]{2,1,0:T(8,128)(2,1)S(1)}, bf16[1,192,192]{2,1,0:T(8,128)(2,1)}, u32[]{:S(2)}) copy-start(bf16[1,192,192]{2,1,0:T(8,128)(2,1)} %copy.86) | copy-start | bytes 221188
  96.5 1.8 copy-start.40
  96.8 4.0 %copy-start.39 = (bf16[1,192,192]{1,0,2:T(2,128)(2,1)S(1)}, bf16[1,192,192]{1,0,2:T(2,128)(2,1)}, u32[]{:S(2)}) copy-start(bf16[1,192,192]{1,0,2:T(2,128)(2,1)} %get-tuple-element.40) | copy-start | bytes 221188
  96.9 4.8 %copy-start.38 = (bf16[1,192,192]{1,0,2:T(2,128)(2,1)S(1)}, bf16[1,192,192]{1,0,2:T(2,128)(2,1)}, u32[]{:S(2)}) copy-start(bf16[1,192,192]{1,0,2:T(2,128)(2,1)} %get-tuple-element.39) | copy-start | bytes 221188
  96.9 4.9 %copy-start.37 = (bf16[1,192,192]{1,0,2:T(2,128)(2,1)S(1)}, bf16[1,192,192]{1,0,2:T(2,128)(2,1)}, u32[]{:S(2)}) copy-start(bf16[1,192,192]{1,0,2:T(2,128)(2,1)} %get-tuple-element.38) | copy-start | bytes 221188
  96.9 5.1 %copy-start.36 = (bf16[1,192,192]{1,0,2:T(2,128)(2,1)S(1)}, bf16[1,192,192]{1,0,2:T(2,128)(2,1)}, u32[]{:S(2)}) copy-start(bf16[1,192,192]{1,0,2:T(2,128)(2,1)} %get-tuple-element.37) | copy-start | bytes 221188
  96.9 5.2 %copy-start.35 = (bf16[1,192,192]{1,0,2:T(2,128)(2,1)S(1)}, bf16[1,192,192]{1,0,2:T(2,128)(2,1)}, u32[]{:S(2)}) copy-start(bf16[1,192,192]{1,0,2:T(2,128)(2,1)} %get-tuple-element.36) | copy-start | bytes 221188
  97.2 5.1 %copy-start.34 = (bf16[1,192,192]{1,0,2:T(2,128)(2,1)S(1)}, bf16[1,192,192]{1,0,2:T(2,128)(2,1)}, u32[]{:S(2)}) copy-start(bf16[1,192,192]{1,0,2:T(2,128)(2,1)} %get-tuple-element.35) | copy-start | bytes 221188
  97.2 5.2 %copy-start.33 = (bf16[1,192,192]{1,0,2:T(2,128)(2,1)S(1)}, bf16[1,192,192]{1,0,2:T(2,128)(2,1)}, u32[]{:S(2)}) copy-start(bf16[1,192,192]{1,0,2:T(2,128)(2,1)} %get-tuple-element.34) | copy-start | bytes 221188
  97.2 5.4 %copy-start.32 = (bf16[1,192,192]{1,0,2:T(2,128)(2,1)S(1)}, bf16[1,192,192]{1,0,2:T(2,128)(2,1)}, u32[]{:S(2)}) copy-start(bf16[1,192,192]{1,0,2:T(2,128)(2,1)} %get-tuple-element.33) | copy-start | bytes 221188
  97.3 5.5 %copy-start.31 = (bf16[1,192,192]{1,0,2:T(2,128)(2,1)S(1)}, bf16[1,192,192]{1,0,2:T(2,128)(2,1)}, u32[]{:S(2)}) copy-start(bf16[1,192,192]{1,0,2:T(2,128)(2,1)} %get-tuple-element.32) | copy-start | bytes 221188
  97.3 5.6 %copy-start.8 = (bf16[2,16,24,192]{3,2,1,0:T(8,128)(2,1)S(1)}, bf16[2,16,24,192]{3,2,1,0:T(8,128)(2,1)}, u32[]{:S(2)}) copy-start(bf16[2,16,24,192]{3,2,1,0:T(8,128)(2,1)} %get-tuple-element.127) | copy-start | bytes 884740
  99.1 5.0 %copy-start.7 = (bf16[2,16,24,192]{3,2,1,0:T(8,128)(2,1)S(1)}, bf16[2,16,24,192]{3,2,1,0:T(8,128)(2,1)}, u32[]{:S(2)}) copy-start(bf16[2,16,24,192]{3,2,1,0:T(8,128)(2,1)} %get-tuple-element.126) | copy-start | bytes 884740
  102.1 2.4 %copy-start.6 = (bf16[2,16,24,192]{3,2,1,0:T(8,128)(2,1)S(1)}, bf16[2,16,24,192]{3,2,1,0:T(8,128)(2,1)}, u32[]{:S(2)}) copy-start(bf16[2,16,24,192]{3,2,1,0:T(8,128)(2,1)} %get-tuple-element.125) | copy-start | bytes 884740
  102.3 2.2 %copy-start.77 = (bf16[1,192,192]{2,1,0:T(8,128)(2,1)S(1)}, bf16[1,192,192]{2,1,0:T(8,128)(2,1)}, u32[]{:S(2)}) copy-start(bf16[1,192,192]{2,1,0:T(8,128)(2,1)} %copy.100) | copy-start | bytes 221188
  102.4 1.7 copy-start.78
  102.9 1.9 copy-start.30
  102.9 1.9 copy-start.76
  108.7 36.5 %collective-permute-start.1 = (bf16[2,16,24,192]{3,2,1,0:T(8,128)(2,1)S(1)}, bf16[2,16,24,192]{3,2,1,0:T(8,128)(2,1)}, u32[]{:S(2)}, u32[]{:S(2)}) collective-permute-start(bf16[2,16,24,192]{3,2,1,0:T(8,128)(2,1)S(1)} %multiply_convert_fusion), channel_id=1, source_target_pairs={{0,1},{1,2},{2,3},{3,4},{4,5},{5,6},{6,7},{7,8},{8,9},{9,10},{10,1... | collective-permute-start | bytes 884744 | tf_op jit(solution)/shard_map/ppermute | solution.py:10
  111.6 9.6 %copy-start.1 = (bf16[27,192,192]{1,0,2:T(8,128)(2,1)S(1)}, bf16[27,192,192]{1,0,2:T(8,128)(2,1)}, u32[]{:S(2)}) copy-start(bf16[27,192,192]{1,0,2:T(8,128)(2,1)} %all-gather.6.cloned.1.call-done) | copy-start | bytes 5971972
  123.4 19.7 %copy-start.48 = (bf16[1,192,192]{1,0,2:T(2,128)(2,1)S(1)}, bf16[1,192,192]{1,0,2:T(2,128)(2,1)}, u32[]{:S(2)}) copy-start(bf16[1,192,192]{1,0,2:T(2,128)(2,1)} %get-tuple-element.14) | copy-start | bytes 221188
  124.2 19.7 %copy-start.47 = (bf16[1,192,192]{1,0,2:T(2,128)(2,1)S(1)}, bf16[1,192,192]{1,0,2:T(2,128)(2,1)}, u32[]{:S(2)}) copy-start(bf16[1,192,192]{1,0,2:T(2,128)(2,1)} %get-tuple-element.13) | copy-start | bytes 221188
  124.9 19.0 %copy-start.46 = (bf16[1,192,192]{1,0,2:T(2,128)(2,1)S(1)}, bf16[1,192,192]{1,0,2:T(2,128)(2,1)}, u32[]{:S(2)}) copy-start(bf16[1,192,192]{1,0,2:T(2,128)(2,1)} %get-tuple-element.12) | copy-start | bytes 221188
  125.7 18.4 %copy-start.45 = (bf16[1,192,192]{1,0,2:T(2,128)(2,1)S(1)}, bf16[1,192,192]{1,0,2:T(2,128)(2,1)}, u32[]{:S(2)}) copy-start(bf16[1,192,192]{1,0,2:T(2,128)(2,1)} %get-tuple-element.11) | copy-start | bytes 221188
  126.5 17.8 %copy-start.44 = (bf16[1,192,192]{1,0,2:T(2,128)(2,1)S(1)}, bf16[1,192,192]{1,0,2:T(2,128)(2,1)}, u32[]{:S(2)}) copy-start(bf16[1,192,192]{1,0,2:T(2,128)(2,1)} %get-tuple-element.10) | copy-start | bytes 221188
  127.3 17.2 %copy-start.43 = (bf16[1,192,192]{1,0,2:T(2,128)(2,1)S(1)}, bf16[1,192,192]{1,0,2:T(2,128)(2,1)}, u32[]{:S(2)}) copy-start(bf16[1,192,192]{1,0,2:T(2,128)(2,1)} %get-tuple-element.9) | copy-start | bytes 221188
  128.0 16.5 %copy-start.42 = (bf16[1,192,192]{1,0,2:T(2,128)(2,1)S(1)}, bf16[1,192,192]{1,0,2:T(2,128)(2,1)}, u32[]{:S(2)}) copy-start(bf16[1,192,192]{1,0,2:T(2,128)(2,1)} %get-tuple-element.8) | copy-start | bytes 221188
  128.8 13.5 %copy-start.49 = (bf16[1,192,192]{1,0,2:T(2,128)(2,1)S(1)}, bf16[1,192,192]{1,0,2:T(2,128)(2,1)}, u32[]{:S(2)}) copy-start(bf16[1,192,192]{1,0,2:T(2,128)(2,1)} %get-tuple-element.15) | copy-start | bytes 221188
  148.1 1.2 copy-start.66
  148.5 1.5 copy-start.64
  157.7 2.9 %copy-start.85 = (s32[192]{0:T(256)S(1)}, s32[192]{0:T(256)}, u32[]{:S(2)}) copy-start(s32[192]{0:T(256)} %compare_select_fusion) | copy-start | bytes 2308
  157.7 2.9 %copy-start.79 = (bf16[27,192,16]{1,2,0:T(8,128)(2,1)S(1)}, bf16[27,192,16]{1,2,0:T(8,128)(2,1)}, u32[]{:S(2)}) copy-start(bf16[27,192,16]{1,2,0:T(8,128)(2,1)} %param.19) | copy-start | bytes 497668
  158.0 4.1 %copy-start.82 = (pred[2]{0:T(512)(128)(4,1)S(1)}, pred[2]{0:T(512)(128)(4,1)}, u32[]{:S(2)}) copy-start(pred[2]{0:T(512)(128)(4,1)} %copy-done.81) | copy-start | bytes 10
  158.0 4.1 %copy-start.84 = (pred[2]{0:T(512)(128)(4,1)S(1)}, pred[2]{0:T(512)(128)(4,1)}, u32[]{:S(2)}) copy-start(pred[2]{0:T(512)(128)(4,1)} %copy-done.83) | copy-start | bytes 10
  158.6 3.0 %collective-permute-start.2 = (bf16[2,16,24,192]{3,2,1,0:T(8,128)(2,1)S(1)}, bf16[2,16,24,192]{3,2,1,0:T(8,128)(2,1)S(1)}, u32[]{:S(2)}, u32[]{:S(2)}) collective-permute-start(bf16[2,16,24,192]{3,2,1,0:T(8,128)(2,1)S(1)} %fusion.30), channel_id=1, source_target_pairs={{0,1},{1,2},{2,3},{3,4},{4,5},{5,6},{6,7},{7,8},{8,9},{9,10},{10,1... | collective-permute-start | bytes 884744 | tf_op jit(solution)/shard_map/ppermute | solution.py:10
  (46 other events, 46.8 us)
Sparse Core Ops, SparseCore 0:
  9.6 47.8 all-gather.3
  59.8 44.0 all-gather.5
where the time goes:
time: 209 us; the launch traced here: 207 us
  local copies, waits for them, and re-layouts  85.2 us (41%)
  waiting for transfers between devices  37.3 us (18%)
  blocking collectives  26 us (12%)
  matrix products  25.8 us (12%)
  between operations  14.7 us (7%)
  other arithmetic  10.9 us (5%)
  starting transfers between devices  7.34 us (4%)
    unnamed x234, local copies, waits for them, and re-layouts  51.5 us
    all_gather x2, waiting for transfers between devices, conv_columns(): lax.all_gather(weight_shard, 'ctx', axis=2, tiled=True)  35.8 us
    all_gather x1, blocking collectives, body(): all_patches = lax.all_gather(patches, 'ctx', axis=0, tiled=True)  26 us
    dot_general x81, matrix products, conv_block(): jnp.dot(shifted, weight[frame_tap * 9 + row_tap * 3 + col_tap], preferred...  25.3 us
    slice x4, local copies, waits for them, and re-layouts, conv_block(): weight[frame_tap * 9 + row_tap * 3 + col_tap]  23 us
    slice x8, local copies, waits for them, and re-layouts, conv_block(): source[:, row_tap:row_tap + height, col_tap:col_tap + breadth, :]  7.41 us
    ppermute x3, starting transfers between devices, shifted_2(): lax.ppermute(value, axis, [(source, source + steps) for source in range(f...  7.3 us
  transfers between devices with their start and end apart: 5, of which 2 were waited for; matrix products, arithmetic and copies ran while one was open for 46% of the time, Pallas kernels for 0%

commit v1 on v0

v1 whole, which is shorter than its diff:
```python
import functools

import jax
import jax.numpy as jnp
from jax import lax
from jax.experimental import pallas as pl
from jax.experimental.pallas import tpu as pltpu
from jax.sharding import PartitionSpec as P

LANES = 128
SUBLANES = 8
UNIT_ROWS = 256
SCRATCH_ROWS = 288
NT = (((1,), (1,)), ((), ()))
VMEM_SPEC = pl.BlockSpec(memory_space=pltpu.VMEM)
SMEM_SPEC = pl.BlockSpec(memory_space=pltpu.SMEM)
PARAMS = pltpu.CompilerParams(vmem_limit_bytes=56 * 2**20)


def xor_permute(value, axis, mask):
    count = lax.axis_size(axis)
    return lax.ppermute(value, axis, [(source, source ^ mask) for source in range(count)])


def to_next(value, axis):
    count = lax.axis_size(axis)
    return lax.ppermute(value, axis, [(source, source + 1) for source in range(count - 1)])


def unit_geometry(taps, unit_channels):
    pairs = (taps + 1) // 2
    head_rows = -(-unit_channels * taps // SUBLANES) * SUBLANES
    return pairs, head_rows


def pack_kernel(half_ref, *refs, unit_channels):
    count = len(refs) // 2
    staged = refs[-1]
    for weight_ref, unit_ref in zip(refs[:count], refs[count:-1]):
        _, taps, channels = weight_ref.shape
        pairs, head_rows = unit_geometry(taps, unit_channels)
        tail = channels - LANES
        staged[...] = jnp.zeros_like(staged)
        for channel in range(unit_channels):
            rows = weight_ref[half_ref[0] * unit_channels + channel].astype(jnp.float32)
            staged[channel * taps : channel * taps + taps, :] = rows[:, :LANES]
            at = head_rows + channel * pairs
            staged[at : at + pairs, 0:tail] = rows[:pairs, LANES:]
            staged[at : at + taps - pairs, tail : 2 * tail] = rows[pairs:, LANES:]
        unit_ref[...] = staged[...].astype(jnp.bfloat16)


def pack_units(half, weights, unit_channels):
    return pl.pallas_call(
        functools.partial(pack_kernel, unit_channels=unit_channels),
        out_shape=[jax.ShapeDtypeStruct((UNIT_ROWS, LANES), jnp.bfloat16)] * len(weights),
        in_specs=[SMEM_SPEC] + [VMEM_SPEC] * len(weights),
        out_specs=[VMEM_SPEC] * len(weights),
        scratch_shapes=[pltpu.VMEM((UNIT_ROWS, LANES), jnp.float32)],
        compiler_params=PARAMS,
    )(half, *weights)


def pack_whole(weight, units):
    outputs, taps, channels = weight.shape
    unit_channels = outputs // units
    pairs, head_rows = unit_geometry(taps, unit_channels)
    split = weight.reshape(units, unit_channels, taps, channels)
    head = split[..., :LANES].reshape(units, unit_channels * taps, LANES)
    head = jnp.pad(head, ((0, 0), (0, head_rows - unit_channels * taps), (0, 0)))
    low, high = split[:, :, :pairs, LANES:], split[:, :, pairs:, LANES:]
    high = jnp.pad(high, ((0, 0), (0, 0), (0, 2 * pairs - taps), (0, 0)))
    tail = jnp.concatenate([low, high], axis=-1).reshape(units, unit_channels * pairs, LANES)
    both = jnp.concatenate([head, tail], axis=1)
    return jnp.pad(both, ((0, 0), (0, UNIT_ROWS - both.shape[1]), (0, 0)))


def expand_kernel(weight_ref, wide_ref):
    depth, channels = weight_ref.shape[1:]
    wide_ref[...] = jnp.zeros_like(wide_ref)
    for u in range(4):
        for v in range(4):
            for a in range(3):
                for r in range(2):
                    for s in range(2):
                        if 0 <= u - r <= 2 and 0 <= v - s <= 2:
                            at = ((a * 2 + r) * 2 + s) * depth
                            wide_ref[4 * u + v, at : at + depth, :channels] = weight_ref[
                                9 * a + 3 * (u - r) + (v - s)
                            ]


def expand_weight_out(weight):
    _, depth, channels = weight.shape
    return pl.pallas_call(
        expand_kernel,
        out_shape=jax.ShapeDtypeStruct((16, 12 * depth, 2 * LANES), jnp.bfloat16),
        in_specs=[VMEM_SPEC],
        out_specs=VMEM_SPEC,
        compiler_params=PARAMS,
    )(weight)


def rms_silu(values, gain_vector):
    normed = (
        values * lax.rsqrt(jnp.mean(values * values, axis=-1, keepdims=True) + 1e-06) * gain_vector
    )
    return jax.nn.silu(normed)


def same_clip(clips_ref, frame, steps_back):
    earlier = jnp.maximum(frame - steps_back, 0)
    return (frame >= steps_back) & (clips_ref[earlier] == clips_ref[frame])


def split_lanes(values):
    tail = values[:, LANES:]
    fill = jnp.zeros((values.shape[0], 2 * LANES - values.shape[1]), values.dtype)
    return values[:, :LANES], jnp.concatenate([tail, fill], axis=1)


def place_frame(values, at, head_x, low_x, high_x):
    breadth, height = head_x.shape[2] - 2, head_x.shape[3]
    row = lax.broadcasted_iota(jnp.int32, (values.shape[0], LANES), 0) % height
    head, tail = split_lanes(values)
    count = values.shape[0]
    for tap in range(3):
        for part, part_x in ((head, head_x), (tail, low_x)):
            if tap == 0:
                part = jnp.where(row == 0, 0.0, pltpu.roll(part, 1, 0))
            if tap == 2:
                part = jnp.where(row == height - 1, 0.0, pltpu.roll(part, count - 1, 0))
            part_x[tap, at, 1 : breadth + 1] = part.reshape(breadth, height, LANES).astype(
                jnp.bfloat16
            )
            if part_x is low_x:
                high_x[tap, at, 1 : breadth + 1] = (
                    pltpu.roll(part, LANES // 2, 1).reshape(breadth, height, LANES)
                ).astype(jnp.bfloat16)


def clear_rims(arrays):
    for array in arrays:
        frames, wide = array.shape[1], array.shape[2]
        array[:, frames - 1] = jnp.zeros_like(array[:, frames - 1])
        array[:, :, 0] = jnp.zeros_like(array[:, :, 0])
        array[:, :, wide - 1] = jnp.zeros_like(array[:, :, wide - 1])


def unpack_units(unit_refs, rhs, staged, taps, unit_channels):
    pairs, head_rows = unit_geometry(taps, unit_channels)
    staged[:, UNIT_ROWS:] = jnp.zeros_like(staged[:, UNIT_ROWS:])
    done = 0
    for unit_ref in unit_refs:
        couples = unit_ref.shape[0] // 2

        def couple_step(couple, carry, unit_ref=unit_ref, done=done):
            for one in range(2):
                staged[one, :UNIT_ROWS] = unit_ref[2 * couple + one].astype(jnp.float32)
            to = pl.ds(pl.multiple_of((done + couple) * 16, 16), 16)
            for tap in range(taps):
                rows = [staged[one, pl.ds(tap, 8, stride=taps), :] for one in range(2)]
                rhs[tap, to, :] = jnp.concatenate(rows, axis=0).astype(jnp.bfloat16)
            for pair in range(pairs):
                rows = [staged[one, pl.ds(head_rows + pair, 8, stride=pairs), :] for one in range(2)]
                rhs[taps + pair, to, :] = jnp.concatenate(rows, axis=0).astype(jnp.bfloat16)
            return carry

        lax.fori_loop(0, couples, couple_step, 0)
        done += couples


def convolve(clips_ref, first, head_x, low_x, high_x, rhs, frames, taps):
    zero_frame = head_x.shape[1] - 1
    breadth, height = head_x.shape[2] - 2, head_x.shape[3]
    pairs = (taps + 1) // 2
    source = [
        [
            jnp.where(same_clip(clips_ref, first + frame, 2 - tap), frame + tap, zero_frame)
            for tap in range(3)
        ]
        for frame in range(frames)
    ]

    def shifted(array, tap):
        a, b, e = tap // 9, tap // 3 % 3, tap % 3
        return jnp.concatenate(
            [
                array[b, source[frame][a], e : e + breadth].reshape(breadth * height, LANES)
                for frame in range(frames)
            ],
            axis=0,
        )

    def chunk(index):
        if index < taps:
            return shifted(head_x, index)
        pair = index - taps
        low = shifted(low_x, pair)
        return low + shifted(high_x, pair + pairs) if pair + pairs < taps else low

    total = taps + pairs
    summed = None
    for begin in range(0, total, 14):
        end = min(begin + 14, total)
        part = lax.dot_general(
            jnp.concatenate([chunk(index) for index in range(begin, end)], axis=1),
            jnp.concatenate([rhs[index] for index in range(begin, end)], axis=1),
            NT,
            preferred_element_type=jnp.float32,
        )
        summed = part if summed is None else summed + part
    return summed


def first_kernel(
    clips_ref, first_ref, own_ref, rim_ref, gain_first_ref, gain_second_ref, pick_ref, *rest,
    taps, unit_channels,
):
    *unit_refs, out_ref, head_x, low_x, high_x, rhs, staged = rest
    frames, breadth, height, channels = own_ref.shape
    clear_rims((head_x, low_x, high_x))
    for frame in range(frames + 2):
        values = rim_ref[frame] if frame < 2 else own_ref[frame - 2]
        values = values.astype(jnp.float32).reshape(breadth * height, channels)
        place_frame(rms_silu(values, gain_first_ref[...]), frame, head_x, low_x, high_x)
    unpack_units(unit_refs, rhs, staged, taps, unit_channels)
    summed = convolve(clips_ref, first_ref[0], head_x, low_x, high_x, rhs, frames, taps)
    first_out = jnp.dot(
        summed.astype(jnp.bfloat16), pick_ref[...], preferred_element_type=jnp.float32
    )
    out_ref[...] = (
        rms_silu(first_out, gain_second_ref[...])
        .astype(jnp.bfloat16)
        .reshape(frames, breadth, height, channels)
    )


def second_kernel(
    clips_ref, first_ref, own_ref, rim_ref, features_ref, gain_ref, pick_ref, wide_ref, *rest,
    taps, unit_channels,
):
    *unit_refs, own_out, next_out, head_x, low_x, high_x, rhs, staged, plain, windows = rest
    frames, breadth, height, channels = own_ref.shape
    pixels = breadth * height
    rows, columns = height // 2, breadth // 2
    width = wide_ref.shape[1] // 3
    first = first_ref[0]
    clear_rims((head_x, low_x, high_x))
    for frame in range(frames + 2):
        values = rim_ref[frame] if frame < 2 else own_ref[frame - 2]
        values = values.astype(jnp.float32).reshape(pixels, channels)
        place_frame(values, frame, head_x, low_x, high_x)
    unpack_units(unit_refs, rhs, staged, taps, unit_channels)
    summed = convolve(clips_ref, first, head_x, low_x, high_x, rhs, frames, taps)
    features = lax.dot_general(
        features_ref[...].reshape(frames * pixels, channels),
        pick_ref[...],
        NT,
        preferred_element_type=jnp.float32,
    )
    block_out = jnp.dot(
        (features + summed).astype(jnp.bfloat16), pick_ref[...], preferred_element_type=jnp.float32
    )
    head_in = rms_silu(block_out, gain_ref[...])
    for part, values in enumerate(split_lanes(head_in)):
        plain[part] = values
    windows[...] = jnp.zeros_like(windows)
    half = frames * pixels // 2
    row = lax.broadcasted_iota(jnp.int32, (half, LANES), 0) % rows
    for part in range(2):
        even = plain[part, pl.ds(0, half, stride=2), :]
        odd = plain[part, pl.ds(1, half, stride=2), :]
        before = jnp.where(row == 0, 0.0, pltpu.roll(odd, 1, 0))
        after = jnp.where(row == rows - 1, 0.0, pltpu.roll(even, half - 1, 0))
        for u, values in enumerate((before, even, odd, after)):
            windows[u, part, :, 1 : breadth + 1] = values.reshape(frames, breadth, rows, LANES)
    chunks = []
    for u in range(4):
        for v in range(4):
            for part in range(2):
                chunks.append(
                    jnp.concatenate(
                        [
                            windows[u, part, frame, pl.ds(v, columns, stride=2)].reshape(
                                columns * rows, LANES
                            )
                            for frame in range(frames)
                        ],
                        axis=0,
                    ).astype(jnp.bfloat16)
                )
    outs = lax.dot_general(
        jnp.concatenate(chunks, axis=1),
        jnp.concatenate([wide_ref[window] for window in range(16)], axis=1),
        NT,
        preferred_element_type=jnp.float32,
    )
    spots = columns * rows

    def from_frame(frame, tap):
        return outs[frame * spots : (frame + 1) * spots, tap * width : (tap + 1) * width]

    def gathered(frame, sources):
        total = jnp.zeros((spots, width), jnp.float32)
        for tap in range(3):
            source = frame + tap - 2
            if source in sources:
                kept = same_clip(clips_ref, jnp.minimum(first + frame, clips_ref.shape[0] - 1), 2 - tap)
                total = total + jnp.where(kept, from_frame(source, tap), 0.0)
        return total

    own = range(frames)
    own_out[...] = jnp.concatenate([gathered(frame, own) for frame in own], axis=1)
    next_out[...] = jnp.concatenate(
        [gathered(frame + frames, own) for frame in own], axis=1
    )


def conv_scratch(frames, breadth, height, taps, outputs):
    pairs = (taps + 1) // 2
    image = pltpu.VMEM((3, frames + 3, breadth + 2, height, LANES), jnp.bfloat16)
    return [image] * 3 + [
        pltpu.VMEM((taps + pairs, outputs, LANES), jnp.bfloat16),
        pltpu.VMEM((2, SCRATCH_ROWS, LANES), jnp.float32),
    ]


def embed_kernel(
    spot_ref, lane_ref, embed_ref, scale_ref, shift_ref, *rest
):
    *patch_refs, out_ref = rest
    width = embed_ref.shape[0]
    total = jnp.zeros((out_ref.shape[0], LANES), jnp.float32)
    begin = 0
    for patch_ref in patch_refs:
        count = patch_ref.shape[0]
        spots = lax.broadcasted_iota(jnp.int32, (out_ref.shape[0], count), 1) + begin
        chosen = jnp.where(spots == spot_ref[...], 1.0, 0.0).astype(jnp.bfloat16)
        total = total + jnp.dot(chosen, patch_ref[...], preferred_element_type=jnp.float32)
        begin += count
    turned = pltpu.roll(total, width, 1)
    ordered = jnp.where(lane_ref[...] == 0, total, turned)[:, :width].astype(jnp.bfloat16)
    embedded = jnp.dot(ordered, embed_ref[...], preferred_element_type=jnp.float32)
    center = jnp.mean(embedded, axis=-1, keepdims=True)
    centered = embedded - center
    variance = jnp.mean(centered * centered, axis=-1, keepdims=True)
    normed = centered * lax.rsqrt(variance + 1e-06)
    out_ref[...] = (normed * (1.0 + scale_ref[...]) + shift_ref[...]).astype(out_ref.dtype)


def gather_units(unit):
    line = jnp.stack([unit] + [xor_permute(unit, "ctx", 4 * step) for step in (1, 2, 3)])
    across = xor_permute(line, "ctx", 2)
    other = xor_permute(line, "groups", 1)
    corner_low = xor_permute(other[:2], "ctx", 2)
    corner_high = xor_permute(across[2:], "groups", 1)
    chip = jnp.concatenate([line, across, other, corner_low, corner_high])
    return [chip, xor_permute(chip, "ctx", 1)]


def unit_channel_map(grid, group, device, unit_channels, units):
    unit = jnp.arange(units * SUBLANES, dtype=jnp.int32) // SUBLANES
    within = jnp.arange(units * SUBLANES, dtype=jnp.int32) % SUBLANES
    if grid:
        step, kind, core = unit % 4, unit // 4 % 4, unit // 16
        source = device ^ (4 * step + 2 * (kind % 2) + core)
        unit = source * 2 + (group ^ (kind // 2))
    return jnp.where(within < unit_channels, unit * unit_channels + within, -1)


def body(
    features,
    clip_ids,
    gain_first,
    weight_first,
    gain_second,
    weight_second,
    gain_third,
    weight_out,
    embed_weight,
    shift_mod,
    scale_mod,
    token_order,
):
    frames, height, breadth, channels = features.shape
    taps = weight_first.shape[0]
    groups, devices = lax.axis_size("groups"), lax.axis_size("ctx")
    group, device = lax.axis_index("groups"), lax.axis_index("ctx")
    grid = groups == 2 and devices == 16
    units = 32
    unit_channels = channels // units

    by_output = [weight.transpose(2, 0, 1) for weight in (weight_first, weight_second)]
    if grid:
        half = group.astype(jnp.int32).reshape(1)
        packed = pack_units(half, by_output, unit_channels)
        units_first, units_second = [gather_units(unit) for unit in packed]
    else:
        units_first, units_second = [
            [pack_whole(lax.all_gather(weight, "ctx", axis=0, tiled=True), units)]
            for weight in by_output
        ]
    channel_map = unit_channel_map(grid, group, device, unit_channels, units)
    pick = (channel_map[:, None] == jnp.arange(channels, dtype=jnp.int32)).astype(jnp.bfloat16)
    wide = expand_weight_out(weight_out.transpose(0, 2, 1))

    first = (device * frames).astype(jnp.int32).reshape(1)
    turned = features.transpose(0, 2, 1, 3)
    scratch = conv_scratch(frames, breadth, height, taps, units * SUBLANES)
    image = jax.ShapeDtypeStruct((frames, breadth, height, channels), jnp.bfloat16)
    second_in = pl.pallas_call(
        functools.partial(first_kernel, taps=taps, unit_channels=unit_channels),
        out_shape=image,
        in_specs=[SMEM_SPEC] * 2 + [VMEM_SPEC] * (5 + len(units_first)),
        out_specs=VMEM_SPEC,
        scratch_shapes=scratch,
        compiler_params=PARAMS,
    )(
        clip_ids, first, turned, to_next(turned[frames - 2 :], "ctx"), gain_first.reshape(1, -1),
        gain_second.reshape(1, -1), pick, *units_first,
    )

    depth = weight_out.shape[2]
    spots = (height // 2) * (breadth // 2)
    partial = jax.ShapeDtypeStruct((spots, frames * 4 * depth), jnp.float32)
    own_part, next_part = pl.pallas_call(
        functools.partial(second_kernel, taps=taps, unit_channels=unit_channels),
        out_shape=[partial, partial],
        in_specs=[SMEM_SPEC] * 2 + [VMEM_SPEC] * (6 + len(units_second)),
        out_specs=[VMEM_SPEC] * 2,
        scratch_shapes=scratch
        + [
            pltpu.VMEM((2, frames * breadth * height, LANES), jnp.float32),
            pltpu.VMEM((4, 2, frames, breadth + 2, height // 2, LANES), jnp.float32),
        ],
        compiler_params=PARAMS,
    )(
        clip_ids, first, second_in, to_next(second_in[frames - 2 :], "ctx"), turned,
        gain_third.reshape(1, -1), pick, wide, *units_second,
    )
    patches = (own_part + to_next(next_part, "ctx")).astype(jnp.bfloat16)

    frame, spot = token_order // spots, token_order % spots
    spot = spot % (breadth // 2) * (height // 2) + spot // (breadth // 2)
    owner = frame // frames
    if grid:
        line = jnp.concatenate([patches] + [xor_permute(patches, "ctx", 4 * k) for k in (1, 2, 3)])
        sheet = jnp.concatenate([line, xor_permute(line, "ctx", 2)])
        pieces = [sheet, xor_permute(sheet, "ctx", 1)]
        away = owner ^ device
        place = (away % 2 * 2 + away // 2 % 2) * 4 + away // 4
    else:
        pieces = [lax.all_gather(patches, "ctx", axis=0, tiled=True)]
        place = owner
    spot = (place * spots + spot).reshape(-1, 1)
    lane = (frame % frames).reshape(-1, 1)

    tokens, width = token_order.shape[0], embed_weight.shape[1]
    block = 48 if tokens % 48 == 0 else tokens
    column = pl.BlockSpec((block, 1), lambda i: (i, 0))
    row = pl.BlockSpec((1, width), lambda i: (0, 0))
    return pl.pallas_call(
        embed_kernel,
        out_shape=jax.ShapeDtypeStruct((tokens, width), jnp.bfloat16),
        grid=(tokens // block,),
        in_specs=[column, column, pl.BlockSpec(embed_weight.shape, lambda i: (0, 0)), row, row]
        + [pl.BlockSpec(piece.shape, lambda i: (0, 0)) for piece in pieces],
        out_specs=pl.BlockSpec((block, width), lambda i: (i, 0)),
        compiler_params=PARAMS,
    )(
        spot, lane, embed_weight, scale_mod.reshape(1, -1), shift_mod.reshape(1, -1), *pieces
    )


def solution(mesh):
    in_specs = (
        P(("groups", "ctx"), None, None, None),
        P("groups"),
        P(),
        P(None, None, "ctx"),
        P(),
        P(None, None, "ctx"),
        P(),
        P(),
        P(),
        P(),
        P(),
        P(("groups", "ctx")),
    )
    out_specs = P(("groups", "ctx"), None)
    return jax.shard_map(body, mesh=mesh, in_specs=in_specs, out_specs=out_specs, check_vma=False)
```

time: 209 us -> 106 us (0.51)
  local copies, waits for them, and re-layouts: 85.2 us -> 5.28 us
  starting transfers between devices: 7.34 us -> 49.8 us
  blocking collectives: 26 us -> 0 us
  matrix products: 25.8 us -> 0 us
  Pallas kernels: 0 us -> 25.7 us
  waiting for transfers between devices: 37.3 us -> 21.3 us
  between operations: 14.7 us -> 0.29 us
  other arithmetic: 10.9 us -> 3.4 us
    unnamed x234 -> x35, local copies, waits for them, and re-layouts: 51.5 us -> 3.67 us
    ppermute x3 -> x24, starting transfers between devices: 7.3 us -> 49.8 us  [the longest x21 33 us: xor_permute(): lax.ppermute(value, axis, [(source, source ^ mask) for source in range(co...]
    all_gather x2 -> x0, waiting for transfers between devices: 35.8 us -> none  [conv_columns(): lax.all_gather(weight_shard, 'ctx', axis=2, tiled=True)]
    slice x12 -> x4, local copies, waits for them, and re-layouts: 30.5 us -> 0.04 us  [the longest x2 0.02 us: gather_units(): corner_high = xor_permute(across[2:], 'groups', 1)]
    all_gather x1 -> x0, blocking collectives: 26 us -> none  [body(): all_patches = lax.all_gather(patches, 'ctx', axis=0, tiled=True)]
    dot_general x82 -> x0, matrix products: 25.8 us -> none  [the longest x81 25.3 us: conv_block(): jnp.dot(shifted, weight[frame_tap * 9 + row_tap * 3 + col_tap], preferred...]
    pallas_call x0 -> x5, Pallas kernels: none -> 25.7 us  [the longest x1 8.82 us: body(): pl.pallas_call(functools.partial(second_kernel, taps=taps, unit_channels=...]
    ppermute x3 -> x24, waiting for transfers between devices: 0.8 us -> 21.3 us  [the longest x21 20 us: xor_permute(): lax.ppermute(value, axis, [(source, source ^ mask) for source in range(co...]
  transfers between devices with their start and end apart: 5 -> 24, of which waited for: 2 -> 11; matrix products, arithmetic and copies ran while one was open for 46% -> 5% of each run, Pallas kernels for 0% -> 9%
where the time goes in v1:
time: 106 us
  starting transfers between devices  49.8 us (47%)
  Pallas kernels  25.7 us (24%)
  waiting for transfers between devices  21.3 us (20%)
  local copies, waits for them, and re-layouts  5.28 us (5%)
  other arithmetic  3.4 us (3%)
    ppermute x21, starting transfers between devices, xor_permute(): lax.ppermute(value, axis, [(source, source ^ mask) for source in range(co...  33 us
    ppermute x21, waiting for transfers between devices, xor_permute(): lax.ppermute(value, axis, [(source, source ^ mask) for source in range(co...  20 us
    ppermute x3, starting transfers between devices, to_next(): lax.ppermute(value, axis, [(source, source + 1) for source in range(count...  16.8 us
    pallas_call x1, Pallas kernels, body(): pl.pallas_call(functools.partial(second_kernel, taps=taps, unit_channels=...  8.82 us
    pallas_call x1, Pallas kernels, body(): pl.pallas_call(functools.partial(first_kernel, taps=taps, unit_channels=u...  7.51 us
    pallas_call x1, Pallas kernels, body(): pl.pallas_call(embed_kernel, out_shape=jax.ShapeDtypeStruct((tokens, widt...  5.29 us
    unnamed x35, local copies, waits for them, and re-layouts  3.67 us
    pallas_call x1, Pallas kernels, expand_weight_out(): pl.pallas_call(expand_kernel, out_shape=jax.ShapeDtypeStruct((16, 12 * de...  2.28 us
  transfers between devices with their start and end apart: 24, of which 11 were waited for; matrix products, arithmetic and copies ran while one was open for 5% of the time, Pallas kernels for 9%

profile of v1, /device:TPU:0, one launch (start us, length us, event | category | flops | bytes accessed | tf_op | source)
XLA Modules:
  0.0 105.7 jit_solution(11380326352612060024)
XLA Ops:
  0.0 1.8 %shard_map.118 = (bf16[256,128]{1,0:T(8,128)(2,1)}, bf16[256,128]{1,0:T(8,128)(2,1)}) custom-call(s32[1]{0:T(128)} %bitcast.8.half_ref, bf16[12,27,192]{2,1,0:T(8,128)(2,1)} %bitcast.43, bf16[12,27,192]{2,1,0:T(8,128)(2,1)} %bitcast.44), custom_call_target="tpu_custom_call" | custom-call | tf_op jit(solution)/shard_map/pallas_call | solution.py:54
  1.8 3.0 %collective-permute-start.10 = (bf16[256,128]{1,0:T(8,128)(2,1)}, bf16[256,128]{1,0:T(8,128)(2,1)S(1)}, u32[]{:S(2)}, u32[]{:S(2)}) collective-permute-start(bf16[256,128]{1,0:T(8,128)(2,1)} %get-tuple-element.10), channel_id=1, source_target_pairs={{0,4},{1,5},{2,6},{3,7},{4,0},{5,1},{6,2},{7,3},{8,12},{9,13},{10,... | collective-permute-start | bytes 196616 | tf_op jit(solution)/shard_map/ppermute | solution.py:22
  4.8 2.6 %collective-permute-start.11 = (bf16[256,128]{1,0:T(8,128)(2,1)}, bf16[256,128]{1,0:T(8,128)(2,1)S(1)}, u32[]{:S(2)}, u32[]{:S(2)}) collective-permute-start(bf16[256,128]{1,0:T(8,128)(2,1)} %get-tuple-element.10), channel_id=1, source_target_pairs={{0,8},{1,9},{2,10},{3,11},{4,12},{5,13},{6,14},{7,15},{8,0},{9,1},... | collective-permute-start | bytes 196616 | tf_op jit(solution)/shard_map/ppermute | solution.py:22
  7.4 0.9 collective-permute-start.1
  8.3 3.5 %collective-permute-start.2 = (bf16[256,128]{1,0:T(8,128)(2,1)}, bf16[256,128]{1,0:T(8,128)(2,1)S(1)}, u32[]{:S(2)}, u32[]{:S(2)}) collective-permute-start(bf16[256,128]{1,0:T(8,128)(2,1)} %get-tuple-element.9), channel_id=1, source_target_pairs={{0,8},{1,9},{2,10},{3,11},{4,12},{5,13},{6,14},{7,15},{8,0},{9,1},... | collective-permute-start | bytes 196616 | tf_op jit(solution)/shard_map/ppermute | solution.py:22
  11.8 0.9 constant_dynamic-update-slice_fusion.7
  12.7 1.4 %collective-permute-done.12 = bf16[256,128]{1,0:T(8,128)(2,1)S(1)} collective-permute-done((bf16[256,128]{1,0:T(8,128)(2,1)}, bf16[256,128]{1,0:T(8,128)(2,1)S(1)}, u32[]{:S(2)}, u32[]{:S(2)}) %collective-permute-start.12) | collective-permute-done | bytes 65568 | tf_op jit(solution)/shard_map/ppermute | solution.py:22
  14.2 0.9 pad_maximum_fusion.1
  15.0 1.6 %collective-permute-start.13 = (bf16[4,256,128]{2,1,0:T(8,128)(2,1)S(1)}, bf16[4,256,128]{2,1,0:T(8,128)(2,1)S(1)}, u32[]{:S(2)}, u32[]{:S(2)}) collective-permute-start(bf16[4,256,128]{2,1,0:T(8,128)(2,1)S(1)} %pad_maximum_fusion.1), channel_id=1, source_target_pairs={{0,2},{1,3},{2,0},{3,1},{4,6},{5,7},{6,4},{7,5},{8,10},{9,11},{10,... | collective-permute-start | bytes 786440 | tf_op jit(solution)/shard_map/ppermute | solution.py:22
  16.6 1.5 %collective-permute-start.14 = (bf16[4,256,128]{2,1,0:T(8,128)(2,1)S(1)}, bf16[4,256,128]{2,1,0:T(8,128)(2,1)S(1)}, u32[]{:S(2)}, u32[]{:S(2)}) collective-permute-start(bf16[4,256,128]{2,1,0:T(8,128)(2,1)S(1)} %pad_maximum_fusion.1), channel_id=1, source_target_pairs={{0,16},{16,0},{1,17},{17,1},{2,18},{18,2},{3,19},{19,3},{4,20},{20... | collective-permute-start | bytes 786440 | tf_op jit(solution)/shard_map/ppermute | solution.py:22
  18.1 1.0 collective-permute-done.3
  19.1 0.9 pad_maximum_fusion
  20.0 1.6 %collective-permute-start.4 = (bf16[4,256,128]{2,1,0:T(8,128)(2,1)S(1)}, bf16[4,256,128]{2,1,0:T(8,128)(2,1)S(1)}, u32[]{:S(2)}, u32[]{:S(2)}) collective-permute-start(bf16[4,256,128]{2,1,0:T(8,128)(2,1)S(1)} %pad_maximum_fusion), channel_id=1, source_target_pairs={{0,2},{1,3},{2,0},{3,1},{4,6},{5,7},{6,4},{7,5},{8,10},{9,11},{10,... | collective-permute-start | bytes 786440 | tf_op jit(solution)/shard_map/ppermute | solution.py:22
  21.6 1.5 %collective-permute-start.5 = (bf16[4,256,128]{2,1,0:T(8,128)(2,1)S(1)}, bf16[4,256,128]{2,1,0:T(8,128)(2,1)S(1)}, u32[]{:S(2)}, u32[]{:S(2)}) collective-permute-start(bf16[4,256,128]{2,1,0:T(8,128)(2,1)S(1)} %pad_maximum_fusion), channel_id=1, source_target_pairs={{0,16},{16,0},{1,17},{17,1},{2,18},{18,2},{3,19},{19,3},{4,20},{20... | collective-permute-start | bytes 786440 | tf_op jit(solution)/shard_map/ppermute | solution.py:22
  23.2 1.7 %collective-permute-done.14 = bf16[4,256,128]{2,1,0:T(8,128)(2,1)S(1)} collective-permute-done((bf16[4,256,128]{2,1,0:T(8,128)(2,1)S(1)}, bf16[4,256,128]{2,1,0:T(8,128)(2,1)S(1)}, u32[]{:S(2)}, u32[]{:S(2)}) %collective-permute-start.14) | collective-permute-done | bytes 262176 | tf_op jit(solution)/shard_map/ppermute | solution.py:22
  24.9 0.6 collective-permute-start.15
  25.5 1.6 %collective-permute-start.16 = (bf16[2,256,128]{2,1,0:T(8,128)(2,1)S(1)}, bf16[2,256,128]{2,1,0:T(8,128)(2,1)S(1)}, u32[]{:S(2)}, u32[]{:S(2)}) collective-permute-start(bf16[2,256,128]{2,1,0:T(8,128)(2,1)S(1)} %slice.19), channel_id=1, source_target_pairs={{0,16},{16,0},{1,17},{17,1},{2,18},{18,2},{3,19},{19,3},{4,20},{20... | collective-permute-start | bytes 393224 | tf_op jit(solution)/shard_map/ppermute | solution.py:22
  27.0 3.4 %collective-permute-done.5 = bf16[4,256,128]{2,1,0:T(8,128)(2,1)S(1)} collective-permute-done((bf16[4,256,128]{2,1,0:T(8,128)(2,1)S(1)}, bf16[4,256,128]{2,1,0:T(8,128)(2,1)S(1)}, u32[]{:S(2)}, u32[]{:S(2)}) %collective-permute-start.5) | collective-permute-done | bytes 262176 | tf_op jit(solution)/shard_map/ppermute | solution.py:22
  30.5 0.1 collective-permute-start.6
  30.6 1.6 %collective-permute-start.7 = (bf16[2,256,128]{2,1,0:T(8,128)(2,1)S(1)}, bf16[2,256,128]{2,1,0:T(8,128)(2,1)S(1)}, u32[]{:S(2)}, u32[]{:S(2)}) collective-permute-start(bf16[2,256,128]{2,1,0:T(8,128)(2,1)S(1)} %slice.17), channel_id=1, source_target_pairs={{0,16},{16,0},{1,17},{17,1},{2,18},{18,2},{3,19},{19,3},{4,20},{20... | collective-permute-start | bytes 393224 | tf_op jit(solution)/shard_map/ppermute | solution.py:22
  32.3 3.2 %collective-permute-done.6 = bf16[2,256,128]{2,1,0:T(8,128)(2,1)S(1)} collective-permute-done((bf16[2,256,128]{2,1,0:T(8,128)(2,1)S(1)}, bf16[2,256,128]{2,1,0:T(8,128)(2,1)S(1)}, u32[]{:S(2)}, u32[]{:S(2)}) %collective-permute-start.6) | collective-permute-done | bytes 131104 | tf_op jit(solution)/shard_map/ppermute | solution.py:22
  35.5 0.1 collective-permute-done.7
  35.7 0.1 collective-permute-start.8
  35.9 0.6 collective-permute-start.17
  36.5 0.1 copy.18
  36.6 2.7 %collective-permute-start = (bf16[2,24,16,192]{3,2,1,0:T(8,128)(2,1)S(1)}, bf16[2,24,16,192]{3,2,1,0:T(8,128)(2,1)}, u32[]{:S(2)}, u32[]{:S(2)}) collective-permute-start(bf16[2,24,16,192]{3,2,1,0:T(8,128)(2,1)S(1)} %bitcast.31), channel_id=1, source_target_pairs={{0,1},{1,2},{2,3},{3,4},{4,5},{5,6},{6,7},{7,8},{8,9},{9,10},{10,1... | collective-permute-start | bytes 884744 | tf_op jit(solution)/shard_map/ppermute | solution.py:27
  39.3 0.8 fusion.pick_ref
  40.0 0.2 collective-permute-done.rim_ref
  40.3 1.0 copy-done.3
  41.2 7.5 %shard_map.119.own_ref = bf16[2,24,16,192]{3,2,1,0:T(8,128)(2,1)} custom-call(s32[32]{0:T(128)} %clips_ref.3, s32[1]{0:T(128)} %bitcast.4.first_ref, bf16[2,24,16,192]{3,2,1,0:T(8,128)(2,1)} %bitcast.32, bf16[2,24,16,192]{3,2,1,0:T(8,128)(2,1)} %collective-permute-done.rim_ref, f32[1,192]{1,0:T(1,128)} %bitcast.49, f32[1,192]{1,0:T(1,128)} %bitcast.50, ...), custom_call_target="tpu_custom_call" | custom-call | tf_op jit(solution)/shard_map/pallas_call | solution.py:412
  48.7 6.9 %collective-permute-start.9 = (bf16[2,24,16,192]{3,2,1,0:T(8,128)(2,1)}, bf16[2,24,16,192]{3,2,1,0:T(8,128)(2,1)S(1)}, u32[]{:S(2)}, u32[]{:S(2)}) collective-permute-start(bf16[2,24,16,192]{3,2,1,0:T(8,128)(2,1)} %shard_map.119.own_ref), channel_id=1, source_target_pairs={{0,1},{1,2},{2,3},{3,4},{4,5},{5,6},{6,7},{7,8},{8,9},{9,10},{10,1... | collective-permute-start | bytes 884744 | tf_op jit(solution)/shard_map/ppermute | solution.py:27
  55.7 2.3 %shard_map.120.wide_ref = bf16[16,192,256]{2,1,0:T(8,128)(2,1)} custom-call(bf16[27,16,192]{2,1,0:T(8,128)(2,1)} %bitcast.42), custom_call_target="tpu_custom_call" | custom-call | tf_op jit(solution)/shard_map/pallas_call | solution.py:95
  58.0 0.7 copy-done.4
  58.7 8.8 %shard_map.121 = (f32[96,128]{1,0:T(8,128)}, f32[96,128]{1,0:T(8,128)}) custom-call(s32[32]{0:T(128)} %clips_ref.3, s32[1]{0:T(128)} %bitcast.4.first_ref, bf16[2,24,16,192]{3,2,1,0:T(8,128)(2,1)} %shard_map.119.own_ref, bf16[2,24,16,192]{3,2,1,0:T(8,128)(2,1)} %copy-done.4, bf16[2,24,16,192]{3,2,1,0:T(8,128)(2,1)} %bitcast.33, f32[1,192]{1,0:T(1,128)} %bitcast.51, ...), custom_call_target="tpu_custom_call" | custom-call | tf_op jit(solution)/shard_map/pallas_call | solution.py:427
  67.5 7.2 %collective-permute-start.18 = (f32[96,128]{1,0:T(8,128)}, f32[96,128]{1,0:T(8,128)S(1)}, u32[]{:S(2)}, u32[]{:S(2)}) collective-permute-start(f32[96,128]{1,0:T(8,128)} %get-tuple-element.12), channel_id=1, source_target_pairs={{0,1},{1,2},{2,3},{3,4},{4,5},{5,6},{6,7},{7,8},{8,9},{9,10},{10,1... | collective-permute-start | bytes 147464 | tf_op jit(solution)/shard_map/ppermute | solution.py:27
  74.7 1.1 %collective-permute-done.18 = f32[96,128]{1,0:T(8,128)S(1)} collective-permute-done((f32[96,128]{1,0:T(8,128)}, f32[96,128]{1,0:T(8,128)S(1)}, u32[]{:S(2)}, u32[]{:S(2)}) %collective-permute-start.18) | collective-permute-done | bytes 49184 | tf_op jit(solution)/shard_map/ppermute | solution.py:27
  75.8 0.8 constant_dynamic-update-slice_fusion.20
  76.6 9.4 %collective-permute-start.19 = (bf16[96,128]{1,0:T(8,128)(2,1)S(1)}, bf16[96,128]{1,0:T(8,128)(2,1)S(1)}, u32[]{:S(2)}, u32[]{:S(2)}) collective-permute-start(bf16[96,128]{1,0:T(8,128)(2,1)S(1)} %get-tuple-element.14), channel_id=1, source_target_pairs={{0,4},{1,5},{2,6},{3,7},{4,0},{5,1},{6,2},{7,3},{8,12},{9,13},{10,... | collective-permute-start | bytes 73736 | tf_op jit(solution)/shard_map/ppermute | solution.py:22
  86.0 1.8 %collective-permute-start.20 = (bf16[96,128]{1,0:T(8,128)(2,1)S(1)}, bf16[96,128]{1,0:T(8,128)(2,1)S(1)}, u32[]{:S(2)}, u32[]{:S(2)}) collective-permute-start(bf16[96,128]{1,0:T(8,128)(2,1)S(1)} %get-tuple-element.14), channel_id=1, source_target_pairs={{0,8},{1,9},{2,10},{3,11},{4,12},{5,13},{6,14},{7,15},{8,0},{9,1},... | collective-permute-start | bytes 73736 | tf_op jit(solution)/shard_map/ppermute | solution.py:22
  87.8 1.0 collective-permute-start.21
  88.9 1.9 %collective-permute-done.20 = bf16[96,128]{1,0:T(8,128)(2,1)S(1)} collective-permute-done((bf16[96,128]{1,0:T(8,128)(2,1)S(1)}, bf16[96,128]{1,0:T(8,128)(2,1)S(1)}, u32[]{:S(2)}, u32[]{:S(2)}) %collective-permute-start.20) | collective-permute-done | bytes 24608 | tf_op jit(solution)/shard_map/ppermute | solution.py:22
  90.7 2.7 %collective-permute-done.21 = bf16[96,128]{1,0:T(8,128)(2,1)S(1)} collective-permute-done((bf16[96,128]{1,0:T(8,128)(2,1)S(1)}, bf16[96,128]{1,0:T(8,128)(2,1)S(1)}, u32[]{:S(2)}, u32[]{:S(2)}) %collective-permute-start.21) | collective-permute-done | bytes 24608 | tf_op jit(solution)/shard_map/ppermute | solution.py:22
  93.4 0.1 collective-permute-start.22
  93.5 4.6 %collective-permute-done.22 = bf16[384,128]{1,0:T(8,128)(2,1)S(1)} collective-permute-done((bf16[384,128]{1,0:T(8,128)(2,1)S(1)}, bf16[384,128]{1,0:T(8,128)(2,1)S(1)}, u32[]{:S(2)}, u32[]{:S(2)}) %collective-permute-start.22) | collective-permute-done | bytes 98336 | tf_op jit(solution)/shard_map/ppermute | solution.py:22
  98.2 0.8 copy.15.spot_ref
  99.0 0.8 copy.16.lane_ref
  99.8 0.7 copy-done.7
  100.4 5.3 %shard_map.122 = bf16[192,3072]{1,0:T(8,128)(2,1)} custom-call(s32[192,1]{1,0:T(8,128)} %copy.15.spot_ref, s32[192,1]{1,0:T(8,128)} %copy.16.lane_ref, bf16[64,3072]{1,0:T(8,128)(2,1)} %embed_ref.1, f32[1,3072]{1,0:T(1,128)} %bitcast.45, f32[1,3072]{1,0:T(1,128)} %bitcast.46, bf16[768,128]{1,0:T(8,128)(2,1)} %copy-done.6, bf16[768,128]{1,0:T(8,128)(2,1)} %copy-done.7), custom_call_target="tpu_custom_call" | custom-call | tf_op jit(solution)/shard_map/pallas_call | solution.py:463
  (57 shorter events, 0.7 us)
Async XLA Ops:
  1.8 10.9 %collective-permute-start.10 = (bf16[256,128]{1,0:T(8,128)(2,1)}, bf16[256,128]{1,0:T(8,128)(2,1)S(1)}, u32[]{:S(2)}, u32[]{:S(2)}) collective-permute-start(bf16[256,128]{1,0:T(8,128)(2,1)} %get-tuple-element.10), channel_id=1, source_target_pairs={{0,4},{1,5},{2,6},{3,7},{4,0},{5,1},{6,2},{7,3},{8,12},{9,13},{10,... | collective-permute-start | bytes 196616 | tf_op jit(solution)/shard_map/ppermute | solution.py:22
  4.8 8.0 %collective-permute-start.11 = (bf16[256,128]{1,0:T(8,128)(2,1)}, bf16[256,128]{1,0:T(8,128)(2,1)S(1)}, u32[]{:S(2)}, u32[]{:S(2)}) collective-permute-start(bf16[256,128]{1,0:T(8,128)(2,1)} %get-tuple-element.10), channel_id=1, source_target_pairs={{0,8},{1,9},{2,10},{3,11},{4,12},{5,13},{6,14},{7,15},{8,0},{9,1},... | collective-permute-start | bytes 196616 | tf_op jit(solution)/shard_map/ppermute | solution.py:22
  7.4 6.8 %collective-permute-start.12 = (bf16[256,128]{1,0:T(8,128)(2,1)}, bf16[256,128]{1,0:T(8,128)(2,1)S(1)}, u32[]{:S(2)}, u32[]{:S(2)}) collective-permute-start(bf16[256,128]{1,0:T(8,128)(2,1)} %get-tuple-element.10), channel_id=1, source_target_pairs={{0,12},{1,13},{2,14},{3,15},{4,8},{5,9},{6,10},{7,11},{8,4},{9,5},... | collective-permute-start | bytes 196616 | tf_op jit(solution)/shard_map/ppermute | solution.py:22
  7.4 10.7 %collective-permute-start.1 = (bf16[256,128]{1,0:T(8,128)(2,1)}, bf16[256,128]{1,0:T(8,128)(2,1)S(1)}, u32[]{:S(2)}, u32[]{:S(2)}) collective-permute-start(bf16[256,128]{1,0:T(8,128)(2,1)} %get-tuple-element.9), channel_id=1, source_target_pairs={{0,4},{1,5},{2,6},{3,7},{4,0},{5,1},{6,2},{7,3},{8,12},{9,13},{10,... | collective-permute-start | bytes 196616 | tf_op jit(solution)/shard_map/ppermute | solution.py:22
  8.3 9.8 %collective-permute-start.2 = (bf16[256,128]{1,0:T(8,128)(2,1)}, bf16[256,128]{1,0:T(8,128)(2,1)S(1)}, u32[]{:S(2)}, u32[]{:S(2)}) collective-permute-start(bf16[256,128]{1,0:T(8,128)(2,1)} %get-tuple-element.9), channel_id=1, source_target_pairs={{0,8},{1,9},{2,10},{3,11},{4,12},{5,13},{6,14},{7,15},{8,0},{9,1},... | collective-permute-start | bytes 196616 | tf_op jit(solution)/shard_map/ppermute | solution.py:22
  12.7 6.4 %collective-permute-start.3 = (bf16[256,128]{1,0:T(8,128)(2,1)}, bf16[256,128]{1,0:T(8,128)(2,1)S(1)}, u32[]{:S(2)}, u32[]{:S(2)}) collective-permute-start(bf16[256,128]{1,0:T(8,128)(2,1)} %get-tuple-element.9), channel_id=1, source_target_pairs={{0,12},{1,13},{2,14},{3,15},{4,8},{5,9},{6,10},{7,11},{8,4},{9,5},... | collective-permute-start | bytes 196616 | tf_op jit(solution)/shard_map/ppermute | solution.py:22
  15.0 10.4 %collective-permute-start.13 = (bf16[4,256,128]{2,1,0:T(8,128)(2,1)S(1)}, bf16[4,256,128]{2,1,0:T(8,128)(2,1)S(1)}, u32[]{:S(2)}, u32[]{:S(2)}) collective-permute-start(bf16[4,256,128]{2,1,0:T(8,128)(2,1)S(1)} %pad_maximum_fusion.1), channel_id=1, source_target_pairs={{0,2},{1,3},{2,0},{3,1},{4,6},{5,7},{6,4},{7,5},{8,10},{9,11},{10,... | collective-permute-start | bytes 786440 | tf_op jit(solution)/shard_map/ppermute | solution.py:22
  16.6 8.3 %collective-permute-start.14 = (bf16[4,256,128]{2,1,0:T(8,128)(2,1)S(1)}, bf16[4,256,128]{2,1,0:T(8,128)(2,1)S(1)}, u32[]{:S(2)}, u32[]{:S(2)}) collective-permute-start(bf16[4,256,128]{2,1,0:T(8,128)(2,1)S(1)} %pad_maximum_fusion.1), channel_id=1, source_target_pairs={{0,16},{16,0},{1,17},{17,1},{2,18},{18,2},{3,19},{19,3},{4,20},{20... | collective-permute-start | bytes 786440 | tf_op jit(solution)/shard_map/ppermute | solution.py:22
  20.0 10.6 %collective-permute-start.4 = (bf16[4,256,128]{2,1,0:T(8,128)(2,1)S(1)}, bf16[4,256,128]{2,1,0:T(8,128)(2,1)S(1)}, u32[]{:S(2)}, u32[]{:S(2)}) collective-permute-start(bf16[4,256,128]{2,1,0:T(8,128)(2,1)S(1)} %pad_maximum_fusion), channel_id=1, source_target_pairs={{0,2},{1,3},{2,0},{3,1},{4,6},{5,7},{6,4},{7,5},{8,10},{9,11},{10,... | collective-permute-start | bytes 786440 | tf_op jit(solution)/shard_map/ppermute | solution.py:22
  21.6 8.9 %collective-permute-start.5 = (bf16[4,256,128]{2,1,0:T(8,128)(2,1)S(1)}, bf16[4,256,128]{2,1,0:T(8,128)(2,1)S(1)}, u32[]{:S(2)}, u32[]{:S(2)}) collective-permute-start(bf16[4,256,128]{2,1,0:T(8,128)(2,1)S(1)} %pad_maximum_fusion), channel_id=1, source_target_pairs={{0,16},{16,0},{1,17},{17,1},{2,18},{18,2},{3,19},{19,3},{4,20},{20... | collective-permute-start | bytes 786440 | tf_op jit(solution)/shard_map/ppermute | solution.py:22
  24.9 10.9 %collective-permute-start.15 = (bf16[2,256,128]{2,1,0:T(8,128)(2,1)S(1)}, bf16[2,256,128]{2,1,0:T(8,128)(2,1)S(1)}, u32[]{:S(2)}, u32[]{:S(2)}) collective-permute-start(bf16[2,256,128]{2,1,0:T(8,128)(2,1)S(1)} %slice.18), channel_id=1, source_target_pairs={{0,2},{1,3},{2,0},{3,1},{4,6},{5,7},{6,4},{7,5},{8,10},{9,11},{10,... | collective-permute-start | bytes 393224 | tf_op jit(solution)/shard_map/ppermute | solution.py:22
  25.5 10.4 %collective-permute-start.16 = (bf16[2,256,128]{2,1,0:T(8,128)(2,1)S(1)}, bf16[2,256,128]{2,1,0:T(8,128)(2,1)S(1)}, u32[]{:S(2)}, u32[]{:S(2)}) collective-permute-start(bf16[2,256,128]{2,1,0:T(8,128)(2,1)S(1)} %slice.19), channel_id=1, source_target_pairs={{0,16},{16,0},{1,17},{17,1},{2,18},{18,2},{3,19},{19,3},{4,20},{20... | collective-permute-start | bytes 393224 | tf_op jit(solution)/shard_map/ppermute | solution.py:22
  30.5 5.0 %collective-permute-start.6 = (bf16[2,256,128]{2,1,0:T(8,128)(2,1)S(1)}, bf16[2,256,128]{2,1,0:T(8,128)(2,1)S(1)}, u32[]{:S(2)}, u32[]{:S(2)}) collective-permute-start(bf16[2,256,128]{2,1,0:T(8,128)(2,1)S(1)} %slice.16), channel_id=1, source_target_pairs={{0,2},{1,3},{2,0},{3,1},{4,6},{5,7},{6,4},{7,5},{8,10},{9,11},{10,... | collective-permute-start | bytes 393224 | tf_op jit(solution)/shard_map/ppermute | solution.py:22
  30.6 5.8 %copy-start.5 = (bf16[2,16,24,192]{3,2,1,0:T(8,128)(2,1)S(1)}, bf16[2,16,24,192]{3,2,1,0:T(8,128)(2,1)}, u32[]{:S(2)}) copy-start(bf16[2,16,24,192]{3,2,1,0:T(8,128)(2,1)} %param.12) | copy-start | bytes 884740
  30.6 5.0 %collective-permute-start.7 = (bf16[2,256,128]{2,1,0:T(8,128)(2,1)S(1)}, bf16[2,256,128]{2,1,0:T(8,128)(2,1)S(1)}, u32[]{:S(2)}, u32[]{:S(2)}) collective-permute-start(bf16[2,256,128]{2,1,0:T(8,128)(2,1)S(1)} %slice.17), channel_id=1, source_target_pairs={{0,16},{16,0},{1,17},{17,1},{2,18},{18,2},{3,19},{19,3},{4,20},{20... | collective-permute-start | bytes 393224 | tf_op jit(solution)/shard_map/ppermute | solution.py:22
  35.7 4.6 %copy-start.1 = (bf16[16,256,128]{2,1,0:T(8,128)(2,1)}, bf16[16,256,128]{2,1,0:T(8,128)(2,1)S(1)}, u32[]{:S(2)}) copy-start(bf16[16,256,128]{2,1,0:T(8,128)(2,1)S(1)} %constant_dynamic-update-slice_fusion.rest_0_) | copy-start | bytes 3145732
  35.7 4.6 %collective-permute-start.8 = (bf16[16,256,128]{2,1,0:T(8,128)(2,1)S(1)}, bf16[16,256,128]{2,1,0:T(8,128)(2,1)S(1)}, u32[]{:S(2)}, u32[]{:S(2)}) collective-permute-start(bf16[16,256,128]{2,1,0:T(8,128)(2,1)S(1)} %constant_dynamic-update-slice_fusion.rest_0_), channel_id=1, source_target_pairs={{0,1},{1,0},{2,3},{3,2},{4,5},{5,4},{6,7},{7,6},{8,9},{9,8},{10,11... | collective-permute-start | bytes 3145736 | tf_op jit(solution)/shard_map/ppermute | solution.py:22
  35.9 22.1 %copy-start.2 = (bf16[16,256,128]{2,1,0:T(8,128)(2,1)}, bf16[16,256,128]{2,1,0:T(8,128)(2,1)S(1)}, u32[]{:S(2)}) copy-start(bf16[16,256,128]{2,1,0:T(8,128)(2,1)S(1)} %constant_dynamic-update-slice_fusion.8.rest_0_) | copy-start | bytes 3145732
  35.9 22.0 %collective-permute-start.17 = (bf16[16,256,128]{2,1,0:T(8,128)(2,1)S(1)}, bf16[16,256,128]{2,1,0:T(8,128)(2,1)}, u32[]{:S(2)}, u32[]{:S(2)}) collective-permute-start(bf16[16,256,128]{2,1,0:T(8,128)(2,1)S(1)} %constant_dynamic-update-slice_fusion.8.rest_0_), channel_id=1, source_target_pairs={{0,1},{1,0},{2,3},{3,2},{4,5},{5,4},{6,7},{7,6},{8,9},{9,8},{10,11... | collective-permute-start | bytes 3145736 | tf_op jit(solution)/shard_map/ppermute | solution.py:22
  36.5 3.7 %copy-start = (bf16[2,16,24,192]{3,1,2,0:T(8,128)(2,1)}, bf16[2,16,24,192]{3,1,2,0:T(8,128)(2,1)S(1)}, u32[]{:S(2)}) copy-start(bf16[2,16,24,192]{3,1,2,0:T(8,128)(2,1)S(1)} %copy.18) | copy-start | bytes 884740
  36.6 3.7 %collective-permute-start = (bf16[2,24,16,192]{3,2,1,0:T(8,128)(2,1)S(1)}, bf16[2,24,16,192]{3,2,1,0:T(8,128)(2,1)}, u32[]{:S(2)}, u32[]{:S(2)}) collective-permute-start(bf16[2,24,16,192]{3,2,1,0:T(8,128)(2,1)S(1)} %bitcast.31), channel_id=1, source_target_pairs={{0,1},{1,2},{2,3},{3,4},{4,5},{5,6},{6,7},{7,8},{8,9},{9,10},{10,1... | collective-permute-start | bytes 884744 | tf_op jit(solution)/shard_map/ppermute | solution.py:27
  40.3 1.0 copy-start.3
  48.7 9.2 %collective-permute-start.9 = (bf16[2,24,16,192]{3,2,1,0:T(8,128)(2,1)}, bf16[2,24,16,192]{3,2,1,0:T(8,128)(2,1)S(1)}, u32[]{:S(2)}, u32[]{:S(2)}) collective-permute-start(bf16[2,24,16,192]{3,2,1,0:T(8,128)(2,1)} %shard_map.119.own_ref), channel_id=1, source_target_pairs={{0,1},{1,2},{2,3},{3,4},{4,5},{5,6},{6,7},{7,8},{8,9},{9,10},{10,1... | collective-permute-start | bytes 884744 | tf_op jit(solution)/shard_map/ppermute | solution.py:27
  57.9 0.7 copy-start.4
  58.7 30.1 %copy-start.8 = (s32[192]{0:T(256)S(1)}, s32[192]{0:T(256)}, u32[]{:S(2)}) copy-start(s32[192]{0:T(256)} %param.23) | copy-start | bytes 2308
  67.5 8.3 %collective-permute-start.18 = (f32[96,128]{1,0:T(8,128)}, f32[96,128]{1,0:T(8,128)S(1)}, u32[]{:S(2)}, u32[]{:S(2)}) collective-permute-start(f32[96,128]{1,0:T(8,128)} %get-tuple-element.12), channel_id=1, source_target_pairs={{0,1},{1,2},{2,3},{3,4},{4,5},{5,6},{6,7},{7,8},{8,9},{9,10},{10,1... | collective-permute-start | bytes 147464 | tf_op jit(solution)/shard_map/ppermute | solution.py:27
  76.6 12.3 %collective-permute-start.19 = (bf16[96,128]{1,0:T(8,128)(2,1)S(1)}, bf16[96,128]{1,0:T(8,128)(2,1)S(1)}, u32[]{:S(2)}, u32[]{:S(2)}) collective-permute-start(bf16[96,128]{1,0:T(8,128)(2,1)S(1)} %get-tuple-element.14), channel_id=1, source_target_pairs={{0,4},{1,5},{2,6},{3,7},{4,0},{5,1},{6,2},{7,3},{8,12},{9,13},{10,... | collective-permute-start | bytes 73736 | tf_op jit(solution)/shard_map/ppermute | solution.py:22
  86.0 4.7 %collective-permute-start.20 = (bf16[96,128]{1,0:T(8,128)(2,1)S(1)}, bf16[96,128]{1,0:T(8,128)(2,1)S(1)}, u32[]{:S(2)}, u32[]{:S(2)}) collective-permute-start(bf16[96,128]{1,0:T(8,128)(2,1)S(1)} %get-tuple-element.14), channel_id=1, source_target_pairs={{0,8},{1,9},{2,10},{3,11},{4,12},{5,13},{6,14},{7,15},{8,0},{9,1},... | collective-permute-start | bytes 73736 | tf_op jit(solution)/shard_map/ppermute | solution.py:22
  87.8 5.6 %collective-permute-start.21 = (bf16[96,128]{1,0:T(8,128)(2,1)S(1)}, bf16[96,128]{1,0:T(8,128)(2,1)S(1)}, u32[]{:S(2)}, u32[]{:S(2)}) collective-permute-start(bf16[96,128]{1,0:T(8,128)(2,1)S(1)} %get-tuple-element.14), channel_id=1, source_target_pairs={{0,12},{1,13},{2,14},{3,15},{4,8},{5,9},{6,10},{7,11},{8,4},{9,5},... | collective-permute-start | bytes 73736 | tf_op jit(solution)/shard_map/ppermute | solution.py:22
  93.4 4.7 %collective-permute-start.22 = (bf16[384,128]{1,0:T(8,128)(2,1)S(1)}, bf16[384,128]{1,0:T(8,128)(2,1)S(1)}, u32[]{:S(2)}, u32[]{:S(2)}) collective-permute-start(bf16[384,128]{1,0:T(8,128)(2,1)S(1)} %pad_maximum_fusion.2), channel_id=1, source_target_pairs={{0,2},{1,3},{2,0},{3,1},{4,6},{5,7},{6,4},{7,5},{8,10},{9,11},{10,... | collective-permute-start | bytes 294920 | tf_op jit(solution)/shard_map/ppermute | solution.py:22
  98.1 1.7 %copy-start.6 = (bf16[768,128]{1,0:T(8,128)(2,1)}, bf16[768,128]{1,0:T(8,128)(2,1)S(1)}, u32[]{:S(2)}) copy-start(bf16[768,128]{1,0:T(8,128)(2,1)S(1)} %constant_dynamic-update-slice_fusion.16.rest_0_) | copy-start | bytes 589828
  98.1 1.6 %collective-permute-start.23 = (bf16[768,128]{1,0:T(8,128)(2,1)S(1)}, bf16[768,128]{1,0:T(8,128)(2,1)S(1)}, u32[]{:S(2)}, u32[]{:S(2)}) collective-permute-start(bf16[768,128]{1,0:T(8,128)(2,1)S(1)} %constant_dynamic-update-slice_fusion.16.rest_0_), channel_id=1, source_target_pairs={{0,1},{1,0},{2,3},{3,2},{4,5},{5,4},{6,7},{7,6},{8,9},{9,8},{10,11... | collective-permute-start | bytes 589832 | tf_op jit(solution)/shard_map/ppermute | solution.py:22
  99.8 0.7 copy-start.7

commit v2 on v1

--- a/solution.py
+++ b/solution.py
@@ -240,7 +240,7 @@
     clips_ref, first_ref, own_ref, rim_ref, features_ref, gain_ref, pick_ref, wide_ref, *rest,
     taps, unit_channels,
 ):
-    *unit_refs, own_out, next_out, head_x, low_x, high_x, rhs, staged, plain, windows = rest
+    *unit_refs, parts_out, head_x, low_x, high_x, rhs, staged, plain, windows = rest
     frames, breadth, height, channels = own_ref.shape
     pixels = breadth * height
     rows, columns = height // 2, breadth // 2
@@ -311,10 +311,11 @@
         return total
 
     own = range(frames)
-    own_out[...] = jnp.concatenate([gathered(frame, own) for frame in own], axis=1)
-    next_out[...] = jnp.concatenate(
-        [gathered(frame + frames, own) for frame in own], axis=1
-    )
+    parts = [
+        jnp.concatenate([gathered(frame + ahead, own) for frame in own], axis=1)
+        for ahead in (0, frames)
+    ]
+    parts_out[...] = jnp.concatenate(parts, axis=0).astype(jnp.bfloat16)
 
 
 def conv_scratch(frames, breadth, height, taps, outputs):
@@ -326,21 +327,21 @@
     ]
 
 
-def embed_kernel(
-    spot_ref, lane_ref, embed_ref, scale_ref, shift_ref, *rest
-):
+def embed_kernel(place_ref, embed_ref, scale_ref, shift_ref, *rest):
     *patch_refs, out_ref = rest
     width = embed_ref.shape[0]
-    total = jnp.zeros((out_ref.shape[0], LANES), jnp.float32)
+    tokens = out_ref.shape[0]
+    total = jnp.zeros((tokens, LANES), jnp.float32)
     begin = 0
     for patch_ref in patch_refs:
         count = patch_ref.shape[0]
-        spots = lax.broadcasted_iota(jnp.int32, (out_ref.shape[0], count), 1) + begin
-        chosen = jnp.where(spots == spot_ref[...], 1.0, 0.0).astype(jnp.bfloat16)
+        spots = lax.broadcasted_iota(jnp.int32, (tokens, count), 1) + begin
+        chosen = (spots == place_ref[:, 0:1]) | (spots == place_ref[:, 1:2])
+        chosen = jnp.where(chosen, 1.0, 0.0).astype(jnp.bfloat16)
         total = total + jnp.dot(chosen, patch_ref[...], preferred_element_type=jnp.float32)
         begin += count
     turned = pltpu.roll(total, width, 1)
-    ordered = jnp.where(lane_ref[...] == 0, total, turned)[:, :width].astype(jnp.bfloat16)
+    ordered = jnp.where(place_ref[:, 2:3] == 0, total, turned)[:, :width].astype(jnp.bfloat16)
     embedded = jnp.dot(ordered, embed_ref[...], preferred_element_type=jnp.float32)
     center = jnp.mean(embedded, axis=-1, keepdims=True)
     centered = embedded - center
@@ -349,10 +350,15 @@
     out_ref[...] = (normed * (1.0 + scale_ref[...]) + shift_ref[...]).astype(out_ref.dtype)
 
 
-def gather_units(unit):
-    line = jnp.stack([unit] + [xor_permute(unit, "ctx", 4 * step) for step in (1, 2, 3)])
-    across = xor_permute(line, "ctx", 2)
-    other = xor_permute(line, "groups", 1)
+def along_line(unit):
+    return jnp.stack([unit] + [xor_permute(unit, "ctx", 4 * step) for step in (1, 2, 3)])
+
+
+def round_square(line):
+    return xor_permute(line, "ctx", 2), xor_permute(line, "groups", 1)
+
+
+def whole_chip(line, across, other):
     corner_low = xor_permute(other[:2], "ctx", 2)
     corner_high = xor_permute(across[2:], "groups", 1)
     chip = jnp.concatenate([line, across, other, corner_low, corner_high])
@@ -392,21 +398,46 @@
     unit_channels = channels // units
 
     by_output = [weight.transpose(2, 0, 1) for weight in (weight_first, weight_second)]
+    channel_map = unit_channel_map(grid, group, device, unit_channels, units)
+    pick = (channel_map[:, None] == jnp.arange(channels, dtype=jnp.int32)).astype(jnp.bfloat16)
+    wide = expand_weight_out(weight_out.transpose(0, 2, 1))
+    turned = features.transpose(0, 2, 1, 3)
+    turned_rim = to_next(turned[frames - 2 :], "ctx")
+
+    spots = (height // 2) * (breadth // 2)
+    frame, spot = token_order // spots, token_order % spots
+    spot = spot % (breadth // 2) * (height // 2) + spot // (breadth // 2)
+    owner = frame // frames
+
+    def piece_of(source):
+        if not grid:
+            return source
+        away = source ^ device
+        return (away % 2 * 2 + away // 2 % 2) * 4 + away // 4
+
+    own_place = piece_of(owner) * 2 * spots + spot
+    sent_place = jnp.where(owner > 0, (piece_of(jnp.maximum(owner - 1, 0)) * 2 + 1) * spots + spot, -1)
+    place = jnp.stack([own_place, sent_place, frame % frames], axis=1)
+
     if grid:
         half = group.astype(jnp.int32).reshape(1)
-        packed = pack_units(half, by_output, unit_channels)
-        units_first, units_second = [gather_units(unit) for unit in packed]
+        packed_first, packed_second = pack_units(half, by_output, unit_channels)
+        line_first = along_line(packed_first)
+        line_first, wide, pick, place = lax.optimization_barrier((line_first, wide, pick, place))
+        square_first = round_square(line_first)
+        line_second = along_line(packed_second)
+        line_second, square_first, turned_rim = lax.optimization_barrier(
+            (line_second, square_first, turned_rim)
+        )
+        units_first = whole_chip(line_first, *square_first)
+        units_second = whole_chip(line_second, *round_square(line_second))
     else:
         units_first, units_second = [
             [pack_whole(lax.all_gather(weight, "ctx", axis=0, tiled=True), units)]
             for weight in by_output
         ]
-    channel_map = unit_channel_map(grid, group, device, unit_channels, units)
-    pick = (channel_map[:, None] == jnp.arange(channels, dtype=jnp.int32)).astype(jnp.bfloat16)
-    wide = expand_weight_out(weight_out.transpose(0, 2, 1))
 
     first = (device * frames).astype(jnp.int32).reshape(1)
-    turned = features.transpose(0, 2, 1, 3)
     scratch = conv_scratch(frames, breadth, height, taps, units * SUBLANES)
     image = jax.ShapeDtypeStruct((frames, breadth, height, channels), jnp.bfloat16)
     second_in = pl.pallas_call(
@@ -417,18 +448,16 @@
         scratch_shapes=scratch,
         compiler_params=PARAMS,
     )(
-        clip_ids, first, turned, to_next(turned[frames - 2 :], "ctx"), gain_first.reshape(1, -1),
+        clip_ids, first, turned, turned_rim, gain_first.reshape(1, -1),
         gain_second.reshape(1, -1), pick, *units_first,
     )
 
     depth = weight_out.shape[2]
-    spots = (height // 2) * (breadth // 2)
-    partial = jax.ShapeDtypeStruct((spots, frames * 4 * depth), jnp.float32)
-    own_part, next_part = pl.pallas_call(
+    parts = pl.pallas_call(
         functools.partial(second_kernel, taps=taps, unit_channels=unit_channels),
-        out_shape=[partial, partial],
+        out_shape=jax.ShapeDtypeStruct((2 * spots, frames * 4 * depth), jnp.bfloat16),
         in_specs=[SMEM_SPEC] * 2 + [VMEM_SPEC] * (6 + len(units_second)),
-        out_specs=[VMEM_SPEC] * 2,
+        out_specs=VMEM_SPEC,
         scratch_shapes=scratch
         + [
             pltpu.VMEM((2, frames * breadth * height, LANES), jnp.float32),
@@ -439,37 +468,22 @@
         clip_ids, first, second_in, to_next(second_in[frames - 2 :], "ctx"), turned,
         gain_third.reshape(1, -1), pick, wide, *units_second,
     )
-    patches = (own_part + to_next(next_part, "ctx")).astype(jnp.bfloat16)
-
-    frame, spot = token_order // spots, token_order % spots
-    spot = spot % (breadth // 2) * (height // 2) + spot // (breadth // 2)
-    owner = frame // frames
     if grid:
-        line = jnp.concatenate([patches] + [xor_permute(patches, "ctx", 4 * k) for k in (1, 2, 3)])
+        line = jnp.concatenate([parts] + [xor_permute(parts, "ctx", 4 * k) for k in (1, 2, 3)])
         sheet = jnp.concatenate([line, xor_permute(line, "ctx", 2)])
         pieces = [sheet, xor_permute(sheet, "ctx", 1)]
-        away = owner ^ device
-        place = (away % 2 * 2 + away // 2 % 2) * 4 + away // 4
     else:
-        pieces = [lax.all_gather(patches, "ctx", axis=0, tiled=True)]
-        place = owner
-    spot = (place * spots + spot).reshape(-1, 1)
-    lane = (frame % frames).reshape(-1, 1)
+        pieces = [lax.all_gather(parts, "ctx", axis=0, tiled=True)]
 
     tokens, width = token_order.shape[0], embed_weight.shape[1]
-    block = 48 if tokens % 48 == 0 else tokens
-    column = pl.BlockSpec((block, 1), lambda i: (i, 0))
-    row = pl.BlockSpec((1, width), lambda i: (0, 0))
     return pl.pallas_call(
         embed_kernel,
         out_shape=jax.ShapeDtypeStruct((tokens, width), jnp.bfloat16),
-        grid=(tokens // block,),
-        in_specs=[column, column, pl.BlockSpec(embed_weight.shape, lambda i: (0, 0)), row, row]
-        + [pl.BlockSpec(piece.shape, lambda i: (0, 0)) for piece in pieces],
-        out_specs=pl.BlockSpec((block, width), lambda i: (i, 0)),
+        in_specs=[VMEM_SPEC] * (4 + len(pieces)),
+        out_specs=VMEM_SPEC,
         compiler_params=PARAMS,
     )(
-        spot, lane, embed_weight, scale_mod.reshape(1, -1), shift_mod.reshape(1, -1), *pieces
+        place, embed_weight, scale_mod.reshape(1, -1), shift_mod.reshape(1, -1), *pieces
     )
 
 

time: 106 us -> 95.9 us (0.905)
  starting transfers between devices: 49.8 us -> 33.3 us
  waiting for transfers between devices: 21.3 us -> 30.1 us
  other arithmetic: 3.4 us -> 1.75 us
  Pallas kernels: 25.7 us -> 24.4 us
    ppermute x3 -> x2, starting transfers between devices: 16.8 us -> 3.62 us  [to_next(): lax.ppermute(value, axis, [(source, source + 1) for source in range(count...]
    ppermute x21, waiting for transfers between devices: 20 us -> 28.6 us  [xor_permute(): lax.ppermute(value, axis, [(source, source ^ mask) for source in range(co...]
    ppermute x21, starting transfers between devices: 33 us -> 29.6 us  [xor_permute(): lax.ppermute(value, axis, [(source, source ^ mask) for source in range(co...]
    another operation x2 -> x3, other arithmetic: 1.75 us -> 0.08 us  [the longest x2 0.07 us: along_line(): jnp.stack([unit] + [xor_permute(unit, 'ctx', 4 * step) for step in (1, 2,...]
    reshape x2 -> x0, local copies, waits for them, and re-layouts: 1.52 us -> none  [the longest x1 0.76 us: body(): spot = (place * spots + spot).reshape(-1, 1)]
    pallas_call x1, Pallas kernels: 5.29 us -> 4.09 us  [body(): pl.pallas_call(embed_kernel, out_shape=jax.ShapeDtypeStruct((tokens, widt...]
    unnamed x35, local copies, waits for them, and re-layouts: 3.67 us -> 4.74 us
  transfers between devices with their start and end apart: 24 -> 23, of which waited for: 11 -> 12; matrix products, arithmetic and copies ran while one was open for 5% -> 4% of each run, Pallas kernels for 9% -> 10%
where the time goes in v2:
time: 95.9 us; the launch traced here: 95.5 us
  starting transfers between devices  33.3 us (35%)
  waiting for transfers between devices  30.1 us (31%)
  Pallas kernels  24.4 us (25%)
  local copies, waits for them, and re-layouts  5.62 us (6%)
  other arithmetic  1.75 us (2%)
    ppermute x21, starting transfers between devices, xor_permute(): lax.ppermute(value, axis, [(source, source ^ mask) for source in range(co...  29.6 us
    ppermute x21, waiting for transfers between devices, xor_permute(): lax.ppermute(value, axis, [(source, source ^ mask) for source in range(co...  28.6 us
    pallas_call x1, Pallas kernels, body(): pl.pallas_call(functools.partial(second_kernel, taps=taps, unit_channels=...  8.78 us
    pallas_call x1, Pallas kernels, body(): pl.pallas_call(functools.partial(first_kernel, taps=taps, unit_channels=u...  7.51 us
    unnamed x35, local copies, waits for them, and re-layouts  4.74 us
    pallas_call x1, Pallas kernels, body(): pl.pallas_call(embed_kernel, out_shape=jax.ShapeDtypeStruct((tokens, widt...  4.09 us
    ppermute x2, starting transfers between devices, to_next(): lax.ppermute(value, axis, [(source, source + 1) for source in range(count...  3.62 us
    pallas_call x1, Pallas kernels, expand_weight_out(): pl.pallas_call(expand_kernel, out_shape=jax.ShapeDtypeStruct((16, 12 * de...  2.27 us
  transfers between devices with their start and end apart: 23, of which 12 were waited for; matrix products, arithmetic and copies ran while one was open for 4% of the time, Pallas kernels for 10%

profile of v2, /device:TPU:0, one launch (start us, length us, event | category | flops | bytes accessed | tf_op | source)
XLA Modules:
  0.0 95.5 jit_solution(9405663549605060535)
XLA Ops:
  0.0 1.8 %shard_map.118 = (bf16[256,128]{1,0:T(8,128)(2,1)}, bf16[256,128]{1,0:T(8,128)(2,1)}) custom-call(s32[1]{0:T(128)} %bitcast.half_ref, bf16[12,27,192]{2,1,0:T(8,128)(2,1)} %bitcast.28, bf16[12,27,192]{2,1,0:T(8,128)(2,1)} %bitcast.29), custom_call_target="tpu_custom_call" | custom-call | tf_op jit(solution)/shard_map/pallas_call | solution.py:54
  1.8 5.0 %collective-permute-start.2 = (bf16[256,128]{1,0:T(8,128)(2,1)}, bf16[256,128]{1,0:T(8,128)(2,1)S(1)}, u32[]{:S(2)}, u32[]{:S(2)}) collective-permute-start(bf16[256,128]{1,0:T(8,128)(2,1)} %get-tuple-element.15), channel_id=1, source_target_pairs={{0,12},{1,13},{2,14},{3,15},{4,8},{5,9},{6,10},{7,11},{8,4},{9,5},... | collective-permute-start | bytes 196616 | tf_op jit(solution)/shard_map/ppermute | solution.py:22
  6.8 0.6 collective-permute-start
  7.4 3.8 %collective-permute-start.5 = (bf16[256,128]{1,0:T(8,128)(2,1)}, bf16[256,128]{1,0:T(8,128)(2,1)S(1)}, u32[]{:S(2)}, u32[]{:S(2)}) collective-permute-start(bf16[256,128]{1,0:T(8,128)(2,1)} %get-tuple-element.17), channel_id=1, source_target_pairs={{0,12},{1,13},{2,14},{3,15},{4,8},{5,9},{6,10},{7,11},{8,4},{9,5},... | collective-permute-start | bytes 196616 | tf_op jit(solution)/shard_map/ppermute | solution.py:22
  11.2 1.1 %copy.21 = bf16[2,16,24,192]{3,1,2,0:T(8,128)(2,1)S(1)} copy(bf16[2,16,24,192]{3,2,1,0:T(8,128)(2,1)} %param.12) | data formatting | bytes 589824 | tf_op args[0]
  12.3 1.3 %collective-permute-start.8 = (bf16[2,24,16,192]{3,2,1,0:T(8,128)(2,1)S(1)}, bf16[2,24,16,192]{3,2,1,0:T(8,128)(2,1)S(1)}, u32[]{:S(2)}, u32[]{:S(2)}) collective-permute-start(bf16[2,24,16,192]{3,2,1,0:T(8,128)(2,1)S(1)} %bitcast.24), channel_id=1, source_target_pairs={{0,1},{1,2},{2,3},{3,4},{4,5},{5,6},{6,7},{7,8},{8,9},{9,10},{10,1... | collective-permute-start | bytes 884744 | tf_op jit(solution)/shard_map/ppermute | solution.py:27
  13.6 2.3 %shard_map.119.wide_ref = bf16[16,192,256]{2,1,0:T(8,128)(2,1)} custom-call(bf16[27,16,192]{2,1,0:T(8,128)(2,1)} %bitcast.27), custom_call_target="tpu_custom_call" | custom-call | tf_op jit(solution)/shard_map/pallas_call | solution.py:95
  15.9 0.8 fusion.pick_ref
  16.8 0.0 collective-permute-done.1
  16.9 2.2 %collective-permute-start.6 = (bf16[4,256,128]{2,1,0:T(8,128)(2,1)S(1)}, bf16[4,256,128]{2,1,0:T(8,128)(2,1)S(1)}, u32[]{:S(2)}, u32[]{:S(2)}) collective-permute-start(bf16[4,256,128]{2,1,0:T(8,128)(2,1)S(1)} %pad_maximum_fusion), channel_id=1, source_target_pairs={{0,2},{1,3},{2,0},{3,1},{4,6},{5,7},{6,4},{7,5},{8,10},{9,11},{10,... | collective-permute-start | bytes 786440 | tf_op jit(solution)/shard_map/ppermute | solution.py:22
  19.0 1.5 %collective-permute-start.7 = (bf16[4,256,128]{2,1,0:T(8,128)(2,1)S(1)}, bf16[4,256,128]{2,1,0:T(8,128)(2,1)S(1)}, u32[]{:S(2)}, u32[]{:S(2)}) collective-permute-start(bf16[4,256,128]{2,1,0:T(8,128)(2,1)S(1)} %pad_maximum_fusion), channel_id=1, source_target_pairs={{0,16},{16,0},{1,17},{17,1},{2,18},{18,2},{3,19},{19,3},{4,20},{20... | collective-permute-start | bytes 786440 | tf_op jit(solution)/shard_map/ppermute | solution.py:22
  20.5 0.8 collective-permute-start.3
  21.3 4.4 %collective-permute-done.4 = bf16[256,128]{1,0:T(8,128)(2,1)S(1)} collective-permute-done((bf16[256,128]{1,0:T(8,128)(2,1)S(1)}, bf16[256,128]{1,0:T(8,128)(2,1)S(1)}, u32[]{:S(2)}, u32[]{:S(2)}) %collective-permute-start.4) | collective-permute-done | bytes 65568 | tf_op jit(solution)/shard_map/ppermute | solution.py:22
  25.8 0.5 collective-permute-done.3
  26.3 1.1 %collective-permute-done.7 = bf16[4,256,128]{2,1,0:T(8,128)(2,1)S(1)} collective-permute-done((bf16[4,256,128]{2,1,0:T(8,128)(2,1)S(1)}, bf16[4,256,128]{2,1,0:T(8,128)(2,1)S(1)}, u32[]{:S(2)}, u32[]{:S(2)}) %collective-permute-start.7) | collective-permute-done | bytes 262176 | tf_op jit(solution)/shard_map/ppermute | solution.py:22
  27.5 0.9 collective-permute-start.13
  28.4 1.5 %collective-permute-start.14 = (bf16[4,256,128]{2,1,0:T(8,128)(2,1)S(1)}, bf16[4,256,128]{2,1,0:T(8,128)(2,1)S(1)}, u32[]{:S(2)}, u32[]{:S(2)}) collective-permute-start(bf16[4,256,128]{2,1,0:T(8,128)(2,1)S(1)} %pad_maximum_fusion.1), channel_id=1, source_target_pairs={{0,16},{16,0},{1,17},{17,1},{2,18},{18,2},{3,19},{19,3},{4,20},{20... | collective-permute-start | bytes 786440 | tf_op jit(solution)/shard_map/ppermute | solution.py:22
  29.9 1.2 %collective-permute-start.9 = (bf16[2,256,128]{2,1,0:T(8,128)(2,1)S(1)}, bf16[2,256,128]{2,1,0:T(8,128)(2,1)S(1)}, u32[]{:S(2)}, u32[]{:S(2)}) collective-permute-start(bf16[2,256,128]{2,1,0:T(8,128)(2,1)S(1)} %slice.12), channel_id=1, source_target_pairs={{0,2},{1,3},{2,0},{3,1},{4,6},{5,7},{6,4},{7,5},{8,10},{9,11},{10,... | collective-permute-start | bytes 393224 | tf_op jit(solution)/shard_map/ppermute | solution.py:22
  31.2 0.6 collective-permute-start.10
  31.8 6.1 %collective-permute-done.9 = bf16[2,256,128]{2,1,0:T(8,128)(2,1)S(1)} collective-permute-done((bf16[2,256,128]{2,1,0:T(8,128)(2,1)S(1)}, bf16[2,256,128]{2,1,0:T(8,128)(2,1)S(1)}, u32[]{:S(2)}, u32[]{:S(2)}) %collective-permute-start.9) | collective-permute-done | bytes 131104 | tf_op jit(solution)/shard_map/ppermute | solution.py:22
  37.9 1.3 %collective-permute-done.10 = bf16[2,256,128]{2,1,0:T(8,128)(2,1)S(1)} collective-permute-done((bf16[2,256,128]{2,1,0:T(8,128)(2,1)S(1)}, bf16[2,256,128]{2,1,0:T(8,128)(2,1)S(1)}, u32[]{:S(2)}, u32[]{:S(2)}) %collective-permute-start.10) | collective-permute-done | bytes 131104 | tf_op jit(solution)/shard_map/ppermute | solution.py:22
  39.3 0.0 copy-start.1
  39.3 0.1 collective-permute-start.11
  39.4 0.5 collective-permute-start.15
  39.9 1.6 %collective-permute-start.16 = (bf16[2,256,128]{2,1,0:T(8,128)(2,1)S(1)}, bf16[2,256,128]{2,1,0:T(8,128)(2,1)S(1)}, u32[]{:S(2)}, u32[]{:S(2)}) collective-permute-start(bf16[2,256,128]{2,1,0:T(8,128)(2,1)S(1)} %slice.17), channel_id=1, source_target_pairs={{0,16},{16,0},{1,17},{17,1},{2,18},{18,2},{3,19},{19,3},{4,20},{20... | collective-permute-start | bytes 393224 | tf_op jit(solution)/shard_map/ppermute | solution.py:22
  41.5 3.8 %collective-permute-done.15 = bf16[2,256,128]{2,1,0:T(8,128)(2,1)S(1)} collective-permute-done((bf16[2,256,128]{2,1,0:T(8,128)(2,1)S(1)}, bf16[2,256,128]{2,1,0:T(8,128)(2,1)S(1)}, u32[]{:S(2)}, u32[]{:S(2)}) %collective-permute-start.15) | collective-permute-done | bytes 131104 | tf_op jit(solution)/shard_map/ppermute | solution.py:22
  45.4 0.2 collective-permute-done.16
  45.6 0.1 collective-permute-start.17
  45.7 1.1 %copy-done.3 = bf16[16,256,128]{2,1,0:T(8,128)(2,1)} copy-done((bf16[16,256,128]{2,1,0:T(8,128)(2,1)}, bf16[16,256,128]{2,1,0:T(8,128)(2,1)S(1)}, u32[]{:S(2)}) %copy-start.3) | copy-done | bytes 1048600
  46.8 7.5 %shard_map.120.own_ref = bf16[2,24,16,192]{3,2,1,0:T(8,128)(2,1)} custom-call(s32[32]{0:T(128)} %clips_ref.3, s32[1]{0:T(128)} %bitcast.13.first_ref, bf16[2,24,16,192]{3,2,1,0:T(8,128)(2,1)} %bitcast.25, bf16[2,24,16,192]{3,2,1,0:T(8,128)(2,1)} %copy-done.7, f32[1,192]{1,0:T(1,128)} %bitcast.43, f32[1,192]{1,0:T(1,128)} %bitcast.44, ...), custom_call_target="tpu_custom_call" | custom-call | tf_op jit(solution)/shard_map/pallas_call | solution.py:443
  54.3 2.3 %collective-permute-start.12 = (bf16[2,24,16,192]{3,2,1,0:T(8,128)(2,1)}, bf16[2,24,16,192]{3,2,1,0:T(8,128)(2,1)S(1)}, u32[]{:S(2)}, u32[]{:S(2)}) collective-permute-start(bf16[2,24,16,192]{3,2,1,0:T(8,128)(2,1)} %shard_map.120.own_ref), channel_id=1, source_target_pairs={{0,1},{1,2},{2,3},{3,4},{4,5},{5,6},{6,7},{7,8},{8,9},{9,10},{10,1... | collective-permute-start | bytes 884744 | tf_op jit(solution)/shard_map/ppermute | solution.py:27
  56.6 1.5 %collective-permute-done.12.rim_ref = bf16[2,24,16,192]{3,2,1,0:T(8,128)(2,1)S(1)} collective-permute-done((bf16[2,24,16,192]{3,2,1,0:T(8,128)(2,1)}, bf16[2,24,16,192]{3,2,1,0:T(8,128)(2,1)S(1)}, u32[]{:S(2)}, u32[]{:S(2)}) %collective-permute-start.12) | collective-permute-done | bytes 294944 | tf_op jit(solution)/shard_map/ppermute | solution.py:27
  58.1 0.7 copy-done.5
  58.8 8.8 %shard_map.121 = bf16[192,128]{1,0:T(8,128)(2,1)} custom-call(s32[32]{0:T(128)} %clips_ref.3, s32[1]{0:T(128)} %bitcast.13.first_ref, bf16[2,24,16,192]{3,2,1,0:T(8,128)(2,1)} %shard_map.120.own_ref, bf16[2,24,16,192]{3,2,1,0:T(8,128)(2,1)} %copy-done.5, bf16[2,24,16,192]{3,2,1,0:T(8,128)(2,1)} %bitcast.26, f32[1,192]{1,0:T(1,128)} %bitcast.45, ...), custom_call_target="tpu_custom_call" | custom-call | tf_op jit(solution)/shard_map/pallas_call | solution.py:456
  67.6 6.8 %collective-permute-start.18 = (bf16[192,128]{1,0:T(8,128)(2,1)}, bf16[192,128]{1,0:T(8,128)(2,1)S(1)}, u32[]{:S(2)}, u32[]{:S(2)}) collective-permute-start(bf16[192,128]{1,0:T(8,128)(2,1)} %shard_map.121), channel_id=1, source_target_pairs={{0,4},{1,5},{2,6},{3,7},{4,0},{5,1},{6,2},{7,3},{8,12},{9,13},{10,... | collective-permute-start | bytes 147464 | tf_op jit(solution)/shard_map/ppermute | solution.py:22
  74.4 1.7 %collective-permute-start.19 = (bf16[192,128]{1,0:T(8,128)(2,1)}, bf16[192,128]{1,0:T(8,128)(2,1)S(1)}, u32[]{:S(2)}, u32[]{:S(2)}) collective-permute-start(bf16[192,128]{1,0:T(8,128)(2,1)} %shard_map.121), channel_id=1, source_target_pairs={{0,8},{1,9},{2,10},{3,11},{4,12},{5,13},{6,14},{7,15},{8,0},{9,1},... | collective-permute-start | bytes 147464 | tf_op jit(solution)/shard_map/ppermute | solution.py:22
  76.2 0.6 collective-permute-start.20
  76.8 0.8 constant_dynamic-update-slice_fusion.14
  77.6 2.4 %collective-permute-done.19 = bf16[192,128]{1,0:T(8,128)(2,1)S(1)} collective-permute-done((bf16[192,128]{1,0:T(8,128)(2,1)}, bf16[192,128]{1,0:T(8,128)(2,1)S(1)}, u32[]{:S(2)}, u32[]{:S(2)}) %collective-permute-start.19) | collective-permute-done | bytes 49184 | tf_op jit(solution)/shard_map/ppermute | solution.py:22
  80.1 2.2 %collective-permute-done.20 = bf16[192,128]{1,0:T(8,128)(2,1)S(1)} collective-permute-done((bf16[192,128]{1,0:T(8,128)(2,1)}, bf16[192,128]{1,0:T(8,128)(2,1)S(1)}, u32[]{:S(2)}, u32[]{:S(2)}) %collective-permute-start.20) | collective-permute-done | bytes 49184 | tf_op jit(solution)/shard_map/ppermute | solution.py:22
  82.3 0.8 pad_maximum_fusion.2
  83.1 0.1 collective-permute-start.21
  83.2 5.6 %collective-permute-done.21 = bf16[768,128]{1,0:T(8,128)(2,1)S(1)} collective-permute-done((bf16[768,128]{1,0:T(8,128)(2,1)S(1)}, bf16[768,128]{1,0:T(8,128)(2,1)S(1)}, u32[]{:S(2)}, u32[]{:S(2)}) %collective-permute-start.21) | collective-permute-done | bytes 196640 | tf_op jit(solution)/shard_map/ppermute | solution.py:22
  88.9 0.1 collective-permute-start.22
  89.0 0.8 copy.19.place_ref
  89.7 0.9 collective-permute-done.22.rest_1_
  90.7 0.7 copy-done.6
  91.4 4.1 %shard_map.122 = bf16[192,3072]{1,0:T(8,128)(2,1)} custom-call(s32[192,3]{1,0:T(8,128)} %copy.19.place_ref, bf16[64,3072]{1,0:T(8,128)(2,1)} %embed_ref.1, f32[1,3072]{1,0:T(1,128)} %bitcast.38, f32[1,3072]{1,0:T(1,128)} %bitcast.39, bf16[1536,128]{1,0:T(8,128)(2,1)} %copy-done.4, bf16[1536,128]{1,0:T(8,128)(2,1)} %copy-done.6), custom_call_target="tpu_custom_call" | custom-call | tf_op jit(solution)/shard_map/pallas_call | solution.py:479
  (54 shorter events, 0.6 us)
Async XLA Ops:
  0.0 16.7 %copy-start.10 = (s32[192]{0:T(256)S(1)}, s32[192]{0:T(256)}, u32[]{:S(2)}) copy-start(s32[192]{0:T(256)} %param.23) | copy-start | bytes 2308
  1.8 15.0 %copy-start.9 = (bf16[256,128]{1,0:T(8,128)(2,1)S(1)}, bf16[256,128]{1,0:T(8,128)(2,1)}, u32[]{:S(2)}) copy-start(bf16[256,128]{1,0:T(8,128)(2,1)} %get-tuple-element.15) | copy-start | bytes 196612
  1.8 15.0 %collective-permute-start.2 = (bf16[256,128]{1,0:T(8,128)(2,1)}, bf16[256,128]{1,0:T(8,128)(2,1)S(1)}, u32[]{:S(2)}, u32[]{:S(2)}) collective-permute-start(bf16[256,128]{1,0:T(8,128)(2,1)} %get-tuple-element.15), channel_id=1, source_target_pairs={{0,12},{1,13},{2,14},{3,15},{4,8},{5,9},{6,10},{7,11},{8,4},{9,5},... | collective-permute-start | bytes 196616 | tf_op jit(solution)/shard_map/ppermute | solution.py:22
  6.8 10.0 %collective-permute-start.1 = (bf16[256,128]{1,0:T(8,128)(2,1)}, bf16[256,128]{1,0:T(8,128)(2,1)S(1)}, u32[]{:S(2)}, u32[]{:S(2)}) collective-permute-start(bf16[256,128]{1,0:T(8,128)(2,1)} %get-tuple-element.15), channel_id=1, source_target_pairs={{0,8},{1,9},{2,10},{3,11},{4,12},{5,13},{6,14},{7,15},{8,0},{9,1},... | collective-permute-start | bytes 196616 | tf_op jit(solution)/shard_map/ppermute | solution.py:22
  6.8 10.0 %collective-permute-start = (bf16[256,128]{1,0:T(8,128)(2,1)}, bf16[256,128]{1,0:T(8,128)(2,1)S(1)}, u32[]{:S(2)}, u32[]{:S(2)}) collective-permute-start(bf16[256,128]{1,0:T(8,128)(2,1)} %get-tuple-element.15), channel_id=1, source_target_pairs={{0,4},{1,5},{2,6},{3,7},{4,0},{5,1},{6,2},{7,3},{8,12},{9,13},{10,... | collective-permute-start | bytes 196616 | tf_op jit(solution)/shard_map/ppermute | solution.py:22
  7.4 13.1 %copy-start.8 = (bf16[256,128]{1,0:T(8,128)(2,1)S(1)}, bf16[256,128]{1,0:T(8,128)(2,1)}, u32[]{:S(2)}) copy-start(bf16[256,128]{1,0:T(8,128)(2,1)} %get-tuple-element.17) | copy-start | bytes 196612
  7.4 13.1 %collective-permute-start.5 = (bf16[256,128]{1,0:T(8,128)(2,1)}, bf16[256,128]{1,0:T(8,128)(2,1)S(1)}, u32[]{:S(2)}, u32[]{:S(2)}) collective-permute-start(bf16[256,128]{1,0:T(8,128)(2,1)} %get-tuple-element.17), channel_id=1, source_target_pairs={{0,12},{1,13},{2,14},{3,15},{4,8},{5,9},{6,10},{7,11},{8,4},{9,5},... | collective-permute-start | bytes 196616 | tf_op jit(solution)/shard_map/ppermute | solution.py:22
  12.3 14.0 %copy-start = (bf16[2,16,24,192]{3,1,2,0:T(8,128)(2,1)}, bf16[2,16,24,192]{3,1,2,0:T(8,128)(2,1)S(1)}, u32[]{:S(2)}) copy-start(bf16[2,16,24,192]{3,1,2,0:T(8,128)(2,1)S(1)} %copy.21) | copy-start | bytes 884740
  12.3 14.0 %collective-permute-start.8 = (bf16[2,24,16,192]{3,2,1,0:T(8,128)(2,1)S(1)}, bf16[2,24,16,192]{3,2,1,0:T(8,128)(2,1)S(1)}, u32[]{:S(2)}, u32[]{:S(2)}) collective-permute-start(bf16[2,24,16,192]{3,2,1,0:T(8,128)(2,1)S(1)} %bitcast.24), channel_id=1, source_target_pairs={{0,1},{1,2},{2,3},{3,4},{4,5},{5,6},{6,7},{7,8},{8,9},{9,10},{10,1... | collective-permute-start | bytes 884744 | tf_op jit(solution)/shard_map/ppermute | solution.py:27
  16.9 9.5 %collective-permute-start.6 = (bf16[4,256,128]{2,1,0:T(8,128)(2,1)S(1)}, bf16[4,256,128]{2,1,0:T(8,128)(2,1)S(1)}, u32[]{:S(2)}, u32[]{:S(2)}) collective-permute-start(bf16[4,256,128]{2,1,0:T(8,128)(2,1)S(1)} %pad_maximum_fusion), channel_id=1, source_target_pairs={{0,2},{1,3},{2,0},{3,1},{4,6},{5,7},{6,4},{7,5},{8,10},{9,11},{10,... | collective-permute-start | bytes 786440 | tf_op jit(solution)/shard_map/ppermute | solution.py:22
  19.0 8.4 %collective-permute-start.7 = (bf16[4,256,128]{2,1,0:T(8,128)(2,1)S(1)}, bf16[4,256,128]{2,1,0:T(8,128)(2,1)S(1)}, u32[]{:S(2)}, u32[]{:S(2)}) collective-permute-start(bf16[4,256,128]{2,1,0:T(8,128)(2,1)S(1)} %pad_maximum_fusion), channel_id=1, source_target_pairs={{0,16},{16,0},{1,17},{17,1},{2,18},{18,2},{3,19},{19,3},{4,20},{20... | collective-permute-start | bytes 786440 | tf_op jit(solution)/shard_map/ppermute | solution.py:22
  20.5 5.2 %collective-permute-start.4 = (bf16[256,128]{1,0:T(8,128)(2,1)S(1)}, bf16[256,128]{1,0:T(8,128)(2,1)S(1)}, u32[]{:S(2)}, u32[]{:S(2)}) collective-permute-start(bf16[256,128]{1,0:T(8,128)(2,1)S(1)} %copy-done.8), channel_id=1, source_target_pairs={{0,8},{1,9},{2,10},{3,11},{4,12},{5,13},{6,14},{7,15},{8,0},{9,1},... | collective-permute-start | bytes 196616 | tf_op jit(solution)/shard_map/ppermute | solution.py:22
  20.5 5.7 %collective-permute-start.3 = (bf16[256,128]{1,0:T(8,128)(2,1)S(1)}, bf16[256,128]{1,0:T(8,128)(2,1)S(1)}, u32[]{:S(2)}, u32[]{:S(2)}) collective-permute-start(bf16[256,128]{1,0:T(8,128)(2,1)S(1)} %copy-done.8), channel_id=1, source_target_pairs={{0,4},{1,5},{2,6},{3,7},{4,0},{5,1},{6,2},{7,3},{8,12},{9,13},{10,... | collective-permute-start | bytes 196616 | tf_op jit(solution)/shard_map/ppermute | solution.py:22
  26.3 13.6 %copy-start.7 = (bf16[2,24,16,192]{3,2,1,0:T(8,128)(2,1)}, bf16[2,24,16,192]{3,2,1,0:T(8,128)(2,1)S(1)}, u32[]{:S(2)}) copy-start(bf16[2,24,16,192]{3,2,1,0:T(8,128)(2,1)S(1)} %collective-permute-done.8.rim_ref) | copy-start | bytes 884740
  27.5 12.4 %collective-permute-start.13 = (bf16[4,256,128]{2,1,0:T(8,128)(2,1)S(1)}, bf16[4,256,128]{2,1,0:T(8,128)(2,1)S(1)}, u32[]{:S(2)}, u32[]{:S(2)}) collective-permute-start(bf16[4,256,128]{2,1,0:T(8,128)(2,1)S(1)} %pad_maximum_fusion.1), channel_id=1, source_target_pairs={{0,2},{1,3},{2,0},{3,1},{4,6},{5,7},{6,4},{7,5},{8,10},{9,11},{10,... | collective-permute-start | bytes 786440 | tf_op jit(solution)/shard_map/ppermute | solution.py:22
  28.4 11.0 %collective-permute-start.14 = (bf16[4,256,128]{2,1,0:T(8,128)(2,1)S(1)}, bf16[4,256,128]{2,1,0:T(8,128)(2,1)S(1)}, u32[]{:S(2)}, u32[]{:S(2)}) collective-permute-start(bf16[4,256,128]{2,1,0:T(8,128)(2,1)S(1)} %pad_maximum_fusion.1), channel_id=1, source_target_pairs={{0,16},{16,0},{1,17},{17,1},{2,18},{18,2},{3,19},{19,3},{4,20},{20... | collective-permute-start | bytes 786440 | tf_op jit(solution)/shard_map/ppermute | solution.py:22
  29.9 8.0 %collective-permute-start.9 = (bf16[2,256,128]{2,1,0:T(8,128)(2,1)S(1)}, bf16[2,256,128]{2,1,0:T(8,128)(2,1)S(1)}, u32[]{:S(2)}, u32[]{:S(2)}) collective-permute-start(bf16[2,256,128]{2,1,0:T(8,128)(2,1)S(1)} %slice.12), channel_id=1, source_target_pairs={{0,2},{1,3},{2,0},{3,1},{4,6},{5,7},{6,4},{7,5},{8,10},{9,11},{10,... | collective-permute-start | bytes 393224 | tf_op jit(solution)/shard_map/ppermute | solution.py:22
  31.2 8.1 %collective-permute-start.10 = (bf16[2,256,128]{2,1,0:T(8,128)(2,1)S(1)}, bf16[2,256,128]{2,1,0:T(8,128)(2,1)S(1)}, u32[]{:S(2)}, u32[]{:S(2)}) collective-permute-start(bf16[2,256,128]{2,1,0:T(8,128)(2,1)S(1)} %slice.13), channel_id=1, source_target_pairs={{0,16},{16,0},{1,17},{17,1},{2,18},{18,2},{3,19},{19,3},{4,20},{20... | collective-permute-start | bytes 393224 | tf_op jit(solution)/shard_map/ppermute | solution.py:22
  39.3 6.4 %copy-start.1 = (bf16[16,256,128]{2,1,0:T(8,128)(2,1)}, bf16[16,256,128]{2,1,0:T(8,128)(2,1)S(1)}, u32[]{:S(2)}) copy-start(bf16[16,256,128]{2,1,0:T(8,128)(2,1)S(1)} %constant_dynamic-update-slice_fusion.rest_0_) | copy-start | bytes 3145732
  39.3 6.4 %collective-permute-start.11 = (bf16[16,256,128]{2,1,0:T(8,128)(2,1)S(1)}, bf16[16,256,128]{2,1,0:T(8,128)(2,1)S(1)}, u32[]{:S(2)}, u32[]{:S(2)}) collective-permute-start(bf16[16,256,128]{2,1,0:T(8,128)(2,1)S(1)} %constant_dynamic-update-slice_fusion.rest_0_), channel_id=1, source_target_pairs={{0,1},{1,0},{2,3},{3,2},{4,5},{5,4},{6,7},{7,6},{8,9},{9,8},{10,11... | collective-permute-start | bytes 3145736 | tf_op jit(solution)/shard_map/ppermute | solution.py:22
  39.4 6.0 %collective-permute-start.15 = (bf16[2,256,128]{2,1,0:T(8,128)(2,1)S(1)}, bf16[2,256,128]{2,1,0:T(8,128)(2,1)S(1)}, u32[]{:S(2)}, u32[]{:S(2)}) collective-permute-start(bf16[2,256,128]{2,1,0:T(8,128)(2,1)S(1)} %slice.16), channel_id=1, source_target_pairs={{0,2},{1,3},{2,0},{3,1},{4,6},{5,7},{6,4},{7,5},{8,10},{9,11},{10,... | collective-permute-start | bytes 393224 | tf_op jit(solution)/shard_map/ppermute | solution.py:22
  39.9 5.7 %collective-permute-start.16 = (bf16[2,256,128]{2,1,0:T(8,128)(2,1)S(1)}, bf16[2,256,128]{2,1,0:T(8,128)(2,1)S(1)}, u32[]{:S(2)}, u32[]{:S(2)}) collective-permute-start(bf16[2,256,128]{2,1,0:T(8,128)(2,1)S(1)} %slice.17), channel_id=1, source_target_pairs={{0,16},{16,0},{1,17},{17,1},{2,18},{18,2},{3,19},{19,3},{4,20},{20... | collective-permute-start | bytes 393224 | tf_op jit(solution)/shard_map/ppermute | solution.py:22
  45.6 8.7 %copy-start.2 = (bf16[16,256,128]{2,1,0:T(8,128)(2,1)}, bf16[16,256,128]{2,1,0:T(8,128)(2,1)S(1)}, u32[]{:S(2)}) copy-start(bf16[16,256,128]{2,1,0:T(8,128)(2,1)S(1)} %constant_dynamic-update-slice_fusion.5.rest_0_) | copy-start | bytes 3145732
  45.6 11.0 %collective-permute-start.17 = (bf16[16,256,128]{2,1,0:T(8,128)(2,1)S(1)}, bf16[16,256,128]{2,1,0:T(8,128)(2,1)}, u32[]{:S(2)}, u32[]{:S(2)}) collective-permute-start(bf16[16,256,128]{2,1,0:T(8,128)(2,1)S(1)} %constant_dynamic-update-slice_fusion.5.rest_0_), channel_id=1, source_target_pairs={{0,1},{1,0},{2,3},{3,2},{4,5},{5,4},{6,7},{7,6},{8,9},{9,8},{10,11... | collective-permute-start | bytes 3145736 | tf_op jit(solution)/shard_map/ppermute | solution.py:22
  45.7 1.1 %copy-start.3 = (bf16[16,256,128]{2,1,0:T(8,128)(2,1)}, bf16[16,256,128]{2,1,0:T(8,128)(2,1)S(1)}, u32[]{:S(2)}) copy-start(bf16[16,256,128]{2,1,0:T(8,128)(2,1)S(1)} %collective-permute-done.11.rest_1_) | copy-start | bytes 3145732
  54.3 3.8 %collective-permute-start.12 = (bf16[2,24,16,192]{3,2,1,0:T(8,128)(2,1)}, bf16[2,24,16,192]{3,2,1,0:T(8,128)(2,1)S(1)}, u32[]{:S(2)}, u32[]{:S(2)}) collective-permute-start(bf16[2,24,16,192]{3,2,1,0:T(8,128)(2,1)} %shard_map.120.own_ref), channel_id=1, source_target_pairs={{0,1},{1,2},{2,3},{3,4},{4,5},{5,6},{6,7},{7,8},{8,9},{9,10},{10,1... | collective-permute-start | bytes 884744 | tf_op jit(solution)/shard_map/ppermute | solution.py:27
  58.1 0.7 copy-start.5
  67.6 10.0 %collective-permute-start.18 = (bf16[192,128]{1,0:T(8,128)(2,1)}, bf16[192,128]{1,0:T(8,128)(2,1)S(1)}, u32[]{:S(2)}, u32[]{:S(2)}) collective-permute-start(bf16[192,128]{1,0:T(8,128)(2,1)} %shard_map.121), channel_id=1, source_target_pairs={{0,4},{1,5},{2,6},{3,7},{4,0},{5,1},{6,2},{7,3},{8,12},{9,13},{10,... | collective-permute-start | bytes 147464 | tf_op jit(solution)/shard_map/ppermute | solution.py:22
  74.4 5.6 %collective-permute-start.19 = (bf16[192,128]{1,0:T(8,128)(2,1)}, bf16[192,128]{1,0:T(8,128)(2,1)S(1)}, u32[]{:S(2)}, u32[]{:S(2)}) collective-permute-start(bf16[192,128]{1,0:T(8,128)(2,1)} %shard_map.121), channel_id=1, source_target_pairs={{0,8},{1,9},{2,10},{3,11},{4,12},{5,13},{6,14},{7,15},{8,0},{9,1},... | collective-permute-start | bytes 147464 | tf_op jit(solution)/shard_map/ppermute | solution.py:22
  76.2 6.1 %collective-permute-start.20 = (bf16[192,128]{1,0:T(8,128)(2,1)}, bf16[192,128]{1,0:T(8,128)(2,1)S(1)}, u32[]{:S(2)}, u32[]{:S(2)}) collective-permute-start(bf16[192,128]{1,0:T(8,128)(2,1)} %shard_map.121), channel_id=1, source_target_pairs={{0,12},{1,13},{2,14},{3,15},{4,8},{5,9},{6,10},{7,11},{8,4},{9,5},... | collective-permute-start | bytes 147464 | tf_op jit(solution)/shard_map/ppermute | solution.py:22
  83.1 5.7 %collective-permute-start.21 = (bf16[768,128]{1,0:T(8,128)(2,1)S(1)}, bf16[768,128]{1,0:T(8,128)(2,1)S(1)}, u32[]{:S(2)}, u32[]{:S(2)}) collective-permute-start(bf16[768,128]{1,0:T(8,128)(2,1)S(1)} %pad_maximum_fusion.2), channel_id=1, source_target_pairs={{0,2},{1,3},{2,0},{3,1},{4,6},{5,7},{6,4},{7,5},{8,10},{9,11},{10,... | collective-permute-start | bytes 589832 | tf_op jit(solution)/shard_map/ppermute | solution.py:22
  88.9 1.8 %copy-start.4 = (bf16[1536,128]{1,0:T(8,128)(2,1)}, bf16[1536,128]{1,0:T(8,128)(2,1)S(1)}, u32[]{:S(2)}) copy-start(bf16[1536,128]{1,0:T(8,128)(2,1)S(1)} %constant_dynamic-update-slice_fusion.10.rest_0_) | copy-start | bytes 1179652
  88.9 1.8 %collective-permute-start.22 = (bf16[1536,128]{1,0:T(8,128)(2,1)S(1)}, bf16[1536,128]{1,0:T(8,128)(2,1)S(1)}, u32[]{:S(2)}, u32[]{:S(2)}) collective-permute-start(bf16[1536,128]{1,0:T(8,128)(2,1)S(1)} %constant_dynamic-update-slice_fusion.10.rest_0_), channel_id=1, source_target_pairs={{0,1},{1,0},{2,3},{3,2},{4,5},{5,4},{6,7},{7,6},{8,9},{9,8},{10,11... | collective-permute-start | bytes 1179656 | tf_op jit(solution)/shard_map/ppermute | solution.py:22
  90.7 0.8 copy-start.6

commit v3 on v2

--- a/solution.py
+++ b/solution.py
@@ -12,8 +12,10 @@
 UNIT_ROWS = 256
 SCRATCH_ROWS = 288
 NT = (((1,), (1,)), ((), ()))
+TN = (((0,), (0,)), ((), ()))
 VMEM_SPEC = pl.BlockSpec(memory_space=pltpu.VMEM)
 SMEM_SPEC = pl.BlockSpec(memory_space=pltpu.SMEM)
+IN_VMEM = functools.partial(pltpu.with_memory_space_constraint, memory_space=pltpu.VMEM)
 PARAMS = pltpu.CompilerParams(vmem_limit_bytes=56 * 2**20)
 
 
@@ -53,7 +55,7 @@
 def pack_units(half, weights, unit_channels):
     return pl.pallas_call(
         functools.partial(pack_kernel, unit_channels=unit_channels),
-        out_shape=[jax.ShapeDtypeStruct((UNIT_ROWS, LANES), jnp.bfloat16)] * len(weights),
+        out_shape=[pltpu.VMEM((UNIT_ROWS, LANES), jnp.bfloat16)] * len(weights),
         in_specs=[SMEM_SPEC] + [VMEM_SPEC] * len(weights),
         out_specs=[VMEM_SPEC] * len(weights),
         scratch_shapes=[pltpu.VMEM((UNIT_ROWS, LANES), jnp.float32)],
@@ -94,7 +96,7 @@
     _, depth, channels = weight.shape
     return pl.pallas_call(
         expand_kernel,
-        out_shape=jax.ShapeDtypeStruct((16, 12 * depth, 2 * LANES), jnp.bfloat16),
+        out_shape=pltpu.VMEM((16, 12 * depth, 2 * LANES), jnp.bfloat16),
         in_specs=[VMEM_SPEC],
         out_specs=VMEM_SPEC,
         compiler_params=PARAMS,
@@ -331,18 +333,19 @@
     *patch_refs, out_ref = rest
     width = embed_ref.shape[0]
     tokens = out_ref.shape[0]
-    total = jnp.zeros((tokens, LANES), jnp.float32)
+    total = jnp.zeros((LANES, tokens), jnp.float32)
     begin = 0
     for patch_ref in patch_refs:
         count = patch_ref.shape[0]
-        spots = lax.broadcasted_iota(jnp.int32, (tokens, count), 1) + begin
-        chosen = (spots == place_ref[:, 0:1]) | (spots == place_ref[:, 1:2])
+        spots = lax.broadcasted_iota(jnp.int32, (count, tokens), 0) + begin
+        chosen = (spots == place_ref[0:1, :]) | (spots == place_ref[1:2, :])
         chosen = jnp.where(chosen, 1.0, 0.0).astype(jnp.bfloat16)
-        total = total + jnp.dot(chosen, patch_ref[...], preferred_element_type=jnp.float32)
+        total = total + lax.dot_general(
+            patch_ref[...], chosen, TN, preferred_element_type=jnp.float32
+        )
         begin += count
-    turned = pltpu.roll(total, width, 1)
-    ordered = jnp.where(place_ref[:, 2:3] == 0, total, turned)[:, :width].astype(jnp.bfloat16)
-    embedded = jnp.dot(ordered, embed_ref[...], preferred_element_type=jnp.float32)
+    ordered = jnp.where(place_ref[2:3, :] == 0, total[:width], total[width:]).astype(jnp.bfloat16)
+    embedded = lax.dot_general(ordered, embed_ref[...], TN, preferred_element_type=jnp.float32)
     center = jnp.mean(embedded, axis=-1, keepdims=True)
     centered = embedded - center
     variance = jnp.mean(centered * centered, axis=-1, keepdims=True)
@@ -351,18 +354,19 @@
 
 
 def along_line(unit):
-    return jnp.stack([unit] + [xor_permute(unit, "ctx", 4 * step) for step in (1, 2, 3)])
+    return [unit] + [xor_permute(unit, "ctx", 4 * step) for step in (1, 2, 3)]
 
 
 def round_square(line):
     return xor_permute(line, "ctx", 2), xor_permute(line, "groups", 1)
 
 
-def whole_chip(line, across, other):
-    corner_low = xor_permute(other[:2], "ctx", 2)
-    corner_high = xor_permute(across[2:], "groups", 1)
-    chip = jnp.concatenate([line, across, other, corner_low, corner_high])
-    return [chip, xor_permute(chip, "ctx", 1)]
+def to_corner(across, other):
+    return xor_permute(other[:2], "ctx", 2), xor_permute(across[2:], "groups", 1)
+
+
+def both_cores(pieces):
+    return list(pieces) + [xor_permute(piece, "ctx", 1) for piece in pieces]
 
 
 def unit_channel_map(grid, group, device, unit_channels, units):
@@ -402,7 +406,6 @@
     pick = (channel_map[:, None] == jnp.arange(channels, dtype=jnp.int32)).astype(jnp.bfloat16)
     wide = expand_weight_out(weight_out.transpose(0, 2, 1))
     turned = features.transpose(0, 2, 1, 3)
-    turned_rim = to_next(turned[frames - 2 :], "ctx")
 
     spots = (height // 2) * (breadth // 2)
     frame, spot = token_order // spots, token_order % spots
@@ -417,29 +420,38 @@
 
     own_place = piece_of(owner) * 2 * spots + spot
     sent_place = jnp.where(owner > 0, (piece_of(jnp.maximum(owner - 1, 0)) * 2 + 1) * spots + spot, -1)
-    place = jnp.stack([own_place, sent_place, frame % frames], axis=1)
+    place = jnp.stack([own_place, sent_place, frame % frames])
 
     if grid:
         half = group.astype(jnp.int32).reshape(1)
         packed_first, packed_second = pack_units(half, by_output, unit_channels)
         line_first = along_line(packed_first)
-        line_first, wide, pick, place = lax.optimization_barrier((line_first, wide, pick, place))
+        line_first, wide, pick, place, turned = lax.optimization_barrier(
+            (line_first, wide, pick, place, turned)
+        )
+        line_first = jnp.stack(line_first)
+        packed_second, rim_source, line_first = lax.optimization_barrier(
+            (packed_second, turned, line_first)
+        )
         square_first = round_square(line_first)
-        line_second = along_line(packed_second)
-        line_second, square_first, turned_rim = lax.optimization_barrier(
-            (line_second, square_first, turned_rim)
+        line_second = jnp.stack(along_line(packed_second))
+        turned_rim = to_next(rim_source[frames - 2 :], "ctx")
+        corner_first = to_corner(*square_first)
+        line_second, corner_first, turned_rim = lax.optimization_barrier(
+            (line_second, corner_first, turned_rim)
         )
-        units_first = whole_chip(line_first, *square_first)
-        units_second = whole_chip(line_second, *round_square(line_second))
+        square_second = round_square(line_second)
+        units_first = both_cores((line_first, *square_first, *corner_first))
     else:
         units_first, units_second = [
             [pack_whole(lax.all_gather(weight, "ctx", axis=0, tiled=True), units)]
             for weight in by_output
         ]
+        turned_rim = to_next(turned[frames - 2 :], "ctx")
 
     first = (device * frames).astype(jnp.int32).reshape(1)
     scratch = conv_scratch(frames, breadth, height, taps, units * SUBLANES)
-    image = jax.ShapeDtypeStruct((frames, breadth, height, channels), jnp.bfloat16)
+    image = pltpu.VMEM((frames, breadth, height, channels), jnp.bfloat16)
     second_in = pl.pallas_call(
         functools.partial(first_kernel, taps=taps, unit_channels=unit_channels),
         out_shape=image,
@@ -448,14 +460,19 @@
         scratch_shapes=scratch,
         compiler_params=PARAMS,
     )(
-        clip_ids, first, turned, turned_rim, gain_first.reshape(1, -1),
-        gain_second.reshape(1, -1), pick, *units_first,
-    )
+        clip_ids, first, IN_VMEM(turned), IN_VMEM(turned_rim), gain_first.reshape(1, -1),
+        gain_second.reshape(1, -1), IN_VMEM(pick), *map(IN_VMEM, units_first),
+    )
+    second_rim = to_next(second_in[frames - 2 :], "ctx")
+    if grid:
+        square_second, second_in = lax.optimization_barrier((square_second, second_in))
+        corner_second = to_corner(*square_second)
+        units_second = both_cores((line_second, *square_second, *corner_second))
 
     depth = weight_out.shape[2]
     parts = pl.pallas_call(
         functools.partial(second_kernel, taps=taps, unit_channels=unit_channels),
-        out_shape=jax.ShapeDtypeStruct((2 * spots, frames * 4 * depth), jnp.bfloat16),
+        out_shape=pltpu.VMEM((2 * spots, frames * 4 * depth), jnp.bfloat16),
         in_specs=[SMEM_SPEC] * 2 + [VMEM_SPEC] * (6 + len(units_second)),
         out_specs=VMEM_SPEC,
         scratch_shapes=scratch
@@ -465,13 +482,12 @@
         ],
         compiler_params=PARAMS,
     )(
-        clip_ids, first, second_in, to_next(second_in[frames - 2 :], "ctx"), turned,
-        gain_third.reshape(1, -1), pick, wide, *units_second,
+        clip_ids, first, IN_VMEM(second_in), IN_VMEM(second_rim), IN_VMEM(turned),
+        gain_third.reshape(1, -1), IN_VMEM(pick), IN_VMEM(wide), *map(IN_VMEM, units_second),
     )
     if grid:
-        line = jnp.concatenate([parts] + [xor_permute(parts, "ctx", 4 * k) for k in (1, 2, 3)])
-        sheet = jnp.concatenate([line, xor_permute(line, "ctx", 2)])
-        pieces = [sheet, xor_permute(sheet, "ctx", 1)]
+        line = jnp.concatenate(along_line(parts))
+        pieces = both_cores((line, xor_permute(line, "ctx", 2)))
     else:
         pieces = [lax.all_gather(parts, "ctx", axis=0, tiled=True)]
 
@@ -483,7 +499,8 @@
         out_specs=VMEM_SPEC,
         compiler_params=PARAMS,
     )(
-        place, embed_weight, scale_mod.reshape(1, -1), shift_mod.reshape(1, -1), *pieces
+        IN_VMEM(place), IN_VMEM(embed_weight), scale_mod.reshape(1, -1), shift_mod.reshape(1, -1),
+        *map(IN_VMEM, pieces),
     )
 
 

time: 95.9 us -> 97.6 us (1.018)
  Pallas kernels: 24.4 us -> 18.8 us
  waiting for transfers between devices: 30.1 us -> 34.3 us
  local copies, waits for them, and re-layouts: 5.62 us -> 8.77 us
    ppermute x21 -> x30, waiting for transfers between devices: 28.6 us -> 34.3 us  [xor_permute(): lax.ppermute(value, axis, [(source, source ^ mask) for source in range(co...]
    unnamed x35 -> x23, local copies, waits for them, and re-layouts: 4.74 us -> 8.73 us
    pallas_call x1, Pallas kernels: 8.78 us -> 6.72 us  [body(): pl.pallas_call(functools.partial(second_kernel, taps=taps, unit_channels=...]
    pallas_call x1, Pallas kernels: 7.51 us -> 5.94 us  [body(): pl.pallas_call(functools.partial(first_kernel, taps=taps, unit_channels=u...]
    ppermute x2, waiting for transfers between devices: 1.51 us -> 0.01 us  [to_next(): lax.ppermute(value, axis, [(source, source + 1) for source in range(count...]
    pallas_call x1, Pallas kernels: 2.27 us -> 1.1 us  [expand_weight_out(): pl.pallas_call(expand_kernel, out_shape=pltpu.VMEM((16, 12 * depth, 2 * L...]
    ppermute x21 -> x30, starting transfers between devices: 29.6 us -> 30.5 us  [xor_permute(): lax.ppermute(value, axis, [(source, source ^ mask) for source in range(co...]
  transfers between devices with their start and end apart: 23 -> 32, of which waited for: 12 -> 15; matrix products, arithmetic and copies ran while one was open for 4% -> 2% of each run, Pallas kernels for 10% -> 7%
where the time goes in v3:
time: 97.6 us; the launch traced here: 97.1 us
  waiting for transfers between devices  34.3 us (35%)
  starting transfers between devices  34 us (35%)
  Pallas kernels  18.8 us (19%)
  local copies, waits for them, and re-layouts  8.77 us (9%)
  other arithmetic  0.98 us (1%)
    ppermute x30, waiting for transfers between devices, xor_permute(): lax.ppermute(value, axis, [(source, source ^ mask) for source in range(co...  34.3 us
    ppermute x30, starting transfers between devices, xor_permute(): lax.ppermute(value, axis, [(source, source ^ mask) for source in range(co...  30.5 us
    unnamed x23, local copies, waits for them, and re-layouts  8.73 us
    pallas_call x1, Pallas kernels, body(): pl.pallas_call(functools.partial(second_kernel, taps=taps, unit_channels=...  6.72 us
    pallas_call x1, Pallas kernels, body(): pl.pallas_call(functools.partial(first_kernel, taps=taps, unit_channels=u...  5.94 us
    pallas_call x1, Pallas kernels, body(): pl.pallas_call(embed_kernel, out_shape=jax.ShapeDtypeStruct((tokens, widt...  3.9 us
    ppermute x2, starting transfers between devices, to_next(): lax.ppermute(value, axis, [(source, source + 1) for source in range(count...  3.56 us
  transfers between devices with their start and end apart: 32, of which 15 were waited for; matrix products, arithmetic and copies ran while one was open for 2% of the time, Pallas kernels for 7%

profile of v3, /device:TPU:0, one launch (start us, length us, event | category | flops | bytes accessed | tf_op | source)
XLA Modules:
  0.0 97.1 jit_solution(689901481238787373)
XLA Ops:
  0.0 1.1 %shard_map.118 = (bf16[256,128]{1,0:T(8,128)(2,1)S(1)}, bf16[256,128]{1,0:T(8,128)(2,1)S(1)}) custom-call(s32[1]{0:T(128)} %bitcast.half_ref, bf16[12,27,192]{2,1,0:T(8,128)(2,1)} %bitcast.30, bf16[12,27,192]{2,1,0:T(8,128)(2,1)} %bitcast.31), custom_call_target="tpu_custom_call" | custom-call | tf_op jit(solution)/shard_map/pallas_call | solution.py:56
  1.1 5.1 %collective-permute-start.2 = (bf16[256,128]{1,0:T(8,128)(2,1)S(1)}, bf16[256,128]{1,0:T(8,128)(2,1)S(1)}, u32[]{:S(2)}, u32[]{:S(2)}) collective-permute-start(bf16[256,128]{1,0:T(8,128)(2,1)S(1)} %get-tuple-element.29), channel_id=1, source_target_pairs={{0,12},{1,13},{2,14},{3,15},{4,8},{5,9},{6,10},{7,11},{8,4},{9,5},... | collective-permute-start | bytes 196616 | tf_op jit(solution)/shard_map/ppermute | solution.py:24
  6.3 0.6 collective-permute-start
  6.9 0.7 multiply_add_fusion
  7.7 1.1 %copy.15 = bf16[2,16,24,192]{3,1,2,0:T(8,128)(2,1)S(1)} copy(bf16[2,16,24,192]{3,2,1,0:T(8,128)(2,1)} %param.12) | data formatting | bytes 589824 | tf_op args[0]
  8.8 1.1 %shard_map.119.wide_ref = bf16[16,192,256]{2,1,0:T(8,128)(2,1)S(1)} custom-call(bf16[27,16,192]{2,1,0:T(8,128)(2,1)} %bitcast.29), custom_call_target="tpu_custom_call" | custom-call | tf_op jit(solution)/shard_map/pallas_call | solution.py:97
  10.0 1.9 %collective-permute-done.1 = bf16[256,128]{1,0:T(8,128)(2,1)S(1)} collective-permute-done((bf16[256,128]{1,0:T(8,128)(2,1)S(1)}, bf16[256,128]{1,0:T(8,128)(2,1)S(1)}, u32[]{:S(2)}, u32[]{:S(2)}) %collective-permute-start.1) | collective-permute-done | bytes 65568 | tf_op jit(solution)/shard_map/ppermute | solution.py:24
  11.9 1.6 %collective-permute-start.8 = (bf16[4,256,128]{2,1,0:T(8,128)(2,1)S(1)}, bf16[4,256,128]{2,1,0:T(8,128)(2,1)S(1)}, u32[]{:S(2)}, u32[]{:S(2)}) collective-permute-start(bf16[4,256,128]{2,1,0:T(8,128)(2,1)S(1)} %pad_maximum_fusion.rest_0_), channel_id=1, source_target_pairs={{0,2},{1,3},{2,0},{3,1},{4,6},{5,7},{6,4},{7,5},{8,10},{9,11},{10,... | collective-permute-start | bytes 786440 | tf_op jit(solution)/shard_map/ppermute | solution.py:24
  13.5 1.5 %collective-permute-start.6 = (bf16[4,256,128]{2,1,0:T(8,128)(2,1)S(1)}, bf16[4,256,128]{2,1,0:T(8,128)(2,1)S(1)}, u32[]{:S(2)}, u32[]{:S(2)}) collective-permute-start(bf16[4,256,128]{2,1,0:T(8,128)(2,1)S(1)} %pad_maximum_fusion.rest_0_), channel_id=1, source_target_pairs={{0,16},{16,0},{1,17},{17,1},{2,18},{18,2},{3,19},{19,3},{4,20},{20... | collective-permute-start | bytes 786440 | tf_op jit(solution)/shard_map/ppermute | solution.py:24
  15.0 1.3 %collective-permute-start.10 = (bf16[2,24,16,192]{3,2,1,0:T(8,128)(2,1)S(1)}, bf16[2,24,16,192]{3,2,1,0:T(8,128)(2,1)S(1)}, u32[]{:S(2)}, u32[]{:S(2)}) collective-permute-start(bf16[2,24,16,192]{3,2,1,0:T(8,128)(2,1)S(1)} %bitcast.24), channel_id=1, source_target_pairs={{0,1},{1,2},{2,3},{3,4},{4,5},{5,6},{6,7},{7,8},{8,9},{9,10},{10,1... | collective-permute-start | bytes 884744 | tf_op jit(solution)/shard_map/ppermute | solution.py:29
  16.3 3.4 %collective-permute-start.5 = (bf16[256,128]{1,0:T(8,128)(2,1)S(1)}, bf16[256,128]{1,0:T(8,128)(2,1)S(1)}, u32[]{:S(2)}, u32[]{:S(2)}) collective-permute-start(bf16[256,128]{1,0:T(8,128)(2,1)S(1)} %get-tuple-element.33), channel_id=1, source_target_pairs={{0,12},{1,13},{2,14},{3,15},{4,8},{5,9},{6,10},{7,11},{8,4},{9,5},... | collective-permute-start | bytes 196616 | tf_op jit(solution)/shard_map/ppermute | solution.py:24
  19.7 3.3 %collective-permute-done.5 = bf16[256,128]{1,0:T(8,128)(2,1)S(1)} collective-permute-done((bf16[256,128]{1,0:T(8,128)(2,1)S(1)}, bf16[256,128]{1,0:T(8,128)(2,1)S(1)}, u32[]{:S(2)}, u32[]{:S(2)}) %collective-permute-start.5) | collective-permute-done | bytes 65568 | tf_op jit(solution)/shard_map/ppermute | solution.py:24
  23.2 3.1 %collective-permute-done.4 = bf16[256,128]{1,0:T(8,128)(2,1)S(1)} collective-permute-done((bf16[256,128]{1,0:T(8,128)(2,1)S(1)}, bf16[256,128]{1,0:T(8,128)(2,1)S(1)}, u32[]{:S(2)}, u32[]{:S(2)}) %collective-permute-start.4) | collective-permute-done | bytes 65568 | tf_op jit(solution)/shard_map/ppermute | solution.py:24
  26.3 0.5 collective-permute-start.15
  26.8 3.7 %collective-permute-done.3 = bf16[256,128]{1,0:T(8,128)(2,1)S(1)} collective-permute-done((bf16[256,128]{1,0:T(8,128)(2,1)S(1)}, bf16[256,128]{1,0:T(8,128)(2,1)S(1)}, u32[]{:S(2)}, u32[]{:S(2)}) %collective-permute-start.3) | collective-permute-done | bytes 65568 | tf_op jit(solution)/shard_map/ppermute | solution.py:24
  30.6 0.5 collective-permute-start.9
  31.1 0.7 copy-done.3
  31.8 2.3 %collective-permute-start.7 = (bf16[2,256,128]{2,1,0:T(8,128)(2,1)S(1)}, bf16[2,256,128]{2,1,0:T(8,128)(2,1)}, u32[]{:S(2)}, u32[]{:S(2)}) collective-permute-start(bf16[2,256,128]{2,1,0:T(8,128)(2,1)S(1)} %slice.16), channel_id=1, source_target_pairs={{0,2},{1,3},{2,0},{3,1},{4,6},{5,7},{6,4},{7,5},{8,10},{9,11},{10,... | collective-permute-start | bytes 393224 | tf_op jit(solution)/shard_map/ppermute | solution.py:24
  34.2 1.3 %collective-permute-done.9.rest_4_ = bf16[2,256,128]{2,1,0:T(8,128)(2,1)S(1)} collective-permute-done((bf16[2,256,128]{2,1,0:T(8,128)(2,1)S(1)}, bf16[2,256,128]{2,1,0:T(8,128)(2,1)S(1)}, u32[]{:S(2)}, u32[]{:S(2)}) %collective-permute-start.9) | collective-permute-done | bytes 131104 | tf_op jit(solution)/shard_map/ppermute | solution.py:24
  35.5 2.2 %collective-permute-done.7.rest_3_ = bf16[2,256,128]{2,1,0:T(8,128)(2,1)} collective-permute-done((bf16[2,256,128]{2,1,0:T(8,128)(2,1)S(1)}, bf16[2,256,128]{2,1,0:T(8,128)(2,1)}, u32[]{:S(2)}, u32[]{:S(2)}) %collective-permute-start.7) | collective-permute-done | bytes 131104 | tf_op jit(solution)/shard_map/ppermute | solution.py:24
  37.8 1.5 %collective-permute-start.12 = (bf16[4,256,128]{2,1,0:T(8,128)(2,1)S(1)}, bf16[4,256,128]{2,1,0:T(8,128)(2,1)S(1)}, u32[]{:S(2)}, u32[]{:S(2)}) collective-permute-start(bf16[4,256,128]{2,1,0:T(8,128)(2,1)S(1)} %pad_maximum_fusion.1.rest_0_), channel_id=1, source_target_pairs={{0,16},{16,0},{1,17},{17,1},{2,18},{18,2},{3,19},{19,3},{4,20},{20... | collective-permute-start | bytes 786440 | tf_op jit(solution)/shard_map/ppermute | solution.py:24
  39.2 1.7 %collective-permute-start.11 = (bf16[4,256,128]{2,1,0:T(8,128)(2,1)S(1)}, bf16[4,256,128]{2,1,0:T(8,128)(2,1)S(1)}, u32[]{:S(2)}, u32[]{:S(2)}) collective-permute-start(bf16[4,256,128]{2,1,0:T(8,128)(2,1)S(1)} %pad_maximum_fusion.1.rest_0_), channel_id=1, source_target_pairs={{0,2},{1,3},{2,0},{3,1},{4,6},{5,7},{6,4},{7,5},{8,10},{9,11},{10,... | collective-permute-start | bytes 786440 | tf_op jit(solution)/shard_map/ppermute | solution.py:24
  41.0 0.7 copy-done.5
  41.7 0.7 copy-done.7
  42.4 0.5 collective-permute-start.16
  42.9 0.7 copy-done.9
  43.6 0.6 collective-permute-done.16.rest_8_
  44.3 0.9 collective-permute-done.17.rest_9_
  45.1 0.9 copy-done.1
  46.1 1.0 %copy-done.4 = bf16[2,24,16,192]{3,2,1,0:T(8,128)(2,1)S(1)} copy-done((bf16[2,24,16,192]{3,2,1,0:T(8,128)(2,1)S(1)}, bf16[2,24,16,192]{3,2,1,0:T(8,128)(2,1)}, u32[]{:S(2)}) %copy-start.4) | copy-done | bytes 294936
  47.1 0.9 copy-done.6
  48.0 0.9 copy-done.8
  49.0 0.9 copy-done.10
  49.9 5.9 %shard_map.120.own_ref = bf16[2,24,16,192]{3,2,1,0:T(8,128)(2,1)S(1)} custom-call(s32[32]{0:T(128)} %clips_ref.3, s32[1]{0:T(128)} %bitcast.10.first_ref, bf16[2,24,16,192]{3,2,1,0:T(8,128)(2,1)S(1)} %bitcast.25, bf16[2,24,16,192]{3,2,1,0:T(8,128)(2,1)S(1)} %copy-done.4, f32[1,192]{1,0:T(1,128)} %bitcast.43, f32[1,192]{1,0:T(1,128)} %bitcast.44, ...), custom_call_target="tpu_custom_call" | custom-call | tf_op jit(solution)/shard_map/pallas_call | solution.py:455
  55.9 2.3 %collective-permute-start.18 = (bf16[2,24,16,192]{3,2,1,0:T(8,128)(2,1)S(1)}, bf16[2,24,16,192]{3,2,1,0:T(8,128)(2,1)S(1)}, u32[]{:S(2)}, u32[]{:S(2)}) collective-permute-start(bf16[2,24,16,192]{3,2,1,0:T(8,128)(2,1)S(1)} %shard_map.120.own_ref), channel_id=1, source_target_pairs={{0,1},{1,2},{2,3},{3,4},{4,5},{5,6},{6,7},{7,8},{8,9},{9,10},{10,1... | collective-permute-start | bytes 884744 | tf_op jit(solution)/shard_map/ppermute | solution.py:29
  58.5 0.6 collective-permute-start.20
  59.1 2.1 %collective-permute-start.22 = (bf16[4,256,128]{2,1,0:T(8,128)(2,1)S(1)}, bf16[4,256,128]{2,1,0:T(8,128)(2,1)S(1)}, u32[]{:S(2)}, u32[]{:S(2)}) collective-permute-start(bf16[4,256,128]{2,1,0:T(8,128)(2,1)S(1)} %collective-permute-done.11.rest_1_), channel_id=1, source_target_pairs={{0,1},{1,0},{2,3},{3,2},{4,5},{5,4},{6,7},{7,6},{8,9},{9,8},{10,11... | collective-permute-start | bytes 786440 | tf_op jit(solution)/shard_map/ppermute | solution.py:24
  61.2 3.2 %collective-permute-done.19.rest_3_ = bf16[2,256,128]{2,1,0:T(8,128)(2,1)S(1)} collective-permute-done((bf16[2,256,128]{2,1,0:T(8,128)(2,1)S(1)}, bf16[2,256,128]{2,1,0:T(8,128)(2,1)S(1)}, u32[]{:S(2)}, u32[]{:S(2)}) %collective-permute-start.19) | collective-permute-done | bytes 131104 | tf_op jit(solution)/shard_map/ppermute | solution.py:24
  64.4 1.3 %collective-permute-start.24 = (bf16[2,256,128]{2,1,0:T(8,128)(2,1)S(1)}, bf16[2,256,128]{2,1,0:T(8,128)(2,1)S(1)}, u32[]{:S(2)}, u32[]{:S(2)}) collective-permute-start(bf16[2,256,128]{2,1,0:T(8,128)(2,1)S(1)} %collective-permute-done.19.rest_3_), channel_id=1, source_target_pairs={{0,1},{1,0},{2,3},{3,2},{4,5},{5,4},{6,7},{7,6},{8,9},{9,8},{10,11... | collective-permute-start | bytes 393224 | tf_op jit(solution)/shard_map/ppermute | solution.py:24
  65.7 1.0 %collective-permute-done.24.rest_8_ = bf16[2,256,128]{2,1,0:T(8,128)(2,1)S(1)} collective-permute-done((bf16[2,256,128]{2,1,0:T(8,128)(2,1)S(1)}, bf16[2,256,128]{2,1,0:T(8,128)(2,1)S(1)}, u32[]{:S(2)}, u32[]{:S(2)}) %collective-permute-start.24) | collective-permute-done | bytes 131104 | tf_op jit(solution)/shard_map/ppermute | solution.py:24
  67.1 6.7 %shard_map.121 = bf16[192,128]{1,0:T(8,128)(2,1)S(1)} custom-call(s32[32]{0:T(128)} %clips_ref.3, s32[1]{0:T(128)} %bitcast.10.first_ref, bf16[2,24,16,192]{3,2,1,0:T(8,128)(2,1)S(1)} %shard_map.120.own_ref, bf16[2,24,16,192]{3,2,1,0:T(8,128)(2,1)S(1)} %collective-permute-done.18.rim_ref, bf16[2,24,16,192]{3,2,1,0:T(8,128)(2,1)S(1)} %bitcast.26, ...), custom_call_target="tpu_custom_call" | custom-call | tf_op jit(solution)/shard_map/pallas_call | solution.py:473
  73.8 5.9 %collective-permute-start.28 = (bf16[192,128]{1,0:T(8,128)(2,1)S(1)}, bf16[192,128]{1,0:T(8,128)(2,1)S(1)}, u32[]{:S(2)}, u32[]{:S(2)}) collective-permute-start(bf16[192,128]{1,0:T(8,128)(2,1)S(1)} %shard_map.121), channel_id=1, source_target_pairs={{0,12},{1,13},{2,14},{3,15},{4,8},{5,9},{6,10},{7,11},{8,4},{9,5},... | collective-permute-start | bytes 147464 | tf_op jit(solution)/shard_map/ppermute | solution.py:24
  79.9 0.4 collective-permute-start.26
  80.3 1.7 %collective-permute-done.28 = bf16[192,128]{1,0:T(8,128)(2,1)S(1)} collective-permute-done((bf16[192,128]{1,0:T(8,128)(2,1)S(1)}, bf16[192,128]{1,0:T(8,128)(2,1)S(1)}, u32[]{:S(2)}, u32[]{:S(2)}) %collective-permute-start.28) | collective-permute-done | bytes 49184 | tf_op jit(solution)/shard_map/ppermute | solution.py:24
  82.0 3.3 %collective-permute-done.27 = bf16[192,128]{1,0:T(8,128)(2,1)S(1)} collective-permute-done((bf16[192,128]{1,0:T(8,128)(2,1)S(1)}, bf16[192,128]{1,0:T(8,128)(2,1)S(1)}, u32[]{:S(2)}, u32[]{:S(2)}) %collective-permute-start.27) | collective-permute-done | bytes 49184 | tf_op jit(solution)/shard_map/ppermute | solution.py:24
  85.5 6.3 %collective-permute-done.29.rest_1_ = bf16[768,128]{1,0:T(8,128)(2,1)S(1)} collective-permute-done((bf16[768,128]{1,0:T(8,128)(2,1)S(1)}, bf16[768,128]{1,0:T(8,128)(2,1)S(1)}, u32[]{:S(2)}, u32[]{:S(2)}) %collective-permute-start.29) | collective-permute-done | bytes 196640 | tf_op jit(solution)/shard_map/ppermute | solution.py:24
  91.7 1.4 %collective-permute-done.31.rest_3_ = bf16[768,128]{1,0:T(8,128)(2,1)S(1)} collective-permute-done((bf16[768,128]{1,0:T(8,128)(2,1)S(1)}, bf16[768,128]{1,0:T(8,128)(2,1)S(1)}, u32[]{:S(2)}, u32[]{:S(2)}) %collective-permute-start.31) | collective-permute-done | bytes 196640 | tf_op jit(solution)/shard_map/ppermute | solution.py:24
  93.2 3.9 %shard_map.122 = bf16[192,3072]{1,0:T(8,128)(2,1)} custom-call(s32[3,192]{1,0:T(4,128)S(1)} %pad_add_fusion.place_ref, bf16[64,3072]{1,0:T(8,128)(2,1)S(1)} %copy-done.2, f32[1,3072]{1,0:T(1,128)} %bitcast.38, f32[1,3072]{1,0:T(1,128)} %bitcast.39, bf16[768,128]{1,0:T(8,128)(2,1)S(1)} %pad_maximum_fusion.2.rest_0_, ...), custom_call_target="tpu_custom_call" | custom-call | tf_op jit(solution)/shard_map/pallas_call | solution.py:495
  (56 shorter events, 1.7 us)
Async XLA Ops:
  1.1 8.8 %collective-permute-start.2 = (bf16[256,128]{1,0:T(8,128)(2,1)S(1)}, bf16[256,128]{1,0:T(8,128)(2,1)S(1)}, u32[]{:S(2)}, u32[]{:S(2)}) collective-permute-start(bf16[256,128]{1,0:T(8,128)(2,1)S(1)} %get-tuple-element.29), channel_id=1, source_target_pairs={{0,12},{1,13},{2,14},{3,15},{4,8},{5,9},{6,10},{7,11},{8,4},{9,5},... | collective-permute-start | bytes 196616 | tf_op jit(solution)/shard_map/ppermute | solution.py:24
  6.2 5.6 %collective-permute-start.1 = (bf16[256,128]{1,0:T(8,128)(2,1)S(1)}, bf16[256,128]{1,0:T(8,128)(2,1)S(1)}, u32[]{:S(2)}, u32[]{:S(2)}) collective-permute-start(bf16[256,128]{1,0:T(8,128)(2,1)S(1)} %get-tuple-element.29), channel_id=1, source_target_pairs={{0,8},{1,9},{2,10},{3,11},{4,12},{5,13},{6,14},{7,15},{8,0},{9,1},... | collective-permute-start | bytes 196616 | tf_op jit(solution)/shard_map/ppermute | solution.py:24
  6.3 5.6 %collective-permute-start = (bf16[256,128]{1,0:T(8,128)(2,1)S(1)}, bf16[256,128]{1,0:T(8,128)(2,1)S(1)}, u32[]{:S(2)}, u32[]{:S(2)}) collective-permute-start(bf16[256,128]{1,0:T(8,128)(2,1)S(1)} %get-tuple-element.29), channel_id=1, source_target_pairs={{0,4},{1,5},{2,6},{3,7},{4,0},{5,1},{6,2},{7,3},{8,12},{9,13},{10,... | collective-permute-start | bytes 196616 | tf_op jit(solution)/shard_map/ppermute | solution.py:24
  11.9 14.4 %collective-permute-start.8 = (bf16[4,256,128]{2,1,0:T(8,128)(2,1)S(1)}, bf16[4,256,128]{2,1,0:T(8,128)(2,1)S(1)}, u32[]{:S(2)}, u32[]{:S(2)}) collective-permute-start(bf16[4,256,128]{2,1,0:T(8,128)(2,1)S(1)} %pad_maximum_fusion.rest_0_), channel_id=1, source_target_pairs={{0,2},{1,3},{2,0},{3,1},{4,6},{5,7},{6,4},{7,5},{8,10},{9,11},{10,... | collective-permute-start | bytes 786440 | tf_op jit(solution)/shard_map/ppermute | solution.py:24
  13.5 12.8 %collective-permute-start.6 = (bf16[4,256,128]{2,1,0:T(8,128)(2,1)S(1)}, bf16[4,256,128]{2,1,0:T(8,128)(2,1)S(1)}, u32[]{:S(2)}, u32[]{:S(2)}) collective-permute-start(bf16[4,256,128]{2,1,0:T(8,128)(2,1)S(1)} %pad_maximum_fusion.rest_0_), channel_id=1, source_target_pairs={{0,16},{16,0},{1,17},{17,1},{2,18},{18,2},{3,19},{19,3},{4,20},{20... | collective-permute-start | bytes 786440 | tf_op jit(solution)/shard_map/ppermute | solution.py:24
  15.0 16.1 %collective-permute-start.10 = (bf16[2,24,16,192]{3,2,1,0:T(8,128)(2,1)S(1)}, bf16[2,24,16,192]{3,2,1,0:T(8,128)(2,1)S(1)}, u32[]{:S(2)}, u32[]{:S(2)}) collective-permute-start(bf16[2,24,16,192]{3,2,1,0:T(8,128)(2,1)S(1)} %bitcast.24), channel_id=1, source_target_pairs={{0,1},{1,2},{2,3},{3,4},{4,5},{5,6},{6,7},{7,8},{8,9},{9,10},{10,1... | collective-permute-start | bytes 884744 | tf_op jit(solution)/shard_map/ppermute | solution.py:29
  16.3 6.7 %collective-permute-start.5 = (bf16[256,128]{1,0:T(8,128)(2,1)S(1)}, bf16[256,128]{1,0:T(8,128)(2,1)S(1)}, u32[]{:S(2)}, u32[]{:S(2)}) collective-permute-start(bf16[256,128]{1,0:T(8,128)(2,1)S(1)} %get-tuple-element.33), channel_id=1, source_target_pairs={{0,12},{1,13},{2,14},{3,15},{4,8},{5,9},{6,10},{7,11},{8,4},{9,5},... | collective-permute-start | bytes 196616 | tf_op jit(solution)/shard_map/ppermute | solution.py:24
  19.7 6.6 %collective-permute-start.4 = (bf16[256,128]{1,0:T(8,128)(2,1)S(1)}, bf16[256,128]{1,0:T(8,128)(2,1)S(1)}, u32[]{:S(2)}, u32[]{:S(2)}) collective-permute-start(bf16[256,128]{1,0:T(8,128)(2,1)S(1)} %get-tuple-element.33), channel_id=1, source_target_pairs={{0,8},{1,9},{2,10},{3,11},{4,12},{5,13},{6,14},{7,15},{8,0},{9,1},... | collective-permute-start | bytes 196616 | tf_op jit(solution)/shard_map/ppermute | solution.py:24
  23.0 18.0 %collective-permute-start.13 = (bf16[4,256,128]{2,1,0:T(8,128)(2,1)S(1)}, bf16[4,256,128]{2,1,0:T(8,128)(2,1)S(1)}, u32[]{:S(2)}, u32[]{:S(2)}) collective-permute-start(bf16[4,256,128]{2,1,0:T(8,128)(2,1)S(1)} %pad_maximum_fusion.rest_0_), channel_id=1, source_target_pairs={{0,1},{1,0},{2,3},{3,2},{4,5},{5,4},{6,7},{7,6},{8,9},{9,8},{10,11... | collective-permute-start | bytes 786440 | tf_op jit(solution)/shard_map/ppermute | solution.py:24
  26.3 4.3 %collective-permute-start.3 = (bf16[256,128]{1,0:T(8,128)(2,1)S(1)}, bf16[256,128]{1,0:T(8,128)(2,1)S(1)}, u32[]{:S(2)}, u32[]{:S(2)}) collective-permute-start(bf16[256,128]{1,0:T(8,128)(2,1)S(1)} %get-tuple-element.33), channel_id=1, source_target_pairs={{0,4},{1,5},{2,6},{3,7},{4,0},{5,1},{6,2},{7,3},{8,12},{9,13},{10,... | collective-permute-start | bytes 196616 | tf_op jit(solution)/shard_map/ppermute | solution.py:24
  26.3 15.4 %collective-permute-start.14 = (bf16[4,256,128]{2,1,0:T(8,128)(2,1)S(1)}, bf16[4,256,128]{2,1,0:T(8,128)(2,1)S(1)}, u32[]{:S(2)}, u32[]{:S(2)}) collective-permute-start(bf16[4,256,128]{2,1,0:T(8,128)(2,1)S(1)} %collective-permute-done.8.rest_1_), channel_id=1, source_target_pairs={{0,1},{1,0},{2,3},{3,2},{4,5},{5,4},{6,7},{7,6},{8,9},{9,8},{10,11... | collective-permute-start | bytes 786440 | tf_op jit(solution)/shard_map/ppermute | solution.py:24
  26.3 15.4 %copy-start = (bf16[4,256,128]{2,1,0:T(8,128)(2,1)}, bf16[4,256,128]{2,1,0:T(8,128)(2,1)S(1)}, u32[]{:S(2)}) copy-start(bf16[4,256,128]{2,1,0:T(8,128)(2,1)S(1)} %collective-permute-done.6.rest_2_) | copy-start | bytes 786436
  26.3 16.6 %collective-permute-start.15 = (bf16[4,256,128]{2,1,0:T(8,128)(2,1)S(1)}, bf16[4,256,128]{2,1,0:T(8,128)(2,1)S(1)}, u32[]{:S(2)}, u32[]{:S(2)}) collective-permute-start(bf16[4,256,128]{2,1,0:T(8,128)(2,1)S(1)} %collective-permute-done.6.rest_2_), channel_id=1, source_target_pairs={{0,1},{1,0},{2,3},{3,2},{4,5},{5,4},{6,7},{7,6},{8,9},{9,8},{10,11... | collective-permute-start | bytes 786440 | tf_op jit(solution)/shard_map/ppermute | solution.py:24
  30.6 5.0 %collective-permute-start.9 = (bf16[2,256,128]{2,1,0:T(8,128)(2,1)S(1)}, bf16[2,256,128]{2,1,0:T(8,128)(2,1)S(1)}, u32[]{:S(2)}, u32[]{:S(2)}) collective-permute-start(bf16[2,256,128]{2,1,0:T(8,128)(2,1)S(1)} %slice.17), channel_id=1, source_target_pairs={{0,16},{16,0},{1,17},{17,1},{2,18},{18,2},{3,19},{19,3},{4,20},{20... | collective-permute-start | bytes 393224 | tf_op jit(solution)/shard_map/ppermute | solution.py:24
  31.1 0.7 copy-start.3
  31.8 5.9 %collective-permute-start.7 = (bf16[2,256,128]{2,1,0:T(8,128)(2,1)S(1)}, bf16[2,256,128]{2,1,0:T(8,128)(2,1)}, u32[]{:S(2)}, u32[]{:S(2)}) collective-permute-start(bf16[2,256,128]{2,1,0:T(8,128)(2,1)S(1)} %slice.16), channel_id=1, source_target_pairs={{0,2},{1,3},{2,0},{3,1},{4,6},{5,7},{6,4},{7,5},{8,10},{9,11},{10,... | collective-permute-start | bytes 393224 | tf_op jit(solution)/shard_map/ppermute | solution.py:24
  37.8 20.4 %collective-permute-start.12 = (bf16[4,256,128]{2,1,0:T(8,128)(2,1)S(1)}, bf16[4,256,128]{2,1,0:T(8,128)(2,1)S(1)}, u32[]{:S(2)}, u32[]{:S(2)}) collective-permute-start(bf16[4,256,128]{2,1,0:T(8,128)(2,1)S(1)} %pad_maximum_fusion.1.rest_0_), channel_id=1, source_target_pairs={{0,16},{16,0},{1,17},{17,1},{2,18},{18,2},{3,19},{19,3},{4,20},{20... | collective-permute-start | bytes 786440 | tf_op jit(solution)/shard_map/ppermute | solution.py:24
  39.2 18.9 %collective-permute-start.11 = (bf16[4,256,128]{2,1,0:T(8,128)(2,1)S(1)}, bf16[4,256,128]{2,1,0:T(8,128)(2,1)S(1)}, u32[]{:S(2)}, u32[]{:S(2)}) collective-permute-start(bf16[4,256,128]{2,1,0:T(8,128)(2,1)S(1)} %pad_maximum_fusion.1.rest_0_), channel_id=1, source_target_pairs={{0,2},{1,3},{2,0},{3,1},{4,6},{5,7},{6,4},{7,5},{8,10},{9,11},{10,... | collective-permute-start | bytes 786440 | tf_op jit(solution)/shard_map/ppermute | solution.py:24
  41.0 0.7 copy-start.5
  41.7 19.5 %collective-permute-start.21 = (bf16[4,256,128]{2,1,0:T(8,128)(2,1)S(1)}, bf16[4,256,128]{2,1,0:T(8,128)(2,1)}, u32[]{:S(2)}, u32[]{:S(2)}) collective-permute-start(bf16[4,256,128]{2,1,0:T(8,128)(2,1)S(1)} %pad_maximum_fusion.1.rest_0_), channel_id=1, source_target_pairs={{0,1},{1,0},{2,3},{3,2},{4,5},{5,4},{6,7},{7,6},{8,9},{9,8},{10,11... | collective-permute-start | bytes 786440 | tf_op jit(solution)/shard_map/ppermute | solution.py:24
  41.7 0.7 copy-start.7
  42.4 1.8 %collective-permute-start.16 = (bf16[2,256,128]{2,1,0:T(8,128)(2,1)}, bf16[2,256,128]{2,1,0:T(8,128)(2,1)}, u32[]{:S(2)}, u32[]{:S(2)}) collective-permute-start(bf16[2,256,128]{2,1,0:T(8,128)(2,1)} %collective-permute-done.7.rest_3_), channel_id=1, source_target_pairs={{0,1},{1,0},{2,3},{3,2},{4,5},{5,4},{6,7},{7,6},{8,9},{9,8},{10,11... | collective-permute-start | bytes 393224 | tf_op jit(solution)/shard_map/ppermute | solution.py:24
  42.9 0.7 copy-start.9
  43.6 1.5 %collective-permute-start.17 = (bf16[2,256,128]{2,1,0:T(8,128)(2,1)S(1)}, bf16[2,256,128]{2,1,0:T(8,128)(2,1)}, u32[]{:S(2)}, u32[]{:S(2)}) collective-permute-start(bf16[2,256,128]{2,1,0:T(8,128)(2,1)S(1)} %collective-permute-done.9.rest_4_), channel_id=1, source_target_pairs={{0,1},{1,0},{2,3},{3,2},{4,5},{5,4},{6,7},{7,6},{8,9},{9,8},{10,11... | collective-permute-start | bytes 393224 | tf_op jit(solution)/shard_map/ppermute | solution.py:24
  45.1 1.0 copy-start.1
  46.1 1.0 %copy-start.4 = (bf16[2,24,16,192]{3,2,1,0:T(8,128)(2,1)S(1)}, bf16[2,24,16,192]{3,2,1,0:T(8,128)(2,1)}, u32[]{:S(2)}) copy-start(bf16[2,24,16,192]{3,2,1,0:T(8,128)(2,1)} %copy-done.3) | copy-start | bytes 884740
  47.1 0.9 copy-start.6
  48.0 0.9 copy-start.8
  49.0 0.9 copy-start.10
  55.9 9.8 %collective-permute-start.18 = (bf16[2,24,16,192]{3,2,1,0:T(8,128)(2,1)S(1)}, bf16[2,24,16,192]{3,2,1,0:T(8,128)(2,1)S(1)}, u32[]{:S(2)}, u32[]{:S(2)}) collective-permute-start(bf16[2,24,16,192]{3,2,1,0:T(8,128)(2,1)S(1)} %shard_map.120.own_ref), channel_id=1, source_target_pairs={{0,1},{1,2},{2,3},{3,4},{4,5},{5,6},{6,7},{7,8},{8,9},{9,10},{10,1... | collective-permute-start | bytes 884744 | tf_op jit(solution)/shard_map/ppermute | solution.py:29
  58.2 6.2 %collective-permute-start.19 = (bf16[2,256,128]{2,1,0:T(8,128)(2,1)S(1)}, bf16[2,256,128]{2,1,0:T(8,128)(2,1)S(1)}, u32[]{:S(2)}, u32[]{:S(2)}) collective-permute-start(bf16[2,256,128]{2,1,0:T(8,128)(2,1)S(1)} %slice.14), channel_id=1, source_target_pairs={{0,2},{1,3},{2,0},{3,1},{4,6},{5,7},{6,4},{7,5},{8,10},{9,11},{10,... | collective-permute-start | bytes 393224 | tf_op jit(solution)/shard_map/ppermute | solution.py:24
  58.5 7.2 %collective-permute-start.20 = (bf16[2,256,128]{2,1,0:T(8,128)(2,1)S(1)}, bf16[2,256,128]{2,1,0:T(8,128)(2,1)S(1)}, u32[]{:S(2)}, u32[]{:S(2)}) collective-permute-start(bf16[2,256,128]{2,1,0:T(8,128)(2,1)S(1)} %slice.15), channel_id=1, source_target_pairs={{0,16},{16,0},{1,17},{17,1},{2,18},{18,2},{3,19},{19,3},{4,20},{20... | collective-permute-start | bytes 393224 | tf_op jit(solution)/shard_map/ppermute | solution.py:24
  59.1 7.9 %collective-permute-start.22 = (bf16[4,256,128]{2,1,0:T(8,128)(2,1)S(1)}, bf16[4,256,128]{2,1,0:T(8,128)(2,1)S(1)}, u32[]{:S(2)}, u32[]{:S(2)}) collective-permute-start(bf16[4,256,128]{2,1,0:T(8,128)(2,1)S(1)} %collective-permute-done.11.rest_1_), channel_id=1, source_target_pairs={{0,1},{1,0},{2,3},{3,2},{4,5},{5,4},{6,7},{7,6},{8,9},{9,8},{10,11... | collective-permute-start | bytes 786440 | tf_op jit(solution)/shard_map/ppermute | solution.py:24
  61.2 5.9 %collective-permute-start.23 = (bf16[4,256,128]{2,1,0:T(8,128)(2,1)S(1)}, bf16[4,256,128]{2,1,0:T(8,128)(2,1)S(1)}, u32[]{:S(2)}, u32[]{:S(2)}) collective-permute-start(bf16[4,256,128]{2,1,0:T(8,128)(2,1)S(1)} %collective-permute-done.12.rest_2_), channel_id=1, source_target_pairs={{0,1},{1,0},{2,3},{3,2},{4,5},{5,4},{6,7},{7,6},{8,9},{9,8},{10,11... | collective-permute-start | bytes 786440 | tf_op jit(solution)/shard_map/ppermute | solution.py:24
  64.4 2.3 %collective-permute-start.24 = (bf16[2,256,128]{2,1,0:T(8,128)(2,1)S(1)}, bf16[2,256,128]{2,1,0:T(8,128)(2,1)S(1)}, u32[]{:S(2)}, u32[]{:S(2)}) collective-permute-start(bf16[2,256,128]{2,1,0:T(8,128)(2,1)S(1)} %collective-permute-done.19.rest_3_), channel_id=1, source_target_pairs={{0,1},{1,0},{2,3},{3,2},{4,5},{5,4},{6,7},{7,6},{8,9},{9,8},{10,11... | collective-permute-start | bytes 393224 | tf_op jit(solution)/shard_map/ppermute | solution.py:24
  65.7 1.3 %collective-permute-start.25 = (bf16[2,256,128]{2,1,0:T(8,128)(2,1)S(1)}, bf16[2,256,128]{2,1,0:T(8,128)(2,1)S(1)}, u32[]{:S(2)}, u32[]{:S(2)}) collective-permute-start(bf16[2,256,128]{2,1,0:T(8,128)(2,1)S(1)} %collective-permute-done.20.rest_4_), channel_id=1, source_target_pairs={{0,1},{1,0},{2,3},{3,2},{4,5},{5,4},{6,7},{7,6},{8,9},{9,8},{10,11... | collective-permute-start | bytes 393224 | tf_op jit(solution)/shard_map/ppermute | solution.py:24
  67.1 26.1 %copy-start.2 = (bf16[64,3072]{1,0:T(8,128)(2,1)S(1)}, bf16[64,3072]{1,0:T(8,128)(2,1)}, u32[]{:S(2)}) copy-start(bf16[64,3072]{1,0:T(8,128)(2,1)} %embed_ref.1) | copy-start | bytes 1179652
  73.8 8.2 %collective-permute-start.28 = (bf16[192,128]{1,0:T(8,128)(2,1)S(1)}, bf16[192,128]{1,0:T(8,128)(2,1)S(1)}, u32[]{:S(2)}, u32[]{:S(2)}) collective-permute-start(bf16[192,128]{1,0:T(8,128)(2,1)S(1)} %shard_map.121), channel_id=1, source_target_pairs={{0,12},{1,13},{2,14},{3,15},{4,8},{5,9},{6,10},{7,11},{8,4},{9,5},... | collective-permute-start | bytes 147464 | tf_op jit(solution)/shard_map/ppermute | solution.py:24
  79.6 5.6 %collective-permute-start.27 = (bf16[192,128]{1,0:T(8,128)(2,1)S(1)}, bf16[192,128]{1,0:T(8,128)(2,1)S(1)}, u32[]{:S(2)}, u32[]{:S(2)}) collective-permute-start(bf16[192,128]{1,0:T(8,128)(2,1)S(1)} %shard_map.121), channel_id=1, source_target_pairs={{0,8},{1,9},{2,10},{3,11},{4,12},{5,13},{6,14},{7,15},{8,0},{9,1},... | collective-permute-start | bytes 147464 | tf_op jit(solution)/shard_map/ppermute | solution.py:24
  79.9 5.4 %collective-permute-start.26 = (bf16[192,128]{1,0:T(8,128)(2,1)S(1)}, bf16[192,128]{1,0:T(8,128)(2,1)S(1)}, u32[]{:S(2)}, u32[]{:S(2)}) collective-permute-start(bf16[192,128]{1,0:T(8,128)(2,1)S(1)} %shard_map.121), channel_id=1, source_target_pairs={{0,4},{1,5},{2,6},{3,7},{4,0},{5,1},{6,2},{7,3},{8,12},{9,13},{10,... | collective-permute-start | bytes 147464 | tf_op jit(solution)/shard_map/ppermute | solution.py:24
  85.3 6.4 %collective-permute-start.29 = (bf16[768,128]{1,0:T(8,128)(2,1)S(1)}, bf16[768,128]{1,0:T(8,128)(2,1)S(1)}, u32[]{:S(2)}, u32[]{:S(2)}) collective-permute-start(bf16[768,128]{1,0:T(8,128)(2,1)S(1)} %pad_maximum_fusion.2.rest_0_), channel_id=1, source_target_pairs={{0,2},{1,3},{2,0},{3,1},{4,6},{5,7},{6,4},{7,5},{8,10},{9,11},{10,... | collective-permute-start | bytes 589832 | tf_op jit(solution)/shard_map/ppermute | solution.py:24
  85.4 6.3 %collective-permute-start.30 = (bf16[768,128]{1,0:T(8,128)(2,1)S(1)}, bf16[768,128]{1,0:T(8,128)(2,1)S(1)}, u32[]{:S(2)}, u32[]{:S(2)}) collective-permute-start(bf16[768,128]{1,0:T(8,128)(2,1)S(1)} %pad_maximum_fusion.2.rest_0_), channel_id=1, source_target_pairs={{0,1},{1,0},{2,3},{3,2},{4,5},{5,4},{6,7},{7,6},{8,9},{9,8},{10,11... | collective-permute-start | bytes 589832 | tf_op jit(solution)/shard_map/ppermute | solution.py:24
  91.7 1.4 %collective-permute-start.31 = (bf16[768,128]{1,0:T(8,128)(2,1)S(1)}, bf16[768,128]{1,0:T(8,128)(2,1)S(1)}, u32[]{:S(2)}, u32[]{:S(2)}) collective-permute-start(bf16[768,128]{1,0:T(8,128)(2,1)S(1)} %collective-permute-done.29.rest_1_), channel_id=1, source_target_pairs={{0,1},{1,0},{2,3},{3,2},{4,5},{5,4},{6,7},{7,6},{8,9},{9,8},{10,11... | collective-permute-start | bytes 589832 | tf_op jit(solution)/shard_map/ppermute | solution.py:24

commit v4 on v3

--- a/solution.py
+++ b/solution.py
@@ -16,7 +16,8 @@
 VMEM_SPEC = pl.BlockSpec(memory_space=pltpu.VMEM)
 SMEM_SPEC = pl.BlockSpec(memory_space=pltpu.SMEM)
 IN_VMEM = functools.partial(pltpu.with_memory_space_constraint, memory_space=pltpu.VMEM)
-PARAMS = pltpu.CompilerParams(vmem_limit_bytes=56 * 2**20)
+SMALL = pltpu.CompilerParams(vmem_limit_bytes=4 * 2**20)
+LARGE = pltpu.CompilerParams(vmem_limit_bytes=24 * 2**20)
 
 
 def xor_permute(value, axis, mask):
@@ -59,7 +60,7 @@
         in_specs=[SMEM_SPEC] + [VMEM_SPEC] * len(weights),
         out_specs=[VMEM_SPEC] * len(weights),
         scratch_shapes=[pltpu.VMEM((UNIT_ROWS, LANES), jnp.float32)],
-        compiler_params=PARAMS,
+        compiler_params=SMALL,
     )(half, *weights)
 
 
@@ -99,7 +100,7 @@
         out_shape=pltpu.VMEM((16, 12 * depth, 2 * LANES), jnp.bfloat16),
         in_specs=[VMEM_SPEC],
         out_specs=VMEM_SPEC,
-        compiler_params=PARAMS,
+        compiler_params=SMALL,
     )(weight)
 
 
@@ -406,6 +407,7 @@
     pick = (channel_map[:, None] == jnp.arange(channels, dtype=jnp.int32)).astype(jnp.bfloat16)
     wide = expand_weight_out(weight_out.transpose(0, 2, 1))
     turned = features.transpose(0, 2, 1, 3)
+    turned_rim = to_next(features[frames - 2 :], "ctx").transpose(0, 2, 1, 3)
 
     spots = (height // 2) * (breadth // 2)
     frame, spot = token_order // spots, token_order % spots
@@ -426,20 +428,19 @@
         half = group.astype(jnp.int32).reshape(1)
         packed_first, packed_second = pack_units(half, by_output, unit_channels)
         line_first = along_line(packed_first)
-        line_first, wide, pick, place, turned = lax.optimization_barrier(
-            (line_first, wide, pick, place, turned)
+        line_first, wide, pick, place, turned, turned_rim = lax.optimization_barrier(
+            (line_first, wide, pick, place, turned, turned_rim)
         )
         line_first = jnp.stack(line_first)
-        packed_second, rim_source, line_first = lax.optimization_barrier(
-            (packed_second, turned, line_first)
+        packed_second, line_first = lax.optimization_barrier((packed_second, line_first))
+        square_first = round_square(line_first)
+        line_second = along_line(packed_second)
+        line_first, square_first, line_second = lax.optimization_barrier(
+            (line_first, square_first, line_second)
         )
-        square_first = round_square(line_first)
-        line_second = jnp.stack(along_line(packed_second))
-        turned_rim = to_next(rim_source[frames - 2 :], "ctx")
         corner_first = to_corner(*square_first)
-        line_second, corner_first, turned_rim = lax.optimization_barrier(
-            (line_second, corner_first, turned_rim)
-        )
+        line_second, corner_first = lax.optimization_barrier((line_second, corner_first))
+        line_second = jnp.stack(line_second)
         square_second = round_square(line_second)
         units_first = both_cores((line_first, *square_first, *corner_first))
     else:
@@ -447,7 +448,6 @@
             [pack_whole(lax.all_gather(weight, "ctx", axis=0, tiled=True), units)]
             for weight in by_output
         ]
-        turned_rim = to_next(turned[frames - 2 :], "ctx")
 
     first = (device * frames).astype(jnp.int32).reshape(1)
     scratch = conv_scratch(frames, breadth, height, taps, units * SUBLANES)
@@ -458,14 +458,16 @@
         in_specs=[SMEM_SPEC] * 2 + [VMEM_SPEC] * (5 + len(units_first)),
         out_specs=VMEM_SPEC,
         scratch_shapes=scratch,
-        compiler_params=PARAMS,
+        compiler_params=LARGE,
     )(
         clip_ids, first, IN_VMEM(turned), IN_VMEM(turned_rim), gain_first.reshape(1, -1),
         gain_second.reshape(1, -1), IN_VMEM(pick), *map(IN_VMEM, units_first),
     )
     second_rim = to_next(second_in[frames - 2 :], "ctx")
     if grid:
-        square_second, second_in = lax.optimization_barrier((square_second, second_in))
+        line_second, square_second, second_in = lax.optimization_barrier(
+            (line_second, square_second, second_in)
+        )
         corner_second = to_corner(*square_second)
         units_second = both_cores((line_second, *square_second, *corner_second))
 
@@ -480,7 +482,7 @@
             pltpu.VMEM((2, frames * breadth * height, LANES), jnp.float32),
             pltpu.VMEM((4, 2, frames, breadth + 2, height // 2, LANES), jnp.float32),
         ],
-        compiler_params=PARAMS,
+        compiler_params=LARGE,
     )(
         clip_ids, first, IN_VMEM(second_in), IN_VMEM(second_rim), IN_VMEM(turned),
         gain_third.reshape(1, -1), IN_VMEM(pick), IN_VMEM(wide), *map(IN_VMEM, units_second),
@@ -497,7 +499,7 @@
         out_shape=jax.ShapeDtypeStruct((tokens, width), jnp.bfloat16),
         in_specs=[VMEM_SPEC] * (4 + len(pieces)),
         out_specs=VMEM_SPEC,
-        compiler_params=PARAMS,
+        compiler_params=LARGE,
     )(
         IN_VMEM(place), IN_VMEM(embed_weight), scale_mod.reshape(1, -1), shift_mod.reshape(1, -1),
         *map(IN_VMEM, pieces),

time: 97.6 us -> 93.1 us (0.954)
  waiting for transfers between devices: 34.3 us -> 29.3 us
  Pallas kernels: 18.8 us -> 15.8 us
  local copies, waits for them, and re-layouts: 8.77 us -> 10.6 us
  starting transfers between devices: 34 us -> 35.7 us
    ppermute x30, waiting for transfers between devices: 34.3 us -> 29.3 us  [xor_permute(): lax.ppermute(value, axis, [(source, source ^ mask) for source in range(co...]
    ppermute x30, starting transfers between devices: 30.5 us -> 32.6 us  [xor_permute(): lax.ppermute(value, axis, [(source, source ^ mask) for source in range(co...]
    pallas_call x1, Pallas kernels: 1.13 us -> 0.11 us  [pack_units(): pl.pallas_call(functools.partial(pack_kernel, unit_channels=unit_channels...]
    unnamed x23 -> x37, local copies, waits for them, and re-layouts: 8.73 us -> 9.65 us
  transfers between devices with their start and end apart: 32 -> 32, of which waited for: 15 -> 14; matrix products, arithmetic and copies ran while one was open for 2% -> 3% of each run, Pallas kernels for 7% -> 7%
where the time goes in v4:
time: 93.1 us; the launch traced here: 92.6 us
  starting transfers between devices  35.7 us (38%)
  waiting for transfers between devices  29.3 us (31%)
  Pallas kernels  15.8 us (17%)
  local copies, waits for them, and re-layouts  10.6 us (11%)
  other arithmetic  0.98 us (1%)
    ppermute x30, starting transfers between devices, xor_permute(): lax.ppermute(value, axis, [(source, source ^ mask) for source in range(co...  32.6 us
    ppermute x30, waiting for transfers between devices, xor_permute(): lax.ppermute(value, axis, [(source, source ^ mask) for source in range(co...  29.3 us
    unnamed x37, local copies, waits for them, and re-layouts  9.65 us
    pallas_call x1, Pallas kernels, body(): pl.pallas_call(functools.partial(second_kernel, taps=taps, unit_channels=...  6.26 us
    pallas_call x1, Pallas kernels, body(): pl.pallas_call(functools.partial(first_kernel, taps=taps, unit_channels=u...  6.09 us
    pallas_call x1, Pallas kernels, body(): pl.pallas_call(embed_kernel, out_shape=jax.ShapeDtypeStruct((tokens, widt...  3.18 us
    ppermute x2, starting transfers between devices, to_next(): lax.ppermute(value, axis, [(source, source + 1) for source in range(count...  3.1 us
  transfers between devices with their start and end apart: 32, of which 14 were waited for; matrix products, arithmetic and copies ran while one was open for 3% of the time, Pallas kernels for 7%

profile of v4, /device:TPU:0, one launch (start us, length us, event | category | flops | bytes accessed | tf_op | source)
XLA Modules:
  0.0 92.6 jit_solution(13646182843315520862)
XLA Ops:
  0.0 0.9 copy-done.4
  0.9 0.9 copy-done.5
  2.0 3.1 %collective-permute-start = (bf16[256,128]{1,0:T(8,128)(2,1)S(1)}, bf16[256,128]{1,0:T(8,128)(2,1)S(1)}, u32[]{:S(2)}, u32[]{:S(2)}) collective-permute-start(bf16[256,128]{1,0:T(8,128)(2,1)S(1)} %get-tuple-element.38), channel_id=1, source_target_pairs={{0,4},{1,5},{2,6},{3,7},{4,0},{5,1},{6,2},{7,3},{8,12},{9,13},{10,... | collective-permute-start | bytes 196616 | tf_op jit(solution)/shard_map/ppermute | solution.py:25
  5.1 2.6 %collective-permute-start.1 = (bf16[256,128]{1,0:T(8,128)(2,1)S(1)}, bf16[256,128]{1,0:T(8,128)(2,1)S(1)}, u32[]{:S(2)}, u32[]{:S(2)}) collective-permute-start(bf16[256,128]{1,0:T(8,128)(2,1)S(1)} %get-tuple-element.38), channel_id=1, source_target_pairs={{0,8},{1,9},{2,10},{3,11},{4,12},{5,13},{6,14},{7,15},{8,0},{9,1},... | collective-permute-start | bytes 196616 | tf_op jit(solution)/shard_map/ppermute | solution.py:25
  7.7 1.1 %copy.17 = bf16[2,16,24,192]{3,1,2,0:T(8,128)(2,1)S(1)} copy(bf16[2,16,24,192]{3,2,1,0:T(8,128)(2,1)} %param.12) | data formatting | bytes 589824 | tf_op args[0]
  8.7 1.3 %collective-permute-start.3 = (bf16[2,16,24,192]{3,1,2,0:T(8,128)(2,1)S(1)}, bf16[2,16,24,192]{3,1,2,0:T(8,128)(2,1)S(1)}, u32[]{:S(2)}, u32[]{:S(2)}) collective-permute-start(bf16[2,16,24,192]{3,1,2,0:T(8,128)(2,1)S(1)} %copy.17), channel_id=1, source_target_pairs={{0,1},{1,2},{2,3},{3,4},{4,5},{5,6},{6,7},{7,8},{8,9},{9,10},{10,1... | collective-permute-start | bytes 884744 | tf_op jit(solution)/shard_map/ppermute | solution.py:30
  10.1 0.7 multiply_add_fusion
  10.9 0.9 %copy-done.3 = bf16[27,192,16]{1,2,0:T(8,128)(2,1)S(1)} copy-done((bf16[27,192,16]{1,2,0:T(8,128)(2,1)S(1)}, bf16[27,192,16]{1,2,0:T(8,128)(2,1)}, u32[]{:S(2)}) %copy-start.3) | copy-done | bytes 165912
  12.3 1.4 %collective-permute-done.2 = bf16[256,128]{1,0:T(8,128)(2,1)S(1)} collective-permute-done((bf16[256,128]{1,0:T(8,128)(2,1)S(1)}, bf16[256,128]{1,0:T(8,128)(2,1)S(1)}, u32[]{:S(2)}, u32[]{:S(2)}) %collective-permute-start.2) | collective-permute-done | bytes 65568 | tf_op jit(solution)/shard_map/ppermute | solution.py:25
  13.7 0.7 copy-done.1
  14.5 5.9 %collective-permute-start.4 = (bf16[4,256,128]{2,1,0:T(8,128)(2,1)S(1)}, bf16[4,256,128]{2,1,0:T(8,128)(2,1)S(1)}, u32[]{:S(2)}, u32[]{:S(2)}) collective-permute-start(bf16[4,256,128]{2,1,0:T(8,128)(2,1)S(1)} %pad_maximum_fusion.rest_0_), channel_id=1, source_target_pairs={{0,2},{1,3},{2,0},{3,1},{4,6},{5,7},{6,4},{7,5},{8,10},{9,11},{10,... | collective-permute-start | bytes 786440 | tf_op jit(solution)/shard_map/ppermute | solution.py:25
  20.4 1.5 %collective-permute-start.5 = (bf16[4,256,128]{2,1,0:T(8,128)(2,1)S(1)}, bf16[4,256,128]{2,1,0:T(8,128)(2,1)}, u32[]{:S(2)}, u32[]{:S(2)}) collective-permute-start(bf16[4,256,128]{2,1,0:T(8,128)(2,1)S(1)} %pad_maximum_fusion.rest_0_), channel_id=1, source_target_pairs={{0,16},{16,0},{1,17},{17,1},{2,18},{18,2},{3,19},{19,3},{4,20},{20... | collective-permute-start | bytes 786440 | tf_op jit(solution)/shard_map/ppermute | solution.py:25
  21.9 0.7 collective-permute-start.6
  22.6 3.5 %collective-permute-start.7 = (bf16[256,128]{1,0:T(8,128)(2,1)S(1)}, bf16[256,128]{1,0:T(8,128)(2,1)S(1)}, u32[]{:S(2)}, u32[]{:S(2)}) collective-permute-start(bf16[256,128]{1,0:T(8,128)(2,1)S(1)} %get-tuple-element.50), channel_id=1, source_target_pairs={{0,8},{1,9},{2,10},{3,11},{4,12},{5,13},{6,14},{7,15},{8,0},{9,1},... | collective-permute-start | bytes 196616 | tf_op jit(solution)/shard_map/ppermute | solution.py:25
  26.3 3.3 %collective-permute-done.7 = bf16[256,128]{1,0:T(8,128)(2,1)S(1)} collective-permute-done((bf16[256,128]{1,0:T(8,128)(2,1)S(1)}, bf16[256,128]{1,0:T(8,128)(2,1)S(1)}, u32[]{:S(2)}, u32[]{:S(2)}) %collective-permute-start.7) | collective-permute-done | bytes 65568 | tf_op jit(solution)/shard_map/ppermute | solution.py:25
  29.6 2.6 %collective-permute-done.8 = bf16[256,128]{1,0:T(8,128)(2,1)S(1)} collective-permute-done((bf16[256,128]{1,0:T(8,128)(2,1)S(1)}, bf16[256,128]{1,0:T(8,128)(2,1)S(1)}, u32[]{:S(2)}, u32[]{:S(2)}) %collective-permute-start.8) | collective-permute-done | bytes 65568 | tf_op jit(solution)/shard_map/ppermute | solution.py:25
  32.2 0.6 collective-permute-start.10
  32.8 0.9 slice.12
  33.7 1.5 %collective-permute-start.9 = (bf16[2,256,128]{2,1,0:T(8,128)(2,1)S(1)}, bf16[2,256,128]{2,1,0:T(8,128)(2,1)S(1)}, u32[]{:S(2)}, u32[]{:S(2)}) collective-permute-start(bf16[2,256,128]{2,1,0:T(8,128)(2,1)S(1)} %slice.12), channel_id=1, source_target_pairs={{0,2},{1,3},{2,0},{3,1},{4,6},{5,7},{6,4},{7,5},{8,10},{9,11},{10,... | collective-permute-start | bytes 393224 | tf_op jit(solution)/shard_map/ppermute | solution.py:25
  35.1 2.0 %collective-permute-done.10.rest_4_ = bf16[2,256,128]{2,1,0:T(8,128)(2,1)S(1)} collective-permute-done((bf16[2,256,128]{2,1,0:T(8,128)(2,1)S(1)}, bf16[2,256,128]{2,1,0:T(8,128)(2,1)S(1)}, u32[]{:S(2)}, u32[]{:S(2)}) %collective-permute-start.10) | collective-permute-done | bytes 131104 | tf_op jit(solution)/shard_map/ppermute | solution.py:25
  37.2 1.5 %collective-permute-done.9.rest_3_ = bf16[2,256,128]{2,1,0:T(8,128)(2,1)S(1)} collective-permute-done((bf16[2,256,128]{2,1,0:T(8,128)(2,1)S(1)}, bf16[2,256,128]{2,1,0:T(8,128)(2,1)S(1)}, u32[]{:S(2)}, u32[]{:S(2)}) %collective-permute-start.9) | collective-permute-done | bytes 131104 | tf_op jit(solution)/shard_map/ppermute | solution.py:25
  38.7 0.5 collective-permute-start.17
  39.2 0.5 collective-permute-start.15
  40.1 0.7 copy-done.8
  40.7 1.4 %collective-permute-start.11 = (bf16[4,256,128]{2,1,0:T(8,128)(2,1)S(1)}, bf16[4,256,128]{2,1,0:T(8,128)(2,1)S(1)}, u32[]{:S(2)}, u32[]{:S(2)}) collective-permute-start(bf16[4,256,128]{2,1,0:T(8,128)(2,1)S(1)} %pad_maximum_fusion.1.rest_0_), channel_id=1, source_target_pairs={{0,2},{1,3},{2,0},{3,1},{4,6},{5,7},{6,4},{7,5},{8,10},{9,11},{10,... | collective-permute-start | bytes 786440 | tf_op jit(solution)/shard_map/ppermute | solution.py:25
  42.1 0.7 copy-done.10
  42.8 1.5 %collective-permute-start.12 = (bf16[4,256,128]{2,1,0:T(8,128)(2,1)S(1)}, bf16[4,256,128]{2,1,0:T(8,128)(2,1)S(1)}, u32[]{:S(2)}, u32[]{:S(2)}) collective-permute-start(bf16[4,256,128]{2,1,0:T(8,128)(2,1)S(1)} %pad_maximum_fusion.1.rest_0_), channel_id=1, source_target_pairs={{0,16},{16,0},{1,17},{17,1},{2,18},{18,2},{3,19},{19,3},{4,20},{20... | collective-permute-start | bytes 786440 | tf_op jit(solution)/shard_map/ppermute | solution.py:25
  44.3 1.0 %copy-done.2 = bf16[2,16,24,192]{3,1,2,0:T(8,128)(2,1)S(1)} copy-done((bf16[2,16,24,192]{3,1,2,0:T(8,128)(2,1)S(1)}, bf16[2,16,24,192]{3,1,2,0:T(8,128)(2,1)}, u32[]{:S(2)}) %copy-start.2) | copy-done | bytes 294936
  45.3 0.9 copy-done.7
  46.2 0.9 copy-done.9
  47.1 0.9 copy-done.11
  48.0 6.1 %shard_map.120.own_ref = bf16[2,24,16,192]{3,2,1,0:T(8,128)(2,1)S(1)} custom-call(s32[32]{0:T(128)S(1)} %copy-done.14, s32[1]{0:T(128)} %bitcast.11.first_ref, bf16[2,24,16,192]{3,2,1,0:T(8,128)(2,1)S(1)} %bitcast.24, bf16[2,24,16,192]{3,2,1,0:T(8,128)(2,1)S(1)} %bitcast.26, f32[1,192]{1,0:T(1,128)S(1)} %bitcast.34, f32[1,192]{1,0:T(1,128)S(1)} %bitcast.35, ...), custom_call_target="tpu_custom_call" | custom-call | tf_op jit(solution)/shard_map/pallas_call | solution.py:455
  54.1 1.8 %collective-permute-start.18 = (bf16[2,24,16,192]{3,2,1,0:T(8,128)(2,1)S(1)}, bf16[2,24,16,192]{3,2,1,0:T(8,128)(2,1)S(1)}, u32[]{:S(2)}, u32[]{:S(2)}) collective-permute-start(bf16[2,24,16,192]{3,2,1,0:T(8,128)(2,1)S(1)} %shard_map.120.own_ref), channel_id=1, source_target_pairs={{0,1},{1,2},{2,3},{3,4},{4,5},{5,6},{6,7},{7,8},{8,9},{9,10},{10,1... | collective-permute-start | bytes 884744 | tf_op jit(solution)/shard_map/ppermute | solution.py:30
  56.0 1.0 %collective-permute-start.19 = (bf16[2,256,128]{2,1,0:T(8,128)(2,1)S(1)}, bf16[2,256,128]{2,1,0:T(8,128)(2,1)S(1)}, u32[]{:S(2)}, u32[]{:S(2)}) collective-permute-start(bf16[2,256,128]{2,1,0:T(8,128)(2,1)S(1)} %slice.14), channel_id=1, source_target_pairs={{0,2},{1,3},{2,0},{3,1},{4,6},{5,7},{6,4},{7,5},{8,10},{9,11},{10,... | collective-permute-start | bytes 393224 | tf_op jit(solution)/shard_map/ppermute | solution.py:25
  57.0 0.6 collective-permute-start.20
  57.6 0.5 collective-permute-start.21
  58.1 4.3 %collective-permute-done.19.rest_3_ = bf16[2,256,128]{2,1,0:T(8,128)(2,1)S(1)} collective-permute-done((bf16[2,256,128]{2,1,0:T(8,128)(2,1)S(1)}, bf16[2,256,128]{2,1,0:T(8,128)(2,1)S(1)}, u32[]{:S(2)}, u32[]{:S(2)}) %collective-permute-start.19) | collective-permute-done | bytes 131104 | tf_op jit(solution)/shard_map/ppermute | solution.py:25
  62.3 1.9 %collective-permute-start.23 = (bf16[4,256,128]{2,1,0:T(8,128)(2,1)S(1)}, bf16[4,256,128]{2,1,0:T(8,128)(2,1)S(1)}, u32[]{:S(2)}, u32[]{:S(2)}) collective-permute-start(bf16[4,256,128]{2,1,0:T(8,128)(2,1)S(1)} %collective-permute-done.12.rest_2_), channel_id=1, source_target_pairs={{0,1},{1,0},{2,3},{3,2},{4,5},{5,4},{6,7},{7,6},{8,9},{9,8},{10,11... | collective-permute-start | bytes 786440 | tf_op jit(solution)/shard_map/ppermute | solution.py:25
  64.3 0.5 collective-permute-start.25
  64.8 0.8 collective-permute-done.24.rest_8_
  65.9 6.3 %shard_map.121 = bf16[192,128]{1,0:T(8,128)(2,1)S(1)} custom-call(s32[32]{0:T(128)S(1)} %copy-done.14, s32[1]{0:T(128)} %bitcast.11.first_ref, bf16[2,24,16,192]{3,2,1,0:T(8,128)(2,1)S(1)} %shard_map.120.own_ref, bf16[2,24,16,192]{3,2,1,0:T(8,128)(2,1)S(1)} %collective-permute-done.18.rim_ref, bf16[2,24,16,192]{3,2,1,0:T(8,128)(2,1)S(1)} %bitcast.25, ...), custom_call_target="tpu_custom_call" | custom-call | tf_op jit(solution)/shard_map/pallas_call | solution.py:475
  72.1 1.6 %collective-permute-start.26 = (bf16[192,128]{1,0:T(8,128)(2,1)S(1)}, bf16[192,128]{1,0:T(8,128)(2,1)S(1)}, u32[]{:S(2)}, u32[]{:S(2)}) collective-permute-start(bf16[192,128]{1,0:T(8,128)(2,1)S(1)} %shard_map.121), channel_id=1, source_target_pairs={{0,4},{1,5},{2,6},{3,7},{4,0},{5,1},{6,2},{7,3},{8,12},{9,13},{10,... | collective-permute-start | bytes 147464 | tf_op jit(solution)/shard_map/ppermute | solution.py:25
  73.8 2.6 %collective-permute-start.27 = (bf16[192,128]{1,0:T(8,128)(2,1)S(1)}, bf16[192,128]{1,0:T(8,128)(2,1)S(1)}, u32[]{:S(2)}, u32[]{:S(2)}) collective-permute-start(bf16[192,128]{1,0:T(8,128)(2,1)S(1)} %shard_map.121), channel_id=1, source_target_pairs={{0,8},{1,9},{2,10},{3,11},{4,12},{5,13},{6,14},{7,15},{8,0},{9,1},... | collective-permute-start | bytes 147464 | tf_op jit(solution)/shard_map/ppermute | solution.py:25
  76.6 3.2 %collective-permute-done.27 = bf16[192,128]{1,0:T(8,128)(2,1)S(1)} collective-permute-done((bf16[192,128]{1,0:T(8,128)(2,1)S(1)}, bf16[192,128]{1,0:T(8,128)(2,1)S(1)}, u32[]{:S(2)}, u32[]{:S(2)}) %collective-permute-start.27) | collective-permute-done | bytes 49184 | tf_op jit(solution)/shard_map/ppermute | solution.py:25
  79.8 2.4 %collective-permute-done.28 = bf16[192,128]{1,0:T(8,128)(2,1)S(1)} collective-permute-done((bf16[192,128]{1,0:T(8,128)(2,1)S(1)}, bf16[192,128]{1,0:T(8,128)(2,1)S(1)}, u32[]{:S(2)}, u32[]{:S(2)}) %collective-permute-start.28) | collective-permute-done | bytes 49184 | tf_op jit(solution)/shard_map/ppermute | solution.py:25
  82.4 5.6 %collective-permute-done.29.rest_1_ = bf16[768,128]{1,0:T(8,128)(2,1)S(1)} collective-permute-done((bf16[768,128]{1,0:T(8,128)(2,1)S(1)}, bf16[768,128]{1,0:T(8,128)(2,1)S(1)}, u32[]{:S(2)}, u32[]{:S(2)}) %collective-permute-start.29) | collective-permute-done | bytes 196640 | tf_op jit(solution)/shard_map/ppermute | solution.py:25
  88.0 1.4 %collective-permute-done.31.rest_3_ = bf16[768,128]{1,0:T(8,128)(2,1)S(1)} collective-permute-done((bf16[768,128]{1,0:T(8,128)(2,1)S(1)}, bf16[768,128]{1,0:T(8,128)(2,1)S(1)}, u32[]{:S(2)}, u32[]{:S(2)}) %collective-permute-start.31) | collective-permute-done | bytes 196640 | tf_op jit(solution)/shard_map/ppermute | solution.py:25
  89.5 3.2 %shard_map.122 = bf16[192,3072]{1,0:T(8,128)(2,1)} custom-call(s32[3,192]{1,0:T(4,128)S(1)} %pad_add_fusion.place_ref, bf16[64,3072]{1,0:T(8,128)(2,1)S(1)} %copy-done, f32[1,3072]{1,0:T(1,128)S(1)} %bitcast.32, f32[1,3072]{1,0:T(1,128)S(1)} %bitcast.33, bf16[768,128]{1,0:T(8,128)(2,1)S(1)} %pad_maximum_fusion.2.rest_0_, ...), custom_call_target="tpu_custom_call" | custom-call | tf_op jit(solution)/shard_map/pallas_call | solution.py:497
  (70 shorter events, 2.0 us)
Async XLA Ops:
  0.0 0.9 %copy-start.4 = (bf16[27,192,12]{1,0,2:T(8,128)(2,1)S(1)}, bf16[27,192,12]{1,0,2:T(8,128)(2,1)}, u32[]{:S(2)}) copy-start(bf16[27,192,12]{1,0,2:T(8,128)(2,1)} %param.15) | copy-start | bytes 373252
  0.9 0.9 %copy-start.5 = (bf16[27,192,12]{1,0,2:T(8,128)(2,1)S(1)}, bf16[27,192,12]{1,0,2:T(8,128)(2,1)}, u32[]{:S(2)}) copy-start(bf16[27,192,12]{1,0,2:T(8,128)(2,1)} %param.17) | copy-start | bytes 373252
  2.0 10.1 %collective-permute-start = (bf16[256,128]{1,0:T(8,128)(2,1)S(1)}, bf16[256,128]{1,0:T(8,128)(2,1)S(1)}, u32[]{:S(2)}, u32[]{:S(2)}) collective-permute-start(bf16[256,128]{1,0:T(8,128)(2,1)S(1)} %get-tuple-element.38), channel_id=1, source_target_pairs={{0,4},{1,5},{2,6},{3,7},{4,0},{5,1},{6,2},{7,3},{8,12},{9,13},{10,... | collective-permute-start | bytes 196616 | tf_op jit(solution)/shard_map/ppermute | solution.py:25
  5.1 7.3 %collective-permute-start.1 = (bf16[256,128]{1,0:T(8,128)(2,1)S(1)}, bf16[256,128]{1,0:T(8,128)(2,1)S(1)}, u32[]{:S(2)}, u32[]{:S(2)}) collective-permute-start(bf16[256,128]{1,0:T(8,128)(2,1)S(1)} %get-tuple-element.38), channel_id=1, source_target_pairs={{0,8},{1,9},{2,10},{3,11},{4,12},{5,13},{6,14},{7,15},{8,0},{9,1},... | collective-permute-start | bytes 196616 | tf_op jit(solution)/shard_map/ppermute | solution.py:25
  7.6 6.1 %collective-permute-start.2 = (bf16[256,128]{1,0:T(8,128)(2,1)S(1)}, bf16[256,128]{1,0:T(8,128)(2,1)S(1)}, u32[]{:S(2)}, u32[]{:S(2)}) collective-permute-start(bf16[256,128]{1,0:T(8,128)(2,1)S(1)} %get-tuple-element.38), channel_id=1, source_target_pairs={{0,12},{1,13},{2,14},{3,15},{4,8},{5,9},{6,10},{7,11},{8,4},{9,5},... | collective-permute-start | bytes 196616 | tf_op jit(solution)/shard_map/ppermute | solution.py:25
  8.7 5.0 %collective-permute-start.3 = (bf16[2,16,24,192]{3,1,2,0:T(8,128)(2,1)S(1)}, bf16[2,16,24,192]{3,1,2,0:T(8,128)(2,1)S(1)}, u32[]{:S(2)}, u32[]{:S(2)}) collective-permute-start(bf16[2,16,24,192]{3,1,2,0:T(8,128)(2,1)S(1)} %copy.17), channel_id=1, source_target_pairs={{0,1},{1,2},{2,3},{3,4},{4,5},{5,6},{6,7},{7,8},{8,9},{9,10},{10,1... | collective-permute-start | bytes 884744 | tf_op jit(solution)/shard_map/ppermute | solution.py:30
  10.9 0.9 %copy-start.3 = (bf16[27,192,16]{1,2,0:T(8,128)(2,1)S(1)}, bf16[27,192,16]{1,2,0:T(8,128)(2,1)}, u32[]{:S(2)}) copy-start(bf16[27,192,16]{1,2,0:T(8,128)(2,1)} %param.19) | copy-start | bytes 497668
  11.8 32.4 %copy-start.14 = (s32[32]{0:T(128)S(1)}, s32[32]{0:T(128)}, u32[]{:S(2)}) copy-start(s32[32]{0:T(128)} %clips_ref.3) | copy-start | bytes 388
  11.9 32.4 %copy-start.15 = (f32[192]{0:T(256)S(1)}, f32[192]{0:T(256)}, u32[]{:S(2)}) copy-start(f32[192]{0:T(256)} %param.14) | copy-start | bytes 2308
  11.9 32.5 %copy-start.16 = (f32[192]{0:T(256)S(1)}, f32[192]{0:T(256)}, u32[]{:S(2)}) copy-start(f32[192]{0:T(256)} %param.16) | copy-start | bytes 2308
  13.7 0.7 copy-start.1
  14.5 17.6 %collective-permute-start.4 = (bf16[4,256,128]{2,1,0:T(8,128)(2,1)S(1)}, bf16[4,256,128]{2,1,0:T(8,128)(2,1)S(1)}, u32[]{:S(2)}, u32[]{:S(2)}) collective-permute-start(bf16[4,256,128]{2,1,0:T(8,128)(2,1)S(1)} %pad_maximum_fusion.rest_0_), channel_id=1, source_target_pairs={{0,2},{1,3},{2,0},{3,1},{4,6},{5,7},{6,4},{7,5},{8,10},{9,11},{10,... | collective-permute-start | bytes 786440 | tf_op jit(solution)/shard_map/ppermute | solution.py:25
  20.4 11.7 %collective-permute-start.5 = (bf16[4,256,128]{2,1,0:T(8,128)(2,1)S(1)}, bf16[4,256,128]{2,1,0:T(8,128)(2,1)}, u32[]{:S(2)}, u32[]{:S(2)}) collective-permute-start(bf16[4,256,128]{2,1,0:T(8,128)(2,1)S(1)} %pad_maximum_fusion.rest_0_), channel_id=1, source_target_pairs={{0,16},{16,0},{1,17},{17,1},{2,18},{18,2},{3,19},{19,3},{4,20},{20... | collective-permute-start | bytes 786440 | tf_op jit(solution)/shard_map/ppermute | solution.py:25
  21.9 4.4 %collective-permute-start.6 = (bf16[256,128]{1,0:T(8,128)(2,1)S(1)}, bf16[256,128]{1,0:T(8,128)(2,1)S(1)}, u32[]{:S(2)}, u32[]{:S(2)}) collective-permute-start(bf16[256,128]{1,0:T(8,128)(2,1)S(1)} %get-tuple-element.50), channel_id=1, source_target_pairs={{0,4},{1,5},{2,6},{3,7},{4,0},{5,1},{6,2},{7,3},{8,12},{9,13},{10,... | collective-permute-start | bytes 196616 | tf_op jit(solution)/shard_map/ppermute | solution.py:25
  22.6 7.0 %collective-permute-start.7 = (bf16[256,128]{1,0:T(8,128)(2,1)S(1)}, bf16[256,128]{1,0:T(8,128)(2,1)S(1)}, u32[]{:S(2)}, u32[]{:S(2)}) collective-permute-start(bf16[256,128]{1,0:T(8,128)(2,1)S(1)} %get-tuple-element.50), channel_id=1, source_target_pairs={{0,8},{1,9},{2,10},{3,11},{4,12},{5,13},{6,14},{7,15},{8,0},{9,1},... | collective-permute-start | bytes 196616 | tf_op jit(solution)/shard_map/ppermute | solution.py:25
  26.1 6.1 %collective-permute-start.8 = (bf16[256,128]{1,0:T(8,128)(2,1)S(1)}, bf16[256,128]{1,0:T(8,128)(2,1)S(1)}, u32[]{:S(2)}, u32[]{:S(2)}) collective-permute-start(bf16[256,128]{1,0:T(8,128)(2,1)S(1)} %get-tuple-element.50), channel_id=1, source_target_pairs={{0,12},{1,13},{2,14},{3,15},{4,8},{5,9},{6,10},{7,11},{8,4},{9,5},... | collective-permute-start | bytes 196616 | tf_op jit(solution)/shard_map/ppermute | solution.py:25
  32.2 5.0 %collective-permute-start.10 = (bf16[2,256,128]{2,1,0:T(8,128)(2,1)S(1)}, bf16[2,256,128]{2,1,0:T(8,128)(2,1)S(1)}, u32[]{:S(2)}, u32[]{:S(2)}) collective-permute-start(bf16[2,256,128]{2,1,0:T(8,128)(2,1)S(1)} %slice.13), channel_id=1, source_target_pairs={{0,16},{16,0},{1,17},{17,1},{2,18},{18,2},{3,19},{19,3},{4,20},{20... | collective-permute-start | bytes 393224 | tf_op jit(solution)/shard_map/ppermute | solution.py:25
  33.7 5.0 %collective-permute-start.9 = (bf16[2,256,128]{2,1,0:T(8,128)(2,1)S(1)}, bf16[2,256,128]{2,1,0:T(8,128)(2,1)S(1)}, u32[]{:S(2)}, u32[]{:S(2)}) collective-permute-start(bf16[2,256,128]{2,1,0:T(8,128)(2,1)S(1)} %slice.12), channel_id=1, source_target_pairs={{0,2},{1,3},{2,0},{3,1},{4,6},{5,7},{6,4},{7,5},{8,10},{9,11},{10,... | collective-permute-start | bytes 393224 | tf_op jit(solution)/shard_map/ppermute | solution.py:25
  38.7 1.1 %copy-start.6 = (bf16[2,256,128]{2,1,0:T(8,128)(2,1)}, bf16[2,256,128]{2,1,0:T(8,128)(2,1)S(1)}, u32[]{:S(2)}) copy-start(bf16[2,256,128]{2,1,0:T(8,128)(2,1)S(1)} %collective-permute-done.9.rest_3_) | copy-start | bytes 393220
  38.7 1.3 %collective-permute-start.16 = (bf16[2,256,128]{2,1,0:T(8,128)(2,1)S(1)}, bf16[2,256,128]{2,1,0:T(8,128)(2,1)S(1)}, u32[]{:S(2)}, u32[]{:S(2)}) collective-permute-start(bf16[2,256,128]{2,1,0:T(8,128)(2,1)S(1)} %collective-permute-done.9.rest_3_), channel_id=1, source_target_pairs={{0,1},{1,0},{2,3},{3,2},{4,5},{5,4},{6,7},{7,6},{8,9},{9,8},{10,11... | collective-permute-start | bytes 393224 | tf_op jit(solution)/shard_map/ppermute | solution.py:25
  38.7 3.4 %collective-permute-start.17 = (bf16[2,256,128]{2,1,0:T(8,128)(2,1)S(1)}, bf16[2,256,128]{2,1,0:T(8,128)(2,1)S(1)}, u32[]{:S(2)}, u32[]{:S(2)}) collective-permute-start(bf16[2,256,128]{2,1,0:T(8,128)(2,1)S(1)} %collective-permute-done.10.rest_4_), channel_id=1, source_target_pairs={{0,1},{1,0},{2,3},{3,2},{4,5},{5,4},{6,7},{7,6},{8,9},{9,8},{10,11... | collective-permute-start | bytes 393224 | tf_op jit(solution)/shard_map/ppermute | solution.py:25
  39.2 5.1 %collective-permute-start.14 = (bf16[4,256,128]{2,1,0:T(8,128)(2,1)S(1)}, bf16[4,256,128]{2,1,0:T(8,128)(2,1)}, u32[]{:S(2)}, u32[]{:S(2)}) collective-permute-start(bf16[4,256,128]{2,1,0:T(8,128)(2,1)S(1)} %collective-permute-done.4.rest_1_), channel_id=1, source_target_pairs={{0,1},{1,0},{2,3},{3,2},{4,5},{5,4},{6,7},{7,6},{8,9},{9,8},{10,11... | collective-permute-start | bytes 786440 | tf_op jit(solution)/shard_map/ppermute | solution.py:25
  39.2 5.1 %collective-permute-start.15 = (bf16[4,256,128]{2,1,0:T(8,128)(2,1)}, bf16[4,256,128]{2,1,0:T(8,128)(2,1)}, u32[]{:S(2)}, u32[]{:S(2)}) collective-permute-start(bf16[4,256,128]{2,1,0:T(8,128)(2,1)} %collective-permute-done.5.rest_2_), channel_id=1, source_target_pairs={{0,1},{1,0},{2,3},{3,2},{4,5},{5,4},{6,7},{7,6},{8,9},{9,8},{10,11... | collective-permute-start | bytes 786440 | tf_op jit(solution)/shard_map/ppermute | solution.py:25
  39.7 4.5 %collective-permute-start.13 = (bf16[4,256,128]{2,1,0:T(8,128)(2,1)S(1)}, bf16[4,256,128]{2,1,0:T(8,128)(2,1)}, u32[]{:S(2)}, u32[]{:S(2)}) collective-permute-start(bf16[4,256,128]{2,1,0:T(8,128)(2,1)S(1)} %pad_maximum_fusion.rest_0_), channel_id=1, source_target_pairs={{0,1},{1,0},{2,3},{3,2},{4,5},{5,4},{6,7},{7,6},{8,9},{9,8},{10,11... | collective-permute-start | bytes 786440 | tf_op jit(solution)/shard_map/ppermute | solution.py:25
  40.7 15.2 %collective-permute-start.11 = (bf16[4,256,128]{2,1,0:T(8,128)(2,1)S(1)}, bf16[4,256,128]{2,1,0:T(8,128)(2,1)S(1)}, u32[]{:S(2)}, u32[]{:S(2)}) collective-permute-start(bf16[4,256,128]{2,1,0:T(8,128)(2,1)S(1)} %pad_maximum_fusion.1.rest_0_), channel_id=1, source_target_pairs={{0,2},{1,3},{2,0},{3,1},{4,6},{5,7},{6,4},{7,5},{8,10},{9,11},{10,... | collective-permute-start | bytes 786440 | tf_op jit(solution)/shard_map/ppermute | solution.py:25
  42.8 13.2 %collective-permute-start.12 = (bf16[4,256,128]{2,1,0:T(8,128)(2,1)S(1)}, bf16[4,256,128]{2,1,0:T(8,128)(2,1)S(1)}, u32[]{:S(2)}, u32[]{:S(2)}) collective-permute-start(bf16[4,256,128]{2,1,0:T(8,128)(2,1)S(1)} %pad_maximum_fusion.1.rest_0_), channel_id=1, source_target_pairs={{0,16},{16,0},{1,17},{17,1},{2,18},{18,2},{3,19},{19,3},{4,20},{20... | collective-permute-start | bytes 786440 | tf_op jit(solution)/shard_map/ppermute | solution.py:25
  44.3 1.0 %copy-start.2 = (bf16[2,16,24,192]{3,1,2,0:T(8,128)(2,1)S(1)}, bf16[2,16,24,192]{3,1,2,0:T(8,128)(2,1)}, u32[]{:S(2)}) copy-start(bf16[2,16,24,192]{3,1,2,0:T(8,128)(2,1)} %copy-done.1) | copy-start | bytes 884740
  45.3 0.9 copy-start.7
  46.2 0.9 copy-start.9
  47.1 0.9 copy-start.11
  48.0 17.8 %copy-start.17 = (f32[192]{0:T(256)S(1)}, f32[192]{0:T(256)}, u32[]{:S(2)}) copy-start(f32[192]{0:T(256)} %param.18) | copy-start | bytes 2308
  54.1 10.2 %collective-permute-start.18 = (bf16[2,24,16,192]{3,2,1,0:T(8,128)(2,1)S(1)}, bf16[2,24,16,192]{3,2,1,0:T(8,128)(2,1)S(1)}, u32[]{:S(2)}, u32[]{:S(2)}) collective-permute-start(bf16[2,24,16,192]{3,2,1,0:T(8,128)(2,1)S(1)} %shard_map.120.own_ref), channel_id=1, source_target_pairs={{0,1},{1,2},{2,3},{3,4},{4,5},{5,6},{6,7},{7,8},{8,9},{9,10},{10,1... | collective-permute-start | bytes 884744 | tf_op jit(solution)/shard_map/ppermute | solution.py:30
  56.0 6.4 %collective-permute-start.19 = (bf16[2,256,128]{2,1,0:T(8,128)(2,1)S(1)}, bf16[2,256,128]{2,1,0:T(8,128)(2,1)S(1)}, u32[]{:S(2)}, u32[]{:S(2)}) collective-permute-start(bf16[2,256,128]{2,1,0:T(8,128)(2,1)S(1)} %slice.14), channel_id=1, source_target_pairs={{0,2},{1,3},{2,0},{3,1},{4,6},{5,7},{6,4},{7,5},{8,10},{9,11},{10,... | collective-permute-start | bytes 393224 | tf_op jit(solution)/shard_map/ppermute | solution.py:25
  57.0 7.3 %collective-permute-start.20 = (bf16[2,256,128]{2,1,0:T(8,128)(2,1)S(1)}, bf16[2,256,128]{2,1,0:T(8,128)(2,1)S(1)}, u32[]{:S(2)}, u32[]{:S(2)}) collective-permute-start(bf16[2,256,128]{2,1,0:T(8,128)(2,1)S(1)} %slice.15), channel_id=1, source_target_pairs={{0,16},{16,0},{1,17},{17,1},{2,18},{18,2},{3,19},{19,3},{4,20},{20... | collective-permute-start | bytes 393224 | tf_op jit(solution)/shard_map/ppermute | solution.py:25
  57.6 8.3 %collective-permute-start.22 = (bf16[4,256,128]{2,1,0:T(8,128)(2,1)S(1)}, bf16[4,256,128]{2,1,0:T(8,128)(2,1)S(1)}, u32[]{:S(2)}, u32[]{:S(2)}) collective-permute-start(bf16[4,256,128]{2,1,0:T(8,128)(2,1)S(1)} %collective-permute-done.11.rest_1_), channel_id=1, source_target_pairs={{0,1},{1,0},{2,3},{3,2},{4,5},{5,4},{6,7},{7,6},{8,9},{9,8},{10,11... | collective-permute-start | bytes 786440 | tf_op jit(solution)/shard_map/ppermute | solution.py:25
  57.6 8.3 %collective-permute-start.21 = (bf16[4,256,128]{2,1,0:T(8,128)(2,1)S(1)}, bf16[4,256,128]{2,1,0:T(8,128)(2,1)S(1)}, u32[]{:S(2)}, u32[]{:S(2)}) collective-permute-start(bf16[4,256,128]{2,1,0:T(8,128)(2,1)S(1)} %pad_maximum_fusion.1.rest_0_), channel_id=1, source_target_pairs={{0,1},{1,0},{2,3},{3,2},{4,5},{5,4},{6,7},{7,6},{8,9},{9,8},{10,11... | collective-permute-start | bytes 786440 | tf_op jit(solution)/shard_map/ppermute | solution.py:25
  62.3 3.5 %collective-permute-start.23 = (bf16[4,256,128]{2,1,0:T(8,128)(2,1)S(1)}, bf16[4,256,128]{2,1,0:T(8,128)(2,1)S(1)}, u32[]{:S(2)}, u32[]{:S(2)}) collective-permute-start(bf16[4,256,128]{2,1,0:T(8,128)(2,1)S(1)} %collective-permute-done.12.rest_2_), channel_id=1, source_target_pairs={{0,1},{1,0},{2,3},{3,2},{4,5},{5,4},{6,7},{7,6},{8,9},{9,8},{10,11... | collective-permute-start | bytes 786440 | tf_op jit(solution)/shard_map/ppermute | solution.py:25
  64.3 1.3 %collective-permute-start.24 = (bf16[2,256,128]{2,1,0:T(8,128)(2,1)S(1)}, bf16[2,256,128]{2,1,0:T(8,128)(2,1)S(1)}, u32[]{:S(2)}, u32[]{:S(2)}) collective-permute-start(bf16[2,256,128]{2,1,0:T(8,128)(2,1)S(1)} %collective-permute-done.19.rest_3_), channel_id=1, source_target_pairs={{0,1},{1,0},{2,3},{3,2},{4,5},{5,4},{6,7},{7,6},{8,9},{9,8},{10,11... | collective-permute-start | bytes 393224 | tf_op jit(solution)/shard_map/ppermute | solution.py:25
  64.3 1.5 %collective-permute-start.25 = (bf16[2,256,128]{2,1,0:T(8,128)(2,1)S(1)}, bf16[2,256,128]{2,1,0:T(8,128)(2,1)S(1)}, u32[]{:S(2)}, u32[]{:S(2)}) collective-permute-start(bf16[2,256,128]{2,1,0:T(8,128)(2,1)S(1)} %collective-permute-done.20.rest_4_), channel_id=1, source_target_pairs={{0,1},{1,0},{2,3},{3,2},{4,5},{5,4},{6,7},{7,6},{8,9},{9,8},{10,11... | collective-permute-start | bytes 393224 | tf_op jit(solution)/shard_map/ppermute | solution.py:25
  65.8 23.6 %copy-start = (bf16[64,3072]{1,0:T(8,128)(2,1)S(1)}, bf16[64,3072]{1,0:T(8,128)(2,1)}, u32[]{:S(2)}) copy-start(bf16[64,3072]{1,0:T(8,128)(2,1)} %embed_ref.1) | copy-start | bytes 1179652
  65.9 23.6 %copy-start.12 = (f32[3072]{0:T(1024)S(1)}, f32[3072]{0:T(1024)}, u32[]{:S(2)}) copy-start(f32[3072]{0:T(1024)} %param.22) | copy-start | bytes 36868
  65.9 23.6 %copy-start.13 = (f32[3072]{0:T(1024)S(1)}, f32[3072]{0:T(1024)}, u32[]{:S(2)}) copy-start(f32[3072]{0:T(1024)} %param.21) | copy-start | bytes 36868
  72.1 4.5 %collective-permute-start.26 = (bf16[192,128]{1,0:T(8,128)(2,1)S(1)}, bf16[192,128]{1,0:T(8,128)(2,1)S(1)}, u32[]{:S(2)}, u32[]{:S(2)}) collective-permute-start(bf16[192,128]{1,0:T(8,128)(2,1)S(1)} %shard_map.121), channel_id=1, source_target_pairs={{0,4},{1,5},{2,6},{3,7},{4,0},{5,1},{6,2},{7,3},{8,12},{9,13},{10,... | collective-permute-start | bytes 147464 | tf_op jit(solution)/shard_map/ppermute | solution.py:25
  73.8 6.1 %collective-permute-start.27 = (bf16[192,128]{1,0:T(8,128)(2,1)S(1)}, bf16[192,128]{1,0:T(8,128)(2,1)S(1)}, u32[]{:S(2)}, u32[]{:S(2)}) collective-permute-start(bf16[192,128]{1,0:T(8,128)(2,1)S(1)} %shard_map.121), channel_id=1, source_target_pairs={{0,8},{1,9},{2,10},{3,11},{4,12},{5,13},{6,14},{7,15},{8,0},{9,1},... | collective-permute-start | bytes 147464 | tf_op jit(solution)/shard_map/ppermute | solution.py:25
  76.4 5.9 %collective-permute-start.28 = (bf16[192,128]{1,0:T(8,128)(2,1)S(1)}, bf16[192,128]{1,0:T(8,128)(2,1)S(1)}, u32[]{:S(2)}, u32[]{:S(2)}) collective-permute-start(bf16[192,128]{1,0:T(8,128)(2,1)S(1)} %shard_map.121), channel_id=1, source_target_pairs={{0,12},{1,13},{2,14},{3,15},{4,8},{5,9},{6,10},{7,11},{8,4},{9,5},... | collective-permute-start | bytes 147464 | tf_op jit(solution)/shard_map/ppermute | solution.py:25
  82.3 5.7 %collective-permute-start.29 = (bf16[768,128]{1,0:T(8,128)(2,1)S(1)}, bf16[768,128]{1,0:T(8,128)(2,1)S(1)}, u32[]{:S(2)}, u32[]{:S(2)}) collective-permute-start(bf16[768,128]{1,0:T(8,128)(2,1)S(1)} %pad_maximum_fusion.2.rest_0_), channel_id=1, source_target_pairs={{0,2},{1,3},{2,0},{3,1},{4,6},{5,7},{6,4},{7,5},{8,10},{9,11},{10,... | collective-permute-start | bytes 589832 | tf_op jit(solution)/shard_map/ppermute | solution.py:25
  82.3 5.7 %collective-permute-start.30 = (bf16[768,128]{1,0:T(8,128)(2,1)S(1)}, bf16[768,128]{1,0:T(8,128)(2,1)S(1)}, u32[]{:S(2)}, u32[]{:S(2)}) collective-permute-start(bf16[768,128]{1,0:T(8,128)(2,1)S(1)} %pad_maximum_fusion.2.rest_0_), channel_id=1, source_target_pairs={{0,1},{1,0},{2,3},{3,2},{4,5},{5,4},{6,7},{7,6},{8,9},{9,8},{10,11... | collective-permute-start | bytes 589832 | tf_op jit(solution)/shard_map/ppermute | solution.py:25
  88.0 1.4 %collective-permute-start.31 = (bf16[768,128]{1,0:T(8,128)(2,1)S(1)}, bf16[768,128]{1,0:T(8,128)(2,1)S(1)}, u32[]{:S(2)}, u32[]{:S(2)}) collective-permute-start(bf16[768,128]{1,0:T(8,128)(2,1)S(1)} %collective-permute-done.29.rest_1_), channel_id=1, source_target_pairs={{0,1},{1,0},{2,3},{3,2},{4,5},{5,4},{6,7},{7,6},{8,9},{9,8},{10,11... | collective-permute-start | bytes 589832 | tf_op jit(solution)/shard_map/ppermute | solution.py:25
  (2 other events, 1.3 us)

commit v5 on v4

--- a/solution.py
+++ b/solution.py
@@ -16,6 +16,7 @@
 VMEM_SPEC = pl.BlockSpec(memory_space=pltpu.VMEM)
 SMEM_SPEC = pl.BlockSpec(memory_space=pltpu.SMEM)
 IN_VMEM = functools.partial(pltpu.with_memory_space_constraint, memory_space=pltpu.VMEM)
+IN_HBM = functools.partial(pltpu.with_memory_space_constraint, memory_space=pltpu.HBM)
 SMALL = pltpu.CompilerParams(vmem_limit_bytes=4 * 2**20)
 LARGE = pltpu.CompilerParams(vmem_limit_bytes=24 * 2**20)
 
@@ -37,9 +38,8 @@
 
 
 def pack_kernel(half_ref, *refs, unit_channels):
-    count = len(refs) // 2
-    staged = refs[-1]
-    for weight_ref, unit_ref in zip(refs[:count], refs[count:-1]):
+    *weight_refs, unit_ref, staged = refs
+    for index, weight_ref in enumerate(weight_refs):
         _, taps, channels = weight_ref.shape
         pairs, head_rows = unit_geometry(taps, unit_channels)
         tail = channels - LANES
@@ -50,18 +50,18 @@
             at = head_rows + channel * pairs
             staged[at : at + pairs, 0:tail] = rows[:pairs, LANES:]
             staged[at : at + taps - pairs, tail : 2 * tail] = rows[pairs:, LANES:]
-        unit_ref[...] = staged[...].astype(jnp.bfloat16)
+        unit_ref[index] = staged[...].astype(jnp.bfloat16)
 
 
 def pack_units(half, weights, unit_channels):
     return pl.pallas_call(
         functools.partial(pack_kernel, unit_channels=unit_channels),
-        out_shape=[pltpu.VMEM((UNIT_ROWS, LANES), jnp.bfloat16)] * len(weights),
+        out_shape=pltpu.VMEM((len(weights), UNIT_ROWS, LANES), jnp.bfloat16),
         in_specs=[SMEM_SPEC] + [VMEM_SPEC] * len(weights),
-        out_specs=[VMEM_SPEC] * len(weights),
+        out_specs=VMEM_SPEC,
         scratch_shapes=[pltpu.VMEM((UNIT_ROWS, LANES), jnp.float32)],
         compiler_params=SMALL,
-    )(half, *weights)
+    )(half, *map(IN_HBM, weights))
 
 
 def pack_whole(weight, units):
@@ -101,7 +101,7 @@
         in_specs=[VMEM_SPEC],
         out_specs=VMEM_SPEC,
         compiler_params=SMALL,
-    )(weight)
+    )(IN_HBM(weight))
 
 
 def rms_silu(values, gain_vector):
@@ -358,12 +358,12 @@
     return [unit] + [xor_permute(unit, "ctx", 4 * step) for step in (1, 2, 3)]
 
 
-def round_square(line):
-    return xor_permute(line, "ctx", 2), xor_permute(line, "groups", 1)
-
-
-def to_corner(across, other):
-    return xor_permute(other[:2], "ctx", 2), xor_permute(across[2:], "groups", 1)
+def round_square(half_line):
+    return xor_permute(half_line, "ctx", 2), xor_permute(half_line, "groups", 1)
+
+
+def in_unit_order(low, high, across, other, corners):
+    return [low, high, *across, *other, *corners]
 
 
 def both_cores(pieces):
@@ -426,23 +426,23 @@
 
     if grid:
         half = group.astype(jnp.int32).reshape(1)
-        packed_first, packed_second = pack_units(half, by_output, unit_channels)
-        line_first = along_line(packed_first)
-        line_first, wide, pick, place, turned, turned_rim = lax.optimization_barrier(
-            (line_first, wide, pick, place, turned, turned_rim)
+        line = along_line(pack_units(half, by_output, unit_channels))
+        lows = [jnp.stack([part[index] for part in line[:2]]) for index in range(2)]
+        low_squares = round_square(lows[0])
+        line, wide, pick, place, turned = lax.optimization_barrier(
+            (line, wide, pick, place, turned)
         )
-        line_first = jnp.stack(line_first)
-        packed_second, line_first = lax.optimization_barrier((packed_second, line_first))
-        square_first = round_square(line_first)
-        line_second = along_line(packed_second)
-        line_first, square_first, line_second = lax.optimization_barrier(
-            (line_first, square_first, line_second)
+        highs = [jnp.stack([part[index] for part in line[2:]]) for index in range(2)]
+        high_squares = round_square(highs[0])
+        across, other = zip(low_squares, high_squares)
+        corners = xor_permute(other[0], "ctx", 2), xor_permute(across[1], "groups", 1)
+        lows, highs, corners, turned_rim = lax.optimization_barrier(
+            (lows, highs, corners, turned_rim)
         )
-        corner_first = to_corner(*square_first)
-        line_second, corner_first = lax.optimization_barrier((line_second, corner_first))
-        line_second = jnp.stack(line_second)
-        square_second = round_square(line_second)
-        units_first = both_cores((line_first, *square_first, *corner_first))
+        units_first = both_cores(in_unit_order(lows[0], highs[0], across, other, corners))
+        across, other = zip(round_square(lows[1]), round_square(highs[1]))
+        corners = xor_permute(other[0], "ctx", 2), xor_permute(across[1], "groups", 1)
+        units_second = in_unit_order(lows[1], highs[1], across, other, corners)
     else:
         units_first, units_second = [
             [pack_whole(lax.all_gather(weight, "ctx", axis=0, tiled=True), units)]
@@ -460,16 +460,13 @@
         scratch_shapes=scratch,
         compiler_params=LARGE,
     )(
-        clip_ids, first, IN_VMEM(turned), IN_VMEM(turned_rim), gain_first.reshape(1, -1),
-        gain_second.reshape(1, -1), IN_VMEM(pick), *map(IN_VMEM, units_first),
+        clip_ids, first, IN_VMEM(turned), IN_HBM(turned_rim), gain_first.reshape(1, -1),
+        gain_second.reshape(1, -1), IN_VMEM(pick), *map(IN_HBM, units_first),
     )
     second_rim = to_next(second_in[frames - 2 :], "ctx")
     if grid:
-        line_second, square_second, second_in = lax.optimization_barrier(
-            (line_second, square_second, second_in)
-        )
-        corner_second = to_corner(*square_second)
-        units_second = both_cores((line_second, *square_second, *corner_second))
+        units_second, second_in = lax.optimization_barrier((units_second, second_in))
+        units_second = both_cores(units_second)
 
     depth = weight_out.shape[2]
     parts = pl.pallas_call(
@@ -485,7 +482,7 @@
         compiler_params=LARGE,
     )(
         clip_ids, first, IN_VMEM(second_in), IN_VMEM(second_rim), IN_VMEM(turned),
-        gain_third.reshape(1, -1), IN_VMEM(pick), IN_VMEM(wide), *map(IN_VMEM, units_second),
+        gain_third.reshape(1, -1), IN_VMEM(pick), IN_VMEM(wide), *map(IN_HBM, units_second),
     )
     if grid:
         line = jnp.concatenate(along_line(parts))

time: 93.1 us -> 81.7 us (0.88)
  local copies, waits for them, and re-layouts: 10.6 us -> 1.83 us
  waiting for transfers between devices: 29.3 us -> 24.8 us
  Pallas kernels: 15.8 us -> 18.9 us
    unnamed x37 -> x71, local copies, waits for them, and re-layouts: 9.65 us -> 1.79 us
    ppermute x30 -> x37, waiting for transfers between devices: 29.3 us -> 24.8 us  [xor_permute(): lax.ppermute(value, axis, [(source, source ^ mask) for source in range(co...]
    pallas_call x1, Pallas kernels: 0.11 us -> 1.15 us  [pack_units(): pl.pallas_call(functools.partial(pack_kernel, unit_channels=unit_channels...]
    pallas_call x1, Pallas kernels: 6.26 us -> 7.24 us  [body(): pl.pallas_call(functools.partial(second_kernel, taps=taps, unit_channels=...]
    pallas_call x1, Pallas kernels: 0.16 us -> 1.11 us  [expand_weight_out(): pl.pallas_call(expand_kernel, out_shape=pltpu.VMEM((16, 12 * depth, 2 * L...]
    ppermute x30 -> x37, starting transfers between devices: 32.6 us -> 32.3 us  [xor_permute(): lax.ppermute(value, axis, [(source, source ^ mask) for source in range(co...]
  transfers between devices with their start and end apart: 32 -> 39, of which waited for: 14 -> 18; matrix products, arithmetic and copies ran while one was open for 3% -> 2% of each run, Pallas kernels for 7% -> 9%
where the time goes in v5:
time: 81.7 us; the launch traced here: 81.4 us
  starting transfers between devices  35.1 us (43%)
  waiting for transfers between devices  24.8 us (30%)
  Pallas kernels  18.9 us (23%)
  local copies, waits for them, and re-layouts  1.83 us (2%)
    ppermute x37, starting transfers between devices, xor_permute(): lax.ppermute(value, axis, [(source, source ^ mask) for source in range(co...  32.3 us
    ppermute x37, waiting for transfers between devices, xor_permute(): lax.ppermute(value, axis, [(source, source ^ mask) for source in range(co...  24.8 us
    pallas_call x1, Pallas kernels, body(): pl.pallas_call(functools.partial(second_kernel, taps=taps, unit_channels=...  7.24 us
    pallas_call x1, Pallas kernels, body(): pl.pallas_call(functools.partial(first_kernel, taps=taps, unit_channels=u...  6.23 us
    pallas_call x1, Pallas kernels, body(): pl.pallas_call(embed_kernel, out_shape=jax.ShapeDtypeStruct((tokens, widt...  3.17 us
    ppermute x2, starting transfers between devices, to_next(): lax.ppermute(value, axis, [(source, source + 1) for source in range(count...  2.81 us
    unnamed x71, local copies, waits for them, and re-layouts  1.79 us
  transfers between devices with their start and end apart: 39, of which 18 were waited for; matrix products, arithmetic and copies ran while one was open for 2% of the time, Pallas kernels for 9%

profile of v5, /device:TPU:0, one launch (start us, length us, event | category | flops | bytes accessed | tf_op | source)
XLA Modules:
  0.0 81.4 jit_solution(17639414540077836036)
XLA Ops:
  0.0 1.1 %shard_map.118 = bf16[2,256,128]{2,1,0:T(8,128)(2,1)S(1)} custom-call(s32[1]{0:T(128)} %bitcast.half_ref, bf16[12,27,192]{2,1,0:T(8,128)(2,1)} %bitcast.25, bf16[12,27,192]{2,1,0:T(8,128)(2,1)} %bitcast.26), custom_call_target="tpu_custom_call" | custom-call | tf_op jit(solution)/shard_map/pallas_call | solution.py:57
  1.1 5.1 %collective-permute-start.2 = (bf16[2,256,128]{2,1,0:T(8,128)(2,1)S(1)}, bf16[2,256,128]{2,1,0:T(8,128)(2,1)S(1)}, u32[]{:S(2)}, u32[]{:S(2)}) collective-permute-start(bf16[2,256,128]{2,1,0:T(8,128)(2,1)S(1)} %shard_map.118), channel_id=1, source_target_pairs={{0,12},{1,13},{2,14},{3,15},{4,8},{5,9},{6,10},{7,11},{8,4},{9,5},... | collective-permute-start | bytes 393224 | tf_op jit(solution)/shard_map/ppermute | solution.py:26
  6.3 0.6 collective-permute-start
  6.9 1.1 %copy.17 = bf16[2,16,24,192]{3,1,2,0:T(8,128)(2,1)S(1)} copy(bf16[2,16,24,192]{3,2,1,0:T(8,128)(2,1)} %param.12) | data formatting | bytes 589824 | tf_op args[0]
  8.0 1.3 %collective-permute-start.7 = (bf16[2,16,24,192]{3,1,2,0:T(8,128)(2,1)S(1)}, bf16[2,16,24,192]{3,1,2,0:T(8,128)(2,1)S(1)}, u32[]{:S(2)}, u32[]{:S(2)}) collective-permute-start(bf16[2,16,24,192]{3,1,2,0:T(8,128)(2,1)S(1)} %copy.17), channel_id=1, source_target_pairs={{0,1},{1,2},{2,3},{3,4},{4,5},{5,6},{6,7},{7,8},{8,9},{9,10},{10,1... | collective-permute-start | bytes 884744 | tf_op jit(solution)/shard_map/ppermute | solution.py:31
  9.6 1.1 %shard_map.119.wide_ref = bf16[16,192,256]{2,1,0:T(8,128)(2,1)S(1)} custom-call(bf16[27,16,192]{2,1,0:T(8,128)(2,1)} %bitcast.24), custom_call_target="tpu_custom_call" | custom-call | tf_op jit(solution)/shard_map/pallas_call | solution.py:98
  10.7 4.0 %collective-permute-done = bf16[2,256,128]{2,1,0:T(8,128)(2,1)S(1)} collective-permute-done((bf16[2,256,128]{2,1,0:T(8,128)(2,1)S(1)}, bf16[2,256,128]{2,1,0:T(8,128)(2,1)S(1)}, u32[]{:S(2)}, u32[]{:S(2)}) %collective-permute-start) | collective-permute-done | bytes 131104 | tf_op jit(solution)/shard_map/ppermute | solution.py:26
  14.7 1.6 %collective-permute-start.3 = (bf16[2,256,128]{2,1,0:T(8,128)(2,1)S(1)}, bf16[2,256,128]{2,1,0:T(8,128)(2,1)S(1)}, u32[]{:S(2)}, u32[]{:S(2)}) collective-permute-start(bf16[2,256,128]{2,1,0:T(8,128)(2,1)S(1)} %pad_maximum_fusion.1.rest_0_), channel_id=1, source_target_pairs={{0,16},{16,0},{1,17},{17,1},{2,18},{18,2},{3,19},{19,3},{4,20},{20... | collective-permute-start | bytes 393224 | tf_op jit(solution)/shard_map/ppermute | solution.py:26
  16.3 1.0 %collective-permute-done.1 = bf16[2,256,128]{2,1,0:T(8,128)(2,1)S(1)} collective-permute-done((bf16[2,256,128]{2,1,0:T(8,128)(2,1)S(1)}, bf16[2,256,128]{2,1,0:T(8,128)(2,1)S(1)}, u32[]{:S(2)}, u32[]{:S(2)}) %collective-permute-start.1) | collective-permute-done | bytes 131104 | tf_op jit(solution)/shard_map/ppermute | solution.py:26
  17.4 1.6 %collective-permute-start.5 = (bf16[2,256,128]{2,1,0:T(8,128)(2,1)S(1)}, bf16[2,256,128]{2,1,0:T(8,128)(2,1)S(1)}, u32[]{:S(2)}, u32[]{:S(2)}) collective-permute-start(bf16[2,256,128]{2,1,0:T(8,128)(2,1)S(1)} %pad_maximum_fusion.3.rest_1_), channel_id=1, source_target_pairs={{0,2},{1,3},{2,0},{3,1},{4,6},{5,7},{6,4},{7,5},{8,10},{9,11},{10,... | collective-permute-start | bytes 393224 | tf_op jit(solution)/shard_map/ppermute | solution.py:26
  19.1 0.5 collective-permute-start.14
  19.5 1.5 %collective-permute-start.15 = (bf16[2,256,128]{2,1,0:T(8,128)(2,1)S(1)}, bf16[2,256,128]{2,1,0:T(8,128)(2,1)S(1)}, u32[]{:S(2)}, u32[]{:S(2)}) collective-permute-start(bf16[2,256,128]{2,1,0:T(8,128)(2,1)S(1)} %pad_maximum_fusion.3.rest_1_), channel_id=1, source_target_pairs={{0,16},{16,0},{1,17},{17,1},{2,18},{18,2},{3,19},{19,3},{4,20},{20... | collective-permute-start | bytes 393224 | tf_op jit(solution)/shard_map/ppermute | solution.py:26
  21.0 1.5 %collective-permute-start.4 = (bf16[2,256,128]{2,1,0:T(8,128)(2,1)S(1)}, bf16[2,256,128]{2,1,0:T(8,128)(2,1)S(1)}, u32[]{:S(2)}, u32[]{:S(2)}) collective-permute-start(bf16[2,256,128]{2,1,0:T(8,128)(2,1)S(1)} %collective-permute-done.3.rest_4_), channel_id=1, source_target_pairs={{0,2},{1,3},{2,0},{3,1},{4,6},{5,7},{6,4},{7,5},{8,10},{9,11},{10,... | collective-permute-start | bytes 393224 | tf_op jit(solution)/shard_map/ppermute | solution.py:26
  22.6 1.4 %collective-permute-done.5.rest_3_ = bf16[2,256,128]{2,1,0:T(8,128)(2,1)S(1)} collective-permute-done((bf16[2,256,128]{2,1,0:T(8,128)(2,1)S(1)}, bf16[2,256,128]{2,1,0:T(8,128)(2,1)S(1)}, u32[]{:S(2)}, u32[]{:S(2)}) %collective-permute-start.5) | collective-permute-done | bytes 131104 | tf_op jit(solution)/shard_map/ppermute | solution.py:26
  23.9 1.5 %collective-permute-start.6 = (bf16[2,256,128]{2,1,0:T(8,128)(2,1)S(1)}, bf16[2,256,128]{2,1,0:T(8,128)(2,1)}, u32[]{:S(2)}, u32[]{:S(2)}) collective-permute-start(bf16[2,256,128]{2,1,0:T(8,128)(2,1)S(1)} %collective-permute-done.5.rest_3_), channel_id=1, source_target_pairs={{0,16},{16,0},{1,17},{17,1},{2,18},{18,2},{3,19},{19,3},{4,20},{20... | collective-permute-start | bytes 393224 | tf_op jit(solution)/shard_map/ppermute | solution.py:26
  25.4 0.8 collective-permute-done.14.rest_2_
  26.3 0.5 collective-permute-start.19
  26.8 0.8 collective-permute-done.4.rest_6_
  27.7 1.3 %collective-permute-done.6.rest_7_ = bf16[2,256,128]{2,1,0:T(8,128)(2,1)} collective-permute-done((bf16[2,256,128]{2,1,0:T(8,128)(2,1)S(1)}, bf16[2,256,128]{2,1,0:T(8,128)(2,1)}, u32[]{:S(2)}, u32[]{:S(2)}) %collective-permute-start.6) | collective-permute-done | bytes 131104 | tf_op jit(solution)/shard_map/ppermute | solution.py:26
  29.0 0.5 collective-permute-start.17
  29.6 1.6 %collective-permute-start.10 = (bf16[2,256,128]{2,1,0:T(8,128)(2,1)S(1)}, bf16[2,256,128]{2,1,0:T(8,128)(2,1)S(1)}, u32[]{:S(2)}, u32[]{:S(2)}) collective-permute-start(bf16[2,256,128]{2,1,0:T(8,128)(2,1)S(1)} %pad_maximum_fusion.2.rest_0_), channel_id=1, source_target_pairs={{0,16},{16,0},{1,17},{17,1},{2,18},{18,2},{3,19},{19,3},{4,20},{20... | collective-permute-start | bytes 393224 | tf_op jit(solution)/shard_map/ppermute | solution.py:26
  31.2 1.5 %collective-permute-start.9 = (bf16[2,256,128]{2,1,0:T(8,128)(2,1)S(1)}, bf16[2,256,128]{2,1,0:T(8,128)(2,1)S(1)}, u32[]{:S(2)}, u32[]{:S(2)}) collective-permute-start(bf16[2,256,128]{2,1,0:T(8,128)(2,1)S(1)} %pad_maximum_fusion.4.rest_1_), channel_id=1, source_target_pairs={{0,2},{1,3},{2,0},{3,1},{4,6},{5,7},{6,4},{7,5},{8,10},{9,11},{10,... | collective-permute-start | bytes 393224 | tf_op jit(solution)/shard_map/ppermute | solution.py:26
  32.7 0.6 collective-permute-start.8
  33.3 0.5 collective-permute-start.11
  33.8 1.7 %collective-permute-done.10.rest_4_ = bf16[2,256,128]{2,1,0:T(8,128)(2,1)S(1)} collective-permute-done((bf16[2,256,128]{2,1,0:T(8,128)(2,1)S(1)}, bf16[2,256,128]{2,1,0:T(8,128)(2,1)S(1)}, u32[]{:S(2)}, u32[]{:S(2)}) %collective-permute-start.10) | collective-permute-done | bytes 131104 | tf_op jit(solution)/shard_map/ppermute | solution.py:26
  35.5 1.6 %collective-permute-start.12 = (bf16[2,256,128]{2,1,0:T(8,128)(2,1)S(1)}, bf16[2,256,128]{2,1,0:T(8,128)(2,1)}, u32[]{:S(2)}, u32[]{:S(2)}) collective-permute-start(bf16[2,256,128]{2,1,0:T(8,128)(2,1)S(1)} %collective-permute-done.10.rest_4_), channel_id=1, source_target_pairs={{0,2},{1,3},{2,0},{3,1},{4,6},{5,7},{6,4},{7,5},{8,10},{9,11},{10,... | collective-permute-start | bytes 393224 | tf_op jit(solution)/shard_map/ppermute | solution.py:26
  37.1 0.4 collective-permute-done.9.rest_3_
  37.6 1.4 %collective-permute-start.13 = (bf16[2,256,128]{2,1,0:T(8,128)(2,1)S(1)}, bf16[2,256,128]{2,1,0:T(8,128)(2,1)}, u32[]{:S(2)}, u32[]{:S(2)}) collective-permute-start(bf16[2,256,128]{2,1,0:T(8,128)(2,1)S(1)} %collective-permute-done.9.rest_3_), channel_id=1, source_target_pairs={{0,16},{16,0},{1,17},{17,1},{2,18},{18,2},{3,19},{19,3},{4,20},{20... | collective-permute-start | bytes 393224 | tf_op jit(solution)/shard_map/ppermute | solution.py:26
  39.0 6.2 %shard_map.120.own_ref = bf16[2,24,16,192]{3,2,1,0:T(8,128)(2,1)S(1)} custom-call(s32[32]{0:T(128)S(1)} %copy-done.3, s32[1]{0:T(128)} %bitcast.10.first_ref, bf16[2,24,16,192]{3,2,1,0:T(8,128)(2,1)S(1)} %bitcast.16, bf16[2,24,16,192]{3,2,1,0:T(8,128)(2,1)} %bitcast.23, f32[1,192]{1,0:T(1,128)S(1)} %bitcast.20, f32[1,192]{1,0:T(1,128)S(1)} %bitcast.21, ...), custom_call_target="tpu_custom_call" | custom-call | tf_op jit(solution)/shard_map/pallas_call | solution.py:455
  45.3 1.5 %collective-permute-start.24 = (bf16[2,24,16,192]{3,2,1,0:T(8,128)(2,1)S(1)}, bf16[2,24,16,192]{3,2,1,0:T(8,128)(2,1)S(1)}, u32[]{:S(2)}, u32[]{:S(2)}) collective-permute-start(bf16[2,24,16,192]{3,2,1,0:T(8,128)(2,1)S(1)} %shard_map.120.own_ref), channel_id=1, source_target_pairs={{0,1},{1,2},{2,3},{3,4},{4,5},{5,6},{6,7},{7,8},{8,9},{9,10},{10,1... | collective-permute-start | bytes 884744 | tf_op jit(solution)/shard_map/ppermute | solution.py:31
  46.8 1.6 %collective-permute-start.25 = (bf16[2,256,128]{2,1,0:T(8,128)(2,1)S(1)}, bf16[2,256,128]{2,1,0:T(8,128)(2,1)S(1)}, u32[]{:S(2)}, u32[]{:S(2)}) collective-permute-start(bf16[2,256,128]{2,1,0:T(8,128)(2,1)S(1)} %pad_maximum_fusion.2.rest_0_), channel_id=1, source_target_pairs={{0,1},{1,0},{2,3},{3,2},{4,5},{5,4},{6,7},{7,6},{8,9},{9,8},{10,11... | collective-permute-start | bytes 393224 | tf_op jit(solution)/shard_map/ppermute | solution.py:26
  48.5 0.4 collective-permute-start.27
  49.0 0.4 collective-permute-done.25.rest_8_
  49.4 0.4 collective-permute-start.29
  50.2 0.3 collective-permute-start.31
  50.7 0.6 collective-permute-done.30.rest_13_
  51.3 0.4 collective-permute-done.31.rest_14_
  51.7 0.3 collective-permute-done.32.rest_15_
  52.1 0.3 copy-done.32
  52.4 0.3 copy-done.33
  52.7 7.2 %shard_map.121 = bf16[192,128]{1,0:T(8,128)(2,1)S(1)} custom-call(s32[32]{0:T(128)S(1)} %copy-done.3, s32[1]{0:T(128)} %bitcast.10.first_ref, bf16[2,24,16,192]{3,2,1,0:T(8,128)(2,1)S(1)} %shard_map.120.own_ref, bf16[2,24,16,192]{3,2,1,0:T(8,128)(2,1)S(1)} %collective-permute-done.24.rim_ref, bf16[2,24,16,192]{3,2,1,0:T(8,128)(2,1)S(1)} %bitcast.17, ...), custom_call_target="tpu_custom_call" | custom-call | tf_op jit(solution)/shard_map/pallas_call | solution.py:472
  60.0 6.0 %collective-permute-start.35 = (bf16[192,128]{1,0:T(8,128)(2,1)S(1)}, bf16[192,128]{1,0:T(8,128)(2,1)S(1)}, u32[]{:S(2)}, u32[]{:S(2)}) collective-permute-start(bf16[192,128]{1,0:T(8,128)(2,1)S(1)} %shard_map.121), channel_id=1, source_target_pairs={{0,12},{1,13},{2,14},{3,15},{4,8},{5,9},{6,10},{7,11},{8,4},{9,5},... | collective-permute-start | bytes 147464 | tf_op jit(solution)/shard_map/ppermute | solution.py:26
  66.0 0.6 collective-permute-start.33
  66.6 1.7 %collective-permute-done.35 = bf16[192,128]{1,0:T(8,128)(2,1)S(1)} collective-permute-done((bf16[192,128]{1,0:T(8,128)(2,1)S(1)}, bf16[192,128]{1,0:T(8,128)(2,1)S(1)}, u32[]{:S(2)}, u32[]{:S(2)}) %collective-permute-start.35) | collective-permute-done | bytes 49184 | tf_op jit(solution)/shard_map/ppermute | solution.py:26
  68.3 2.6 %collective-permute-done.34 = bf16[192,128]{1,0:T(8,128)(2,1)S(1)} collective-permute-done((bf16[192,128]{1,0:T(8,128)(2,1)S(1)}, bf16[192,128]{1,0:T(8,128)(2,1)S(1)}, u32[]{:S(2)}, u32[]{:S(2)}) %collective-permute-start.34) | collective-permute-done | bytes 49184 | tf_op jit(solution)/shard_map/ppermute | solution.py:26
  71.2 5.6 %collective-permute-done.36.rest_1_ = bf16[768,128]{1,0:T(8,128)(2,1)S(1)} collective-permute-done((bf16[768,128]{1,0:T(8,128)(2,1)S(1)}, bf16[768,128]{1,0:T(8,128)(2,1)S(1)}, u32[]{:S(2)}, u32[]{:S(2)}) %collective-permute-start.36) | collective-permute-done | bytes 196640 | tf_op jit(solution)/shard_map/ppermute | solution.py:26
  76.7 1.4 %collective-permute-done.38.rest_3_ = bf16[768,128]{1,0:T(8,128)(2,1)S(1)} collective-permute-done((bf16[768,128]{1,0:T(8,128)(2,1)S(1)}, bf16[768,128]{1,0:T(8,128)(2,1)S(1)}, u32[]{:S(2)}, u32[]{:S(2)}) %collective-permute-start.38) | collective-permute-done | bytes 196640 | tf_op jit(solution)/shard_map/ppermute | solution.py:26
  78.2 3.2 %shard_map.122 = bf16[192,3072]{1,0:T(8,128)(2,1)} custom-call(s32[3,192]{1,0:T(4,128)S(1)} %pad_add_fusion.place_ref, bf16[64,3072]{1,0:T(8,128)(2,1)S(1)} %copy-done, f32[1,3072]{1,0:T(1,128)S(1)} %bitcast.18, f32[1,3072]{1,0:T(1,128)S(1)} %bitcast.19, bf16[768,128]{1,0:T(8,128)(2,1)S(1)} %pad_maximum_fusion.rest_0_, ...), custom_call_target="tpu_custom_call" | custom-call | tf_op jit(solution)/shard_map/pallas_call | solution.py:494
  (120 shorter events, 1.7 us)
Async XLA Ops:
  1.1 15.1 %collective-permute-start.2 = (bf16[2,256,128]{2,1,0:T(8,128)(2,1)S(1)}, bf16[2,256,128]{2,1,0:T(8,128)(2,1)S(1)}, u32[]{:S(2)}, u32[]{:S(2)}) collective-permute-start(bf16[2,256,128]{2,1,0:T(8,128)(2,1)S(1)} %shard_map.118), channel_id=1, source_target_pairs={{0,12},{1,13},{2,14},{3,15},{4,8},{5,9},{6,10},{7,11},{8,4},{9,5},... | collective-permute-start | bytes 393224 | tf_op jit(solution)/shard_map/ppermute | solution.py:26
  6.3 11.1 %collective-permute-start.1 = (bf16[2,256,128]{2,1,0:T(8,128)(2,1)S(1)}, bf16[2,256,128]{2,1,0:T(8,128)(2,1)S(1)}, u32[]{:S(2)}, u32[]{:S(2)}) collective-permute-start(bf16[2,256,128]{2,1,0:T(8,128)(2,1)S(1)} %shard_map.118), channel_id=1, source_target_pairs={{0,8},{1,9},{2,10},{3,11},{4,12},{5,13},{6,14},{7,15},{8,0},{9,1},... | collective-permute-start | bytes 393224 | tf_op jit(solution)/shard_map/ppermute | solution.py:26
  6.3 8.4 %collective-permute-start = (bf16[2,256,128]{2,1,0:T(8,128)(2,1)S(1)}, bf16[2,256,128]{2,1,0:T(8,128)(2,1)S(1)}, u32[]{:S(2)}, u32[]{:S(2)}) collective-permute-start(bf16[2,256,128]{2,1,0:T(8,128)(2,1)S(1)} %shard_map.118), channel_id=1, source_target_pairs={{0,4},{1,5},{2,6},{3,7},{4,0},{5,1},{6,2},{7,3},{8,12},{9,13},{10,... | collective-permute-start | bytes 393224 | tf_op jit(solution)/shard_map/ppermute | solution.py:26
  8.0 18.8 %collective-permute-start.7 = (bf16[2,16,24,192]{3,1,2,0:T(8,128)(2,1)S(1)}, bf16[2,16,24,192]{3,1,2,0:T(8,128)(2,1)S(1)}, u32[]{:S(2)}, u32[]{:S(2)}) collective-permute-start(bf16[2,16,24,192]{3,1,2,0:T(8,128)(2,1)S(1)} %copy.17), channel_id=1, source_target_pairs={{0,1},{1,2},{2,3},{3,4},{4,5},{5,6},{6,7},{7,8},{8,9},{9,10},{10,1... | collective-permute-start | bytes 884744 | tf_op jit(solution)/shard_map/ppermute | solution.py:31
  9.5 29.4 %copy-start.3 = (s32[32]{0:T(128)S(1)}, s32[32]{0:T(128)}, u32[]{:S(2)}) copy-start(s32[32]{0:T(128)} %clips_ref.3) | copy-start | bytes 388
  9.6 29.4 %copy-start.4 = (f32[192]{0:T(256)S(1)}, f32[192]{0:T(256)}, u32[]{:S(2)}) copy-start(f32[192]{0:T(256)} %param.14) | copy-start | bytes 2308
  9.6 29.4 %copy-start.5 = (f32[192]{0:T(256)S(1)}, f32[192]{0:T(256)}, u32[]{:S(2)}) copy-start(f32[192]{0:T(256)} %param.16) | copy-start | bytes 2308
  14.7 24.2 %copy-start.9 = (bf16[2,256,128]{2,1,0:T(8,128)(2,1)}, bf16[2,256,128]{2,1,0:T(8,128)(2,1)S(1)}, u32[]{:S(2)}) copy-start(bf16[2,256,128]{2,1,0:T(8,128)(2,1)S(1)} %pad_maximum_fusion.1.rest_0_) | copy-start | bytes 393220
  14.7 6.3 %collective-permute-start.3 = (bf16[2,256,128]{2,1,0:T(8,128)(2,1)S(1)}, bf16[2,256,128]{2,1,0:T(8,128)(2,1)S(1)}, u32[]{:S(2)}, u32[]{:S(2)}) collective-permute-start(bf16[2,256,128]{2,1,0:T(8,128)(2,1)S(1)} %pad_maximum_fusion.1.rest_0_), channel_id=1, source_target_pairs={{0,16},{16,0},{1,17},{17,1},{2,18},{18,2},{3,19},{19,3},{4,20},{20... | collective-permute-start | bytes 393224 | tf_op jit(solution)/shard_map/ppermute | solution.py:26
  17.4 21.6 %copy-start.10 = (bf16[2,256,128]{2,1,0:T(8,128)(2,1)}, bf16[2,256,128]{2,1,0:T(8,128)(2,1)S(1)}, u32[]{:S(2)}) copy-start(bf16[2,256,128]{2,1,0:T(8,128)(2,1)S(1)} %pad_maximum_fusion.3.rest_1_) | copy-start | bytes 393220
  17.4 6.5 %collective-permute-start.5 = (bf16[2,256,128]{2,1,0:T(8,128)(2,1)S(1)}, bf16[2,256,128]{2,1,0:T(8,128)(2,1)S(1)}, u32[]{:S(2)}, u32[]{:S(2)}) collective-permute-start(bf16[2,256,128]{2,1,0:T(8,128)(2,1)S(1)} %pad_maximum_fusion.3.rest_1_), channel_id=1, source_target_pairs={{0,2},{1,3},{2,0},{3,1},{4,6},{5,7},{6,4},{7,5},{8,10},{9,11},{10,... | collective-permute-start | bytes 393224 | tf_op jit(solution)/shard_map/ppermute | solution.py:26
  19.1 7.2 %collective-permute-start.14 = (bf16[2,256,128]{2,1,0:T(8,128)(2,1)S(1)}, bf16[2,256,128]{2,1,0:T(8,128)(2,1)S(1)}, u32[]{:S(2)}, u32[]{:S(2)}) collective-permute-start(bf16[2,256,128]{2,1,0:T(8,128)(2,1)S(1)} %pad_maximum_fusion.1.rest_0_), channel_id=1, source_target_pairs={{0,2},{1,3},{2,0},{3,1},{4,6},{5,7},{6,4},{7,5},{8,10},{9,11},{10,... | collective-permute-start | bytes 393224 | tf_op jit(solution)/shard_map/ppermute | solution.py:26
  19.5 6.7 %collective-permute-start.15 = (bf16[2,256,128]{2,1,0:T(8,128)(2,1)S(1)}, bf16[2,256,128]{2,1,0:T(8,128)(2,1)S(1)}, u32[]{:S(2)}, u32[]{:S(2)}) collective-permute-start(bf16[2,256,128]{2,1,0:T(8,128)(2,1)S(1)} %pad_maximum_fusion.3.rest_1_), channel_id=1, source_target_pairs={{0,16},{16,0},{1,17},{17,1},{2,18},{18,2},{3,19},{19,3},{4,20},{20... | collective-permute-start | bytes 393224 | tf_op jit(solution)/shard_map/ppermute | solution.py:26
  21.0 6.6 %collective-permute-start.4 = (bf16[2,256,128]{2,1,0:T(8,128)(2,1)S(1)}, bf16[2,256,128]{2,1,0:T(8,128)(2,1)S(1)}, u32[]{:S(2)}, u32[]{:S(2)}) collective-permute-start(bf16[2,256,128]{2,1,0:T(8,128)(2,1)S(1)} %collective-permute-done.3.rest_4_), channel_id=1, source_target_pairs={{0,2},{1,3},{2,0},{3,1},{4,6},{5,7},{6,4},{7,5},{8,10},{9,11},{10,... | collective-permute-start | bytes 393224 | tf_op jit(solution)/shard_map/ppermute | solution.py:26
  23.9 5.1 %collective-permute-start.6 = (bf16[2,256,128]{2,1,0:T(8,128)(2,1)S(1)}, bf16[2,256,128]{2,1,0:T(8,128)(2,1)}, u32[]{:S(2)}, u32[]{:S(2)}) collective-permute-start(bf16[2,256,128]{2,1,0:T(8,128)(2,1)S(1)} %collective-permute-done.5.rest_3_), channel_id=1, source_target_pairs={{0,16},{16,0},{1,17},{17,1},{2,18},{18,2},{3,19},{19,3},{4,20},{20... | collective-permute-start | bytes 393224 | tf_op jit(solution)/shard_map/ppermute | solution.py:26
  25.4 21.4 %copy-start.7 = (bf16[2,256,128]{2,1,0:T(8,128)(2,1)}, bf16[2,256,128]{2,1,0:T(8,128)(2,1)S(1)}, u32[]{:S(2)}) copy-start(bf16[2,256,128]{2,1,0:T(8,128)(2,1)S(1)} %pad_maximum_fusion.2.rest_0_) | copy-start | bytes 393220
  26.2 3.3 %collective-permute-start.20 = (bf16[2,256,128]{2,1,0:T(8,128)(2,1)S(1)}, bf16[2,256,128]{2,1,0:T(8,128)(2,1)S(1)}, u32[]{:S(2)}, u32[]{:S(2)}) collective-permute-start(bf16[2,256,128]{2,1,0:T(8,128)(2,1)S(1)} %collective-permute-done.3.rest_4_), channel_id=1, source_target_pairs={{0,1},{1,0},{2,3},{3,2},{4,5},{5,4},{6,7},{7,6},{8,9},{9,8},{10,11... | collective-permute-start | bytes 393224 | tf_op jit(solution)/shard_map/ppermute | solution.py:26
  26.3 4.9 %collective-permute-start.19 = (bf16[2,256,128]{2,1,0:T(8,128)(2,1)S(1)}, bf16[2,256,128]{2,1,0:T(8,128)(2,1)S(1)}, u32[]{:S(2)}, u32[]{:S(2)}) collective-permute-start(bf16[2,256,128]{2,1,0:T(8,128)(2,1)S(1)} %collective-permute-done.5.rest_3_), channel_id=1, source_target_pairs={{0,1},{1,0},{2,3},{3,2},{4,5},{5,4},{6,7},{7,6},{8,9},{9,8},{10,11... | collective-permute-start | bytes 393224 | tf_op jit(solution)/shard_map/ppermute | solution.py:26
  26.8 2.3 %collective-permute-start.18 = (bf16[2,256,128]{2,1,0:T(8,128)(2,1)S(1)}, bf16[2,256,128]{2,1,0:T(8,128)(2,1)S(1)}, u32[]{:S(2)}, u32[]{:S(2)}) collective-permute-start(bf16[2,256,128]{2,1,0:T(8,128)(2,1)S(1)} %collective-permute-done.14.rest_2_), channel_id=1, source_target_pairs={{0,1},{1,0},{2,3},{3,2},{4,5},{5,4},{6,7},{7,6},{8,9},{9,8},{10,11... | collective-permute-start | bytes 393224 | tf_op jit(solution)/shard_map/ppermute | solution.py:26
  27.6 2.0 %collective-permute-start.21 = (bf16[2,256,128]{2,1,0:T(8,128)(2,1)S(1)}, bf16[2,256,128]{2,1,0:T(8,128)(2,1)S(1)}, u32[]{:S(2)}, u32[]{:S(2)}) collective-permute-start(bf16[2,256,128]{2,1,0:T(8,128)(2,1)S(1)} %collective-permute-done.15.rest_5_), channel_id=1, source_target_pairs={{0,1},{1,0},{2,3},{3,2},{4,5},{5,4},{6,7},{7,6},{8,9},{9,8},{10,11... | collective-permute-start | bytes 393224 | tf_op jit(solution)/shard_map/ppermute | solution.py:26
  29.0 3.7 %collective-permute-start.16 = (bf16[2,256,128]{2,1,0:T(8,128)(2,1)S(1)}, bf16[2,256,128]{2,1,0:T(8,128)(2,1)S(1)}, u32[]{:S(2)}, u32[]{:S(2)}) collective-permute-start(bf16[2,256,128]{2,1,0:T(8,128)(2,1)S(1)} %pad_maximum_fusion.1.rest_0_), channel_id=1, source_target_pairs={{0,1},{1,0},{2,3},{3,2},{4,5},{5,4},{6,7},{7,6},{8,9},{9,8},{10,11... | collective-permute-start | bytes 393224 | tf_op jit(solution)/shard_map/ppermute | solution.py:26
  29.0 3.7 %collective-permute-start.17 = (bf16[2,256,128]{2,1,0:T(8,128)(2,1)S(1)}, bf16[2,256,128]{2,1,0:T(8,128)(2,1)S(1)}, u32[]{:S(2)}, u32[]{:S(2)}) collective-permute-start(bf16[2,256,128]{2,1,0:T(8,128)(2,1)S(1)} %pad_maximum_fusion.3.rest_1_), channel_id=1, source_target_pairs={{0,1},{1,0},{2,3},{3,2},{4,5},{5,4},{6,7},{7,6},{8,9},{9,8},{10,11... | collective-permute-start | bytes 393224 | tf_op jit(solution)/shard_map/ppermute | solution.py:26
  29.5 3.8 %collective-permute-start.22 = (bf16[2,256,128]{2,1,0:T(8,128)(2,1)S(1)}, bf16[2,256,128]{2,1,0:T(8,128)(2,1)S(1)}, u32[]{:S(2)}, u32[]{:S(2)}) collective-permute-start(bf16[2,256,128]{2,1,0:T(8,128)(2,1)S(1)} %collective-permute-done.4.rest_6_), channel_id=1, source_target_pairs={{0,1},{1,0},{2,3},{3,2},{4,5},{5,4},{6,7},{7,6},{8,9},{9,8},{10,11... | collective-permute-start | bytes 393224 | tf_op jit(solution)/shard_map/ppermute | solution.py:26
  29.6 5.9 %collective-permute-start.10 = (bf16[2,256,128]{2,1,0:T(8,128)(2,1)S(1)}, bf16[2,256,128]{2,1,0:T(8,128)(2,1)S(1)}, u32[]{:S(2)}, u32[]{:S(2)}) collective-permute-start(bf16[2,256,128]{2,1,0:T(8,128)(2,1)S(1)} %pad_maximum_fusion.2.rest_0_), channel_id=1, source_target_pairs={{0,16},{16,0},{1,17},{17,1},{2,18},{18,2},{3,19},{19,3},{4,20},{20... | collective-permute-start | bytes 393224 | tf_op jit(solution)/shard_map/ppermute | solution.py:26
  31.2 6.3 %collective-permute-start.9 = (bf16[2,256,128]{2,1,0:T(8,128)(2,1)S(1)}, bf16[2,256,128]{2,1,0:T(8,128)(2,1)S(1)}, u32[]{:S(2)}, u32[]{:S(2)}) collective-permute-start(bf16[2,256,128]{2,1,0:T(8,128)(2,1)S(1)} %pad_maximum_fusion.4.rest_1_), channel_id=1, source_target_pairs={{0,2},{1,3},{2,0},{3,1},{4,6},{5,7},{6,4},{7,5},{8,10},{9,11},{10,... | collective-permute-start | bytes 393224 | tf_op jit(solution)/shard_map/ppermute | solution.py:26
  32.7 6.3 %collective-permute-start.23 = (bf16[2,256,128]{2,1,0:T(8,128)(2,1)}, bf16[2,256,128]{2,1,0:T(8,128)(2,1)}, u32[]{:S(2)}, u32[]{:S(2)}) collective-permute-start(bf16[2,256,128]{2,1,0:T(8,128)(2,1)} %collective-permute-done.6.rest_7_), channel_id=1, source_target_pairs={{0,1},{1,0},{2,3},{3,2},{4,5},{5,4},{6,7},{7,6},{8,9},{9,8},{10,11... | collective-permute-start | bytes 393224 | tf_op jit(solution)/shard_map/ppermute | solution.py:26
  32.7 14.1 %collective-permute-start.8 = (bf16[2,256,128]{2,1,0:T(8,128)(2,1)S(1)}, bf16[2,256,128]{2,1,0:T(8,128)(2,1)}, u32[]{:S(2)}, u32[]{:S(2)}) collective-permute-start(bf16[2,256,128]{2,1,0:T(8,128)(2,1)S(1)} %pad_maximum_fusion.2.rest_0_), channel_id=1, source_target_pairs={{0,2},{1,3},{2,0},{3,1},{4,6},{5,7},{6,4},{7,5},{8,10},{9,11},{10,... | collective-permute-start | bytes 393224 | tf_op jit(solution)/shard_map/ppermute | solution.py:26
  33.3 13.5 %collective-permute-start.11 = (bf16[2,256,128]{2,1,0:T(8,128)(2,1)S(1)}, bf16[2,256,128]{2,1,0:T(8,128)(2,1)}, u32[]{:S(2)}, u32[]{:S(2)}) collective-permute-start(bf16[2,256,128]{2,1,0:T(8,128)(2,1)S(1)} %pad_maximum_fusion.4.rest_1_), channel_id=1, source_target_pairs={{0,16},{16,0},{1,17},{17,1},{2,18},{18,2},{3,19},{19,3},{4,20},{20... | collective-permute-start | bytes 393224 | tf_op jit(solution)/shard_map/ppermute | solution.py:26
  35.5 11.3 %collective-permute-start.12 = (bf16[2,256,128]{2,1,0:T(8,128)(2,1)S(1)}, bf16[2,256,128]{2,1,0:T(8,128)(2,1)}, u32[]{:S(2)}, u32[]{:S(2)}) collective-permute-start(bf16[2,256,128]{2,1,0:T(8,128)(2,1)S(1)} %collective-permute-done.10.rest_4_), channel_id=1, source_target_pairs={{0,2},{1,3},{2,0},{3,1},{4,6},{5,7},{6,4},{7,5},{8,10},{9,11},{10,... | collective-permute-start | bytes 393224 | tf_op jit(solution)/shard_map/ppermute | solution.py:26
  37.6 9.2 %collective-permute-start.13 = (bf16[2,256,128]{2,1,0:T(8,128)(2,1)S(1)}, bf16[2,256,128]{2,1,0:T(8,128)(2,1)}, u32[]{:S(2)}, u32[]{:S(2)}) collective-permute-start(bf16[2,256,128]{2,1,0:T(8,128)(2,1)S(1)} %collective-permute-done.9.rest_3_), channel_id=1, source_target_pairs={{0,16},{16,0},{1,17},{17,1},{2,18},{18,2},{3,19},{19,3},{4,20},{20... | collective-permute-start | bytes 393224 | tf_op jit(solution)/shard_map/ppermute | solution.py:26
  45.3 6.8 %collective-permute-start.24 = (bf16[2,24,16,192]{3,2,1,0:T(8,128)(2,1)S(1)}, bf16[2,24,16,192]{3,2,1,0:T(8,128)(2,1)S(1)}, u32[]{:S(2)}, u32[]{:S(2)}) collective-permute-start(bf16[2,24,16,192]{3,2,1,0:T(8,128)(2,1)S(1)} %shard_map.120.own_ref), channel_id=1, source_target_pairs={{0,1},{1,2},{2,3},{3,4},{4,5},{5,6},{6,7},{7,8},{8,9},{9,10},{10,1... | collective-permute-start | bytes 884744 | tf_op jit(solution)/shard_map/ppermute | solution.py:31
  46.8 2.6 %collective-permute-start.25 = (bf16[2,256,128]{2,1,0:T(8,128)(2,1)S(1)}, bf16[2,256,128]{2,1,0:T(8,128)(2,1)S(1)}, u32[]{:S(2)}, u32[]{:S(2)}) collective-permute-start(bf16[2,256,128]{2,1,0:T(8,128)(2,1)S(1)} %pad_maximum_fusion.2.rest_0_), channel_id=1, source_target_pairs={{0,1},{1,0},{2,3},{3,2},{4,5},{5,4},{6,7},{7,6},{8,9},{9,8},{10,11... | collective-permute-start | bytes 393224 | tf_op jit(solution)/shard_map/ppermute | solution.py:26
  48.4 1.4 %collective-permute-start.26 = (bf16[2,256,128]{2,1,0:T(8,128)(2,1)S(1)}, bf16[2,256,128]{2,1,0:T(8,128)(2,1)S(1)}, u32[]{:S(2)}, u32[]{:S(2)}) collective-permute-start(bf16[2,256,128]{2,1,0:T(8,128)(2,1)S(1)} %pad_maximum_fusion.4.rest_1_), channel_id=1, source_target_pairs={{0,1},{1,0},{2,3},{3,2},{4,5},{5,4},{6,7},{7,6},{8,9},{9,8},{10,11... | collective-permute-start | bytes 393224 | tf_op jit(solution)/shard_map/ppermute | solution.py:26
  48.5 1.7 %collective-permute-start.27 = (bf16[2,256,128]{2,1,0:T(8,128)(2,1)}, bf16[2,256,128]{2,1,0:T(8,128)(2,1)S(1)}, u32[]{:S(2)}, u32[]{:S(2)}) collective-permute-start(bf16[2,256,128]{2,1,0:T(8,128)(2,1)} %collective-permute-done.8.rest_2_), channel_id=1, source_target_pairs={{0,1},{1,0},{2,3},{3,2},{4,5},{5,4},{6,7},{7,6},{8,9},{9,8},{10,11... | collective-permute-start | bytes 393224 | tf_op jit(solution)/shard_map/ppermute | solution.py:26
  48.9 1.6 %collective-permute-start.28 = (bf16[2,256,128]{2,1,0:T(8,128)(2,1)S(1)}, bf16[2,256,128]{2,1,0:T(8,128)(2,1)S(1)}, u32[]{:S(2)}, u32[]{:S(2)}) collective-permute-start(bf16[2,256,128]{2,1,0:T(8,128)(2,1)S(1)} %collective-permute-done.9.rest_3_), channel_id=1, source_target_pairs={{0,1},{1,0},{2,3},{3,2},{4,5},{5,4},{6,7},{7,6},{8,9},{9,8},{10,11... | collective-permute-start | bytes 393224 | tf_op jit(solution)/shard_map/ppermute | solution.py:26
  49.4 1.3 %collective-permute-start.29 = (bf16[2,256,128]{2,1,0:T(8,128)(2,1)S(1)}, bf16[2,256,128]{2,1,0:T(8,128)(2,1)S(1)}, u32[]{:S(2)}, u32[]{:S(2)}) collective-permute-start(bf16[2,256,128]{2,1,0:T(8,128)(2,1)S(1)} %collective-permute-done.10.rest_4_), channel_id=1, source_target_pairs={{0,1},{1,0},{2,3},{3,2},{4,5},{5,4},{6,7},{7,6},{8,9},{9,8},{10,11... | collective-permute-start | bytes 393224 | tf_op jit(solution)/shard_map/ppermute | solution.py:26
  49.8 1.6 %collective-permute-start.30 = (bf16[2,256,128]{2,1,0:T(8,128)(2,1)}, bf16[2,256,128]{2,1,0:T(8,128)(2,1)S(1)}, u32[]{:S(2)}, u32[]{:S(2)}) collective-permute-start(bf16[2,256,128]{2,1,0:T(8,128)(2,1)} %collective-permute-done.11.rest_5_), channel_id=1, source_target_pairs={{0,1},{1,0},{2,3},{3,2},{4,5},{5,4},{6,7},{7,6},{8,9},{9,8},{10,11... | collective-permute-start | bytes 393224 | tf_op jit(solution)/shard_map/ppermute | solution.py:26
  50.2 1.6 %collective-permute-start.31 = (bf16[2,256,128]{2,1,0:T(8,128)(2,1)}, bf16[2,256,128]{2,1,0:T(8,128)(2,1)S(1)}, u32[]{:S(2)}, u32[]{:S(2)}) collective-permute-start(bf16[2,256,128]{2,1,0:T(8,128)(2,1)} %collective-permute-done.12.rest_6_), channel_id=1, source_target_pairs={{0,1},{1,0},{2,3},{3,2},{4,5},{5,4},{6,7},{7,6},{8,9},{9,8},{10,11... | collective-permute-start | bytes 393224 | tf_op jit(solution)/shard_map/ppermute | solution.py:26
  50.5 1.6 %collective-permute-start.32 = (bf16[2,256,128]{2,1,0:T(8,128)(2,1)}, bf16[2,256,128]{2,1,0:T(8,128)(2,1)S(1)}, u32[]{:S(2)}, u32[]{:S(2)}) collective-permute-start(bf16[2,256,128]{2,1,0:T(8,128)(2,1)} %collective-permute-done.13.rest_7_), channel_id=1, source_target_pairs={{0,1},{1,0},{2,3},{3,2},{4,5},{5,4},{6,7},{7,6},{8,9},{9,8},{10,11... | collective-permute-start | bytes 393224 | tf_op jit(solution)/shard_map/ppermute | solution.py:26
  52.7 25.5 %copy-start = (bf16[64,3072]{1,0:T(8,128)(2,1)S(1)}, bf16[64,3072]{1,0:T(8,128)(2,1)}, u32[]{:S(2)}) copy-start(bf16[64,3072]{1,0:T(8,128)(2,1)} %embed_ref.1) | copy-start | bytes 1179652
  52.7 25.5 %copy-start.1 = (f32[3072]{0:T(1024)S(1)}, f32[3072]{0:T(1024)}, u32[]{:S(2)}) copy-start(f32[3072]{0:T(1024)} %param.22) | copy-start | bytes 36868
  52.7 25.5 %copy-start.2 = (f32[3072]{0:T(1024)S(1)}, f32[3072]{0:T(1024)}, u32[]{:S(2)}) copy-start(f32[3072]{0:T(1024)} %param.21) | copy-start | bytes 36868
  60.0 8.4 %collective-permute-start.35 = (bf16[192,128]{1,0:T(8,128)(2,1)S(1)}, bf16[192,128]{1,0:T(8,128)(2,1)S(1)}, u32[]{:S(2)}, u32[]{:S(2)}) collective-permute-start(bf16[192,128]{1,0:T(8,128)(2,1)S(1)} %shard_map.121), channel_id=1, source_target_pairs={{0,12},{1,13},{2,14},{3,15},{4,8},{5,9},{6,10},{7,11},{8,4},{9,5},... | collective-permute-start | bytes 147464 | tf_op jit(solution)/shard_map/ppermute | solution.py:26
  66.0 5.0 %collective-permute-start.34 = (bf16[192,128]{1,0:T(8,128)(2,1)S(1)}, bf16[192,128]{1,0:T(8,128)(2,1)S(1)}, u32[]{:S(2)}, u32[]{:S(2)}) collective-permute-start(bf16[192,128]{1,0:T(8,128)(2,1)S(1)} %shard_map.121), channel_id=1, source_target_pairs={{0,8},{1,9},{2,10},{3,11},{4,12},{5,13},{6,14},{7,15},{8,0},{9,1},... | collective-permute-start | bytes 147464 | tf_op jit(solution)/shard_map/ppermute | solution.py:26
  66.0 5.0 %collective-permute-start.33 = (bf16[192,128]{1,0:T(8,128)(2,1)S(1)}, bf16[192,128]{1,0:T(8,128)(2,1)S(1)}, u32[]{:S(2)}, u32[]{:S(2)}) collective-permute-start(bf16[192,128]{1,0:T(8,128)(2,1)S(1)} %shard_map.121), channel_id=1, source_target_pairs={{0,4},{1,5},{2,6},{3,7},{4,0},{5,1},{6,2},{7,3},{8,12},{9,13},{10,... | collective-permute-start | bytes 147464 | tf_op jit(solution)/shard_map/ppermute | solution.py:26
  71.0 5.7 %collective-permute-start.36 = (bf16[768,128]{1,0:T(8,128)(2,1)S(1)}, bf16[768,128]{1,0:T(8,128)(2,1)S(1)}, u32[]{:S(2)}, u32[]{:S(2)}) collective-permute-start(bf16[768,128]{1,0:T(8,128)(2,1)S(1)} %pad_maximum_fusion.rest_0_), channel_id=1, source_target_pairs={{0,2},{1,3},{2,0},{3,1},{4,6},{5,7},{6,4},{7,5},{8,10},{9,11},{10,... | collective-permute-start | bytes 589832 | tf_op jit(solution)/shard_map/ppermute | solution.py:26
  71.1 5.7 %collective-permute-start.37 = (bf16[768,128]{1,0:T(8,128)(2,1)S(1)}, bf16[768,128]{1,0:T(8,128)(2,1)S(1)}, u32[]{:S(2)}, u32[]{:S(2)}) collective-permute-start(bf16[768,128]{1,0:T(8,128)(2,1)S(1)} %pad_maximum_fusion.rest_0_), channel_id=1, source_target_pairs={{0,1},{1,0},{2,3},{3,2},{4,5},{5,4},{6,7},{7,6},{8,9},{9,8},{10,11... | collective-permute-start | bytes 589832 | tf_op jit(solution)/shard_map/ppermute | solution.py:26
  76.7 1.4 %collective-permute-start.38 = (bf16[768,128]{1,0:T(8,128)(2,1)S(1)}, bf16[768,128]{1,0:T(8,128)(2,1)S(1)}, u32[]{:S(2)}, u32[]{:S(2)}) collective-permute-start(bf16[768,128]{1,0:T(8,128)(2,1)S(1)} %collective-permute-done.36.rest_1_), channel_id=1, source_target_pairs={{0,1},{1,0},{2,3},{3,2},{4,5},{5,4},{6,7},{7,6},{8,9},{9,8},{10,11... | collective-permute-start | bytes 589832 | tf_op jit(solution)/shard_map/ppermute | solution.py:26
  (26 other events, 195.5 us)

commit v6 on v5

--- a/solution.py
+++ b/solution.py
@@ -122,11 +122,10 @@
     return values[:, :LANES], jnp.concatenate([tail, fill], axis=1)
 
 
-def place_frame(values, at, head_x, low_x, high_x):
+def place_frame(head, tail, at, head_x, low_x, high_x):
     breadth, height = head_x.shape[2] - 2, head_x.shape[3]
-    row = lax.broadcasted_iota(jnp.int32, (values.shape[0], LANES), 0) % height
-    head, tail = split_lanes(values)
-    count = values.shape[0]
+    row = lax.broadcasted_iota(jnp.int32, head.shape, 0) % height
+    count = head.shape[0]
     for tap in range(3):
         for part, part_x in ((head, head_x), (tail, low_x)):
             if tap == 0:
@@ -150,7 +149,8 @@
         array[:, :, wide - 1] = jnp.zeros_like(array[:, :, wide - 1])
 
 
-def unpack_units(unit_refs, rhs, staged, taps, unit_channels):
+def unpack_kernel(*refs, taps, unit_channels):
+    *unit_refs, rhs, staged = refs
     pairs, head_rows = unit_geometry(taps, unit_channels)
     staged[:, UNIT_ROWS:] = jnp.zeros_like(staged[:, UNIT_ROWS:])
     done = 0
@@ -173,42 +173,52 @@
         done += couples
 
 
-def convolve(clips_ref, first, head_x, low_x, high_x, rhs, frames, taps):
-    zero_frame = head_x.shape[1] - 1
+def unpack_units(pieces, taps, unit_channels, keep=IN_HBM):
+    count = sum(piece.shape[0] for piece in pieces)
+    return pl.pallas_call(
+        functools.partial(unpack_kernel, taps=taps, unit_channels=unit_channels),
+        out_shape=pltpu.VMEM((taps + (taps + 1) // 2, count * SUBLANES, LANES), jnp.bfloat16),
+        in_specs=[VMEM_SPEC] * len(pieces),
+        out_specs=VMEM_SPEC,
+        scratch_shapes=[pltpu.VMEM((2, SCRATCH_ROWS, LANES), jnp.float32)],
+        compiler_params=SMALL,
+    )(*map(keep, pieces))
+
+
+def convolve(clips_ref, first, frame, held, head_x, low_x, high_x, rhs_refs, taps):
+    empty = head_x.shape[1] - 1
     breadth, height = head_x.shape[2] - 2, head_x.shape[3]
     pairs = (taps + 1) // 2
-    source = [
-        [
-            jnp.where(same_clip(clips_ref, first + frame, 2 - tap), frame + tap, zero_frame)
-            for tap in range(3)
-        ]
-        for frame in range(frames)
+    sources = [
+        jnp.where(same_clip(clips_ref, first + frame, 2 - tap), frame + tap - held[0], empty)
+        for tap in range(3)
     ]
+
+    def here(tap):
+        return tap < taps and frame + tap // 9 in held
 
     def shifted(array, tap):
         a, b, e = tap // 9, tap // 3 % 3, tap % 3
-        return jnp.concatenate(
-            [
-                array[b, source[frame][a], e : e + breadth].reshape(breadth * height, LANES)
-                for frame in range(frames)
-            ],
-            axis=0,
-        )
-
-    def chunk(index):
-        if index < taps:
-            return shifted(head_x, index)
-        pair = index - taps
-        low = shifted(low_x, pair)
-        return low + shifted(high_x, pair + pairs) if pair + pairs < taps else low
-
-    total = taps + pairs
+        return array[b, sources[a], e : e + breadth].reshape(breadth * height, LANES)
+
+    chunks = [(shifted(head_x, tap), tap) for tap in range(taps) if here(tap)]
+    for pair in range(pairs):
+        parts = []
+        if here(pair):
+            parts.append(shifted(low_x, pair))
+        if here(pair + pairs):
+            parts.append(shifted(high_x, pair + pairs))
+        if parts:
+            chunks.append((sum(parts[1:], parts[0]), taps + pair))
     summed = None
-    for begin in range(0, total, 14):
-        end = min(begin + 14, total)
+    for begin in range(0, len(chunks), 14):
+        group = chunks[begin : begin + 14]
         part = lax.dot_general(
-            jnp.concatenate([chunk(index) for index in range(begin, end)], axis=1),
-            jnp.concatenate([rhs[index] for index in range(begin, end)], axis=1),
+            jnp.concatenate([values for values, _ in group], axis=1),
+            jnp.concatenate(
+                [jnp.concatenate([rhs[index] for _, index in group], axis=1) for rhs in rhs_refs],
+                axis=0,
+            ),
             NT,
             preferred_element_type=jnp.float32,
         )
@@ -220,55 +230,93 @@
     clips_ref, first_ref, own_ref, rim_ref, gain_first_ref, gain_second_ref, pick_ref, *rest,
     taps, unit_channels,
 ):
-    *unit_refs, out_ref, head_x, low_x, high_x, rhs, staged = rest
+    *unit_refs, out_ref, sent_ref, head_x, low_x, high_x, rhs, staged = rest
     frames, breadth, height, channels = own_ref.shape
     clear_rims((head_x, low_x, high_x))
     for frame in range(frames + 2):
         values = rim_ref[frame] if frame < 2 else own_ref[frame - 2]
         values = values.astype(jnp.float32).reshape(breadth * height, channels)
-        place_frame(rms_silu(values, gain_first_ref[...]), frame, head_x, low_x, high_x)
-    unpack_units(unit_refs, rhs, staged, taps, unit_channels)
-    summed = convolve(clips_ref, first_ref[0], head_x, low_x, high_x, rhs, frames, taps)
+        values = split_lanes(rms_silu(values, gain_first_ref[...]))
+        place_frame(*values, frame, head_x, low_x, high_x)
+    unpack_kernel(*unit_refs, rhs, staged, taps=taps, unit_channels=unit_channels)
+    held = range(frames + 2)
+    summed = jnp.concatenate(
+        [
+            convolve(clips_ref, first_ref[0], frame, held, head_x, low_x, high_x, [rhs], taps)
+            for frame in range(frames)
+        ],
+        axis=0,
+    )
     first_out = jnp.dot(
         summed.astype(jnp.bfloat16), pick_ref[...], preferred_element_type=jnp.float32
     )
-    out_ref[...] = (
-        rms_silu(first_out, gain_second_ref[...])
-        .astype(jnp.bfloat16)
-        .reshape(frames, breadth, height, channels)
-    )
-
-
-def second_kernel(
-    clips_ref, first_ref, own_ref, rim_ref, features_ref, gain_ref, pick_ref, wide_ref, *rest,
-    taps, unit_channels,
+    second_in = rms_silu(first_out, gain_second_ref[...])
+    out_ref[...] = second_in.astype(jnp.bfloat16).reshape(frames, breadth, height, channels)
+    pixels = breadth * height
+    last = [second_in[at * pixels : (at + 1) * pixels] for at in (frames - 2, frames - 1)]
+    sent_ref[0] = last[0][:, :LANES].astype(jnp.bfloat16)
+    sent_ref[1] = last[1][:, :LANES].astype(jnp.bfloat16)
+    tails = jnp.concatenate([values[:, LANES:] for values in last], axis=1)
+    sent_ref[2] = tails.astype(jnp.bfloat16)
+
+
+def own_kernel(
+    clips_ref, first_ref, own_ref, features_ref, pick_ref, *rest, taps
 ):
-    *unit_refs, parts_out, head_x, low_x, high_x, rhs, staged, plain, windows = rest
+    *rhs, summed_ref, head_x, low_x, high_x = rest
     frames, breadth, height, channels = own_ref.shape
     pixels = breadth * height
+    clear_rims((head_x, low_x, high_x))
+    for frame in range(frames):
+        values = own_ref[frame].astype(jnp.float32).reshape(pixels, channels)
+        place_frame(*split_lanes(values), frame, head_x, low_x, high_x)
+    held = range(2, frames + 2)
+    for frame in range(frames):
+        features = lax.dot_general(
+            features_ref[frame].reshape(pixels, channels),
+            pick_ref[...],
+            NT,
+            preferred_element_type=jnp.float32,
+        )
+        summed_ref[frame * pixels : (frame + 1) * pixels] = features + convolve(
+            clips_ref, first_ref[0], frame, held, head_x, low_x, high_x, rhs, taps
+        )
+
+
+def second_kernel(
+    clips_ref, first_ref, rim_ref, gain_ref, pick_ref, wide_ref, summed_ref, *rest, taps
+):
+    *rhs, parts_out, head_x, low_x, high_x, plain, windows = rest
+    breadth, height = head_x.shape[2] - 2, head_x.shape[3]
+    pixels = breadth * height
+    frames = summed_ref.shape[0] // pixels
     rows, columns = height // 2, breadth // 2
     width = wide_ref.shape[1] // 3
     first = first_ref[0]
     clear_rims((head_x, low_x, high_x))
-    for frame in range(frames + 2):
-        values = rim_ref[frame] if frame < 2 else own_ref[frame - 2]
-        values = values.astype(jnp.float32).reshape(pixels, channels)
-        place_frame(values, frame, head_x, low_x, high_x)
-    unpack_units(unit_refs, rhs, staged, taps, unit_channels)
-    summed = convolve(clips_ref, first, head_x, low_x, high_x, rhs, frames, taps)
-    features = lax.dot_general(
-        features_ref[...].reshape(frames * pixels, channels),
-        pick_ref[...],
-        NT,
-        preferred_element_type=jnp.float32,
-    )
+    for frame in range(2):
+        tail = rim_ref[2].astype(jnp.float32)
+        if frame == 1:
+            tail = pltpu.roll(tail, LANES // 2, 1)
+        lane = lax.broadcasted_iota(jnp.int32, tail.shape, 1)
+        tail = jnp.where(lane < LANES // 2, tail, 0.0)
+        place_frame(rim_ref[frame].astype(jnp.float32), tail, frame, head_x, low_x, high_x)
+    sums = []
+    for frame in range(frames):
+        total = summed_ref[frame * pixels : (frame + 1) * pixels]
+        if frame < 2:
+            total = total + convolve(
+                clips_ref, first, frame, range(2), head_x, low_x, high_x, rhs, taps
+            )
+        sums.append(total.astype(jnp.bfloat16))
     block_out = jnp.dot(
-        (features + summed).astype(jnp.bfloat16), pick_ref[...], preferred_element_type=jnp.float32
+        jnp.concatenate(sums, axis=0), pick_ref[...], preferred_element_type=jnp.float32
     )
     head_in = rms_silu(block_out, gain_ref[...])
     for part, values in enumerate(split_lanes(head_in)):
         plain[part] = values
-    windows[...] = jnp.zeros_like(windows)
+    for at in (0, breadth + 1):
+        windows[:, :, :, at] = jnp.zeros_like(windows[:, :, :, at])
     half = frames * pixels // 2
     row = lax.broadcasted_iota(jnp.int32, (half, LANES), 0) % rows
     for part in range(2):
@@ -321,13 +369,8 @@
     parts_out[...] = jnp.concatenate(parts, axis=0).astype(jnp.bfloat16)
 
 
-def conv_scratch(frames, breadth, height, taps, outputs):
-    pairs = (taps + 1) // 2
-    image = pltpu.VMEM((3, frames + 3, breadth + 2, height, LANES), jnp.bfloat16)
-    return [image] * 3 + [
-        pltpu.VMEM((taps + pairs, outputs, LANES), jnp.bfloat16),
-        pltpu.VMEM((2, SCRATCH_ROWS, LANES), jnp.float32),
-    ]
+def image_scratch(frames, breadth, height):
+    return [pltpu.VMEM((3, frames + 1, breadth + 2, height, LANES), jnp.bfloat16)] * 3
 
 
 def embed_kernel(place_ref, embed_ref, scale_ref, shift_ref, *rest):
@@ -401,6 +444,7 @@
     grid = groups == 2 and devices == 16
     units = 32
     unit_channels = channels // units
+    unpack = functools.partial(unpack_units, taps=taps, unit_channels=unit_channels)
 
     by_output = [weight.transpose(2, 0, 1) for weight in (weight_first, weight_second)]
     channel_map = unit_channel_map(grid, group, device, unit_channels, units)
@@ -450,39 +494,54 @@
         ]
 
     first = (device * frames).astype(jnp.int32).reshape(1)
-    scratch = conv_scratch(frames, breadth, height, taps, units * SUBLANES)
     image = pltpu.VMEM((frames, breadth, height, channels), jnp.bfloat16)
-    second_in = pl.pallas_call(
+    second_in, sent = pl.pallas_call(
         functools.partial(first_kernel, taps=taps, unit_channels=unit_channels),
-        out_shape=image,
+        out_shape=[image, pltpu.VMEM((3, breadth * height, LANES), jnp.bfloat16)],
         in_specs=[SMEM_SPEC] * 2 + [VMEM_SPEC] * (5 + len(units_first)),
-        out_specs=VMEM_SPEC,
-        scratch_shapes=scratch,
+        out_specs=[VMEM_SPEC] * 2,
+        scratch_shapes=image_scratch(frames + 2, breadth, height)
+        + [
+            pltpu.VMEM((taps + (taps + 1) // 2, units * SUBLANES, LANES), jnp.bfloat16),
+            pltpu.VMEM((2, SCRATCH_ROWS, LANES), jnp.float32),
+        ],
         compiler_params=LARGE,
     )(
         clip_ids, first, IN_VMEM(turned), IN_HBM(turned_rim), gain_first.reshape(1, -1),
         gain_second.reshape(1, -1), IN_VMEM(pick), *map(IN_HBM, units_first),
     )
-    second_rim = to_next(second_in[frames - 2 :], "ctx")
+    second_rim = to_next(sent, "ctx")
+    units_second, second_in = lax.optimization_barrier((units_second, second_in))
+    rhs_second = [unpack(units_second)]
     if grid:
-        units_second, second_in = lax.optimization_barrier((units_second, second_in))
-        units_second = both_cores(units_second)
+        rhs_second = both_cores(rhs_second)
 
     depth = weight_out.shape[2]
+    summed = pl.pallas_call(
+        functools.partial(own_kernel, taps=taps),
+        out_shape=pltpu.VMEM((frames * breadth * height, units * SUBLANES), jnp.float32),
+        in_specs=[SMEM_SPEC] * 2 + [VMEM_SPEC] * (3 + len(rhs_second)),
+        out_specs=VMEM_SPEC,
+        scratch_shapes=image_scratch(frames, breadth, height),
+        compiler_params=LARGE,
+    )(
+        clip_ids, first, IN_VMEM(second_in), IN_VMEM(turned), IN_VMEM(pick),
+        *map(IN_VMEM, rhs_second),
+    )
     parts = pl.pallas_call(
-        functools.partial(second_kernel, taps=taps, unit_channels=unit_channels),
+        functools.partial(second_kernel, taps=taps),
         out_shape=pltpu.VMEM((2 * spots, frames * 4 * depth), jnp.bfloat16),
-        in_specs=[SMEM_SPEC] * 2 + [VMEM_SPEC] * (6 + len(units_second)),
+        in_specs=[SMEM_SPEC] * 2 + [VMEM_SPEC] * (5 + len(rhs_second)),
         out_specs=VMEM_SPEC,
-        scratch_shapes=scratch
+        scratch_shapes=image_scratch(2, breadth, height)
         + [
             pltpu.VMEM((2, frames * breadth * height, LANES), jnp.float32),
             pltpu.VMEM((4, 2, frames, breadth + 2, height // 2, LANES), jnp.float32),
         ],
         compiler_params=LARGE,
     )(
-        clip_ids, first, IN_VMEM(second_in), IN_VMEM(second_rim), IN_VMEM(turned),
-        gain_third.reshape(1, -1), IN_VMEM(pick), IN_VMEM(wide), *map(IN_HBM, units_second),
+        clip_ids, first, IN_VMEM(second_rim), gain_third.reshape(1, -1), IN_VMEM(pick),
+        IN_VMEM(wide), IN_VMEM(summed), *map(IN_VMEM, rhs_second),
     )
     if grid:
         line = jnp.concatenate(along_line(parts))

time: 81.7 us -> 81.2 us (level)
  starting transfers between devices: 35.1 us -> 33.7 us
  waiting for transfers between devices: 24.8 us -> 25.8 us
    ppermute x37 -> x30, starting transfers between devices: 32.3 us -> 29.7 us  [xor_permute(): lax.ppermute(value, axis, [(source, source ^ mask) for source in range(co...]
    ppermute x2, starting transfers between devices: 2.81 us -> 4.02 us  [to_next(): lax.ppermute(value, axis, [(source, source + 1) for source in range(count...]
    ppermute x37 -> x30, waiting for transfers between devices: 24.8 us -> 25.8 us  [xor_permute(): lax.ppermute(value, axis, [(source, source ^ mask) for source in range(co...]
    pallas_call x1 -> x3, Pallas kernels: 7.24 us -> 7.97 us  [the longest x1 3.91 us: body(): pl.pallas_call(functools.partial(second_kernel, taps=taps), out_shape=plt...]
    unnamed x71 -> x51, local copies, waits for them, and re-layouts: 1.79 us -> 1.18 us
  transfers between devices with their start and end apart: 39 -> 32, of which waited for: 18 -> 13; matrix products, arithmetic and copies ran while one was open for 2% -> 2% of each run, Pallas kernels for 9% -> 12%
where the time goes in v6:
time: 81.2 us; the launch traced here: 80.9 us
  starting transfers between devices  33.7 us (42%)
  waiting for transfers between devices  25.8 us (32%)
  Pallas kernels  19.4 us (24%)
  local copies, waits for them, and re-layouts  1.22 us (2%)
    ppermute x30, starting transfers between devices, xor_permute(): lax.ppermute(value, axis, [(source, source ^ mask) for source in range(co...  29.7 us
    ppermute x30, waiting for transfers between devices, xor_permute(): lax.ppermute(value, axis, [(source, source ^ mask) for source in range(co...  25.8 us
    pallas_call x1, Pallas kernels, body(): pl.pallas_call(functools.partial(first_kernel, taps=taps, unit_channels=u...  6.04 us
    ppermute x2, starting transfers between devices, to_next(): lax.ppermute(value, axis, [(source, source + 1) for source in range(count...  4.02 us
    pallas_call x1, Pallas kernels, body(): pl.pallas_call(functools.partial(second_kernel, taps=taps), out_shape=plt...  3.91 us
    pallas_call x1, Pallas kernels, body(): pl.pallas_call(embed_kernel, out_shape=jax.ShapeDtypeStruct((tokens, widt...  3.17 us
    pallas_call x1, Pallas kernels, body(): pl.pallas_call(functools.partial(own_kernel, taps=taps), out_shape=pltpu....  2.43 us
    pallas_call x1, Pallas kernels, unpack_units(): pl.pallas_call(functools.partial(unpack_kernel, taps=taps, unit_channels=...  1.63 us
  transfers between devices with their start and end apart: 32, of which 13 were waited for; matrix products, arithmetic and copies ran while one was open for 2% of the time, Pallas kernels for 12%

profile of v6, /device:TPU:0, one launch (start us, length us, event | category | flops | bytes accessed | tf_op | source)
XLA Modules:
  0.0 80.9 jit_solution(6943174378685364948)
XLA Ops:
  0.0 1.1 %shard_map.118 = bf16[2,256,128]{2,1,0:T(8,128)(2,1)S(1)} custom-call(s32[1]{0:T(128)} %bitcast.half_ref, bf16[12,27,192]{2,1,0:T(8,128)(2,1)} %bitcast.25, bf16[12,27,192]{2,1,0:T(8,128)(2,1)} %bitcast.26), custom_call_target="tpu_custom_call" | custom-call | tf_op jit(solution)/shard_map/pallas_call | solution.py:57
  1.1 5.1 %collective-permute-start.2 = (bf16[2,256,128]{2,1,0:T(8,128)(2,1)S(1)}, bf16[2,256,128]{2,1,0:T(8,128)(2,1)S(1)}, u32[]{:S(2)}, u32[]{:S(2)}) collective-permute-start(bf16[2,256,128]{2,1,0:T(8,128)(2,1)S(1)} %shard_map.118), channel_id=1, source_target_pairs={{0,12},{1,13},{2,14},{3,15},{4,8},{5,9},{6,10},{7,11},{8,4},{9,5},... | collective-permute-start | bytes 393224 | tf_op jit(solution)/shard_map/ppermute | solution.py:26
  6.3 0.6 collective-permute-start
  6.9 1.1 %copy.17 = bf16[2,16,24,192]{3,1,2,0:T(8,128)(2,1)S(1)} copy(bf16[2,16,24,192]{3,2,1,0:T(8,128)(2,1)} %param.12) | data formatting | bytes 589824 | tf_op args[0]
  8.0 1.3 %collective-permute-start.7 = (bf16[2,16,24,192]{3,1,2,0:T(8,128)(2,1)S(1)}, bf16[2,16,24,192]{3,1,2,0:T(8,128)(2,1)S(1)}, u32[]{:S(2)}, u32[]{:S(2)}) collective-permute-start(bf16[2,16,24,192]{3,1,2,0:T(8,128)(2,1)S(1)} %copy.17), channel_id=1, source_target_pairs={{0,1},{1,2},{2,3},{3,4},{4,5},{5,6},{6,7},{7,8},{8,9},{9,10},{10,1... | collective-permute-start | bytes 884744 | tf_op jit(solution)/shard_map/ppermute | solution.py:31
  9.4 0.1 fusion.pick_ref
  9.5 1.1 %shard_map.119.wide_ref = bf16[16,192,256]{2,1,0:T(8,128)(2,1)S(1)} custom-call(bf16[27,16,192]{2,1,0:T(8,128)(2,1)} %bitcast.24), custom_call_target="tpu_custom_call" | custom-call | tf_op jit(solution)/shard_map/pallas_call | solution.py:98
  10.6 0.0 copy-start.3
  10.7 4.0 %collective-permute-done = bf16[2,256,128]{2,1,0:T(8,128)(2,1)S(1)} collective-permute-done((bf16[2,256,128]{2,1,0:T(8,128)(2,1)S(1)}, bf16[2,256,128]{2,1,0:T(8,128)(2,1)S(1)}, u32[]{:S(2)}, u32[]{:S(2)}) %collective-permute-start) | collective-permute-done | bytes 131104 | tf_op jit(solution)/shard_map/ppermute | solution.py:26
  14.7 2.7 %collective-permute-start.8 = (bf16[2,256,128]{2,1,0:T(8,128)(2,1)S(1)}, bf16[2,256,128]{2,1,0:T(8,128)(2,1)S(1)}, u32[]{:S(2)}, u32[]{:S(2)}) collective-permute-start(bf16[2,256,128]{2,1,0:T(8,128)(2,1)S(1)} %pad_maximum_fusion.1.rest_0_), channel_id=1, source_target_pairs={{0,2},{1,3},{2,0},{3,1},{4,6},{5,7},{6,4},{7,5},{8,10},{9,11},{10,... | collective-permute-start | bytes 393224 | tf_op jit(solution)/shard_map/ppermute | solution.py:26
  17.4 1.5 %collective-permute-start.3 = (bf16[2,256,128]{2,1,0:T(8,128)(2,1)S(1)}, bf16[2,256,128]{2,1,0:T(8,128)(2,1)S(1)}, u32[]{:S(2)}, u32[]{:S(2)}) collective-permute-start(bf16[2,256,128]{2,1,0:T(8,128)(2,1)S(1)} %pad_maximum_fusion.1.rest_0_), channel_id=1, source_target_pairs={{0,16},{16,0},{1,17},{17,1},{2,18},{18,2},{3,19},{19,3},{4,20},{20... | collective-permute-start | bytes 393224 | tf_op jit(solution)/shard_map/ppermute | solution.py:26
  19.0 0.1 collective-permute-start.5
  19.1 1.4 %collective-permute-start.9 = (bf16[2,256,128]{2,1,0:T(8,128)(2,1)S(1)}, bf16[2,256,128]{2,1,0:T(8,128)(2,1)S(1)}, u32[]{:S(2)}, u32[]{:S(2)}) collective-permute-start(bf16[2,256,128]{2,1,0:T(8,128)(2,1)S(1)} %pad_maximum_fusion.3.rest_1_), channel_id=1, source_target_pairs={{0,16},{16,0},{1,17},{17,1},{2,18},{18,2},{3,19},{19,3},{4,20},{20... | collective-permute-start | bytes 393224 | tf_op jit(solution)/shard_map/ppermute | solution.py:26
  20.5 2.8 %collective-permute-done.3.rest_4_ = bf16[2,256,128]{2,1,0:T(8,128)(2,1)S(1)} collective-permute-done((bf16[2,256,128]{2,1,0:T(8,128)(2,1)S(1)}, bf16[2,256,128]{2,1,0:T(8,128)(2,1)S(1)}, u32[]{:S(2)}, u32[]{:S(2)}) %collective-permute-start.3) | collective-permute-done | bytes 131104 | tf_op jit(solution)/shard_map/ppermute | solution.py:26
  23.3 0.5 collective-permute-start.4
  23.8 0.8 collective-permute-done.5.rest_3_
  24.6 0.1 collective-permute-done.9.rest_5_
  24.7 1.5 %collective-permute-start.6 = (bf16[2,256,128]{2,1,0:T(8,128)(2,1)S(1)}, bf16[2,256,128]{2,1,0:T(8,128)(2,1)}, u32[]{:S(2)}, u32[]{:S(2)}) collective-permute-start(bf16[2,256,128]{2,1,0:T(8,128)(2,1)S(1)} %collective-permute-done.5.rest_3_), channel_id=1, source_target_pairs={{0,16},{16,0},{1,17},{17,1},{2,18},{18,2},{3,19},{19,3},{4,20},{20... | collective-permute-start | bytes 393224 | tf_op jit(solution)/shard_map/ppermute | solution.py:26
  26.2 0.1 collective-permute-start.12
  26.3 2.0 %collective-permute-done.4.rest_6_ = bf16[2,256,128]{2,1,0:T(8,128)(2,1)S(1)} collective-permute-done((bf16[2,256,128]{2,1,0:T(8,128)(2,1)S(1)}, bf16[2,256,128]{2,1,0:T(8,128)(2,1)S(1)}, u32[]{:S(2)}, u32[]{:S(2)}) %collective-permute-start.4) | collective-permute-done | bytes 131104 | tf_op jit(solution)/shard_map/ppermute | solution.py:26
  28.3 2.3 %collective-permute-done.6.rest_7_ = bf16[2,256,128]{2,1,0:T(8,128)(2,1)} collective-permute-done((bf16[2,256,128]{2,1,0:T(8,128)(2,1)S(1)}, bf16[2,256,128]{2,1,0:T(8,128)(2,1)}, u32[]{:S(2)}, u32[]{:S(2)}) %collective-permute-start.6) | collective-permute-done | bytes 131104 | tf_op jit(solution)/shard_map/ppermute | solution.py:26
  30.6 0.5 collective-permute-start.11
  31.1 0.1 collective-permute-start.16
  31.2 1.4 %collective-permute-start.21 = (bf16[2,256,128]{2,1,0:T(8,128)(2,1)S(1)}, bf16[2,256,128]{2,1,0:T(8,128)(2,1)}, u32[]{:S(2)}, u32[]{:S(2)}) collective-permute-start(bf16[2,256,128]{2,1,0:T(8,128)(2,1)S(1)} %pad_maximum_fusion.2.refs_0_), channel_id=1, source_target_pairs={{0,16},{16,0},{1,17},{17,1},{2,18},{18,2},{3,19},{19,3},{4,20},{20... | collective-permute-start | bytes 393224 | tf_op jit(solution)/shard_map/ppermute | solution.py:26
  32.7 1.8 %collective-permute-start.20 = (bf16[2,256,128]{2,1,0:T(8,128)(2,1)S(1)}, bf16[2,256,128]{2,1,0:T(8,128)(2,1)}, u32[]{:S(2)}, u32[]{:S(2)}) collective-permute-start(bf16[2,256,128]{2,1,0:T(8,128)(2,1)S(1)} %pad_maximum_fusion.4.refs_1_), channel_id=1, source_target_pairs={{0,2},{1,3},{2,0},{3,1},{4,6},{5,7},{6,4},{7,5},{8,10},{9,11},{10,... | collective-permute-start | bytes 393224 | tf_op jit(solution)/shard_map/ppermute | solution.py:26
  34.5 0.3 collective-permute-start.19
  34.8 0.6 collective-permute-start.22
  35.4 1.8 %collective-permute-done.21.refs_4_ = bf16[2,256,128]{2,1,0:T(8,128)(2,1)} collective-permute-done((bf16[2,256,128]{2,1,0:T(8,128)(2,1)S(1)}, bf16[2,256,128]{2,1,0:T(8,128)(2,1)}, u32[]{:S(2)}, u32[]{:S(2)}) %collective-permute-start.21) | collective-permute-done | bytes 131104 | tf_op jit(solution)/shard_map/ppermute | solution.py:26
  37.2 1.8 %collective-permute-start.23 = (bf16[2,256,128]{2,1,0:T(8,128)(2,1)}, bf16[2,256,128]{2,1,0:T(8,128)(2,1)}, u32[]{:S(2)}, u32[]{:S(2)}) collective-permute-start(bf16[2,256,128]{2,1,0:T(8,128)(2,1)} %collective-permute-done.21.refs_4_), channel_id=1, source_target_pairs={{0,2},{1,3},{2,0},{3,1},{4,6},{5,7},{6,4},{7,5},{8,10},{9,11},{10,... | collective-permute-start | bytes 393224 | tf_op jit(solution)/shard_map/ppermute | solution.py:26
  39.0 0.2 collective-permute-done.20.refs_3_
  39.2 1.8 %collective-permute-start.24 = (bf16[2,256,128]{2,1,0:T(8,128)(2,1)}, bf16[2,256,128]{2,1,0:T(8,128)(2,1)}, u32[]{:S(2)}, u32[]{:S(2)}) collective-permute-start(bf16[2,256,128]{2,1,0:T(8,128)(2,1)} %collective-permute-done.20.refs_3_), channel_id=1, source_target_pairs={{0,16},{16,0},{1,17},{17,1},{2,18},{18,2},{3,19},{19,3},{4,20},{20... | collective-permute-start | bytes 393224 | tf_op jit(solution)/shard_map/ppermute | solution.py:26
  41.0 6.0 %shard_map.120 = (bf16[2,24,16,192]{3,2,1,0:T(8,128)(2,1)S(1)}, bf16[3,384,128]{2,1,0:T(8,128)(2,1)S(1)}) custom-call(s32[32]{0:T(128)S(1)} %copy-done.3, s32[1]{0:T(128)} %bitcast.10.first_ref, bf16[2,24,16,192]{3,2,1,0:T(8,128)(2,1)S(1)} %bitcast.16, bf16[2,24,16,192]{3,2,1,0:T(8,128)(2,1)} %bitcast.23, f32[1,192]{1,0:T(1,128)S(1)} %bitcast.20, ...), custom_call_target="tpu_custom_call" | custom-call | tf_op jit(solution)/shard_map/pallas_call | solution.py:498
  47.1 1.6 %shard_map.121.rest_0_ = bf16[41,128,128]{2,1,0:T(8,128)(2,1)S(1)} custom-call(bf16[2,256,128]{2,1,0:T(8,128)(2,1)} %copy-done.9, bf16[2,256,128]{2,1,0:T(8,128)(2,1)} %copy-done.10, bf16[2,256,128]{2,1,0:T(8,128)(2,1)} %collective-permute-done.19.refs_2_, bf16[2,256,128]{2,1,0:T(8,128)(2,1)} %collective-permute-done.20.refs_3_, ...), custom_call_target="tpu_custom_call" | custom-call | tf_op jit(solution)/shard_map/pallas_call | solution.py:178
  48.8 0.1 collective-permute-start.25
  48.8 0.0 copy-start.6
  48.8 2.7 %collective-permute-start.18 = (bf16[3,384,128]{2,1,0:T(8,128)(2,1)S(1)}, bf16[3,384,128]{2,1,0:T(8,128)(2,1)S(1)}, u32[]{:S(2)}, u32[]{:S(2)}) collective-permute-start(bf16[3,384,128]{2,1,0:T(8,128)(2,1)S(1)} %get-tuple-element.39), channel_id=1, source_target_pairs={{0,1},{1,2},{2,3},{3,4},{4,5},{5,6},{6,7},{7,8},{8,9},{9,10},{10,1... | collective-permute-start | bytes 884744 | tf_op jit(solution)/shard_map/ppermute | solution.py:31
  51.6 0.3 collective-permute-done.25.rest_1_
  51.9 2.4 %shard_map.122.summed_ref = f32[768,256]{1,0:T(8,128)S(1)} custom-call(s32[32]{0:T(128)S(1)} %copy-done.3, s32[1]{0:T(128)} %bitcast.10.first_ref, bf16[2,24,16,192]{3,2,1,0:T(8,128)(2,1)S(1)} %get-tuple-element.44.own_ref, bf16[2,24,16,192]{3,2,1,0:T(8,128)(2,1)S(1)} %bitcast.17, bf16[256,192]{1,0:T(8,128)(2,1)S(1)} %fusion.pick_ref, ...), custom_call_target="tpu_custom_call" | custom-call | tf_op jit(solution)/shard_map/pallas_call | solution.py:520
  54.4 3.9 %shard_map.123 = bf16[192,128]{1,0:T(8,128)(2,1)S(1)} custom-call(s32[32]{0:T(128)S(1)} %copy-done.3, s32[1]{0:T(128)} %bitcast.10.first_ref, bf16[3,384,128]{2,1,0:T(8,128)(2,1)S(1)} %collective-permute-done.18.rim_ref, f32[1,192]{1,0:T(1,128)S(1)} %bitcast.22, bf16[256,192]{1,0:T(8,128)(2,1)S(1)} %fusion.pick_ref, ...), custom_call_target="tpu_custom_call" | custom-call | tf_op jit(solution)/shard_map/pallas_call | solution.py:531
  58.3 6.7 %collective-permute-start.28 = (bf16[192,128]{1,0:T(8,128)(2,1)S(1)}, bf16[192,128]{1,0:T(8,128)(2,1)S(1)}, u32[]{:S(2)}, u32[]{:S(2)}) collective-permute-start(bf16[192,128]{1,0:T(8,128)(2,1)S(1)} %shard_map.123), channel_id=1, source_target_pairs={{0,12},{1,13},{2,14},{3,15},{4,8},{5,9},{6,10},{7,11},{8,4},{9,5},... | collective-permute-start | bytes 147464 | tf_op jit(solution)/shard_map/ppermute | solution.py:26
  65.0 0.6 collective-permute-start.27
  65.6 0.2 collective-permute-start.26
  65.8 1.9 %collective-permute-done.28 = bf16[192,128]{1,0:T(8,128)(2,1)S(1)} collective-permute-done((bf16[192,128]{1,0:T(8,128)(2,1)S(1)}, bf16[192,128]{1,0:T(8,128)(2,1)S(1)}, u32[]{:S(2)}, u32[]{:S(2)}) %collective-permute-start.28) | collective-permute-done | bytes 49184 | tf_op jit(solution)/shard_map/ppermute | solution.py:26
  67.7 2.9 %collective-permute-done.27 = bf16[192,128]{1,0:T(8,128)(2,1)S(1)} collective-permute-done((bf16[192,128]{1,0:T(8,128)(2,1)S(1)}, bf16[192,128]{1,0:T(8,128)(2,1)S(1)}, u32[]{:S(2)}, u32[]{:S(2)}) %collective-permute-start.27) | collective-permute-done | bytes 49184 | tf_op jit(solution)/shard_map/ppermute | solution.py:26
  70.6 0.4 collective-permute-start.29
  70.9 5.4 %collective-permute-done.29.rest_1_ = bf16[768,128]{1,0:T(8,128)(2,1)S(1)} collective-permute-done((bf16[768,128]{1,0:T(8,128)(2,1)S(1)}, bf16[768,128]{1,0:T(8,128)(2,1)S(1)}, u32[]{:S(2)}, u32[]{:S(2)}) %collective-permute-start.29) | collective-permute-done | bytes 196640 | tf_op jit(solution)/shard_map/ppermute | solution.py:26
  76.3 1.4 %collective-permute-done.31.rest_3_ = bf16[768,128]{1,0:T(8,128)(2,1)S(1)} collective-permute-done((bf16[768,128]{1,0:T(8,128)(2,1)S(1)}, bf16[768,128]{1,0:T(8,128)(2,1)S(1)}, u32[]{:S(2)}, u32[]{:S(2)}) %collective-permute-start.31) | collective-permute-done | bytes 196640 | tf_op jit(solution)/shard_map/ppermute | solution.py:26
  77.8 3.2 %shard_map.124 = bf16[192,3072]{1,0:T(8,128)(2,1)} custom-call(s32[3,192]{1,0:T(4,128)S(1)} %pad_add_fusion.place_ref, bf16[64,3072]{1,0:T(8,128)(2,1)S(1)} %copy-done, f32[1,3072]{1,0:T(1,128)S(1)} %bitcast.18, f32[1,3072]{1,0:T(1,128)S(1)} %bitcast.19, bf16[768,128]{1,0:T(8,128)(2,1)S(1)} %pad_maximum_fusion.rest_0_, ...), custom_call_target="tpu_custom_call" | custom-call | tf_op jit(solution)/shard_map/pallas_call | solution.py:553
  (88 shorter events, 0.4 us)
Async XLA Ops:
  1.1 17.8 %collective-permute-start.2 = (bf16[2,256,128]{2,1,0:T(8,128)(2,1)S(1)}, bf16[2,256,128]{2,1,0:T(8,128)(2,1)S(1)}, u32[]{:S(2)}, u32[]{:S(2)}) collective-permute-start(bf16[2,256,128]{2,1,0:T(8,128)(2,1)S(1)} %shard_map.118), channel_id=1, source_target_pairs={{0,12},{1,13},{2,14},{3,15},{4,8},{5,9},{6,10},{7,11},{8,4},{9,5},... | collective-permute-start | bytes 393224 | tf_op jit(solution)/shard_map/ppermute | solution.py:26
  6.3 12.7 %collective-permute-start.1 = (bf16[2,256,128]{2,1,0:T(8,128)(2,1)S(1)}, bf16[2,256,128]{2,1,0:T(8,128)(2,1)S(1)}, u32[]{:S(2)}, u32[]{:S(2)}) collective-permute-start(bf16[2,256,128]{2,1,0:T(8,128)(2,1)S(1)} %shard_map.118), channel_id=1, source_target_pairs={{0,8},{1,9},{2,10},{3,11},{4,12},{5,13},{6,14},{7,15},{8,0},{9,1},... | collective-permute-start | bytes 393224 | tf_op jit(solution)/shard_map/ppermute | solution.py:26
  6.3 8.4 %collective-permute-start = (bf16[2,256,128]{2,1,0:T(8,128)(2,1)S(1)}, bf16[2,256,128]{2,1,0:T(8,128)(2,1)S(1)}, u32[]{:S(2)}, u32[]{:S(2)}) collective-permute-start(bf16[2,256,128]{2,1,0:T(8,128)(2,1)S(1)} %shard_map.118), channel_id=1, source_target_pairs={{0,4},{1,5},{2,6},{3,7},{4,0},{5,1},{6,2},{7,3},{8,12},{9,13},{10,... | collective-permute-start | bytes 393224 | tf_op jit(solution)/shard_map/ppermute | solution.py:26
  8.0 18.2 %collective-permute-start.7 = (bf16[2,16,24,192]{3,1,2,0:T(8,128)(2,1)S(1)}, bf16[2,16,24,192]{3,1,2,0:T(8,128)(2,1)S(1)}, u32[]{:S(2)}, u32[]{:S(2)}) collective-permute-start(bf16[2,16,24,192]{3,1,2,0:T(8,128)(2,1)S(1)} %copy.17), channel_id=1, source_target_pairs={{0,1},{1,2},{2,3},{3,4},{4,5},{5,6},{6,7},{7,8},{8,9},{9,10},{10,1... | collective-permute-start | bytes 884744 | tf_op jit(solution)/shard_map/ppermute | solution.py:31
  10.6 30.3 %copy-start.3 = (s32[32]{0:T(128)S(1)}, s32[32]{0:T(128)}, u32[]{:S(2)}) copy-start(s32[32]{0:T(128)} %clips_ref.5) | copy-start | bytes 388
  10.7 30.3 %copy-start.4 = (f32[192]{0:T(256)S(1)}, f32[192]{0:T(256)}, u32[]{:S(2)}) copy-start(f32[192]{0:T(256)} %param.14) | copy-start | bytes 2308
  10.7 30.3 %copy-start.5 = (f32[192]{0:T(256)S(1)}, f32[192]{0:T(256)}, u32[]{:S(2)}) copy-start(f32[192]{0:T(256)} %param.16) | copy-start | bytes 2308
  14.7 26.2 %copy-start.7 = (bf16[2,256,128]{2,1,0:T(8,128)(2,1)}, bf16[2,256,128]{2,1,0:T(8,128)(2,1)S(1)}, u32[]{:S(2)}) copy-start(bf16[2,256,128]{2,1,0:T(8,128)(2,1)S(1)} %pad_maximum_fusion.1.rest_0_) | copy-start | bytes 393220
  14.7 9.0 %collective-permute-start.8 = (bf16[2,256,128]{2,1,0:T(8,128)(2,1)S(1)}, bf16[2,256,128]{2,1,0:T(8,128)(2,1)S(1)}, u32[]{:S(2)}, u32[]{:S(2)}) collective-permute-start(bf16[2,256,128]{2,1,0:T(8,128)(2,1)S(1)} %pad_maximum_fusion.1.rest_0_), channel_id=1, source_target_pairs={{0,2},{1,3},{2,0},{3,1},{4,6},{5,7},{6,4},{7,5},{8,10},{9,11},{10,... | collective-permute-start | bytes 393224 | tf_op jit(solution)/shard_map/ppermute | solution.py:26
  17.4 5.8 %collective-permute-start.3 = (bf16[2,256,128]{2,1,0:T(8,128)(2,1)S(1)}, bf16[2,256,128]{2,1,0:T(8,128)(2,1)S(1)}, u32[]{:S(2)}, u32[]{:S(2)}) collective-permute-start(bf16[2,256,128]{2,1,0:T(8,128)(2,1)S(1)} %pad_maximum_fusion.1.rest_0_), channel_id=1, source_target_pairs={{0,16},{16,0},{1,17},{17,1},{2,18},{18,2},{3,19},{19,3},{4,20},{20... | collective-permute-start | bytes 393224 | tf_op jit(solution)/shard_map/ppermute | solution.py:26
  19.0 22.0 %copy-start.8 = (bf16[2,256,128]{2,1,0:T(8,128)(2,1)}, bf16[2,256,128]{2,1,0:T(8,128)(2,1)S(1)}, u32[]{:S(2)}) copy-start(bf16[2,256,128]{2,1,0:T(8,128)(2,1)S(1)} %pad_maximum_fusion.3.rest_1_) | copy-start | bytes 393220
  19.0 5.6 %collective-permute-start.5 = (bf16[2,256,128]{2,1,0:T(8,128)(2,1)S(1)}, bf16[2,256,128]{2,1,0:T(8,128)(2,1)S(1)}, u32[]{:S(2)}, u32[]{:S(2)}) collective-permute-start(bf16[2,256,128]{2,1,0:T(8,128)(2,1)S(1)} %pad_maximum_fusion.3.rest_1_), channel_id=1, source_target_pairs={{0,2},{1,3},{2,0},{3,1},{4,6},{5,7},{6,4},{7,5},{8,10},{9,11},{10,... | collective-permute-start | bytes 393224 | tf_op jit(solution)/shard_map/ppermute | solution.py:26
  19.1 5.5 %collective-permute-start.9 = (bf16[2,256,128]{2,1,0:T(8,128)(2,1)S(1)}, bf16[2,256,128]{2,1,0:T(8,128)(2,1)S(1)}, u32[]{:S(2)}, u32[]{:S(2)}) collective-permute-start(bf16[2,256,128]{2,1,0:T(8,128)(2,1)S(1)} %pad_maximum_fusion.3.rest_1_), channel_id=1, source_target_pairs={{0,16},{16,0},{1,17},{17,1},{2,18},{18,2},{3,19},{19,3},{4,20},{20... | collective-permute-start | bytes 393224 | tf_op jit(solution)/shard_map/ppermute | solution.py:26
  23.3 17.7 %copy-start.13 = (bf16[2,256,128]{2,1,0:T(8,128)(2,1)}, bf16[2,256,128]{2,1,0:T(8,128)(2,1)S(1)}, u32[]{:S(2)}) copy-start(bf16[2,256,128]{2,1,0:T(8,128)(2,1)S(1)} %collective-permute-done.3.rest_4_) | copy-start | bytes 393220
  23.3 5.0 %collective-permute-start.4 = (bf16[2,256,128]{2,1,0:T(8,128)(2,1)S(1)}, bf16[2,256,128]{2,1,0:T(8,128)(2,1)S(1)}, u32[]{:S(2)}, u32[]{:S(2)}) collective-permute-start(bf16[2,256,128]{2,1,0:T(8,128)(2,1)S(1)} %collective-permute-done.3.rest_4_), channel_id=1, source_target_pairs={{0,2},{1,3},{2,0},{3,1},{4,6},{5,7},{6,4},{7,5},{8,10},{9,11},{10,... | collective-permute-start | bytes 393224 | tf_op jit(solution)/shard_map/ppermute | solution.py:26
  23.8 17.2 %copy-start.12 = (bf16[2,256,128]{2,1,0:T(8,128)(2,1)}, bf16[2,256,128]{2,1,0:T(8,128)(2,1)S(1)}, u32[]{:S(2)}) copy-start(bf16[2,256,128]{2,1,0:T(8,128)(2,1)S(1)} %collective-permute-done.8.rest_2_) | copy-start | bytes 393220
  23.8 7.4 %collective-permute-start.14 = (bf16[2,256,128]{2,1,0:T(8,128)(2,1)S(1)}, bf16[2,256,128]{2,1,0:T(8,128)(2,1)S(1)}, u32[]{:S(2)}, u32[]{:S(2)}) collective-permute-start(bf16[2,256,128]{2,1,0:T(8,128)(2,1)S(1)} %collective-permute-done.3.rest_4_), channel_id=1, source_target_pairs={{0,1},{1,0},{2,3},{3,2},{4,5},{5,4},{6,7},{7,6},{8,9},{9,8},{10,11... | collective-permute-start | bytes 393224 | tf_op jit(solution)/shard_map/ppermute | solution.py:26
  24.6 16.4 %copy-start.14 = (bf16[2,256,128]{2,1,0:T(8,128)(2,1)}, bf16[2,256,128]{2,1,0:T(8,128)(2,1)S(1)}, u32[]{:S(2)}) copy-start(bf16[2,256,128]{2,1,0:T(8,128)(2,1)S(1)} %collective-permute-done.5.rest_3_) | copy-start | bytes 393220
  24.6 8.1 %collective-permute-start.13 = (bf16[2,256,128]{2,1,0:T(8,128)(2,1)S(1)}, bf16[2,256,128]{2,1,0:T(8,128)(2,1)S(1)}, u32[]{:S(2)}, u32[]{:S(2)}) collective-permute-start(bf16[2,256,128]{2,1,0:T(8,128)(2,1)S(1)} %collective-permute-done.5.rest_3_), channel_id=1, source_target_pairs={{0,1},{1,0},{2,3},{3,2},{4,5},{5,4},{6,7},{7,6},{8,9},{9,8},{10,11... | collective-permute-start | bytes 393224 | tf_op jit(solution)/shard_map/ppermute | solution.py:26
  24.7 16.3 %copy-start.15 = (bf16[2,256,128]{2,1,0:T(8,128)(2,1)}, bf16[2,256,128]{2,1,0:T(8,128)(2,1)S(1)}, u32[]{:S(2)}) copy-start(bf16[2,256,128]{2,1,0:T(8,128)(2,1)S(1)} %collective-permute-done.9.rest_5_) | copy-start | bytes 393220
  24.7 6.0 %collective-permute-start.6 = (bf16[2,256,128]{2,1,0:T(8,128)(2,1)S(1)}, bf16[2,256,128]{2,1,0:T(8,128)(2,1)}, u32[]{:S(2)}, u32[]{:S(2)}) collective-permute-start(bf16[2,256,128]{2,1,0:T(8,128)(2,1)S(1)} %collective-permute-done.5.rest_3_), channel_id=1, source_target_pairs={{0,16},{16,0},{1,17},{17,1},{2,18},{18,2},{3,19},{19,3},{4,20},{20... | collective-permute-start | bytes 393224 | tf_op jit(solution)/shard_map/ppermute | solution.py:26
  26.2 14.8 %copy-start.11 = (bf16[2,16,24,192]{3,1,2,0:T(8,128)(2,1)}, bf16[2,16,24,192]{3,1,2,0:T(8,128)(2,1)S(1)}, u32[]{:S(2)}) copy-start(bf16[2,16,24,192]{3,1,2,0:T(8,128)(2,1)S(1)} %collective-permute-done.7) | copy-start | bytes 884740
  26.2 4.4 %collective-permute-start.12 = (bf16[2,256,128]{2,1,0:T(8,128)(2,1)S(1)}, bf16[2,256,128]{2,1,0:T(8,128)(2,1)S(1)}, u32[]{:S(2)}, u32[]{:S(2)}) collective-permute-start(bf16[2,256,128]{2,1,0:T(8,128)(2,1)S(1)} %collective-permute-done.8.rest_2_), channel_id=1, source_target_pairs={{0,1},{1,0},{2,3},{3,2},{4,5},{5,4},{6,7},{7,6},{8,9},{9,8},{10,11... | collective-permute-start | bytes 393224 | tf_op jit(solution)/shard_map/ppermute | solution.py:26
  28.2 10.9 %copy-start.16 = (bf16[2,256,128]{2,1,0:T(8,128)(2,1)}, bf16[2,256,128]{2,1,0:T(8,128)(2,1)S(1)}, u32[]{:S(2)}) copy-start(bf16[2,256,128]{2,1,0:T(8,128)(2,1)S(1)} %collective-permute-done.4.rest_6_) | copy-start | bytes 393220
  28.2 3.0 %collective-permute-start.15 = (bf16[2,256,128]{2,1,0:T(8,128)(2,1)S(1)}, bf16[2,256,128]{2,1,0:T(8,128)(2,1)S(1)}, u32[]{:S(2)}, u32[]{:S(2)}) collective-permute-start(bf16[2,256,128]{2,1,0:T(8,128)(2,1)S(1)} %collective-permute-done.9.rest_5_), channel_id=1, source_target_pairs={{0,1},{1,0},{2,3},{3,2},{4,5},{5,4},{6,7},{7,6},{8,9},{9,8},{10,11... | collective-permute-start | bytes 393224 | tf_op jit(solution)/shard_map/ppermute | solution.py:26
  28.3 18.8 %copy-start.9 = (bf16[2,256,128]{2,1,0:T(8,128)(2,1)}, bf16[2,256,128]{2,1,0:T(8,128)(2,1)S(1)}, u32[]{:S(2)}) copy-start(bf16[2,256,128]{2,1,0:T(8,128)(2,1)S(1)} %pad_maximum_fusion.2.refs_0_) | copy-start | bytes 393220
  28.3 18.8 %copy-start.10 = (bf16[2,256,128]{2,1,0:T(8,128)(2,1)}, bf16[2,256,128]{2,1,0:T(8,128)(2,1)S(1)}, u32[]{:S(2)}) copy-start(bf16[2,256,128]{2,1,0:T(8,128)(2,1)S(1)} %pad_maximum_fusion.4.refs_1_) | copy-start | bytes 393220
  30.6 3.9 %collective-permute-start.10 = (bf16[2,256,128]{2,1,0:T(8,128)(2,1)S(1)}, bf16[2,256,128]{2,1,0:T(8,128)(2,1)S(1)}, u32[]{:S(2)}, u32[]{:S(2)}) collective-permute-start(bf16[2,256,128]{2,1,0:T(8,128)(2,1)S(1)} %pad_maximum_fusion.1.rest_0_), channel_id=1, source_target_pairs={{0,1},{1,0},{2,3},{3,2},{4,5},{5,4},{6,7},{7,6},{8,9},{9,8},{10,11... | collective-permute-start | bytes 393224 | tf_op jit(solution)/shard_map/ppermute | solution.py:26
  30.6 3.9 %collective-permute-start.11 = (bf16[2,256,128]{2,1,0:T(8,128)(2,1)S(1)}, bf16[2,256,128]{2,1,0:T(8,128)(2,1)S(1)}, u32[]{:S(2)}, u32[]{:S(2)}) collective-permute-start(bf16[2,256,128]{2,1,0:T(8,128)(2,1)S(1)} %pad_maximum_fusion.3.rest_1_), channel_id=1, source_target_pairs={{0,1},{1,0},{2,3},{3,2},{4,5},{5,4},{6,7},{7,6},{8,9},{9,8},{10,11... | collective-permute-start | bytes 393224 | tf_op jit(solution)/shard_map/ppermute | solution.py:26
  31.1 3.7 %collective-permute-start.16 = (bf16[2,256,128]{2,1,0:T(8,128)(2,1)S(1)}, bf16[2,256,128]{2,1,0:T(8,128)(2,1)S(1)}, u32[]{:S(2)}, u32[]{:S(2)}) collective-permute-start(bf16[2,256,128]{2,1,0:T(8,128)(2,1)S(1)} %collective-permute-done.4.rest_6_), channel_id=1, source_target_pairs={{0,1},{1,0},{2,3},{3,2},{4,5},{5,4},{6,7},{7,6},{8,9},{9,8},{10,11... | collective-permute-start | bytes 393224 | tf_op jit(solution)/shard_map/ppermute | solution.py:26
  31.2 5.9 %collective-permute-start.21 = (bf16[2,256,128]{2,1,0:T(8,128)(2,1)S(1)}, bf16[2,256,128]{2,1,0:T(8,128)(2,1)}, u32[]{:S(2)}, u32[]{:S(2)}) collective-permute-start(bf16[2,256,128]{2,1,0:T(8,128)(2,1)S(1)} %pad_maximum_fusion.2.refs_0_), channel_id=1, source_target_pairs={{0,16},{16,0},{1,17},{17,1},{2,18},{18,2},{3,19},{19,3},{4,20},{20... | collective-permute-start | bytes 393224 | tf_op jit(solution)/shard_map/ppermute | solution.py:26
  32.7 6.4 %collective-permute-start.20 = (bf16[2,256,128]{2,1,0:T(8,128)(2,1)S(1)}, bf16[2,256,128]{2,1,0:T(8,128)(2,1)}, u32[]{:S(2)}, u32[]{:S(2)}) collective-permute-start(bf16[2,256,128]{2,1,0:T(8,128)(2,1)S(1)} %pad_maximum_fusion.4.refs_1_), channel_id=1, source_target_pairs={{0,2},{1,3},{2,0},{3,1},{4,6},{5,7},{6,4},{7,5},{8,10},{9,11},{10,... | collective-permute-start | bytes 393224 | tf_op jit(solution)/shard_map/ppermute | solution.py:26
  34.5 6.4 %collective-permute-start.17 = (bf16[2,256,128]{2,1,0:T(8,128)(2,1)}, bf16[2,256,128]{2,1,0:T(8,128)(2,1)}, u32[]{:S(2)}, u32[]{:S(2)}) collective-permute-start(bf16[2,256,128]{2,1,0:T(8,128)(2,1)} %collective-permute-done.6.rest_7_), channel_id=1, source_target_pairs={{0,1},{1,0},{2,3},{3,2},{4,5},{5,4},{6,7},{7,6},{8,9},{9,8},{10,11... | collective-permute-start | bytes 393224 | tf_op jit(solution)/shard_map/ppermute | solution.py:26
  34.5 12.6 %collective-permute-start.19 = (bf16[2,256,128]{2,1,0:T(8,128)(2,1)S(1)}, bf16[2,256,128]{2,1,0:T(8,128)(2,1)}, u32[]{:S(2)}, u32[]{:S(2)}) collective-permute-start(bf16[2,256,128]{2,1,0:T(8,128)(2,1)S(1)} %pad_maximum_fusion.2.refs_0_), channel_id=1, source_target_pairs={{0,2},{1,3},{2,0},{3,1},{4,6},{5,7},{6,4},{7,5},{8,10},{9,11},{10,... | collective-permute-start | bytes 393224 | tf_op jit(solution)/shard_map/ppermute | solution.py:26
  34.8 12.3 %collective-permute-start.22 = (bf16[2,256,128]{2,1,0:T(8,128)(2,1)S(1)}, bf16[2,256,128]{2,1,0:T(8,128)(2,1)}, u32[]{:S(2)}, u32[]{:S(2)}) collective-permute-start(bf16[2,256,128]{2,1,0:T(8,128)(2,1)S(1)} %pad_maximum_fusion.4.refs_1_), channel_id=1, source_target_pairs={{0,16},{16,0},{1,17},{17,1},{2,18},{18,2},{3,19},{19,3},{4,20},{20... | collective-permute-start | bytes 393224 | tf_op jit(solution)/shard_map/ppermute | solution.py:26
  37.2 9.9 %collective-permute-start.23 = (bf16[2,256,128]{2,1,0:T(8,128)(2,1)}, bf16[2,256,128]{2,1,0:T(8,128)(2,1)}, u32[]{:S(2)}, u32[]{:S(2)}) collective-permute-start(bf16[2,256,128]{2,1,0:T(8,128)(2,1)} %collective-permute-done.21.refs_4_), channel_id=1, source_target_pairs={{0,2},{1,3},{2,0},{3,1},{4,6},{5,7},{6,4},{7,5},{8,10},{9,11},{10,... | collective-permute-start | bytes 393224 | tf_op jit(solution)/shard_map/ppermute | solution.py:26
  39.2 7.9 %collective-permute-start.24 = (bf16[2,256,128]{2,1,0:T(8,128)(2,1)}, bf16[2,256,128]{2,1,0:T(8,128)(2,1)}, u32[]{:S(2)}, u32[]{:S(2)}) collective-permute-start(bf16[2,256,128]{2,1,0:T(8,128)(2,1)} %collective-permute-done.20.refs_3_), channel_id=1, source_target_pairs={{0,16},{16,0},{1,17},{17,1},{2,18},{18,2},{3,19},{19,3},{4,20},{20... | collective-permute-start | bytes 393224 | tf_op jit(solution)/shard_map/ppermute | solution.py:26
  48.8 3.1 %collective-permute-start.25 = (bf16[41,128,128]{2,1,0:T(8,128)(2,1)S(1)}, bf16[41,128,128]{2,1,0:T(8,128)(2,1)S(1)}, u32[]{:S(2)}, u32[]{:S(2)}) collective-permute-start(bf16[41,128,128]{2,1,0:T(8,128)(2,1)S(1)} %shard_map.121.rest_0_), channel_id=1, source_target_pairs={{0,1},{1,0},{2,3},{3,2},{4,5},{5,4},{6,7},{7,6},{8,9},{9,8},{10,11... | collective-permute-start | bytes 4030472 | tf_op jit(solution)/shard_map/ppermute | solution.py:26
  48.8 5.5 %collective-permute-start.18 = (bf16[3,384,128]{2,1,0:T(8,128)(2,1)S(1)}, bf16[3,384,128]{2,1,0:T(8,128)(2,1)S(1)}, u32[]{:S(2)}, u32[]{:S(2)}) collective-permute-start(bf16[3,384,128]{2,1,0:T(8,128)(2,1)S(1)} %get-tuple-element.39), channel_id=1, source_target_pairs={{0,1},{1,2},{2,3},{3,4},{4,5},{5,6},{6,7},{7,8},{8,9},{9,10},{10,1... | collective-permute-start | bytes 884744 | tf_op jit(solution)/shard_map/ppermute | solution.py:31
  54.4 23.4 %copy-start = (bf16[64,3072]{1,0:T(8,128)(2,1)S(1)}, bf16[64,3072]{1,0:T(8,128)(2,1)}, u32[]{:S(2)}) copy-start(bf16[64,3072]{1,0:T(8,128)(2,1)} %embed_ref.1) | copy-start | bytes 1179652
  54.4 23.4 %copy-start.1 = (f32[3072]{0:T(1024)S(1)}, f32[3072]{0:T(1024)}, u32[]{:S(2)}) copy-start(f32[3072]{0:T(1024)} %param.22) | copy-start | bytes 36868
  54.4 23.4 %copy-start.2 = (f32[3072]{0:T(1024)S(1)}, f32[3072]{0:T(1024)}, u32[]{:S(2)}) copy-start(f32[3072]{0:T(1024)} %param.21) | copy-start | bytes 36868
  58.3 9.3 %collective-permute-start.28 = (bf16[192,128]{1,0:T(8,128)(2,1)S(1)}, bf16[192,128]{1,0:T(8,128)(2,1)S(1)}, u32[]{:S(2)}, u32[]{:S(2)}) collective-permute-start(bf16[192,128]{1,0:T(8,128)(2,1)S(1)} %shard_map.123), channel_id=1, source_target_pairs={{0,12},{1,13},{2,14},{3,15},{4,8},{5,9},{6,10},{7,11},{8,4},{9,5},... | collective-permute-start | bytes 147464 | tf_op jit(solution)/shard_map/ppermute | solution.py:26
  65.0 5.5 %collective-permute-start.27 = (bf16[192,128]{1,0:T(8,128)(2,1)S(1)}, bf16[192,128]{1,0:T(8,128)(2,1)S(1)}, u32[]{:S(2)}, u32[]{:S(2)}) collective-permute-start(bf16[192,128]{1,0:T(8,128)(2,1)S(1)} %shard_map.123), channel_id=1, source_target_pairs={{0,8},{1,9},{2,10},{3,11},{4,12},{5,13},{6,14},{7,15},{8,0},{9,1},... | collective-permute-start | bytes 147464 | tf_op jit(solution)/shard_map/ppermute | solution.py:26
  65.6 4.9 %collective-permute-start.26 = (bf16[192,128]{1,0:T(8,128)(2,1)S(1)}, bf16[192,128]{1,0:T(8,128)(2,1)S(1)}, u32[]{:S(2)}, u32[]{:S(2)}) collective-permute-start(bf16[192,128]{1,0:T(8,128)(2,1)S(1)} %shard_map.123), channel_id=1, source_target_pairs={{0,4},{1,5},{2,6},{3,7},{4,0},{5,1},{6,2},{7,3},{8,12},{9,13},{10,... | collective-permute-start | bytes 147464 | tf_op jit(solution)/shard_map/ppermute | solution.py:26
  70.6 5.7 %collective-permute-start.29 = (bf16[768,128]{1,0:T(8,128)(2,1)S(1)}, bf16[768,128]{1,0:T(8,128)(2,1)S(1)}, u32[]{:S(2)}, u32[]{:S(2)}) collective-permute-start(bf16[768,128]{1,0:T(8,128)(2,1)S(1)} %pad_maximum_fusion.rest_0_), channel_id=1, source_target_pairs={{0,2},{1,3},{2,0},{3,1},{4,6},{5,7},{6,4},{7,5},{8,10},{9,11},{10,... | collective-permute-start | bytes 589832 | tf_op jit(solution)/shard_map/ppermute | solution.py:26
  70.9 5.4 %collective-permute-start.30 = (bf16[768,128]{1,0:T(8,128)(2,1)S(1)}, bf16[768,128]{1,0:T(8,128)(2,1)S(1)}, u32[]{:S(2)}, u32[]{:S(2)}) collective-permute-start(bf16[768,128]{1,0:T(8,128)(2,1)S(1)} %pad_maximum_fusion.rest_0_), channel_id=1, source_target_pairs={{0,1},{1,0},{2,3},{3,2},{4,5},{5,4},{6,7},{7,6},{8,9},{9,8},{10,11... | collective-permute-start | bytes 589832 | tf_op jit(solution)/shard_map/ppermute | solution.py:26
  76.3 1.4 %collective-permute-start.31 = (bf16[768,128]{1,0:T(8,128)(2,1)S(1)}, bf16[768,128]{1,0:T(8,128)(2,1)S(1)}, u32[]{:S(2)}, u32[]{:S(2)}) collective-permute-start(bf16[768,128]{1,0:T(8,128)(2,1)S(1)} %collective-permute-done.29.rest_1_), channel_id=1, source_target_pairs={{0,1},{1,0},{2,3},{3,2},{4,5},{5,4},{6,7},{7,6},{8,9},{9,8},{10,11... | collective-permute-start | bytes 589832 | tf_op jit(solution)/shard_map/ppermute | solution.py:26
  (9 other events, 59.3 us)

commit v7 on v6

--- a/solution.py
+++ b/solution.py
@@ -10,7 +10,7 @@
 LANES = 128
 SUBLANES = 8
 UNIT_ROWS = 256
-SCRATCH_ROWS = 288
+SCRATCH_ROWS = 304
 NT = (((1,), (1,)), ((), ()))
 TN = (((0,), (0,)), ((), ()))
 VMEM_SPEC = pl.BlockSpec(memory_space=pltpu.VMEM)
@@ -314,7 +314,7 @@
     )
     head_in = rms_silu(block_out, gain_ref[...])
     for part, values in enumerate(split_lanes(head_in)):
-        plain[part] = values
+        plain[part, : frames * pixels] = values
     for at in (0, breadth + 1):
         windows[:, :, :, at] = jnp.zeros_like(windows[:, :, :, at])
     half = frames * pixels // 2
@@ -535,8 +535,8 @@
         out_specs=VMEM_SPEC,
         scratch_shapes=image_scratch(2, breadth, height)
         + [
-            pltpu.VMEM((2, frames * breadth * height, LANES), jnp.float32),
-            pltpu.VMEM((4, 2, frames, breadth + 2, height // 2, LANES), jnp.float32),
+            pltpu.VMEM((2, frames * breadth * height + SUBLANES, LANES), jnp.float32),
+            pltpu.VMEM((4, 2, frames, breadth + 4, height // 2, LANES), jnp.float32),
         ],
         compiler_params=LARGE,
     )(

time: 81.2 us -> 81.2 us (level)
  no operation moved by 1% of the time
where the time goes in v7:
time: 81.2 us; the launch traced here: 80.9 us
  starting transfers between devices  33.7 us (42%)
  waiting for transfers between devices  25.8 us (32%)
  Pallas kernels  19.4 us (24%)
  local copies, waits for them, and re-layouts  1.22 us (2%)
    ppermute x30, starting transfers between devices, xor_permute(): lax.ppermute(value, axis, [(source, source ^ mask) for source in range(co...  29.7 us
    ppermute x30, waiting for transfers between devices, xor_permute(): lax.ppermute(value, axis, [(source, source ^ mask) for source in range(co...  25.8 us
    pallas_call x1, Pallas kernels, body(): pl.pallas_call(functools.partial(first_kernel, taps=taps, unit_channels=u...  6.03 us
    ppermute x2, starting transfers between devices, to_next(): lax.ppermute(value, axis, [(source, source + 1) for source in range(count...  4.02 us
    pallas_call x1, Pallas kernels, body(): pl.pallas_call(functools.partial(second_kernel, taps=taps), out_shape=plt...  3.91 us
    pallas_call x1, Pallas kernels, body(): pl.pallas_call(embed_kernel, out_shape=jax.ShapeDtypeStruct((tokens, widt...  3.18 us
    pallas_call x1, Pallas kernels, body(): pl.pallas_call(functools.partial(own_kernel, taps=taps), out_shape=pltpu....  2.43 us
    pallas_call x1, Pallas kernels, unpack_units(): pl.pallas_call(functools.partial(unpack_kernel, taps=taps, unit_channels=...  1.63 us
  transfers between devices with their start and end apart: 32, of which 13 were waited for; matrix products, arithmetic and copies ran while one was open for 2% of the time, Pallas kernels for 12%

profile of v7, /device:TPU:0, one launch (start us, length us, event | category | flops | bytes accessed | tf_op | source)
XLA Modules:
  0.0 80.9 jit_solution(5419207476815728456)
XLA Ops:
  0.0 1.1 %shard_map.118 = bf16[2,256,128]{2,1,0:T(8,128)(2,1)S(1)} custom-call(s32[1]{0:T(128)} %bitcast.half_ref, bf16[12,27,192]{2,1,0:T(8,128)(2,1)} %bitcast.25, bf16[12,27,192]{2,1,0:T(8,128)(2,1)} %bitcast.26), custom_call_target="tpu_custom_call" | custom-call | tf_op jit(solution)/shard_map/pallas_call | solution.py:57
  1.1 5.1 %collective-permute-start.2 = (bf16[2,256,128]{2,1,0:T(8,128)(2,1)S(1)}, bf16[2,256,128]{2,1,0:T(8,128)(2,1)S(1)}, u32[]{:S(2)}, u32[]{:S(2)}) collective-permute-start(bf16[2,256,128]{2,1,0:T(8,128)(2,1)S(1)} %shard_map.118), channel_id=1, source_target_pairs={{0,12},{1,13},{2,14},{3,15},{4,8},{5,9},{6,10},{7,11},{8,4},{9,5},... | collective-permute-start | bytes 393224 | tf_op jit(solution)/shard_map/ppermute | solution.py:26
  6.3 0.6 collective-permute-start
  6.9 1.1 %copy.17 = bf16[2,16,24,192]{3,1,2,0:T(8,128)(2,1)S(1)} copy(bf16[2,16,24,192]{3,2,1,0:T(8,128)(2,1)} %param.12) | data formatting | bytes 589824 | tf_op args[0]
  8.0 1.3 %collective-permute-start.7 = (bf16[2,16,24,192]{3,1,2,0:T(8,128)(2,1)S(1)}, bf16[2,16,24,192]{3,1,2,0:T(8,128)(2,1)S(1)}, u32[]{:S(2)}, u32[]{:S(2)}) collective-permute-start(bf16[2,16,24,192]{3,1,2,0:T(8,128)(2,1)S(1)} %copy.17), channel_id=1, source_target_pairs={{0,1},{1,2},{2,3},{3,4},{4,5},{5,6},{6,7},{7,8},{8,9},{9,10},{10,1... | collective-permute-start | bytes 884744 | tf_op jit(solution)/shard_map/ppermute | solution.py:31
  9.4 0.1 fusion.pick_ref
  9.5 1.1 %shard_map.119.wide_ref = bf16[16,192,256]{2,1,0:T(8,128)(2,1)S(1)} custom-call(bf16[27,16,192]{2,1,0:T(8,128)(2,1)} %bitcast.24), custom_call_target="tpu_custom_call" | custom-call | tf_op jit(solution)/shard_map/pallas_call | solution.py:98
  10.6 0.0 copy-start.3
  10.7 0.0 copy-start.5
  10.7 4.0 %collective-permute-done = bf16[2,256,128]{2,1,0:T(8,128)(2,1)S(1)} collective-permute-done((bf16[2,256,128]{2,1,0:T(8,128)(2,1)S(1)}, bf16[2,256,128]{2,1,0:T(8,128)(2,1)S(1)}, u32[]{:S(2)}, u32[]{:S(2)}) %collective-permute-start) | collective-permute-done | bytes 131104 | tf_op jit(solution)/shard_map/ppermute | solution.py:26
  14.7 2.7 %collective-permute-start.8 = (bf16[2,256,128]{2,1,0:T(8,128)(2,1)S(1)}, bf16[2,256,128]{2,1,0:T(8,128)(2,1)S(1)}, u32[]{:S(2)}, u32[]{:S(2)}) collective-permute-start(bf16[2,256,128]{2,1,0:T(8,128)(2,1)S(1)} %pad_maximum_fusion.1.rest_0_), channel_id=1, source_target_pairs={{0,2},{1,3},{2,0},{3,1},{4,6},{5,7},{6,4},{7,5},{8,10},{9,11},{10,... | collective-permute-start | bytes 393224 | tf_op jit(solution)/shard_map/ppermute | solution.py:26
  17.4 1.5 %collective-permute-start.3 = (bf16[2,256,128]{2,1,0:T(8,128)(2,1)S(1)}, bf16[2,256,128]{2,1,0:T(8,128)(2,1)S(1)}, u32[]{:S(2)}, u32[]{:S(2)}) collective-permute-start(bf16[2,256,128]{2,1,0:T(8,128)(2,1)S(1)} %pad_maximum_fusion.1.rest_0_), channel_id=1, source_target_pairs={{0,16},{16,0},{1,17},{17,1},{2,18},{18,2},{3,19},{19,3},{4,20},{20... | collective-permute-start | bytes 393224 | tf_op jit(solution)/shard_map/ppermute | solution.py:26
  19.0 0.1 collective-permute-start.5
  19.1 1.4 %collective-permute-start.9 = (bf16[2,256,128]{2,1,0:T(8,128)(2,1)S(1)}, bf16[2,256,128]{2,1,0:T(8,128)(2,1)S(1)}, u32[]{:S(2)}, u32[]{:S(2)}) collective-permute-start(bf16[2,256,128]{2,1,0:T(8,128)(2,1)S(1)} %pad_maximum_fusion.3.rest_1_), channel_id=1, source_target_pairs={{0,16},{16,0},{1,17},{17,1},{2,18},{18,2},{3,19},{19,3},{4,20},{20... | collective-permute-start | bytes 393224 | tf_op jit(solution)/shard_map/ppermute | solution.py:26
  20.5 2.8 %collective-permute-done.3.rest_4_ = bf16[2,256,128]{2,1,0:T(8,128)(2,1)S(1)} collective-permute-done((bf16[2,256,128]{2,1,0:T(8,128)(2,1)S(1)}, bf16[2,256,128]{2,1,0:T(8,128)(2,1)S(1)}, u32[]{:S(2)}, u32[]{:S(2)}) %collective-permute-start.3) | collective-permute-done | bytes 131104 | tf_op jit(solution)/shard_map/ppermute | solution.py:26
  23.3 0.5 collective-permute-start.4
  23.8 0.8 collective-permute-done.5.rest_3_
  24.6 0.1 collective-permute-done.9.rest_5_
  24.7 1.5 %collective-permute-start.6 = (bf16[2,256,128]{2,1,0:T(8,128)(2,1)S(1)}, bf16[2,256,128]{2,1,0:T(8,128)(2,1)}, u32[]{:S(2)}, u32[]{:S(2)}) collective-permute-start(bf16[2,256,128]{2,1,0:T(8,128)(2,1)S(1)} %collective-permute-done.5.rest_3_), channel_id=1, source_target_pairs={{0,16},{16,0},{1,17},{17,1},{2,18},{18,2},{3,19},{19,3},{4,20},{20... | collective-permute-start | bytes 393224 | tf_op jit(solution)/shard_map/ppermute | solution.py:26
  26.2 0.1 collective-permute-start.12
  26.3 2.0 %collective-permute-done.4.rest_6_ = bf16[2,256,128]{2,1,0:T(8,128)(2,1)S(1)} collective-permute-done((bf16[2,256,128]{2,1,0:T(8,128)(2,1)S(1)}, bf16[2,256,128]{2,1,0:T(8,128)(2,1)S(1)}, u32[]{:S(2)}, u32[]{:S(2)}) %collective-permute-start.4) | collective-permute-done | bytes 131104 | tf_op jit(solution)/shard_map/ppermute | solution.py:26
  28.3 2.3 %collective-permute-done.6.rest_7_ = bf16[2,256,128]{2,1,0:T(8,128)(2,1)} collective-permute-done((bf16[2,256,128]{2,1,0:T(8,128)(2,1)S(1)}, bf16[2,256,128]{2,1,0:T(8,128)(2,1)}, u32[]{:S(2)}, u32[]{:S(2)}) %collective-permute-start.6) | collective-permute-done | bytes 131104 | tf_op jit(solution)/shard_map/ppermute | solution.py:26
  30.6 0.5 collective-permute-start.11
  31.1 0.1 collective-permute-start.16
  31.2 1.4 %collective-permute-start.21 = (bf16[2,256,128]{2,1,0:T(8,128)(2,1)S(1)}, bf16[2,256,128]{2,1,0:T(8,128)(2,1)}, u32[]{:S(2)}, u32[]{:S(2)}) collective-permute-start(bf16[2,256,128]{2,1,0:T(8,128)(2,1)S(1)} %pad_maximum_fusion.2.refs_0_), channel_id=1, source_target_pairs={{0,16},{16,0},{1,17},{17,1},{2,18},{18,2},{3,19},{19,3},{4,20},{20... | collective-permute-start | bytes 393224 | tf_op jit(solution)/shard_map/ppermute | solution.py:26
  32.7 1.8 %collective-permute-start.20 = (bf16[2,256,128]{2,1,0:T(8,128)(2,1)S(1)}, bf16[2,256,128]{2,1,0:T(8,128)(2,1)}, u32[]{:S(2)}, u32[]{:S(2)}) collective-permute-start(bf16[2,256,128]{2,1,0:T(8,128)(2,1)S(1)} %pad_maximum_fusion.4.refs_1_), channel_id=1, source_target_pairs={{0,2},{1,3},{2,0},{3,1},{4,6},{5,7},{6,4},{7,5},{8,10},{9,11},{10,... | collective-permute-start | bytes 393224 | tf_op jit(solution)/shard_map/ppermute | solution.py:26
  34.5 0.3 collective-permute-start.19
  34.8 0.6 collective-permute-start.22
  35.4 1.8 %collective-permute-done.21.refs_4_ = bf16[2,256,128]{2,1,0:T(8,128)(2,1)} collective-permute-done((bf16[2,256,128]{2,1,0:T(8,128)(2,1)S(1)}, bf16[2,256,128]{2,1,0:T(8,128)(2,1)}, u32[]{:S(2)}, u32[]{:S(2)}) %collective-permute-start.21) | collective-permute-done | bytes 131104 | tf_op jit(solution)/shard_map/ppermute | solution.py:26
  37.2 1.8 %collective-permute-start.23 = (bf16[2,256,128]{2,1,0:T(8,128)(2,1)}, bf16[2,256,128]{2,1,0:T(8,128)(2,1)}, u32[]{:S(2)}, u32[]{:S(2)}) collective-permute-start(bf16[2,256,128]{2,1,0:T(8,128)(2,1)} %collective-permute-done.21.refs_4_), channel_id=1, source_target_pairs={{0,2},{1,3},{2,0},{3,1},{4,6},{5,7},{6,4},{7,5},{8,10},{9,11},{10,... | collective-permute-start | bytes 393224 | tf_op jit(solution)/shard_map/ppermute | solution.py:26
  39.0 0.2 collective-permute-done.20.refs_3_
  39.2 1.8 %collective-permute-start.24 = (bf16[2,256,128]{2,1,0:T(8,128)(2,1)}, bf16[2,256,128]{2,1,0:T(8,128)(2,1)}, u32[]{:S(2)}, u32[]{:S(2)}) collective-permute-start(bf16[2,256,128]{2,1,0:T(8,128)(2,1)} %collective-permute-done.20.refs_3_), channel_id=1, source_target_pairs={{0,16},{16,0},{1,17},{17,1},{2,18},{18,2},{3,19},{19,3},{4,20},{20... | collective-permute-start | bytes 393224 | tf_op jit(solution)/shard_map/ppermute | solution.py:26
  41.0 6.0 %shard_map.120 = (bf16[2,24,16,192]{3,2,1,0:T(8,128)(2,1)S(1)}, bf16[3,384,128]{2,1,0:T(8,128)(2,1)S(1)}) custom-call(s32[32]{0:T(128)S(1)} %copy-done.3, s32[1]{0:T(128)} %bitcast.10.first_ref, bf16[2,24,16,192]{3,2,1,0:T(8,128)(2,1)S(1)} %bitcast.16, bf16[2,24,16,192]{3,2,1,0:T(8,128)(2,1)} %bitcast.23, f32[1,192]{1,0:T(1,128)S(1)} %bitcast.20, ...), custom_call_target="tpu_custom_call" | custom-call | tf_op jit(solution)/shard_map/pallas_call | solution.py:498
  47.1 1.6 %shard_map.121.rest_0_ = bf16[41,128,128]{2,1,0:T(8,128)(2,1)S(1)} custom-call(bf16[2,256,128]{2,1,0:T(8,128)(2,1)} %copy-done.9, bf16[2,256,128]{2,1,0:T(8,128)(2,1)} %copy-done.10, bf16[2,256,128]{2,1,0:T(8,128)(2,1)} %collective-permute-done.19.refs_2_, bf16[2,256,128]{2,1,0:T(8,128)(2,1)} %collective-permute-done.20.refs_3_, ...), custom_call_target="tpu_custom_call" | custom-call | tf_op jit(solution)/shard_map/pallas_call | solution.py:178
  48.8 0.1 collective-permute-start.25
  48.8 2.7 %collective-permute-start.18 = (bf16[3,384,128]{2,1,0:T(8,128)(2,1)S(1)}, bf16[3,384,128]{2,1,0:T(8,128)(2,1)S(1)}, u32[]{:S(2)}, u32[]{:S(2)}) collective-permute-start(bf16[3,384,128]{2,1,0:T(8,128)(2,1)S(1)} %get-tuple-element.39), channel_id=1, source_target_pairs={{0,1},{1,2},{2,3},{3,4},{4,5},{5,6},{6,7},{7,8},{8,9},{9,10},{10,1... | collective-permute-start | bytes 884744 | tf_op jit(solution)/shard_map/ppermute | solution.py:31
  51.6 0.3 collective-permute-done.25.rest_1_
  51.9 2.4 %shard_map.122.summed_ref = f32[768,256]{1,0:T(8,128)S(1)} custom-call(s32[32]{0:T(128)S(1)} %copy-done.3, s32[1]{0:T(128)} %bitcast.10.first_ref, bf16[2,24,16,192]{3,2,1,0:T(8,128)(2,1)S(1)} %get-tuple-element.44.own_ref, bf16[2,24,16,192]{3,2,1,0:T(8,128)(2,1)S(1)} %bitcast.17, bf16[256,192]{1,0:T(8,128)(2,1)S(1)} %fusion.pick_ref, ...), custom_call_target="tpu_custom_call" | custom-call | tf_op jit(solution)/shard_map/pallas_call | solution.py:520
  54.4 3.9 %shard_map.123 = bf16[192,128]{1,0:T(8,128)(2,1)S(1)} custom-call(s32[32]{0:T(128)S(1)} %copy-done.3, s32[1]{0:T(128)} %bitcast.10.first_ref, bf16[3,384,128]{2,1,0:T(8,128)(2,1)S(1)} %collective-permute-done.18.rim_ref, f32[1,192]{1,0:T(1,128)S(1)} %bitcast.22, bf16[256,192]{1,0:T(8,128)(2,1)S(1)} %fusion.pick_ref, ...), custom_call_target="tpu_custom_call" | custom-call | tf_op jit(solution)/shard_map/pallas_call | solution.py:531
  58.3 6.7 %collective-permute-start.28 = (bf16[192,128]{1,0:T(8,128)(2,1)S(1)}, bf16[192,128]{1,0:T(8,128)(2,1)S(1)}, u32[]{:S(2)}, u32[]{:S(2)}) collective-permute-start(bf16[192,128]{1,0:T(8,128)(2,1)S(1)} %shard_map.123), channel_id=1, source_target_pairs={{0,12},{1,13},{2,14},{3,15},{4,8},{5,9},{6,10},{7,11},{8,4},{9,5},... | collective-permute-start | bytes 147464 | tf_op jit(solution)/shard_map/ppermute | solution.py:26
  65.0 0.6 collective-permute-start.27
  65.6 0.1 collective-permute-start.26
  65.8 1.9 %collective-permute-done.28 = bf16[192,128]{1,0:T(8,128)(2,1)S(1)} collective-permute-done((bf16[192,128]{1,0:T(8,128)(2,1)S(1)}, bf16[192,128]{1,0:T(8,128)(2,1)S(1)}, u32[]{:S(2)}, u32[]{:S(2)}) %collective-permute-start.28) | collective-permute-done | bytes 49184 | tf_op jit(solution)/shard_map/ppermute | solution.py:26
  67.7 2.9 %collective-permute-done.27 = bf16[192,128]{1,0:T(8,128)(2,1)S(1)} collective-permute-done((bf16[192,128]{1,0:T(8,128)(2,1)S(1)}, bf16[192,128]{1,0:T(8,128)(2,1)S(1)}, u32[]{:S(2)}, u32[]{:S(2)}) %collective-permute-start.27) | collective-permute-done | bytes 49184 | tf_op jit(solution)/shard_map/ppermute | solution.py:26
  70.6 0.3 collective-permute-start.29
  70.9 5.4 %collective-permute-done.29.rest_1_ = bf16[768,128]{1,0:T(8,128)(2,1)S(1)} collective-permute-done((bf16[768,128]{1,0:T(8,128)(2,1)S(1)}, bf16[768,128]{1,0:T(8,128)(2,1)S(1)}, u32[]{:S(2)}, u32[]{:S(2)}) %collective-permute-start.29) | collective-permute-done | bytes 196640 | tf_op jit(solution)/shard_map/ppermute | solution.py:26
  76.3 1.4 %collective-permute-done.31.rest_3_ = bf16[768,128]{1,0:T(8,128)(2,1)S(1)} collective-permute-done((bf16[768,128]{1,0:T(8,128)(2,1)S(1)}, bf16[768,128]{1,0:T(8,128)(2,1)S(1)}, u32[]{:S(2)}, u32[]{:S(2)}) %collective-permute-start.31) | collective-permute-done | bytes 196640 | tf_op jit(solution)/shard_map/ppermute | solution.py:26
  77.8 3.2 %shard_map.124 = bf16[192,3072]{1,0:T(8,128)(2,1)} custom-call(s32[3,192]{1,0:T(4,128)S(1)} %pad_add_fusion.place_ref, bf16[64,3072]{1,0:T(8,128)(2,1)S(1)} %copy-done, f32[1,3072]{1,0:T(1,128)S(1)} %bitcast.18, f32[1,3072]{1,0:T(1,128)S(1)} %bitcast.19, bf16[768,128]{1,0:T(8,128)(2,1)S(1)} %pad_maximum_fusion.rest_0_, ...), custom_call_target="tpu_custom_call" | custom-call | tf_op jit(solution)/shard_map/pallas_call | solution.py:553
  (88 shorter events, 0.4 us)
Async XLA Ops:
  1.1 17.8 %collective-permute-start.2 = (bf16[2,256,128]{2,1,0:T(8,128)(2,1)S(1)}, bf16[2,256,128]{2,1,0:T(8,128)(2,1)S(1)}, u32[]{:S(2)}, u32[]{:S(2)}) collective-permute-start(bf16[2,256,128]{2,1,0:T(8,128)(2,1)S(1)} %shard_map.118), channel_id=1, source_target_pairs={{0,12},{1,13},{2,14},{3,15},{4,8},{5,9},{6,10},{7,11},{8,4},{9,5},... | collective-permute-start | bytes 393224 | tf_op jit(solution)/shard_map/ppermute | solution.py:26
  6.3 12.7 %collective-permute-start.1 = (bf16[2,256,128]{2,1,0:T(8,128)(2,1)S(1)}, bf16[2,256,128]{2,1,0:T(8,128)(2,1)S(1)}, u32[]{:S(2)}, u32[]{:S(2)}) collective-permute-start(bf16[2,256,128]{2,1,0:T(8,128)(2,1)S(1)} %shard_map.118), channel_id=1, source_target_pairs={{0,8},{1,9},{2,10},{3,11},{4,12},{5,13},{6,14},{7,15},{8,0},{9,1},... | collective-permute-start | bytes 393224 | tf_op jit(solution)/shard_map/ppermute | solution.py:26
  6.3 8.4 %collective-permute-start = (bf16[2,256,128]{2,1,0:T(8,128)(2,1)S(1)}, bf16[2,256,128]{2,1,0:T(8,128)(2,1)S(1)}, u32[]{:S(2)}, u32[]{:S(2)}) collective-permute-start(bf16[2,256,128]{2,1,0:T(8,128)(2,1)S(1)} %shard_map.118), channel_id=1, source_target_pairs={{0,4},{1,5},{2,6},{3,7},{4,0},{5,1},{6,2},{7,3},{8,12},{9,13},{10,... | collective-permute-start | bytes 393224 | tf_op jit(solution)/shard_map/ppermute | solution.py:26
  8.0 18.2 %collective-permute-start.7 = (bf16[2,16,24,192]{3,1,2,0:T(8,128)(2,1)S(1)}, bf16[2,16,24,192]{3,1,2,0:T(8,128)(2,1)S(1)}, u32[]{:S(2)}, u32[]{:S(2)}) collective-permute-start(bf16[2,16,24,192]{3,1,2,0:T(8,128)(2,1)S(1)} %copy.17), channel_id=1, source_target_pairs={{0,1},{1,2},{2,3},{3,4},{4,5},{5,6},{6,7},{7,8},{8,9},{9,10},{10,1... | collective-permute-start | bytes 884744 | tf_op jit(solution)/shard_map/ppermute | solution.py:31
  10.6 30.3 %copy-start.3 = (s32[32]{0:T(128)S(1)}, s32[32]{0:T(128)}, u32[]{:S(2)}) copy-start(s32[32]{0:T(128)} %clips_ref.5) | copy-start | bytes 388
  10.7 30.3 %copy-start.4 = (f32[192]{0:T(256)S(1)}, f32[192]{0:T(256)}, u32[]{:S(2)}) copy-start(f32[192]{0:T(256)} %param.14) | copy-start | bytes 2308
  10.7 30.3 %copy-start.5 = (f32[192]{0:T(256)S(1)}, f32[192]{0:T(256)}, u32[]{:S(2)}) copy-start(f32[192]{0:T(256)} %param.16) | copy-start | bytes 2308
  14.7 26.2 %copy-start.7 = (bf16[2,256,128]{2,1,0:T(8,128)(2,1)}, bf16[2,256,128]{2,1,0:T(8,128)(2,1)S(1)}, u32[]{:S(2)}) copy-start(bf16[2,256,128]{2,1,0:T(8,128)(2,1)S(1)} %pad_maximum_fusion.1.rest_0_) | copy-start | bytes 393220
  14.7 9.0 %collective-permute-start.8 = (bf16[2,256,128]{2,1,0:T(8,128)(2,1)S(1)}, bf16[2,256,128]{2,1,0:T(8,128)(2,1)S(1)}, u32[]{:S(2)}, u32[]{:S(2)}) collective-permute-start(bf16[2,256,128]{2,1,0:T(8,128)(2,1)S(1)} %pad_maximum_fusion.1.rest_0_), channel_id=1, source_target_pairs={{0,2},{1,3},{2,0},{3,1},{4,6},{5,7},{6,4},{7,5},{8,10},{9,11},{10,... | collective-permute-start | bytes 393224 | tf_op jit(solution)/shard_map/ppermute | solution.py:26
  17.4 5.8 %collective-permute-start.3 = (bf16[2,256,128]{2,1,0:T(8,128)(2,1)S(1)}, bf16[2,256,128]{2,1,0:T(8,128)(2,1)S(1)}, u32[]{:S(2)}, u32[]{:S(2)}) collective-permute-start(bf16[2,256,128]{2,1,0:T(8,128)(2,1)S(1)} %pad_maximum_fusion.1.rest_0_), channel_id=1, source_target_pairs={{0,16},{16,0},{1,17},{17,1},{2,18},{18,2},{3,19},{19,3},{4,20},{20... | collective-permute-start | bytes 393224 | tf_op jit(solution)/shard_map/ppermute | solution.py:26
  19.0 22.0 %copy-start.8 = (bf16[2,256,128]{2,1,0:T(8,128)(2,1)}, bf16[2,256,128]{2,1,0:T(8,128)(2,1)S(1)}, u32[]{:S(2)}) copy-start(bf16[2,256,128]{2,1,0:T(8,128)(2,1)S(1)} %pad_maximum_fusion.3.rest_1_) | copy-start | bytes 393220
  19.0 5.6 %collective-permute-start.5 = (bf16[2,256,128]{2,1,0:T(8,128)(2,1)S(1)}, bf16[2,256,128]{2,1,0:T(8,128)(2,1)S(1)}, u32[]{:S(2)}, u32[]{:S(2)}) collective-permute-start(bf16[2,256,128]{2,1,0:T(8,128)(2,1)S(1)} %pad_maximum_fusion.3.rest_1_), channel_id=1, source_target_pairs={{0,2},{1,3},{2,0},{3,1},{4,6},{5,7},{6,4},{7,5},{8,10},{9,11},{10,... | collective-permute-start | bytes 393224 | tf_op jit(solution)/shard_map/ppermute | solution.py:26
  19.1 5.5 %collective-permute-start.9 = (bf16[2,256,128]{2,1,0:T(8,128)(2,1)S(1)}, bf16[2,256,128]{2,1,0:T(8,128)(2,1)S(1)}, u32[]{:S(2)}, u32[]{:S(2)}) collective-permute-start(bf16[2,256,128]{2,1,0:T(8,128)(2,1)S(1)} %pad_maximum_fusion.3.rest_1_), channel_id=1, source_target_pairs={{0,16},{16,0},{1,17},{17,1},{2,18},{18,2},{3,19},{19,3},{4,20},{20... | collective-permute-start | bytes 393224 | tf_op jit(solution)/shard_map/ppermute | solution.py:26
  23.3 17.7 %copy-start.13 = (bf16[2,256,128]{2,1,0:T(8,128)(2,1)}, bf16[2,256,128]{2,1,0:T(8,128)(2,1)S(1)}, u32[]{:S(2)}) copy-start(bf16[2,256,128]{2,1,0:T(8,128)(2,1)S(1)} %collective-permute-done.3.rest_4_) | copy-start | bytes 393220
  23.3 5.0 %collective-permute-start.4 = (bf16[2,256,128]{2,1,0:T(8,128)(2,1)S(1)}, bf16[2,256,128]{2,1,0:T(8,128)(2,1)S(1)}, u32[]{:S(2)}, u32[]{:S(2)}) collective-permute-start(bf16[2,256,128]{2,1,0:T(8,128)(2,1)S(1)} %collective-permute-done.3.rest_4_), channel_id=1, source_target_pairs={{0,2},{1,3},{2,0},{3,1},{4,6},{5,7},{6,4},{7,5},{8,10},{9,11},{10,... | collective-permute-start | bytes 393224 | tf_op jit(solution)/shard_map/ppermute | solution.py:26
  23.8 17.2 %copy-start.12 = (bf16[2,256,128]{2,1,0:T(8,128)(2,1)}, bf16[2,256,128]{2,1,0:T(8,128)(2,1)S(1)}, u32[]{:S(2)}) copy-start(bf16[2,256,128]{2,1,0:T(8,128)(2,1)S(1)} %collective-permute-done.8.rest_2_) | copy-start | bytes 393220
  23.8 7.4 %collective-permute-start.14 = (bf16[2,256,128]{2,1,0:T(8,128)(2,1)S(1)}, bf16[2,256,128]{2,1,0:T(8,128)(2,1)S(1)}, u32[]{:S(2)}, u32[]{:S(2)}) collective-permute-start(bf16[2,256,128]{2,1,0:T(8,128)(2,1)S(1)} %collective-permute-done.3.rest_4_), channel_id=1, source_target_pairs={{0,1},{1,0},{2,3},{3,2},{4,5},{5,4},{6,7},{7,6},{8,9},{9,8},{10,11... | collective-permute-start | bytes 393224 | tf_op jit(solution)/shard_map/ppermute | solution.py:26
  24.6 16.4 %copy-start.14 = (bf16[2,256,128]{2,1,0:T(8,128)(2,1)}, bf16[2,256,128]{2,1,0:T(8,128)(2,1)S(1)}, u32[]{:S(2)}) copy-start(bf16[2,256,128]{2,1,0:T(8,128)(2,1)S(1)} %collective-permute-done.5.rest_3_) | copy-start | bytes 393220
  24.6 8.1 %collective-permute-start.13 = (bf16[2,256,128]{2,1,0:T(8,128)(2,1)S(1)}, bf16[2,256,128]{2,1,0:T(8,128)(2,1)S(1)}, u32[]{:S(2)}, u32[]{:S(2)}) collective-permute-start(bf16[2,256,128]{2,1,0:T(8,128)(2,1)S(1)} %collective-permute-done.5.rest_3_), channel_id=1, source_target_pairs={{0,1},{1,0},{2,3},{3,2},{4,5},{5,4},{6,7},{7,6},{8,9},{9,8},{10,11... | collective-permute-start | bytes 393224 | tf_op jit(solution)/shard_map/ppermute | solution.py:26
  24.7 16.3 %copy-start.15 = (bf16[2,256,128]{2,1,0:T(8,128)(2,1)}, bf16[2,256,128]{2,1,0:T(8,128)(2,1)S(1)}, u32[]{:S(2)}) copy-start(bf16[2,256,128]{2,1,0:T(8,128)(2,1)S(1)} %collective-permute-done.9.rest_5_) | copy-start | bytes 393220
  24.7 6.0 %collective-permute-start.6 = (bf16[2,256,128]{2,1,0:T(8,128)(2,1)S(1)}, bf16[2,256,128]{2,1,0:T(8,128)(2,1)}, u32[]{:S(2)}, u32[]{:S(2)}) collective-permute-start(bf16[2,256,128]{2,1,0:T(8,128)(2,1)S(1)} %collective-permute-done.5.rest_3_), channel_id=1, source_target_pairs={{0,16},{16,0},{1,17},{17,1},{2,18},{18,2},{3,19},{19,3},{4,20},{20... | collective-permute-start | bytes 393224 | tf_op jit(solution)/shard_map/ppermute | solution.py:26
  26.2 14.8 %copy-start.11 = (bf16[2,16,24,192]{3,1,2,0:T(8,128)(2,1)}, bf16[2,16,24,192]{3,1,2,0:T(8,128)(2,1)S(1)}, u32[]{:S(2)}) copy-start(bf16[2,16,24,192]{3,1,2,0:T(8,128)(2,1)S(1)} %collective-permute-done.7) | copy-start | bytes 884740
  26.2 4.4 %collective-permute-start.12 = (bf16[2,256,128]{2,1,0:T(8,128)(2,1)S(1)}, bf16[2,256,128]{2,1,0:T(8,128)(2,1)S(1)}, u32[]{:S(2)}, u32[]{:S(2)}) collective-permute-start(bf16[2,256,128]{2,1,0:T(8,128)(2,1)S(1)} %collective-permute-done.8.rest_2_), channel_id=1, source_target_pairs={{0,1},{1,0},{2,3},{3,2},{4,5},{5,4},{6,7},{7,6},{8,9},{9,8},{10,11... | collective-permute-start | bytes 393224 | tf_op jit(solution)/shard_map/ppermute | solution.py:26
  28.2 10.9 %copy-start.16 = (bf16[2,256,128]{2,1,0:T(8,128)(2,1)}, bf16[2,256,128]{2,1,0:T(8,128)(2,1)S(1)}, u32[]{:S(2)}) copy-start(bf16[2,256,128]{2,1,0:T(8,128)(2,1)S(1)} %collective-permute-done.4.rest_6_) | copy-start | bytes 393220
  28.2 3.0 %collective-permute-start.15 = (bf16[2,256,128]{2,1,0:T(8,128)(2,1)S(1)}, bf16[2,256,128]{2,1,0:T(8,128)(2,1)S(1)}, u32[]{:S(2)}, u32[]{:S(2)}) collective-permute-start(bf16[2,256,128]{2,1,0:T(8,128)(2,1)S(1)} %collective-permute-done.9.rest_5_), channel_id=1, source_target_pairs={{0,1},{1,0},{2,3},{3,2},{4,5},{5,4},{6,7},{7,6},{8,9},{9,8},{10,11... | collective-permute-start | bytes 393224 | tf_op jit(solution)/shard_map/ppermute | solution.py:26
  28.3 18.8 %copy-start.9 = (bf16[2,256,128]{2,1,0:T(8,128)(2,1)}, bf16[2,256,128]{2,1,0:T(8,128)(2,1)S(1)}, u32[]{:S(2)}) copy-start(bf16[2,256,128]{2,1,0:T(8,128)(2,1)S(1)} %pad_maximum_fusion.2.refs_0_) | copy-start | bytes 393220
  28.3 18.8 %copy-start.10 = (bf16[2,256,128]{2,1,0:T(8,128)(2,1)}, bf16[2,256,128]{2,1,0:T(8,128)(2,1)S(1)}, u32[]{:S(2)}) copy-start(bf16[2,256,128]{2,1,0:T(8,128)(2,1)S(1)} %pad_maximum_fusion.4.refs_1_) | copy-start | bytes 393220
  30.6 3.9 %collective-permute-start.10 = (bf16[2,256,128]{2,1,0:T(8,128)(2,1)S(1)}, bf16[2,256,128]{2,1,0:T(8,128)(2,1)S(1)}, u32[]{:S(2)}, u32[]{:S(2)}) collective-permute-start(bf16[2,256,128]{2,1,0:T(8,128)(2,1)S(1)} %pad_maximum_fusion.1.rest_0_), channel_id=1, source_target_pairs={{0,1},{1,0},{2,3},{3,2},{4,5},{5,4},{6,7},{7,6},{8,9},{9,8},{10,11... | collective-permute-start | bytes 393224 | tf_op jit(solution)/shard_map/ppermute | solution.py:26
  30.6 3.9 %collective-permute-start.11 = (bf16[2,256,128]{2,1,0:T(8,128)(2,1)S(1)}, bf16[2,256,128]{2,1,0:T(8,128)(2,1)S(1)}, u32[]{:S(2)}, u32[]{:S(2)}) collective-permute-start(bf16[2,256,128]{2,1,0:T(8,128)(2,1)S(1)} %pad_maximum_fusion.3.rest_1_), channel_id=1, source_target_pairs={{0,1},{1,0},{2,3},{3,2},{4,5},{5,4},{6,7},{7,6},{8,9},{9,8},{10,11... | collective-permute-start | bytes 393224 | tf_op jit(solution)/shard_map/ppermute | solution.py:26
  31.1 3.7 %collective-permute-start.16 = (bf16[2,256,128]{2,1,0:T(8,128)(2,1)S(1)}, bf16[2,256,128]{2,1,0:T(8,128)(2,1)S(1)}, u32[]{:S(2)}, u32[]{:S(2)}) collective-permute-start(bf16[2,256,128]{2,1,0:T(8,128)(2,1)S(1)} %collective-permute-done.4.rest_6_), channel_id=1, source_target_pairs={{0,1},{1,0},{2,3},{3,2},{4,5},{5,4},{6,7},{7,6},{8,9},{9,8},{10,11... | collective-permute-start | bytes 393224 | tf_op jit(solution)/shard_map/ppermute | solution.py:26
  31.2 5.9 %collective-permute-start.21 = (bf16[2,256,128]{2,1,0:T(8,128)(2,1)S(1)}, bf16[2,256,128]{2,1,0:T(8,128)(2,1)}, u32[]{:S(2)}, u32[]{:S(2)}) collective-permute-start(bf16[2,256,128]{2,1,0:T(8,128)(2,1)S(1)} %pad_maximum_fusion.2.refs_0_), channel_id=1, source_target_pairs={{0,16},{16,0},{1,17},{17,1},{2,18},{18,2},{3,19},{19,3},{4,20},{20... | collective-permute-start | bytes 393224 | tf_op jit(solution)/shard_map/ppermute | solution.py:26
  32.7 6.4 %collective-permute-start.20 = (bf16[2,256,128]{2,1,0:T(8,128)(2,1)S(1)}, bf16[2,256,128]{2,1,0:T(8,128)(2,1)}, u32[]{:S(2)}, u32[]{:S(2)}) collective-permute-start(bf16[2,256,128]{2,1,0:T(8,128)(2,1)S(1)} %pad_maximum_fusion.4.refs_1_), channel_id=1, source_target_pairs={{0,2},{1,3},{2,0},{3,1},{4,6},{5,7},{6,4},{7,5},{8,10},{9,11},{10,... | collective-permute-start | bytes 393224 | tf_op jit(solution)/shard_map/ppermute | solution.py:26
  34.5 6.4 %collective-permute-start.17 = (bf16[2,256,128]{2,1,0:T(8,128)(2,1)}, bf16[2,256,128]{2,1,0:T(8,128)(2,1)}, u32[]{:S(2)}, u32[]{:S(2)}) collective-permute-start(bf16[2,256,128]{2,1,0:T(8,128)(2,1)} %collective-permute-done.6.rest_7_), channel_id=1, source_target_pairs={{0,1},{1,0},{2,3},{3,2},{4,5},{5,4},{6,7},{7,6},{8,9},{9,8},{10,11... | collective-permute-start | bytes 393224 | tf_op jit(solution)/shard_map/ppermute | solution.py:26
  34.5 12.5 %collective-permute-start.19 = (bf16[2,256,128]{2,1,0:T(8,128)(2,1)S(1)}, bf16[2,256,128]{2,1,0:T(8,128)(2,1)}, u32[]{:S(2)}, u32[]{:S(2)}) collective-permute-start(bf16[2,256,128]{2,1,0:T(8,128)(2,1)S(1)} %pad_maximum_fusion.2.refs_0_), channel_id=1, source_target_pairs={{0,2},{1,3},{2,0},{3,1},{4,6},{5,7},{6,4},{7,5},{8,10},{9,11},{10,... | collective-permute-start | bytes 393224 | tf_op jit(solution)/shard_map/ppermute | solution.py:26
  34.8 12.3 %collective-permute-start.22 = (bf16[2,256,128]{2,1,0:T(8,128)(2,1)S(1)}, bf16[2,256,128]{2,1,0:T(8,128)(2,1)}, u32[]{:S(2)}, u32[]{:S(2)}) collective-permute-start(bf16[2,256,128]{2,1,0:T(8,128)(2,1)S(1)} %pad_maximum_fusion.4.refs_1_), channel_id=1, source_target_pairs={{0,16},{16,0},{1,17},{17,1},{2,18},{18,2},{3,19},{19,3},{4,20},{20... | collective-permute-start | bytes 393224 | tf_op jit(solution)/shard_map/ppermute | solution.py:26
  37.2 9.9 %collective-permute-start.23 = (bf16[2,256,128]{2,1,0:T(8,128)(2,1)}, bf16[2,256,128]{2,1,0:T(8,128)(2,1)}, u32[]{:S(2)}, u32[]{:S(2)}) collective-permute-start(bf16[2,256,128]{2,1,0:T(8,128)(2,1)} %collective-permute-done.21.refs_4_), channel_id=1, source_target_pairs={{0,2},{1,3},{2,0},{3,1},{4,6},{5,7},{6,4},{7,5},{8,10},{9,11},{10,... | collective-permute-start | bytes 393224 | tf_op jit(solution)/shard_map/ppermute | solution.py:26
  39.2 7.9 %collective-permute-start.24 = (bf16[2,256,128]{2,1,0:T(8,128)(2,1)}, bf16[2,256,128]{2,1,0:T(8,128)(2,1)}, u32[]{:S(2)}, u32[]{:S(2)}) collective-permute-start(bf16[2,256,128]{2,1,0:T(8,128)(2,1)} %collective-permute-done.20.refs_3_), channel_id=1, source_target_pairs={{0,16},{16,0},{1,17},{17,1},{2,18},{18,2},{3,19},{19,3},{4,20},{20... | collective-permute-start | bytes 393224 | tf_op jit(solution)/shard_map/ppermute | solution.py:26
  48.8 3.1 %collective-permute-start.25 = (bf16[41,128,128]{2,1,0:T(8,128)(2,1)S(1)}, bf16[41,128,128]{2,1,0:T(8,128)(2,1)S(1)}, u32[]{:S(2)}, u32[]{:S(2)}) collective-permute-start(bf16[41,128,128]{2,1,0:T(8,128)(2,1)S(1)} %shard_map.121.rest_0_), channel_id=1, source_target_pairs={{0,1},{1,0},{2,3},{3,2},{4,5},{5,4},{6,7},{7,6},{8,9},{9,8},{10,11... | collective-permute-start | bytes 4030472 | tf_op jit(solution)/shard_map/ppermute | solution.py:26
  48.8 5.5 %collective-permute-start.18 = (bf16[3,384,128]{2,1,0:T(8,128)(2,1)S(1)}, bf16[3,384,128]{2,1,0:T(8,128)(2,1)S(1)}, u32[]{:S(2)}, u32[]{:S(2)}) collective-permute-start(bf16[3,384,128]{2,1,0:T(8,128)(2,1)S(1)} %get-tuple-element.39), channel_id=1, source_target_pairs={{0,1},{1,2},{2,3},{3,4},{4,5},{5,6},{6,7},{7,8},{8,9},{9,10},{10,1... | collective-permute-start | bytes 884744 | tf_op jit(solution)/shard_map/ppermute | solution.py:31
  54.4 23.4 %copy-start = (bf16[64,3072]{1,0:T(8,128)(2,1)S(1)}, bf16[64,3072]{1,0:T(8,128)(2,1)}, u32[]{:S(2)}) copy-start(bf16[64,3072]{1,0:T(8,128)(2,1)} %embed_ref.1) | copy-start | bytes 1179652
  54.4 23.4 %copy-start.1 = (f32[3072]{0:T(1024)S(1)}, f32[3072]{0:T(1024)}, u32[]{:S(2)}) copy-start(f32[3072]{0:T(1024)} %param.22) | copy-start | bytes 36868
  54.4 23.4 %copy-start.2 = (f32[3072]{0:T(1024)S(1)}, f32[3072]{0:T(1024)}, u32[]{:S(2)}) copy-start(f32[3072]{0:T(1024)} %param.21) | copy-start | bytes 36868
  58.3 9.4 %collective-permute-start.28 = (bf16[192,128]{1,0:T(8,128)(2,1)S(1)}, bf16[192,128]{1,0:T(8,128)(2,1)S(1)}, u32[]{:S(2)}, u32[]{:S(2)}) collective-permute-start(bf16[192,128]{1,0:T(8,128)(2,1)S(1)} %shard_map.123), channel_id=1, source_target_pairs={{0,12},{1,13},{2,14},{3,15},{4,8},{5,9},{6,10},{7,11},{8,4},{9,5},... | collective-permute-start | bytes 147464 | tf_op jit(solution)/shard_map/ppermute | solution.py:26
  65.0 5.5 %collective-permute-start.27 = (bf16[192,128]{1,0:T(8,128)(2,1)S(1)}, bf16[192,128]{1,0:T(8,128)(2,1)S(1)}, u32[]{:S(2)}, u32[]{:S(2)}) collective-permute-start(bf16[192,128]{1,0:T(8,128)(2,1)S(1)} %shard_map.123), channel_id=1, source_target_pairs={{0,8},{1,9},{2,10},{3,11},{4,12},{5,13},{6,14},{7,15},{8,0},{9,1},... | collective-permute-start | bytes 147464 | tf_op jit(solution)/shard_map/ppermute | solution.py:26
  65.6 4.9 %collective-permute-start.26 = (bf16[192,128]{1,0:T(8,128)(2,1)S(1)}, bf16[192,128]{1,0:T(8,128)(2,1)S(1)}, u32[]{:S(2)}, u32[]{:S(2)}) collective-permute-start(bf16[192,128]{1,0:T(8,128)(2,1)S(1)} %shard_map.123), channel_id=1, source_target_pairs={{0,4},{1,5},{2,6},{3,7},{4,0},{5,1},{6,2},{7,3},{8,12},{9,13},{10,... | collective-permute-start | bytes 147464 | tf_op jit(solution)/shard_map/ppermute | solution.py:26
  70.6 5.7 %collective-permute-start.29 = (bf16[768,128]{1,0:T(8,128)(2,1)S(1)}, bf16[768,128]{1,0:T(8,128)(2,1)S(1)}, u32[]{:S(2)}, u32[]{:S(2)}) collective-permute-start(bf16[768,128]{1,0:T(8,128)(2,1)S(1)} %pad_maximum_fusion.rest_0_), channel_id=1, source_target_pairs={{0,2},{1,3},{2,0},{3,1},{4,6},{5,7},{6,4},{7,5},{8,10},{9,11},{10,... | collective-permute-start | bytes 589832 | tf_op jit(solution)/shard_map/ppermute | solution.py:26
  70.9 5.4 %collective-permute-start.30 = (bf16[768,128]{1,0:T(8,128)(2,1)S(1)}, bf16[768,128]{1,0:T(8,128)(2,1)S(1)}, u32[]{:S(2)}, u32[]{:S(2)}) collective-permute-start(bf16[768,128]{1,0:T(8,128)(2,1)S(1)} %pad_maximum_fusion.rest_0_), channel_id=1, source_target_pairs={{0,1},{1,0},{2,3},{3,2},{4,5},{5,4},{6,7},{7,6},{8,9},{9,8},{10,11... | collective-permute-start | bytes 589832 | tf_op jit(solution)/shard_map/ppermute | solution.py:26
  76.3 1.4 %collective-permute-start.31 = (bf16[768,128]{1,0:T(8,128)(2,1)S(1)}, bf16[768,128]{1,0:T(8,128)(2,1)S(1)}, u32[]{:S(2)}, u32[]{:S(2)}) collective-permute-start(bf16[768,128]{1,0:T(8,128)(2,1)S(1)} %collective-permute-done.29.rest_1_), channel_id=1, source_target_pairs={{0,1},{1,0},{2,3},{3,2},{4,5},{5,4},{6,7},{7,6},{8,9},{9,8},{10,11... | collective-permute-start | bytes 589832 | tf_op jit(solution)/shard_map/ppermute | solution.py:26
  (9 other events, 59.3 us)

commit v8 on v7

--- a/solution.py
+++ b/solution.py
@@ -398,7 +398,7 @@
 
 
 def along_line(unit):
-    return [unit] + [xor_permute(unit, "ctx", 4 * step) for step in (1, 2, 3)]
+    return [unit] + [xor_permute(unit, "ctx", 4 * step) for step in (3, 2, 1)][::-1]
 
 
 def round_square(half_line):

time: 81.2 us -> 81.2 us (level)
  no operation moved by 1% of the time
where the time goes in v8:
time: 81.2 us; the launch traced here: 80.9 us
  starting transfers between devices  33.7 us (42%)
  waiting for transfers between devices  25.8 us (32%)
  Pallas kernels  19.4 us (24%)
  local copies, waits for them, and re-layouts  1.22 us (2%)
    ppermute x30, starting transfers between devices, xor_permute(): lax.ppermute(value, axis, [(source, source ^ mask) for source in range(co...  29.7 us
    ppermute x30, waiting for transfers between devices, xor_permute(): lax.ppermute(value, axis, [(source, source ^ mask) for source in range(co...  25.8 us
    pallas_call x1, Pallas kernels, body(): pl.pallas_call(functools.partial(first_kernel, taps=taps, unit_channels=u...  6.03 us
    ppermute x2, starting transfers between devices, to_next(): lax.ppermute(value, axis, [(source, source + 1) for source in range(count...  4.02 us
    pallas_call x1, Pallas kernels, body(): pl.pallas_call(functools.partial(second_kernel, taps=taps), out_shape=plt...  3.91 us
    pallas_call x1, Pallas kernels, body(): pl.pallas_call(embed_kernel, out_shape=jax.ShapeDtypeStruct((tokens, widt...  3.18 us
    pallas_call x1, Pallas kernels, body(): pl.pallas_call(functools.partial(own_kernel, taps=taps), out_shape=pltpu....  2.43 us
    pallas_call x1, Pallas kernels, unpack_units(): pl.pallas_call(functools.partial(unpack_kernel, taps=taps, unit_channels=...  1.63 us
  transfers between devices with their start and end apart: 32, of which 13 were waited for; matrix products, arithmetic and copies ran while one was open for 2% of the time, Pallas kernels for 12%

profile of v8, /device:TPU:0, one launch (start us, length us, event | category | flops | bytes accessed | tf_op | source)
XLA Modules:
  0.0 80.9 jit_solution(5419207476815728456)
XLA Ops:
  0.0 1.1 %shard_map.118 = bf16[2,256,128]{2,1,0:T(8,128)(2,1)S(1)} custom-call(s32[1]{0:T(128)} %bitcast.half_ref, bf16[12,27,192]{2,1,0:T(8,128)(2,1)} %bitcast.25, bf16[12,27,192]{2,1,0:T(8,128)(2,1)} %bitcast.26), custom_call_target="tpu_custom_call" | custom-call | tf_op jit(solution)/shard_map/pallas_call | solution.py:57
  1.1 5.1 %collective-permute-start.2 = (bf16[2,256,128]{2,1,0:T(8,128)(2,1)S(1)}, bf16[2,256,128]{2,1,0:T(8,128)(2,1)S(1)}, u32[]{:S(2)}, u32[]{:S(2)}) collective-permute-start(bf16[2,256,128]{2,1,0:T(8,128)(2,1)S(1)} %shard_map.118), channel_id=1, source_target_pairs={{0,12},{1,13},{2,14},{3,15},{4,8},{5,9},{6,10},{7,11},{8,4},{9,5},... | collective-permute-start | bytes 393224 | tf_op jit(solution)/shard_map/ppermute | solution.py:26
  6.3 0.6 collective-permute-start
  6.9 1.1 %copy.17 = bf16[2,16,24,192]{3,1,2,0:T(8,128)(2,1)S(1)} copy(bf16[2,16,24,192]{3,2,1,0:T(8,128)(2,1)} %param.12) | data formatting | bytes 589824 | tf_op args[0]
  8.0 1.3 %collective-permute-start.7 = (bf16[2,16,24,192]{3,1,2,0:T(8,128)(2,1)S(1)}, bf16[2,16,24,192]{3,1,2,0:T(8,128)(2,1)S(1)}, u32[]{:S(2)}, u32[]{:S(2)}) collective-permute-start(bf16[2,16,24,192]{3,1,2,0:T(8,128)(2,1)S(1)} %copy.17), channel_id=1, source_target_pairs={{0,1},{1,2},{2,3},{3,4},{4,5},{5,6},{6,7},{7,8},{8,9},{9,10},{10,1... | collective-permute-start | bytes 884744 | tf_op jit(solution)/shard_map/ppermute | solution.py:31
  9.4 0.1 fusion.pick_ref
  9.5 1.1 %shard_map.119.wide_ref = bf16[16,192,256]{2,1,0:T(8,128)(2,1)S(1)} custom-call(bf16[27,16,192]{2,1,0:T(8,128)(2,1)} %bitcast.24), custom_call_target="tpu_custom_call" | custom-call | tf_op jit(solution)/shard_map/pallas_call | solution.py:98
  10.6 0.0 copy-start.3
  10.7 0.0 copy-start.4
  10.7 4.0 %collective-permute-done = bf16[2,256,128]{2,1,0:T(8,128)(2,1)S(1)} collective-permute-done((bf16[2,256,128]{2,1,0:T(8,128)(2,1)S(1)}, bf16[2,256,128]{2,1,0:T(8,128)(2,1)S(1)}, u32[]{:S(2)}, u32[]{:S(2)}) %collective-permute-start) | collective-permute-done | bytes 131104 | tf_op jit(solution)/shard_map/ppermute | solution.py:26
  14.7 2.7 %collective-permute-start.8 = (bf16[2,256,128]{2,1,0:T(8,128)(2,1)S(1)}, bf16[2,256,128]{2,1,0:T(8,128)(2,1)S(1)}, u32[]{:S(2)}, u32[]{:S(2)}) collective-permute-start(bf16[2,256,128]{2,1,0:T(8,128)(2,1)S(1)} %pad_maximum_fusion.1.rest_0_), channel_id=1, source_target_pairs={{0,2},{1,3},{2,0},{3,1},{4,6},{5,7},{6,4},{7,5},{8,10},{9,11},{10,... | collective-permute-start | bytes 393224 | tf_op jit(solution)/shard_map/ppermute | solution.py:26
  17.4 1.5 %collective-permute-start.3 = (bf16[2,256,128]{2,1,0:T(8,128)(2,1)S(1)}, bf16[2,256,128]{2,1,0:T(8,128)(2,1)S(1)}, u32[]{:S(2)}, u32[]{:S(2)}) collective-permute-start(bf16[2,256,128]{2,1,0:T(8,128)(2,1)S(1)} %pad_maximum_fusion.1.rest_0_), channel_id=1, source_target_pairs={{0,16},{16,0},{1,17},{17,1},{2,18},{18,2},{3,19},{19,3},{4,20},{20... | collective-permute-start | bytes 393224 | tf_op jit(solution)/shard_map/ppermute | solution.py:26
  19.0 0.1 collective-permute-start.5
  19.1 1.4 %collective-permute-start.9 = (bf16[2,256,128]{2,1,0:T(8,128)(2,1)S(1)}, bf16[2,256,128]{2,1,0:T(8,128)(2,1)S(1)}, u32[]{:S(2)}, u32[]{:S(2)}) collective-permute-start(bf16[2,256,128]{2,1,0:T(8,128)(2,1)S(1)} %pad_maximum_fusion.3.rest_1_), channel_id=1, source_target_pairs={{0,16},{16,0},{1,17},{17,1},{2,18},{18,2},{3,19},{19,3},{4,20},{20... | collective-permute-start | bytes 393224 | tf_op jit(solution)/shard_map/ppermute | solution.py:26
  20.5 2.8 %collective-permute-done.3.rest_4_ = bf16[2,256,128]{2,1,0:T(8,128)(2,1)S(1)} collective-permute-done((bf16[2,256,128]{2,1,0:T(8,128)(2,1)S(1)}, bf16[2,256,128]{2,1,0:T(8,128)(2,1)S(1)}, u32[]{:S(2)}, u32[]{:S(2)}) %collective-permute-start.3) | collective-permute-done | bytes 131104 | tf_op jit(solution)/shard_map/ppermute | solution.py:26
  23.3 0.5 collective-permute-start.4
  23.8 0.8 collective-permute-done.5.rest_3_
  24.6 0.1 collective-permute-done.9.rest_5_
  24.7 1.5 %collective-permute-start.6 = (bf16[2,256,128]{2,1,0:T(8,128)(2,1)S(1)}, bf16[2,256,128]{2,1,0:T(8,128)(2,1)}, u32[]{:S(2)}, u32[]{:S(2)}) collective-permute-start(bf16[2,256,128]{2,1,0:T(8,128)(2,1)S(1)} %collective-permute-done.5.rest_3_), channel_id=1, source_target_pairs={{0,16},{16,0},{1,17},{17,1},{2,18},{18,2},{3,19},{19,3},{4,20},{20... | collective-permute-start | bytes 393224 | tf_op jit(solution)/shard_map/ppermute | solution.py:26
  26.2 0.1 collective-permute-start.12
  26.3 2.0 %collective-permute-done.4.rest_6_ = bf16[2,256,128]{2,1,0:T(8,128)(2,1)S(1)} collective-permute-done((bf16[2,256,128]{2,1,0:T(8,128)(2,1)S(1)}, bf16[2,256,128]{2,1,0:T(8,128)(2,1)S(1)}, u32[]{:S(2)}, u32[]{:S(2)}) %collective-permute-start.4) | collective-permute-done | bytes 131104 | tf_op jit(solution)/shard_map/ppermute | solution.py:26
  28.3 2.3 %collective-permute-done.6.rest_7_ = bf16[2,256,128]{2,1,0:T(8,128)(2,1)} collective-permute-done((bf16[2,256,128]{2,1,0:T(8,128)(2,1)S(1)}, bf16[2,256,128]{2,1,0:T(8,128)(2,1)}, u32[]{:S(2)}, u32[]{:S(2)}) %collective-permute-start.6) | collective-permute-done | bytes 131104 | tf_op jit(solution)/shard_map/ppermute | solution.py:26
  30.6 0.5 collective-permute-start.11
  31.1 0.1 collective-permute-start.16
  31.2 1.4 %collective-permute-start.21 = (bf16[2,256,128]{2,1,0:T(8,128)(2,1)S(1)}, bf16[2,256,128]{2,1,0:T(8,128)(2,1)}, u32[]{:S(2)}, u32[]{:S(2)}) collective-permute-start(bf16[2,256,128]{2,1,0:T(8,128)(2,1)S(1)} %pad_maximum_fusion.2.refs_0_), channel_id=1, source_target_pairs={{0,16},{16,0},{1,17},{17,1},{2,18},{18,2},{3,19},{19,3},{4,20},{20... | collective-permute-start | bytes 393224 | tf_op jit(solution)/shard_map/ppermute | solution.py:26
  32.7 1.8 %collective-permute-start.20 = (bf16[2,256,128]{2,1,0:T(8,128)(2,1)S(1)}, bf16[2,256,128]{2,1,0:T(8,128)(2,1)}, u32[]{:S(2)}, u32[]{:S(2)}) collective-permute-start(bf16[2,256,128]{2,1,0:T(8,128)(2,1)S(1)} %pad_maximum_fusion.4.refs_1_), channel_id=1, source_target_pairs={{0,2},{1,3},{2,0},{3,1},{4,6},{5,7},{6,4},{7,5},{8,10},{9,11},{10,... | collective-permute-start | bytes 393224 | tf_op jit(solution)/shard_map/ppermute | solution.py:26
  34.5 0.3 collective-permute-start.19
  34.8 0.6 collective-permute-start.22
  35.4 1.8 %collective-permute-done.21.refs_4_ = bf16[2,256,128]{2,1,0:T(8,128)(2,1)} collective-permute-done((bf16[2,256,128]{2,1,0:T(8,128)(2,1)S(1)}, bf16[2,256,128]{2,1,0:T(8,128)(2,1)}, u32[]{:S(2)}, u32[]{:S(2)}) %collective-permute-start.21) | collective-permute-done | bytes 131104 | tf_op jit(solution)/shard_map/ppermute | solution.py:26
  37.2 1.8 %collective-permute-start.23 = (bf16[2,256,128]{2,1,0:T(8,128)(2,1)}, bf16[2,256,128]{2,1,0:T(8,128)(2,1)}, u32[]{:S(2)}, u32[]{:S(2)}) collective-permute-start(bf16[2,256,128]{2,1,0:T(8,128)(2,1)} %collective-permute-done.21.refs_4_), channel_id=1, source_target_pairs={{0,2},{1,3},{2,0},{3,1},{4,6},{5,7},{6,4},{7,5},{8,10},{9,11},{10,... | collective-permute-start | bytes 393224 | tf_op jit(solution)/shard_map/ppermute | solution.py:26
  39.0 0.2 collective-permute-done.20.refs_3_
  39.2 1.8 %collective-permute-start.24 = (bf16[2,256,128]{2,1,0:T(8,128)(2,1)}, bf16[2,256,128]{2,1,0:T(8,128)(2,1)}, u32[]{:S(2)}, u32[]{:S(2)}) collective-permute-start(bf16[2,256,128]{2,1,0:T(8,128)(2,1)} %collective-permute-done.20.refs_3_), channel_id=1, source_target_pairs={{0,16},{16,0},{1,17},{17,1},{2,18},{18,2},{3,19},{19,3},{4,20},{20... | collective-permute-start | bytes 393224 | tf_op jit(solution)/shard_map/ppermute | solution.py:26
  41.0 6.0 %shard_map.120 = (bf16[2,24,16,192]{3,2,1,0:T(8,128)(2,1)S(1)}, bf16[3,384,128]{2,1,0:T(8,128)(2,1)S(1)}) custom-call(s32[32]{0:T(128)S(1)} %copy-done.3, s32[1]{0:T(128)} %bitcast.10.first_ref, bf16[2,24,16,192]{3,2,1,0:T(8,128)(2,1)S(1)} %bitcast.16, bf16[2,24,16,192]{3,2,1,0:T(8,128)(2,1)} %bitcast.23, f32[1,192]{1,0:T(1,128)S(1)} %bitcast.20, ...), custom_call_target="tpu_custom_call" | custom-call | tf_op jit(solution)/shard_map/pallas_call | solution.py:498
  47.1 1.6 %shard_map.121.rest_0_ = bf16[41,128,128]{2,1,0:T(8,128)(2,1)S(1)} custom-call(bf16[2,256,128]{2,1,0:T(8,128)(2,1)} %copy-done.9, bf16[2,256,128]{2,1,0:T(8,128)(2,1)} %copy-done.10, bf16[2,256,128]{2,1,0:T(8,128)(2,1)} %collective-permute-done.19.refs_2_, bf16[2,256,128]{2,1,0:T(8,128)(2,1)} %collective-permute-done.20.refs_3_, ...), custom_call_target="tpu_custom_call" | custom-call | tf_op jit(solution)/shard_map/pallas_call | solution.py:178
  48.8 0.1 collective-permute-start.25
  48.8 2.7 %collective-permute-start.18 = (bf16[3,384,128]{2,1,0:T(8,128)(2,1)S(1)}, bf16[3,384,128]{2,1,0:T(8,128)(2,1)S(1)}, u32[]{:S(2)}, u32[]{:S(2)}) collective-permute-start(bf16[3,384,128]{2,1,0:T(8,128)(2,1)S(1)} %get-tuple-element.39), channel_id=1, source_target_pairs={{0,1},{1,2},{2,3},{3,4},{4,5},{5,6},{6,7},{7,8},{8,9},{9,10},{10,1... | collective-permute-start | bytes 884744 | tf_op jit(solution)/shard_map/ppermute | solution.py:31
  51.6 0.3 collective-permute-done.25.rest_1_
  51.9 2.4 %shard_map.122.summed_ref = f32[768,256]{1,0:T(8,128)S(1)} custom-call(s32[32]{0:T(128)S(1)} %copy-done.3, s32[1]{0:T(128)} %bitcast.10.first_ref, bf16[2,24,16,192]{3,2,1,0:T(8,128)(2,1)S(1)} %get-tuple-element.44.own_ref, bf16[2,24,16,192]{3,2,1,0:T(8,128)(2,1)S(1)} %bitcast.17, bf16[256,192]{1,0:T(8,128)(2,1)S(1)} %fusion.pick_ref, ...), custom_call_target="tpu_custom_call" | custom-call | tf_op jit(solution)/shard_map/pallas_call | solution.py:520
  54.4 3.9 %shard_map.123 = bf16[192,128]{1,0:T(8,128)(2,1)S(1)} custom-call(s32[32]{0:T(128)S(1)} %copy-done.3, s32[1]{0:T(128)} %bitcast.10.first_ref, bf16[3,384,128]{2,1,0:T(8,128)(2,1)S(1)} %collective-permute-done.18.rim_ref, f32[1,192]{1,0:T(1,128)S(1)} %bitcast.22, bf16[256,192]{1,0:T(8,128)(2,1)S(1)} %fusion.pick_ref, ...), custom_call_target="tpu_custom_call" | custom-call | tf_op jit(solution)/shard_map/pallas_call | solution.py:531
  58.3 6.7 %collective-permute-start.28 = (bf16[192,128]{1,0:T(8,128)(2,1)S(1)}, bf16[192,128]{1,0:T(8,128)(2,1)S(1)}, u32[]{:S(2)}, u32[]{:S(2)}) collective-permute-start(bf16[192,128]{1,0:T(8,128)(2,1)S(1)} %shard_map.123), channel_id=1, source_target_pairs={{0,12},{1,13},{2,14},{3,15},{4,8},{5,9},{6,10},{7,11},{8,4},{9,5},... | collective-permute-start | bytes 147464 | tf_op jit(solution)/shard_map/ppermute | solution.py:26
  65.0 0.6 collective-permute-start.27
  65.6 0.1 collective-permute-start.26
  65.8 1.9 %collective-permute-done.28 = bf16[192,128]{1,0:T(8,128)(2,1)S(1)} collective-permute-done((bf16[192,128]{1,0:T(8,128)(2,1)S(1)}, bf16[192,128]{1,0:T(8,128)(2,1)S(1)}, u32[]{:S(2)}, u32[]{:S(2)}) %collective-permute-start.28) | collective-permute-done | bytes 49184 | tf_op jit(solution)/shard_map/ppermute | solution.py:26
  67.7 2.9 %collective-permute-done.27 = bf16[192,128]{1,0:T(8,128)(2,1)S(1)} collective-permute-done((bf16[192,128]{1,0:T(8,128)(2,1)S(1)}, bf16[192,128]{1,0:T(8,128)(2,1)S(1)}, u32[]{:S(2)}, u32[]{:S(2)}) %collective-permute-start.27) | collective-permute-done | bytes 49184 | tf_op jit(solution)/shard_map/ppermute | solution.py:26
  70.6 0.4 collective-permute-start.29
  70.9 5.4 %collective-permute-done.29.rest_1_ = bf16[768,128]{1,0:T(8,128)(2,1)S(1)} collective-permute-done((bf16[768,128]{1,0:T(8,128)(2,1)S(1)}, bf16[768,128]{1,0:T(8,128)(2,1)S(1)}, u32[]{:S(2)}, u32[]{:S(2)}) %collective-permute-start.29) | collective-permute-done | bytes 196640 | tf_op jit(solution)/shard_map/ppermute | solution.py:26
  76.3 1.4 %collective-permute-done.31.rest_3_ = bf16[768,128]{1,0:T(8,128)(2,1)S(1)} collective-permute-done((bf16[768,128]{1,0:T(8,128)(2,1)S(1)}, bf16[768,128]{1,0:T(8,128)(2,1)S(1)}, u32[]{:S(2)}, u32[]{:S(2)}) %collective-permute-start.31) | collective-permute-done | bytes 196640 | tf_op jit(solution)/shard_map/ppermute | solution.py:26
  77.7 3.2 %shard_map.124 = bf16[192,3072]{1,0:T(8,128)(2,1)} custom-call(s32[3,192]{1,0:T(4,128)S(1)} %pad_add_fusion.place_ref, bf16[64,3072]{1,0:T(8,128)(2,1)S(1)} %copy-done, f32[1,3072]{1,0:T(1,128)S(1)} %bitcast.18, f32[1,3072]{1,0:T(1,128)S(1)} %bitcast.19, bf16[768,128]{1,0:T(8,128)(2,1)S(1)} %pad_maximum_fusion.rest_0_, ...), custom_call_target="tpu_custom_call" | custom-call | tf_op jit(solution)/shard_map/pallas_call | solution.py:553
  (88 shorter events, 0.4 us)
Async XLA Ops:
  1.1 17.8 %collective-permute-start.2 = (bf16[2,256,128]{2,1,0:T(8,128)(2,1)S(1)}, bf16[2,256,128]{2,1,0:T(8,128)(2,1)S(1)}, u32[]{:S(2)}, u32[]{:S(2)}) collective-permute-start(bf16[2,256,128]{2,1,0:T(8,128)(2,1)S(1)} %shard_map.118), channel_id=1, source_target_pairs={{0,12},{1,13},{2,14},{3,15},{4,8},{5,9},{6,10},{7,11},{8,4},{9,5},... | collective-permute-start | bytes 393224 | tf_op jit(solution)/shard_map/ppermute | solution.py:26
  6.3 12.7 %collective-permute-start.1 = (bf16[2,256,128]{2,1,0:T(8,128)(2,1)S(1)}, bf16[2,256,128]{2,1,0:T(8,128)(2,1)S(1)}, u32[]{:S(2)}, u32[]{:S(2)}) collective-permute-start(bf16[2,256,128]{2,1,0:T(8,128)(2,1)S(1)} %shard_map.118), channel_id=1, source_target_pairs={{0,8},{1,9},{2,10},{3,11},{4,12},{5,13},{6,14},{7,15},{8,0},{9,1},... | collective-permute-start | bytes 393224 | tf_op jit(solution)/shard_map/ppermute | solution.py:26
  6.3 8.4 %collective-permute-start = (bf16[2,256,128]{2,1,0:T(8,128)(2,1)S(1)}, bf16[2,256,128]{2,1,0:T(8,128)(2,1)S(1)}, u32[]{:S(2)}, u32[]{:S(2)}) collective-permute-start(bf16[2,256,128]{2,1,0:T(8,128)(2,1)S(1)} %shard_map.118), channel_id=1, source_target_pairs={{0,4},{1,5},{2,6},{3,7},{4,0},{5,1},{6,2},{7,3},{8,12},{9,13},{10,... | collective-permute-start | bytes 393224 | tf_op jit(solution)/shard_map/ppermute | solution.py:26
  8.0 18.2 %collective-permute-start.7 = (bf16[2,16,24,192]{3,1,2,0:T(8,128)(2,1)S(1)}, bf16[2,16,24,192]{3,1,2,0:T(8,128)(2,1)S(1)}, u32[]{:S(2)}, u32[]{:S(2)}) collective-permute-start(bf16[2,16,24,192]{3,1,2,0:T(8,128)(2,1)S(1)} %copy.17), channel_id=1, source_target_pairs={{0,1},{1,2},{2,3},{3,4},{4,5},{5,6},{6,7},{7,8},{8,9},{9,10},{10,1... | collective-permute-start | bytes 884744 | tf_op jit(solution)/shard_map/ppermute | solution.py:31
  10.6 30.3 %copy-start.3 = (s32[32]{0:T(128)S(1)}, s32[32]{0:T(128)}, u32[]{:S(2)}) copy-start(s32[32]{0:T(128)} %clips_ref.5) | copy-start | bytes 388
  10.7 30.3 %copy-start.4 = (f32[192]{0:T(256)S(1)}, f32[192]{0:T(256)}, u32[]{:S(2)}) copy-start(f32[192]{0:T(256)} %param.14) | copy-start | bytes 2308
  10.7 30.3 %copy-start.5 = (f32[192]{0:T(256)S(1)}, f32[192]{0:T(256)}, u32[]{:S(2)}) copy-start(f32[192]{0:T(256)} %param.16) | copy-start | bytes 2308
  14.7 26.2 %copy-start.7 = (bf16[2,256,128]{2,1,0:T(8,128)(2,1)}, bf16[2,256,128]{2,1,0:T(8,128)(2,1)S(1)}, u32[]{:S(2)}) copy-start(bf16[2,256,128]{2,1,0:T(8,128)(2,1)S(1)} %pad_maximum_fusion.1.rest_0_) | copy-start | bytes 393220
  14.7 9.0 %collective-permute-start.8 = (bf16[2,256,128]{2,1,0:T(8,128)(2,1)S(1)}, bf16[2,256,128]{2,1,0:T(8,128)(2,1)S(1)}, u32[]{:S(2)}, u32[]{:S(2)}) collective-permute-start(bf16[2,256,128]{2,1,0:T(8,128)(2,1)S(1)} %pad_maximum_fusion.1.rest_0_), channel_id=1, source_target_pairs={{0,2},{1,3},{2,0},{3,1},{4,6},{5,7},{6,4},{7,5},{8,10},{9,11},{10,... | collective-permute-start | bytes 393224 | tf_op jit(solution)/shard_map/ppermute | solution.py:26
  17.4 5.8 %collective-permute-start.3 = (bf16[2,256,128]{2,1,0:T(8,128)(2,1)S(1)}, bf16[2,256,128]{2,1,0:T(8,128)(2,1)S(1)}, u32[]{:S(2)}, u32[]{:S(2)}) collective-permute-start(bf16[2,256,128]{2,1,0:T(8,128)(2,1)S(1)} %pad_maximum_fusion.1.rest_0_), channel_id=1, source_target_pairs={{0,16},{16,0},{1,17},{17,1},{2,18},{18,2},{3,19},{19,3},{4,20},{20... | collective-permute-start | bytes 393224 | tf_op jit(solution)/shard_map/ppermute | solution.py:26
  19.0 22.0 %copy-start.8 = (bf16[2,256,128]{2,1,0:T(8,128)(2,1)}, bf16[2,256,128]{2,1,0:T(8,128)(2,1)S(1)}, u32[]{:S(2)}) copy-start(bf16[2,256,128]{2,1,0:T(8,128)(2,1)S(1)} %pad_maximum_fusion.3.rest_1_) | copy-start | bytes 393220
  19.0 5.6 %collective-permute-start.5 = (bf16[2,256,128]{2,1,0:T(8,128)(2,1)S(1)}, bf16[2,256,128]{2,1,0:T(8,128)(2,1)S(1)}, u32[]{:S(2)}, u32[]{:S(2)}) collective-permute-start(bf16[2,256,128]{2,1,0:T(8,128)(2,1)S(1)} %pad_maximum_fusion.3.rest_1_), channel_id=1, source_target_pairs={{0,2},{1,3},{2,0},{3,1},{4,6},{5,7},{6,4},{7,5},{8,10},{9,11},{10,... | collective-permute-start | bytes 393224 | tf_op jit(solution)/shard_map/ppermute | solution.py:26
  19.1 5.5 %collective-permute-start.9 = (bf16[2,256,128]{2,1,0:T(8,128)(2,1)S(1)}, bf16[2,256,128]{2,1,0:T(8,128)(2,1)S(1)}, u32[]{:S(2)}, u32[]{:S(2)}) collective-permute-start(bf16[2,256,128]{2,1,0:T(8,128)(2,1)S(1)} %pad_maximum_fusion.3.rest_1_), channel_id=1, source_target_pairs={{0,16},{16,0},{1,17},{17,1},{2,18},{18,2},{3,19},{19,3},{4,20},{20... | collective-permute-start | bytes 393224 | tf_op jit(solution)/shard_map/ppermute | solution.py:26
  23.3 17.7 %copy-start.13 = (bf16[2,256,128]{2,1,0:T(8,128)(2,1)}, bf16[2,256,128]{2,1,0:T(8,128)(2,1)S(1)}, u32[]{:S(2)}) copy-start(bf16[2,256,128]{2,1,0:T(8,128)(2,1)S(1)} %collective-permute-done.3.rest_4_) | copy-start | bytes 393220
  23.3 5.0 %collective-permute-start.4 = (bf16[2,256,128]{2,1,0:T(8,128)(2,1)S(1)}, bf16[2,256,128]{2,1,0:T(8,128)(2,1)S(1)}, u32[]{:S(2)}, u32[]{:S(2)}) collective-permute-start(bf16[2,256,128]{2,1,0:T(8,128)(2,1)S(1)} %collective-permute-done.3.rest_4_), channel_id=1, source_target_pairs={{0,2},{1,3},{2,0},{3,1},{4,6},{5,7},{6,4},{7,5},{8,10},{9,11},{10,... | collective-permute-start | bytes 393224 | tf_op jit(solution)/shard_map/ppermute | solution.py:26
  23.8 17.2 %copy-start.12 = (bf16[2,256,128]{2,1,0:T(8,128)(2,1)}, bf16[2,256,128]{2,1,0:T(8,128)(2,1)S(1)}, u32[]{:S(2)}) copy-start(bf16[2,256,128]{2,1,0:T(8,128)(2,1)S(1)} %collective-permute-done.8.rest_2_) | copy-start | bytes 393220
  23.8 7.4 %collective-permute-start.14 = (bf16[2,256,128]{2,1,0:T(8,128)(2,1)S(1)}, bf16[2,256,128]{2,1,0:T(8,128)(2,1)S(1)}, u32[]{:S(2)}, u32[]{:S(2)}) collective-permute-start(bf16[2,256,128]{2,1,0:T(8,128)(2,1)S(1)} %collective-permute-done.3.rest_4_), channel_id=1, source_target_pairs={{0,1},{1,0},{2,3},{3,2},{4,5},{5,4},{6,7},{7,6},{8,9},{9,8},{10,11... | collective-permute-start | bytes 393224 | tf_op jit(solution)/shard_map/ppermute | solution.py:26
  24.6 16.4 %copy-start.14 = (bf16[2,256,128]{2,1,0:T(8,128)(2,1)}, bf16[2,256,128]{2,1,0:T(8,128)(2,1)S(1)}, u32[]{:S(2)}) copy-start(bf16[2,256,128]{2,1,0:T(8,128)(2,1)S(1)} %collective-permute-done.5.rest_3_) | copy-start | bytes 393220
  24.6 8.1 %collective-permute-start.13 = (bf16[2,256,128]{2,1,0:T(8,128)(2,1)S(1)}, bf16[2,256,128]{2,1,0:T(8,128)(2,1)S(1)}, u32[]{:S(2)}, u32[]{:S(2)}) collective-permute-start(bf16[2,256,128]{2,1,0:T(8,128)(2,1)S(1)} %collective-permute-done.5.rest_3_), channel_id=1, source_target_pairs={{0,1},{1,0},{2,3},{3,2},{4,5},{5,4},{6,7},{7,6},{8,9},{9,8},{10,11... | collective-permute-start | bytes 393224 | tf_op jit(solution)/shard_map/ppermute | solution.py:26
  24.7 16.3 %copy-start.15 = (bf16[2,256,128]{2,1,0:T(8,128)(2,1)}, bf16[2,256,128]{2,1,0:T(8,128)(2,1)S(1)}, u32[]{:S(2)}) copy-start(bf16[2,256,128]{2,1,0:T(8,128)(2,1)S(1)} %collective-permute-done.9.rest_5_) | copy-start | bytes 393220
  24.7 6.0 %collective-permute-start.6 = (bf16[2,256,128]{2,1,0:T(8,128)(2,1)S(1)}, bf16[2,256,128]{2,1,0:T(8,128)(2,1)}, u32[]{:S(2)}, u32[]{:S(2)}) collective-permute-start(bf16[2,256,128]{2,1,0:T(8,128)(2,1)S(1)} %collective-permute-done.5.rest_3_), channel_id=1, source_target_pairs={{0,16},{16,0},{1,17},{17,1},{2,18},{18,2},{3,19},{19,3},{4,20},{20... | collective-permute-start | bytes 393224 | tf_op jit(solution)/shard_map/ppermute | solution.py:26
  26.2 14.8 %copy-start.11 = (bf16[2,16,24,192]{3,1,2,0:T(8,128)(2,1)}, bf16[2,16,24,192]{3,1,2,0:T(8,128)(2,1)S(1)}, u32[]{:S(2)}) copy-start(bf16[2,16,24,192]{3,1,2,0:T(8,128)(2,1)S(1)} %collective-permute-done.7) | copy-start | bytes 884740
  26.2 4.4 %collective-permute-start.12 = (bf16[2,256,128]{2,1,0:T(8,128)(2,1)S(1)}, bf16[2,256,128]{2,1,0:T(8,128)(2,1)S(1)}, u32[]{:S(2)}, u32[]{:S(2)}) collective-permute-start(bf16[2,256,128]{2,1,0:T(8,128)(2,1)S(1)} %collective-permute-done.8.rest_2_), channel_id=1, source_target_pairs={{0,1},{1,0},{2,3},{3,2},{4,5},{5,4},{6,7},{7,6},{8,9},{9,8},{10,11... | collective-permute-start | bytes 393224 | tf_op jit(solution)/shard_map/ppermute | solution.py:26
  28.2 10.9 %copy-start.16 = (bf16[2,256,128]{2,1,0:T(8,128)(2,1)}, bf16[2,256,128]{2,1,0:T(8,128)(2,1)S(1)}, u32[]{:S(2)}) copy-start(bf16[2,256,128]{2,1,0:T(8,128)(2,1)S(1)} %collective-permute-done.4.rest_6_) | copy-start | bytes 393220
  28.2 3.0 %collective-permute-start.15 = (bf16[2,256,128]{2,1,0:T(8,128)(2,1)S(1)}, bf16[2,256,128]{2,1,0:T(8,128)(2,1)S(1)}, u32[]{:S(2)}, u32[]{:S(2)}) collective-permute-start(bf16[2,256,128]{2,1,0:T(8,128)(2,1)S(1)} %collective-permute-done.9.rest_5_), channel_id=1, source_target_pairs={{0,1},{1,0},{2,3},{3,2},{4,5},{5,4},{6,7},{7,6},{8,9},{9,8},{10,11... | collective-permute-start | bytes 393224 | tf_op jit(solution)/shard_map/ppermute | solution.py:26
  28.3 18.8 %copy-start.9 = (bf16[2,256,128]{2,1,0:T(8,128)(2,1)}, bf16[2,256,128]{2,1,0:T(8,128)(2,1)S(1)}, u32[]{:S(2)}) copy-start(bf16[2,256,128]{2,1,0:T(8,128)(2,1)S(1)} %pad_maximum_fusion.2.refs_0_) | copy-start | bytes 393220
  28.3 18.8 %copy-start.10 = (bf16[2,256,128]{2,1,0:T(8,128)(2,1)}, bf16[2,256,128]{2,1,0:T(8,128)(2,1)S(1)}, u32[]{:S(2)}) copy-start(bf16[2,256,128]{2,1,0:T(8,128)(2,1)S(1)} %pad_maximum_fusion.4.refs_1_) | copy-start | bytes 393220
  30.6 3.9 %collective-permute-start.10 = (bf16[2,256,128]{2,1,0:T(8,128)(2,1)S(1)}, bf16[2,256,128]{2,1,0:T(8,128)(2,1)S(1)}, u32[]{:S(2)}, u32[]{:S(2)}) collective-permute-start(bf16[2,256,128]{2,1,0:T(8,128)(2,1)S(1)} %pad_maximum_fusion.1.rest_0_), channel_id=1, source_target_pairs={{0,1},{1,0},{2,3},{3,2},{4,5},{5,4},{6,7},{7,6},{8,9},{9,8},{10,11... | collective-permute-start | bytes 393224 | tf_op jit(solution)/shard_map/ppermute | solution.py:26
  30.6 3.9 %collective-permute-start.11 = (bf16[2,256,128]{2,1,0:T(8,128)(2,1)S(1)}, bf16[2,256,128]{2,1,0:T(8,128)(2,1)S(1)}, u32[]{:S(2)}, u32[]{:S(2)}) collective-permute-start(bf16[2,256,128]{2,1,0:T(8,128)(2,1)S(1)} %pad_maximum_fusion.3.rest_1_), channel_id=1, source_target_pairs={{0,1},{1,0},{2,3},{3,2},{4,5},{5,4},{6,7},{7,6},{8,9},{9,8},{10,11... | collective-permute-start | bytes 393224 | tf_op jit(solution)/shard_map/ppermute | solution.py:26
  31.1 3.7 %collective-permute-start.16 = (bf16[2,256,128]{2,1,0:T(8,128)(2,1)S(1)}, bf16[2,256,128]{2,1,0:T(8,128)(2,1)S(1)}, u32[]{:S(2)}, u32[]{:S(2)}) collective-permute-start(bf16[2,256,128]{2,1,0:T(8,128)(2,1)S(1)} %collective-permute-done.4.rest_6_), channel_id=1, source_target_pairs={{0,1},{1,0},{2,3},{3,2},{4,5},{5,4},{6,7},{7,6},{8,9},{9,8},{10,11... | collective-permute-start | bytes 393224 | tf_op jit(solution)/shard_map/ppermute | solution.py:26
  31.2 5.9 %collective-permute-start.21 = (bf16[2,256,128]{2,1,0:T(8,128)(2,1)S(1)}, bf16[2,256,128]{2,1,0:T(8,128)(2,1)}, u32[]{:S(2)}, u32[]{:S(2)}) collective-permute-start(bf16[2,256,128]{2,1,0:T(8,128)(2,1)S(1)} %pad_maximum_fusion.2.refs_0_), channel_id=1, source_target_pairs={{0,16},{16,0},{1,17},{17,1},{2,18},{18,2},{3,19},{19,3},{4,20},{20... | collective-permute-start | bytes 393224 | tf_op jit(solution)/shard_map/ppermute | solution.py:26
  32.7 6.4 %collective-permute-start.20 = (bf16[2,256,128]{2,1,0:T(8,128)(2,1)S(1)}, bf16[2,256,128]{2,1,0:T(8,128)(2,1)}, u32[]{:S(2)}, u32[]{:S(2)}) collective-permute-start(bf16[2,256,128]{2,1,0:T(8,128)(2,1)S(1)} %pad_maximum_fusion.4.refs_1_), channel_id=1, source_target_pairs={{0,2},{1,3},{2,0},{3,1},{4,6},{5,7},{6,4},{7,5},{8,10},{9,11},{10,... | collective-permute-start | bytes 393224 | tf_op jit(solution)/shard_map/ppermute | solution.py:26
  34.5 6.4 %collective-permute-start.17 = (bf16[2,256,128]{2,1,0:T(8,128)(2,1)}, bf16[2,256,128]{2,1,0:T(8,128)(2,1)}, u32[]{:S(2)}, u32[]{:S(2)}) collective-permute-start(bf16[2,256,128]{2,1,0:T(8,128)(2,1)} %collective-permute-done.6.rest_7_), channel_id=1, source_target_pairs={{0,1},{1,0},{2,3},{3,2},{4,5},{5,4},{6,7},{7,6},{8,9},{9,8},{10,11... | collective-permute-start | bytes 393224 | tf_op jit(solution)/shard_map/ppermute | solution.py:26
  34.5 12.5 %collective-permute-start.19 = (bf16[2,256,128]{2,1,0:T(8,128)(2,1)S(1)}, bf16[2,256,128]{2,1,0:T(8,128)(2,1)}, u32[]{:S(2)}, u32[]{:S(2)}) collective-permute-start(bf16[2,256,128]{2,1,0:T(8,128)(2,1)S(1)} %pad_maximum_fusion.2.refs_0_), channel_id=1, source_target_pairs={{0,2},{1,3},{2,0},{3,1},{4,6},{5,7},{6,4},{7,5},{8,10},{9,11},{10,... | collective-permute-start | bytes 393224 | tf_op jit(solution)/shard_map/ppermute | solution.py:26
  34.8 12.3 %collective-permute-start.22 = (bf16[2,256,128]{2,1,0:T(8,128)(2,1)S(1)}, bf16[2,256,128]{2,1,0:T(8,128)(2,1)}, u32[]{:S(2)}, u32[]{:S(2)}) collective-permute-start(bf16[2,256,128]{2,1,0:T(8,128)(2,1)S(1)} %pad_maximum_fusion.4.refs_1_), channel_id=1, source_target_pairs={{0,16},{16,0},{1,17},{17,1},{2,18},{18,2},{3,19},{19,3},{4,20},{20... | collective-permute-start | bytes 393224 | tf_op jit(solution)/shard_map/ppermute | solution.py:26
  37.2 9.9 %collective-permute-start.23 = (bf16[2,256,128]{2,1,0:T(8,128)(2,1)}, bf16[2,256,128]{2,1,0:T(8,128)(2,1)}, u32[]{:S(2)}, u32[]{:S(2)}) collective-permute-start(bf16[2,256,128]{2,1,0:T(8,128)(2,1)} %collective-permute-done.21.refs_4_), channel_id=1, source_target_pairs={{0,2},{1,3},{2,0},{3,1},{4,6},{5,7},{6,4},{7,5},{8,10},{9,11},{10,... | collective-permute-start | bytes 393224 | tf_op jit(solution)/shard_map/ppermute | solution.py:26
  39.2 7.9 %collective-permute-start.24 = (bf16[2,256,128]{2,1,0:T(8,128)(2,1)}, bf16[2,256,128]{2,1,0:T(8,128)(2,1)}, u32[]{:S(2)}, u32[]{:S(2)}) collective-permute-start(bf16[2,256,128]{2,1,0:T(8,128)(2,1)} %collective-permute-done.20.refs_3_), channel_id=1, source_target_pairs={{0,16},{16,0},{1,17},{17,1},{2,18},{18,2},{3,19},{19,3},{4,20},{20... | collective-permute-start | bytes 393224 | tf_op jit(solution)/shard_map/ppermute | solution.py:26
  48.8 3.1 %collective-permute-start.25 = (bf16[41,128,128]{2,1,0:T(8,128)(2,1)S(1)}, bf16[41,128,128]{2,1,0:T(8,128)(2,1)S(1)}, u32[]{:S(2)}, u32[]{:S(2)}) collective-permute-start(bf16[41,128,128]{2,1,0:T(8,128)(2,1)S(1)} %shard_map.121.rest_0_), channel_id=1, source_target_pairs={{0,1},{1,0},{2,3},{3,2},{4,5},{5,4},{6,7},{7,6},{8,9},{9,8},{10,11... | collective-permute-start | bytes 4030472 | tf_op jit(solution)/shard_map/ppermute | solution.py:26
  48.8 5.5 %collective-permute-start.18 = (bf16[3,384,128]{2,1,0:T(8,128)(2,1)S(1)}, bf16[3,384,128]{2,1,0:T(8,128)(2,1)S(1)}, u32[]{:S(2)}, u32[]{:S(2)}) collective-permute-start(bf16[3,384,128]{2,1,0:T(8,128)(2,1)S(1)} %get-tuple-element.39), channel_id=1, source_target_pairs={{0,1},{1,2},{2,3},{3,4},{4,5},{5,6},{6,7},{7,8},{8,9},{9,10},{10,1... | collective-permute-start | bytes 884744 | tf_op jit(solution)/shard_map/ppermute | solution.py:31
  54.4 23.4 %copy-start = (bf16[64,3072]{1,0:T(8,128)(2,1)S(1)}, bf16[64,3072]{1,0:T(8,128)(2,1)}, u32[]{:S(2)}) copy-start(bf16[64,3072]{1,0:T(8,128)(2,1)} %embed_ref.1) | copy-start | bytes 1179652
  54.4 23.4 %copy-start.1 = (f32[3072]{0:T(1024)S(1)}, f32[3072]{0:T(1024)}, u32[]{:S(2)}) copy-start(f32[3072]{0:T(1024)} %param.22) | copy-start | bytes 36868
  54.4 23.4 %copy-start.2 = (f32[3072]{0:T(1024)S(1)}, f32[3072]{0:T(1024)}, u32[]{:S(2)}) copy-start(f32[3072]{0:T(1024)} %param.21) | copy-start | bytes 36868
  58.3 9.4 %collective-permute-start.28 = (bf16[192,128]{1,0:T(8,128)(2,1)S(1)}, bf16[192,128]{1,0:T(8,128)(2,1)S(1)}, u32[]{:S(2)}, u32[]{:S(2)}) collective-permute-start(bf16[192,128]{1,0:T(8,128)(2,1)S(1)} %shard_map.123), channel_id=1, source_target_pairs={{0,12},{1,13},{2,14},{3,15},{4,8},{5,9},{6,10},{7,11},{8,4},{9,5},... | collective-permute-start | bytes 147464 | tf_op jit(solution)/shard_map/ppermute | solution.py:26
  65.0 5.5 %collective-permute-start.27 = (bf16[192,128]{1,0:T(8,128)(2,1)S(1)}, bf16[192,128]{1,0:T(8,128)(2,1)S(1)}, u32[]{:S(2)}, u32[]{:S(2)}) collective-permute-start(bf16[192,128]{1,0:T(8,128)(2,1)S(1)} %shard_map.123), channel_id=1, source_target_pairs={{0,8},{1,9},{2,10},{3,11},{4,12},{5,13},{6,14},{7,15},{8,0},{9,1},... | collective-permute-start | bytes 147464 | tf_op jit(solution)/shard_map/ppermute | solution.py:26
  65.6 4.9 %collective-permute-start.26 = (bf16[192,128]{1,0:T(8,128)(2,1)S(1)}, bf16[192,128]{1,0:T(8,128)(2,1)S(1)}, u32[]{:S(2)}, u32[]{:S(2)}) collective-permute-start(bf16[192,128]{1,0:T(8,128)(2,1)S(1)} %shard_map.123), channel_id=1, source_target_pairs={{0,4},{1,5},{2,6},{3,7},{4,0},{5,1},{6,2},{7,3},{8,12},{9,13},{10,... | collective-permute-start | bytes 147464 | tf_op jit(solution)/shard_map/ppermute | solution.py:26
  70.6 5.7 %collective-permute-start.29 = (bf16[768,128]{1,0:T(8,128)(2,1)S(1)}, bf16[768,128]{1,0:T(8,128)(2,1)S(1)}, u32[]{:S(2)}, u32[]{:S(2)}) collective-permute-start(bf16[768,128]{1,0:T(8,128)(2,1)S(1)} %pad_maximum_fusion.rest_0_), channel_id=1, source_target_pairs={{0,2},{1,3},{2,0},{3,1},{4,6},{5,7},{6,4},{7,5},{8,10},{9,11},{10,... | collective-permute-start | bytes 589832 | tf_op jit(solution)/shard_map/ppermute | solution.py:26
  70.9 5.4 %collective-permute-start.30 = (bf16[768,128]{1,0:T(8,128)(2,1)S(1)}, bf16[768,128]{1,0:T(8,128)(2,1)S(1)}, u32[]{:S(2)}, u32[]{:S(2)}) collective-permute-start(bf16[768,128]{1,0:T(8,128)(2,1)S(1)} %pad_maximum_fusion.rest_0_), channel_id=1, source_target_pairs={{0,1},{1,0},{2,3},{3,2},{4,5},{5,4},{6,7},{7,6},{8,9},{9,8},{10,11... | collective-permute-start | bytes 589832 | tf_op jit(solution)/shard_map/ppermute | solution.py:26
  76.3 1.4 %collective-permute-start.31 = (bf16[768,128]{1,0:T(8,128)(2,1)S(1)}, bf16[768,128]{1,0:T(8,128)(2,1)S(1)}, u32[]{:S(2)}, u32[]{:S(2)}) collective-permute-start(bf16[768,128]{1,0:T(8,128)(2,1)S(1)} %collective-permute-done.29.rest_1_), channel_id=1, source_target_pairs={{0,1},{1,0},{2,3},{3,2},{4,5},{5,4},{6,7},{7,6},{8,9},{9,8},{10,11... | collective-permute-start | bytes 589832 | tf_op jit(solution)/shard_map/ppermute | solution.py:26
  (9 other events, 59.3 us)
